TPU v7x, 32 devices: a whole 2x2x4 slice. The times are simulated.
32 devices in a mesh: grp: 8 (over y, x, core), lag: 4 (over z).
Axes of the slice: x: 2, y: 2, z: 4, core: 2. Of those that a mesh axis runs over, the one named last changes fastest.
Arguments:
- weights: bfloat16 [3, 16384, 256], P(None, 'lag'), may hold values from -0.125 to 0.125
- history: bfloat16 [128, 2048, 256], P(('grp', 'lag')), may hold values from -6 to 6
- send_patch: int32 [256, 2], P(('grp', 'lag')), may hold values from 0 to 3
- send_lag: int32 [256, 2], P(('grp', 'lag')), may hold values from 0 to 56
- send_class: int32 [256, 2], P(('grp', 'lag')), may hold values from 0 to 2
- recv_target: int32 [256, 2], P(('grp', 'lag')), may hold values from 0 to 3
- local_src: int32 [1536], P(('grp', 'lag')), may hold values from 0 to 3
- local_lag: int32 [1536], P(('grp', 'lag')), may hold values from 0 to 56
- local_class: int32 [1536], P(('grp', 'lag')), may hold values from 0 to 2
- local_target: int32 [1536], P(('grp', 'lag')), may hold values from 0 to 3
- inverse_blocks: bfloat16 [128, 256, 256], P(('grp', 'lag')), may hold values from -0.375 to 0.375
- incident: bfloat16 [128, 256, 256], P(('grp', 'lag')), may hold values from -6 to 6
Outputs:
- density: bfloat16 [128, 256, 256], P(('grp', 'lag'))
All inputs are finite; a program needn't handle non-finite values.
Results may differ from a plain program's by a relative error of at most 0.0049.
Values may be sent and summed in bfloat16 or wider, within the bound.
No kernel may reach another device: no remote copies, remote signals or barrier semaphores. Data moves between devices by JAX's collectives and lax.ppermute only.
A program may use at most 256 MiB of HBM per device.

v0:
```python
import jax
import jax.numpy as jnp
from jax import lax
from jax.sharding import PartitionSpec as P


def pair_product(gathered, source, key, klass, offset):
    panel_count = gathered.shape[2]
    height = source.shape[1]
    window = lax.dynamic_slice(
        gathered, (klass, offset * panel_count, jnp.int32(0)), (1, height, panel_count)
    )[0]
    rows = lax.dynamic_index_in_dim(source, key, 0, keepdims=False)
    return lax.dot_general(
        window, rows, (((0,), (0,)), ((), ())), preferred_element_type=jnp.float32
    )


def block_width():
    return 8


def block_products(gathered, source, block_keys, block_classes, block_offsets):
    outputs = [
        pair_product(gathered, source, block_keys[i], block_classes[i], block_offsets[i])
        for i in range(block_keys.shape[0])
    ]
    return jnp.stack(outputs, 0)


def compute_pairs(gathered, source, keys, classes, offsets):
    total = keys.shape[0]
    width = block_width()

    def compute_step(carry, inputs):
        block_keys, block_classes, block_offsets = inputs
        return (carry, block_products(gathered, source, block_keys, block_classes, block_offsets))

    _, result = lax.scan(
        compute_step,
        jnp.int32(0),
        (keys.reshape(-1, width), classes.reshape(-1, width), offsets.reshape(-1, width)),
    )
    return result.reshape(total, result.shape[2], result.shape[3])


def collect(owned, targets, contrib):
    select = (jnp.arange(owned, dtype=jnp.int32)[:, None] == targets[None, :]).astype(jnp.float32)
    return jnp.einsum("ts,spc->tpc", select, contrib, precision=lax.Precision.HIGHEST)


def accumulate_pairs(gathered, source, keys, classes, offsets, targets, initial):
    width = block_width()
    owned = initial.shape[0]

    def accumulate_step(carry, inputs):
        block_keys, block_classes, block_offsets, block_targets = inputs
        contrib = block_products(gathered, source, block_keys, block_classes, block_offsets)
        return (carry + collect(owned, block_targets, contrib), None)

    result, _ = lax.scan(
        accumulate_step,
        initial,
        (
            keys.reshape(-1, width),
            classes.reshape(-1, width),
            offsets.reshape(-1, width),
            targets.reshape(-1, width),
        ),
    )
    return result


def per_device(
    weights,
    history,
    send_patch,
    send_lag,
    send_class,
    recv_target,
    local_src,
    local_lag,
    local_class,
    local_target,
    inverse_blocks,
    incident,
):
    owned = history.shape[0]
    panel_count = weights.shape[2]
    excite = history.shape[2]
    peers = send_patch.shape[0]
    slots = send_patch.shape[1]
    gathered = lax.all_gather(weights, "lag", axis=1, tiled=True)
    served_rows = history[send_patch]
    hist_rows = lax.all_to_all(served_rows, "grp", split_axis=0, concat_axis=0, tiled=True)
    offsets = lax.all_to_all(send_lag, "grp", split_axis=0, concat_axis=0, tiled=True)
    classes = lax.all_to_all(send_class, "grp", split_axis=0, concat_axis=0, tiled=True)
    groups = offsets.shape[0]
    count = offsets.shape[1]
    flat_rows = hist_rows.reshape(groups * count, hist_rows.shape[2], hist_rows.shape[3])
    contrib = compute_pairs(
        gathered,
        flat_rows,
        jnp.arange(groups * count, dtype=jnp.int32),
        classes.reshape(groups * count),
        offsets.reshape(groups * count),
    )
    remote = contrib.reshape(groups, count, panel_count, excite)
    near_start = jnp.zeros((owned, panel_count, excite), jnp.float32)
    near_sum = accumulate_pairs(
        gathered, history, local_src, local_class, local_lag, local_target, near_start
    )
    near_sum = near_sum + collect(
        owned,
        recv_target.reshape(peers * slots),
        remote.reshape(peers * slots, panel_count, excite),
    )
    residual = (incident.astype(jnp.float32) - near_sum).astype(jnp.bfloat16)
    density = jnp.einsum(
        "tpq,tqc->tpc", inverse_blocks, residual, preferred_element_type=jnp.float32
    )
    return density.astype(jnp.bfloat16)


def solution(mesh):
    return jax.shard_map(
        per_device,
        mesh=mesh,
        in_specs=(
            P(None, "lag", None),
            P(("grp", "lag"), None, None),
            P(("grp", "lag"), None),
            P(("grp", "lag"), None),
            P(("grp", "lag"), None),
            P(("grp", "lag"), None),
            P(("grp", "lag")),
            P(("grp", "lag")),
            P(("grp", "lag")),
            P(("grp", "lag")),
            P(("grp", "lag"), None, None),
            P(("grp", "lag"), None, None),
        ),
        out_specs=P(("grp", "lag"), None, None),
        check_vma=False,
    )
```

profile of v0, /device:TPU:0, one launch (start us, length us, event | category | flops | bytes accessed | tf_op | source)
XLA Modules:
  0.0 907.9 jit_solution(12558134267319641852)
XLA Ops:
  8.0 5.2 all-to-all-start
  14.0 3.7 all-to-all-done
  17.7 3.2 all-to-all-start.1
  21.0 11.5 %gather_fusion = bf16[16,2048,256]{2,1,0:T(8,128)(2,1)} fusion(bf16[4,2048,256]{2,1,0:T(8,128)(2,1)} %param.17, s32[1024]{0:T(1024)S(1)} %pad_clamp_fusion), kind=kCustom, calls=%fused_computation | custom fusion | bytes 33554496 | tf_op jit(solution)/shard_map/gather | solution.py:94
  32.6 6.1 all-to-all-start.2
  41.1 181.6 %all-to-all-done.2 = bf16[8,2,2048,256]{3,2,1,0:T(8,128)(2,1)} async-done(((bf16[8,2,2048,256]{3,2,1,0:T(8,128)(2,1)}), bf16[8,2,2048,256]{3,2,1,0:T(8,128)(2,1)}, u32[]{:S(2)}, u32[]{:S(2)}) %all-to-all-start.2) | async-done | bytes 16777248 | tf_op jit(solution)/shard_map/all_to_all | solution.py:95
  222.7 214.2 %all-gather.2.cloned.1.call-done = bf16[3,16384,256]{2,1,0:T(8,128)(2,1)} async-done(((bf16[3,4096,256]{2,1,0:T(8,128)(2,1)}), bf16[3,16384,256]{2,1,0:T(8,128)(2,1)}) %all-gather.2.cloned.1.call-update) | async-done | bytes 25165840 | tf_op jit(solution)/shard_map/all_gather | solution.py:93
  436.9 110.1 %while.21 = (s32[]{:T(128)}, f32[2,8,256,256]{3,2,1,0:T(8,128)}, s32[2,8]{1,0:T(2,128)S(1)}, s32[2,8]{1,0:T(2,128)S(1)}, bf16[3,16384,256]{2,1,0:T(8,128)(2,1)},...) while((s32[]{:T(128)}, f32[2,8,256,256]{3,2,1,0:T(8,128)}, ...), condition=%wide.region_3.4_spmd, body=%wide.region_2.3_spmd.sunk | while | flops 2147483648 | bytes 23070708 | solution.py:39
  488.3 2.0 fusion.212
  505.0 2.0 fusion.206
  518.0 2.0 fusion.208
  543.4 2.0 fusion.212
  546.9 346.1 %while.22 = (s32[]{:T(128)}, f32[4,256,256]{2,0,1:T(4,128)}, s32[6,8]{1,0:T(8,128)S(1)}, s32[6,8]{1,0:T(8,128)S(1)}, s32[6,8]{1,0:T(8,128)S(1)}, /*index=5*/bf16...) while((s32[]{:T(128)}, f32[4,256,256]{2,0,1:T(4,128)}, ...), condition=%wide.region_1.2_spmd.clone, body=%wide.region_0.1_spmd.clone.sunk | while | flops 2173173760 | bytes 23070312 | solution.py:61
  598.2 2.0 fusion.241
  600.2 3.4 fusion.243
  654.8 2.0 fusion.241
  656.9 4.6 fusion.243
  712.7 2.0 fusion.241
  714.8 4.6 fusion.243
  770.6 2.0 fusion.241
  772.7 4.6 fusion.243
  830.5 4.6 fusion.243
  888.4 4.6 fusion.243
  893.0 6.6 fusion.113
  (149 shorter events, 139.0 us)
Async XLA Ops:
  6.5 893.1 %copy-start = (bf16[4,256,256]{2,1,0:T(8,128)(2,1)S(1)}, bf16[4,256,256]{2,1,0:T(8,128)(2,1)}, u32[]{:S(2)}) copy-start(bf16[4,256,256]{2,1,0:T(8,128)(2,1)} %param.26) | copy-start | bytes 1572868
  6.5 0.7 copy-start.2
  6.5 6.6 copy-start.5
  6.5 6.8 copy-start.3
  6.5 430.3 %all-gather.2.cloned.1.call-start = ((), (), s32[]{:S(2)}) async-start(), calls=%async_computation.3 | async-start | bytes 31457280 | tf_op jit(solution)/shard_map/all_gather | solution.py:93
  8.0 9.8 %all-to-all-start = ((s32[8,1,2]{2,1,0:T(1,128)}), s32[8,1,2]{2,1,0:T(1,128)S(1)}, u32[]{:S(2)}, u32[]{:S(2)}) async-start(s32[8,1,2]{2,1,0:T(1,128)} %copy.32), calls=%async_computation | async-start | bytes 8192 | tf_op jit(solution)/shard_map/all_to_all | solution.py:97
  17.7 14.8 %all-to-all-start.1 = ((s32[8,1,2]{2,1,0:T(1,128)}), s32[8,1,2]{2,1,0:T(1,128)S(1)}, u32[]{:S(2)}, u32[]{:S(2)}) async-start(s32[8,1,2]{2,1,0:T(1,128)} %copy.33), calls=%async_computation.1 | async-start | bytes 8192 | tf_op jit(solution)/shard_map/all_to_all | solution.py:96
  32.5 6.2 copy-start.6
  32.5 6.3 copy-start.7
  32.5 6.4 copy-start.8
  32.5 6.4 copy-start.9
  32.5 6.5 copy-start.4
  32.6 190.1 %all-to-all-start.2 = ((bf16[8,2,2048,256]{3,2,1,0:T(8,128)(2,1)}), bf16[8,2,2048,256]{3,2,1,0:T(8,128)(2,1)}, u32[]{:S(2)}, u32[]{:S(2)}) async-start(bf16[8,2,2048,256]{3,2,1,0:T(8,128)(2,1)} %bitcast.424), calls=%async_computation.2 | async-start | bytes 33554432 | tf_op jit(solution)/shard_map/all_to_all | solution.py:95
  546.9 346.1 %copy-start.1 = (bf16[4,256,256]{2,1,0:T(8,128)(2,1)S(1)}, bf16[4,256,256]{2,1,0:T(8,128)(2,1)}, u32[]{:S(2)}) copy-start(bf16[4,256,256]{2,1,0:T(8,128)(2,1)} %param.27) | copy-start | bytes 1572868
Sparse Core Ops, SparseCore 0:
  9.0 427.8 all-gather.1
where the time goes:
time: 914 us; the launch traced here: 908 us
  waiting for transfers between devices  400 us (44%)
  loops' own time  281 us (31%)
  matrix products  163 us (18%)
  local copies, waits for them, and re-layouts  34.8 us (4%)
  starting transfers between devices  14.6 us (2%)
  between operations  13.5 us (1%)
    all_gather x1, waiting for transfers between devices, per_device(): gathered = lax.all_gather(weights, 'lag', axis=1, tiled=True)  214 us
    another operation x1, loops' own time, accumulate_pairs(): lax.scan(accumulate_step, initial, (keys.reshape(-1, width), classes.resh...  210 us
    all_to_all x1, waiting for transfers between devices, per_device(): lax.all_to_all(served_rows, 'grp', split_axis=0, concat_axis=0, tiled=True)  182 us
    dot_general x64, matrix products, pair_product(): lax.dot_general(window, rows, (((0,), (0,)), ((), ())), preferred_element...  130 us
    another operation x1, loops' own time, compute_pairs(): lax.scan(compute_step, jnp.int32(0), (keys.reshape(-1, width), classes.re...  70.4 us
    dot_general x7, matrix products, collect(): jnp.einsum('ts,spc->tpc', select, contrib, precision=lax.Precision.HIGHEST)  32.9 us
  transfers between devices with their start and end apart: 4, of which 3 were waited for; matrix products, arithmetic and copies ran while one was open for 2% of the time, Pallas kernels for 0%

commit v1 on v0

v1 whole, which is shorter than its diff:
```python
import functools

import jax
import jax.numpy as jnp
from jax import lax
from jax.experimental import pallas as pl
from jax.experimental.pallas import tpu as pltpu
from jax.sharding import PartitionSpec as P

SMEM = pl.BlockSpec(memory_space=pltpu.SMEM)
VMEM = pl.BlockSpec(memory_space=pltpu.VMEM)
ANY = pl.BlockSpec(memory_space=pl.ANY)
MIB = 1 << 20


def matmul_cost(count, panels, height, excite, moved):
    return pl.CostEstimate(
        flops=2 * count * panels * height * excite, bytes_accessed=moved, transcendentals=0
    )


def local_kernel(klass, src_ref, lag_ref, class_ref, target_ref, table_ref, hist_ref, near_ref):
    panels = table_ref.shape[1]
    height = hist_ref.shape[2]
    near_ref[...] = jnp.zeros_like(near_ref)

    @pl.loop(0, src_ref.shape[0])
    def _(i):
        @pl.when(class_ref[i] == klass)
        def _():
            first = pl.multiple_of(lag_ref[i] * panels, panels)
            window = table_ref[pl.ds(first, height), :]
            near_ref[target_ref[i]] += jnp.dot(
                hist_ref[src_ref[i]], window, preferred_element_type=jnp.float32
            )


def local_sum(klass, src, lag, classes, target, table, hist_t):
    owned, excite, height = hist_t.shape
    panels = table.shape[1]
    return pl.pallas_call(
        functools.partial(local_kernel, klass),
        out_shape=jax.ShapeDtypeStruct((owned, excite, panels), jnp.float32),
        in_specs=[SMEM] * 4 + [VMEM] * 2,
        out_specs=VMEM,
        compiler_params=pltpu.CompilerParams(vmem_limit_bytes=32 * MIB),
        cost_estimate=matmul_cost(
            src.shape[0] // 3, panels, height, excite, 2 * (table.size + hist_t.size)
        ),
    )(src, lag, classes, target, table, hist_t)


def served_kernel(src_ref, lag_ref, class_ref, *refs):
    tables, (hist_ref, out_ref, held, sems) = refs[:-4], refs[-4:]
    count = src_ref.shape[0]
    panels = held.shape[2]
    height = held.shape[1]
    depth = held.shape[0]

    def fetch(i, slot, wait):
        first = pl.multiple_of(lag_ref[i] * panels, panels)
        for k, table in enumerate(tables):
            @pl.when(class_ref[i] == k)
            def _():
                copy = pltpu.make_async_copy(
                    table.at[pl.ds(first, height), :], held.at[slot], sems.at[slot]
                )
                if wait:
                    copy.wait()
                else:
                    copy.start()

    for i in range(min(depth - 1, count)):
        fetch(i, i, False)

    @pl.loop(0, count)
    def _(i):
        @pl.when(i + depth - 1 < count)
        def _():
            ahead = i + depth - 1
            fetch(ahead, lax.rem(ahead, depth), False)

        slot = lax.rem(i, depth)
        fetch(i, slot, True)
        out_ref[i] = jnp.dot(
            hist_ref[src_ref[i]], held[slot], preferred_element_type=jnp.float32
        ).astype(out_ref.dtype)


def served_products(src, lag, classes, tables, hist_t):
    owned, excite, height = hist_t.shape
    panels = tables[0].shape[1]
    count = src.shape[0]
    depth = 4
    return pl.pallas_call(
        served_kernel,
        out_shape=jax.ShapeDtypeStruct((count, excite, panels), jnp.bfloat16),
        in_specs=[SMEM] * 3 + [ANY] * len(tables) + [VMEM],
        out_specs=VMEM,
        scratch_shapes=[
            pltpu.VMEM((depth, height, panels), jnp.bfloat16),
            pltpu.SemaphoreType.DMA((depth,)),
        ],
        compiler_params=pltpu.CompilerParams(vmem_limit_bytes=32 * MIB),
        cost_estimate=matmul_cost(
            count, panels, height, excite, 2 * (count * height * panels + hist_t.size)
        ),
    )(src, lag, classes, *tables, hist_t)


def update_kernel(target_ref, *refs):
    nears, (recv_ref, inverse_ref, incident_ref, out_ref, total) = refs[:-5], refs[-5:]
    total[...] = sum(near[...] for near in nears)

    @pl.loop(0, target_ref.shape[0])
    def _(i):
        total[target_ref[i]] += recv_ref[i].astype(jnp.float32)

    for t in range(out_ref.shape[0]):
        residual = (incident_ref[t].astype(jnp.float32) - total[t].T).astype(jnp.bfloat16)
        out_ref[t] = jnp.dot(
            inverse_ref[t], residual, preferred_element_type=jnp.float32
        ).astype(out_ref.dtype)


def update(target, nears, recv, inverse, incident):
    return pl.pallas_call(
        update_kernel,
        out_shape=jax.ShapeDtypeStruct(incident.shape, jnp.bfloat16),
        in_specs=[SMEM] + [VMEM] * (len(nears) + 3),
        out_specs=VMEM,
        scratch_shapes=[pltpu.VMEM(nears[0].shape, jnp.float32)],
        compiler_params=pltpu.CompilerParams(vmem_limit_bytes=32 * MIB),
    )(target, *nears, recv, inverse, incident)


def per_device(
    weights,
    history,
    send_patch,
    send_lag,
    send_class,
    recv_target,
    local_src,
    local_lag,
    local_class,
    local_target,
    inverse_blocks,
    incident,
):
    classes, rows, panels = weights.shape
    peers, slots = send_patch.shape
    step = rows // peers
    piece = lax.dynamic_slice_in_dim(weights, lax.axis_index("grp") * step, step, 1)
    tables = [
        lax.all_gather(piece[k], ("lag", "grp"), axis=0, tiled=True) for k in range(classes)
    ]
    hist_t = jnp.swapaxes(history, 1, 2)
    served = served_products(
        send_patch.reshape(-1), send_lag.reshape(-1), send_class.reshape(-1), tables, hist_t
    )
    recv = lax.all_to_all(
        served.reshape(peers, slots, *served.shape[1:]), "grp", split_axis=0, concat_axis=0, tiled=True
    ).reshape(served.shape)
    nears = [
        local_sum(k, local_src, local_lag, local_class, local_target, tables[k], hist_t)
        for k in range(classes)
    ]
    return update(recv_target.reshape(-1), nears, recv, inverse_blocks, incident)


def solution(mesh):
    both = ("grp", "lag")
    return jax.shard_map(
        per_device,
        mesh=mesh,
        in_specs=(
            P(None, "lag", None),
            P(both, None, None),
            P(both, None),
            P(both, None),
            P(both, None),
            P(both, None),
            P(both),
            P(both),
            P(both),
            P(both),
            P(both, None, None),
            P(both, None, None),
        ),
        out_specs=P(both, None, None),
        check_vma=False,
    )
```

time: 914 us -> 319 us (0.35)
  loops' own time: 281 us -> 0 us
  waiting for transfers between devices: 400 us -> 231 us
  matrix products: 163 us -> 0 us
  Pallas kernels: 0 us -> 37.6 us
  starting transfers between devices: 14.6 us -> 3.7 us
    another operation x2 -> x0, loops' own time: 281 us -> none  [the longest x1 210 us: accumulate_pairs(): lax.scan(accumulate_step, initial, (keys.reshape(-1, width), classes.resh...]
    all_to_all x3 -> x1, waiting for transfers between devices: 185 us -> 0.01 us  [per_device(): lax.all_to_all(served.reshape(peers, slots, *served.shape[1:]), 'grp', sp...]
    dot_general x72 -> x0, matrix products: 163 us -> none  [the longest x64 130 us: pair_product(): lax.dot_general(window, rows, (((0,), (0,)), ((), ())), preferred_element...]
    pallas_call x0 -> x5, Pallas kernels: none -> 37.6 us  [the longest x3 24.8 us: local_sum(): pl.pallas_call(functools.partial(local_kernel, klass), out_shape=jax.Shap...]
    unnamed x21 -> x41, local copies, waits for them, and re-layouts: 0.13 us -> 29.7 us
    all_gather x1 -> x3, waiting for transfers between devices: 214 us -> 229 us  [per_device(): lax.all_gather(piece[k], ('lag', 'grp'), axis=0, tiled=True)]
    slice x24 -> x1, local copies, waits for them, and re-layouts: 16.3 us -> 2 us  [per_device(): piece[k]]
    gather x1 -> x0, local copies, waits for them, and re-layouts: 11.5 us -> none  [per_device(): served_rows = history[send_patch]]
  transfers between devices with their start and end apart: 4 -> 4, of which waited for: 3 -> 3; matrix products, arithmetic and copies ran while one was open for 2% -> 3% of each run, Pallas kernels for 0% -> 8%
where the time goes in v1:
time: 319 us; the launch traced here: 317 us
  waiting for transfers between devices  231 us (72%)
  Pallas kernels  37.6 us (12%)
  local copies, waits for them, and re-layouts  32.1 us (10%)
  between operations  13.2 us (4%)
  starting transfers between devices  3.7 us (1%)
    all_gather x3, waiting for transfers between devices, per_device(): lax.all_gather(piece[k], ('lag', 'grp'), axis=0, tiled=True)  229 us
    unnamed x41, local copies, waits for them, and re-layouts  29.7 us
    pallas_call x3, Pallas kernels, local_sum(): pl.pallas_call(functools.partial(local_kernel, klass), out_shape=jax.Shap...  24.8 us
    pallas_call x1, Pallas kernels, served_products(): pl.pallas_call(served_kernel, out_shape=jax.ShapeDtypeStruct((count, exci...  10.3 us
  transfers between devices with their start and end apart: 4, of which 3 were waited for; matrix products, arithmetic and copies ran while one was open for 3% of the time, Pallas kernels for 8%

profile of v1, /device:TPU:0, one launch (start us, length us, event | category | flops | bytes accessed | tf_op | source)
XLA Modules:
  0.0 317.4 jit_solution(8003740217241961063)
XLA Ops:
  6.5 2.0 constant_dynamic-slice_fusion.2
  10.1 0.8 copy.20
  10.9 0.8 copy.21
  12.6 6.3 %copy.19 = bf16[4,2048,256]{1,2,0:T(8,128)(2,1)} copy(bf16[4,2048,256]{2,1,0:T(8,128)(2,1)} %param.13) | data formatting | bytes 8388608 | tf_op args[1]
  18.9 71.5 %all-gather.11.cloned.1.call-done = bf16[1,16384,256]{2,1,0:T(8,128)(2,1)} async-done(((bf16[1,512,256]{2,1,0:T(8,128)(2,1)}), bf16[1,16384,256]{2,1,0:T(8,128)(2,1)}) %all-gather.11.cloned.1.call-update) | async-done | bytes 8388624 | tf_op jit(solution)/shard_map/all_gather | solution.py:156
  90.4 78.9 %all-gather.9.cloned.1.call-done = bf16[1,16384,256]{2,1,0:T(8,128)(2,1)} async-done(((bf16[1,512,256]{2,1,0:T(8,128)(2,1)}), bf16[1,16384,256]{2,1,0:T(8,128)(2,1)}) %all-gather.9.cloned.1.call-update) | async-done | bytes 8388624 | tf_op jit(solution)/shard_map/all_gather | solution.py:156
  169.3 78.9 %all-gather.7.cloned.1.call-done = bf16[1,16384,256]{2,1,0:T(8,128)(2,1)} async-done(((bf16[1,512,256]{2,1,0:T(8,128)(2,1)}), bf16[1,16384,256]{2,1,0:T(8,128)(2,1)}) %all-gather.7.cloned.1.call-update) | async-done | bytes 8388624 | tf_op jit(solution)/shard_map/all_gather | solution.py:156
  248.3 2.2 copy-done
  250.5 3.4 %copy-done.5 = bf16[1,16384,256]{2,1,0:T(8,128)(2,1)S(1)} copy-done((bf16[1,16384,256]{2,1,0:T(8,128)(2,1)S(1)}, bf16[1,16384,256]{2,1,0:T(8,128)(2,1)}, u32[]{:S(2)}) %copy-start.5) | copy-done | bytes 8388632
  253.9 10.3 %shard_map.121 = bf16[16,256,256]{2,1,0:T(8,128)(2,1)} custom-call(s32[16]{0:T(128)S(1)} %reshape.19.src_ref, s32[16]{0:T(128)S(1)} %reshape.20.lag_ref, s32[16]{0:T(128)S(1)} %reshape.21.class_ref, bf16[16384,256]{1,0:T(8,128)(2,1)S(1)} %bitcast.14, bf16[16384,256]{1,0:T(8,128)(2,1)} %bitcast.12, bf16[16384,256]{1,0:T(8,128)(2,1)} %bitcast.10, ...), custom_call_target="tpu_custom_call" | custom-call | flops 4294967296 | bytes 20971520 | tf_op jit(solution)/shard_map/pallas_call | solution.py:95
  264.2 3.6 %all-to-all-start = ((bf16[8,2,256,256]{3,2,1,0:T(8,128)(2,1)}), bf16[8,2,256,256]{3,2,1,0:T(8,128)(2,1)S(1)}, u32[]{:S(2)}, u32[]{:S(2)}) async-start(bf16[8,2,256,256]{3,2,1,0:T(8,128)(2,1)} %bitcast.4), calls=%async_computation | async-start | bytes 4194304 | tf_op jit(solution)/shard_map/all_to_all | solution.py:162
  268.0 2.2 copy-done.1
  270.2 3.4 %copy-done.3 = bf16[1,16384,256]{2,1,0:T(8,128)(2,1)S(1)} copy-done((bf16[1,16384,256]{2,1,0:T(8,128)(2,1)S(1)}, bf16[1,16384,256]{2,1,0:T(8,128)(2,1)}, u32[]{:S(2)}) %copy-start.3) | copy-done | bytes 8388632
  273.6 10.9 %shard_map.120.refs_2_ = f32[4,256,256]{2,1,0:T(8,128)S(1)} custom-call(s32[48]{0:T(128)S(1)} %copy-done.13, s32[48]{0:T(128)S(1)} %copy-done.14, s32[48]{0:T(128)S(1)} %copy-done.15, s32[48]{0:T(128)S(1)} %copy-done.16, bf16[16384,256]{1,0:T(8,128)(2,1)S(1)} %bitcast.11, bf16[4,256,2048]{2,1,0:T(8,128)(2,1)S(1)} %bitcast.7), custom_call_target="tpu_custom_call" | custom-call | flops 4294967296 | bytes 12582912 | tf_op jit(solution)/shard_map/pallas_call | solution.py:41
  284.5 5.7 %shard_map.119.refs_1_ = f32[4,256,256]{2,1,0:T(8,128)S(1)} custom-call(s32[48]{0:T(128)S(1)} %copy-done.13, s32[48]{0:T(128)S(1)} %copy-done.14, s32[48]{0:T(128)S(1)} %copy-done.15, s32[48]{0:T(128)S(1)} %copy-done.16, bf16[16384,256]{1,0:T(8,128)(2,1)S(1)} %bitcast.13, bf16[4,256,2048]{2,1,0:T(8,128)(2,1)S(1)} %bitcast.8), custom_call_target="tpu_custom_call" | custom-call | flops 4294967296 | bytes 12582912 | tf_op jit(solution)/shard_map/pallas_call | solution.py:41
  290.2 1.0 copy-done.7
  291.2 3.4 %copy-done.6 = bf16[1,16384,256]{2,1,0:T(8,128)(2,1)S(1)} copy-done((bf16[1,16384,256]{2,1,0:T(8,128)(2,1)S(1)}, bf16[1,16384,256]{2,1,0:T(8,128)(2,1)}, u32[]{:S(2)}) %copy-start.6) | copy-done | bytes 8388632
  294.6 8.3 %shard_map.118.refs_0_ = f32[4,256,256]{2,1,0:T(8,128)S(1)} custom-call(s32[48]{0:T(128)S(1)} %copy-done.13, s32[48]{0:T(128)S(1)} %copy-done.14, s32[48]{0:T(128)S(1)} %copy-done.15, s32[48]{0:T(128)S(1)} %copy-done.16, bf16[16384,256]{1,0:T(8,128)(2,1)S(1)} %bitcast.15, bf16[4,256,2048]{2,1,0:T(8,128)(2,1)S(1)} %bitcast.9), custom_call_target="tpu_custom_call" | custom-call | flops 4294967296 | bytes 12582912 | tf_op jit(solution)/shard_map/pallas_call | solution.py:41
  302.9 1.0 copy-done.9
  303.9 1.2 copy-done.8
  305.1 1.2 copy-done.10
  306.3 1.0 copy-done.11
  307.4 1.0 copy-done.12
  308.4 2.5 shard_map.122
  (38 shorter events, 2.7 us)
Async XLA Ops:
  6.5 83.9 %all-gather.11.cloned.1.call-start = ((), (), s32[]{:S(2)}) async-start(), calls=%async_computation.3 | async-start | bytes 8650752 | tf_op jit(solution)/shard_map/all_gather | solution.py:156
  8.6 160.8 %all-gather.9.cloned.1.call-start = ((), (), s32[]{:S(2)}) async-start(), calls=%async_computation.2 | async-start | bytes 8650752 | tf_op jit(solution)/shard_map/all_gather | solution.py:156
  9.3 239.0 %all-gather.7.cloned.1.call-start = ((), (), s32[]{:S(2)}) async-start(), calls=%async_computation.1 | async-start | bytes 8650752 | tf_op jit(solution)/shard_map/all_gather | solution.py:156
  248.3 2.2 copy-start
  250.5 3.4 %copy-start.5 = (bf16[1,16384,256]{2,1,0:T(8,128)(2,1)S(1)}, bf16[1,16384,256]{2,1,0:T(8,128)(2,1)}, u32[]{:S(2)}) copy-start(bf16[1,16384,256]{2,1,0:T(8,128)(2,1)} %all-gather.7.cloned.1.call-done) | copy-start | bytes 25165828
  253.9 14.0 %copy-start.17 = (s32[8,2]{0,1:T(2,128)S(1)}, s32[8,2]{0,1:T(2,128)}, u32[]{:S(2)}) copy-start(s32[8,2]{0,1:T(2,128)} %param.17) | copy-start | bytes 196
  253.9 14.1 %copy-start.13 = (s32[48]{0:T(128)S(1)}, s32[48]{0:T(128)}, u32[]{:S(2)}) copy-start(s32[48]{0:T(128)} %src_ref.5) | copy-start | bytes 580
  253.9 14.1 %copy-start.14 = (s32[48]{0:T(128)S(1)}, s32[48]{0:T(128)}, u32[]{:S(2)}) copy-start(s32[48]{0:T(128)} %lag_ref.5) | copy-start | bytes 580
  253.9 14.1 %copy-start.15 = (s32[48]{0:T(128)S(1)}, s32[48]{0:T(128)}, u32[]{:S(2)}) copy-start(s32[48]{0:T(128)} %class_ref.5) | copy-start | bytes 580
  253.9 14.1 %copy-start.16 = (s32[48]{0:T(128)S(1)}, s32[48]{0:T(128)}, u32[]{:S(2)}) copy-start(s32[48]{0:T(128)} %target_ref.5) | copy-start | bytes 580
  264.2 39.7 %all-to-all-start = ((bf16[8,2,256,256]{3,2,1,0:T(8,128)(2,1)}), bf16[8,2,256,256]{3,2,1,0:T(8,128)(2,1)S(1)}, u32[]{:S(2)}, u32[]{:S(2)}) async-start(bf16[8,2,256,256]{3,2,1,0:T(8,128)(2,1)} %bitcast.4), calls=%async_computation | async-start | bytes 4194304 | tf_op jit(solution)/shard_map/all_to_all | solution.py:162
  268.0 2.2 copy-start.1
  270.2 3.4 %copy-start.3 = (bf16[1,16384,256]{2,1,0:T(8,128)(2,1)S(1)}, bf16[1,16384,256]{2,1,0:T(8,128)(2,1)}, u32[]{:S(2)}) copy-start(bf16[1,16384,256]{2,1,0:T(8,128)(2,1)} %all-gather.11.cloned.1.call-done) | copy-start | bytes 25165828
  273.6 10.9 %copy-start.4 = (bf16[1,16384,256]{2,1,0:T(8,128)(2,1)S(1)}, bf16[1,16384,256]{2,1,0:T(8,128)(2,1)}, u32[]{:S(2)}) copy-start(bf16[1,16384,256]{2,1,0:T(8,128)(2,1)} %all-gather.9.cloned.1.call-done) | copy-start | bytes 25165828
  284.5 6.7 %copy-start.2 = (bf16[4,2048,256]{1,2,0:T(8,128)(2,1)S(1)}, bf16[4,2048,256]{1,2,0:T(8,128)(2,1)}, u32[]{:S(2)}) copy-start(bf16[4,2048,256]{1,2,0:T(8,128)(2,1)} %copy.19) | copy-start | bytes 12582916
  290.2 1.1 copy-start.7
  291.2 3.4 %copy-start.6 = (bf16[1,16384,256]{2,1,0:T(8,128)(2,1)S(1)}, bf16[1,16384,256]{2,1,0:T(8,128)(2,1)}, u32[]{:S(2)}) copy-start(bf16[1,16384,256]{2,1,0:T(8,128)(2,1)} %all-gather.7.cloned.1.call-done) | copy-start | bytes 25165828
  302.9 1.0 copy-start.9
  303.9 1.2 copy-start.8
  305.1 1.2 copy-start.10
  306.3 1.0 copy-start.11
  307.4 1.0 copy-start.12
Sparse Core Ops, SparseCore 0:
  10.2 80.1 all-gather.10
  93.3 76.0 all-gather.8
  172.2 76.0 all-gather.6

commit v2 on v1

v2 whole, which is shorter than its diff:
```python
import functools

import jax
import jax.numpy as jnp
from jax import lax
from jax.experimental import pallas as pl
from jax.experimental.pallas import tpu as pltpu
from jax.sharding import PartitionSpec as P

SMEM = pl.BlockSpec(memory_space=pltpu.SMEM)
VMEM = pl.BlockSpec(memory_space=pltpu.VMEM)
ANY = pl.BlockSpec(memory_space=pl.ANY)
MIB = 1 << 20


def add_pairs(shard, pairs, hist_ref, table, acc):
    src_ref, lag_ref, class_ref, dest_ref = pairs
    panels = table.shape[2]
    steps = hist_ref.shape[2] // panels
    lags = table.shape[1] // panels

    @pl.loop(0, src_ref.shape[0])
    def _(i):
        offset = lag_ref[i] - shard * lags
        first = jnp.maximum(offset, 0)
        count = jnp.minimum(offset + steps, lags) - first
        for n in range(1, min(steps, lags) + 1):
            @pl.when(count == n)
            def _():
                rows = pl.multiple_of(first * panels, panels)
                columns = pl.multiple_of((first - offset) * panels, panels)
                acc[dest_ref[i]] += jnp.dot(
                    hist_ref[src_ref[i], :, pl.ds(columns, n * panels)],
                    table[class_ref[i], pl.ds(rows, n * panels), :],
                    preferred_element_type=jnp.float32,
                )


def round_kernel(places, groups, begun, *refs):
    refs = list(refs)
    where = refs.pop(0)
    pairs = [[refs.pop(0) for _ in range(4)] for _ in range(groups)]
    hist_ref = refs.pop(0)
    pieces = [refs.pop(0) for _ in places]
    before = [refs.pop(0) for _ in range(groups if begun else 0)]
    outs = [refs.pop(0) for _ in range(groups)]
    table, sems, acc_sems = refs[:3]
    accs = refs[3:] or outs
    shard, group = where[0], where[1]

    copies = []
    for n, ((mask, first, height), piece) in enumerate(zip(places, pieces)):
        start = pl.multiple_of((group ^ mask) * height + first, 16)
        rows = piece.shape[1]
        copies.append(
            pltpu.make_async_copy(piece, table.at[:, pl.ds(start, rows), :], sems.at[n])
        )
    for n, (old, acc) in enumerate(zip(before, accs)):
        copies.append(pltpu.make_async_copy(old, acc, acc_sems.at[n]))
    for copy in copies:
        copy.start()
    if not begun:
        for acc in accs:
            acc[...] = jnp.zeros_like(acc)
    for copy in copies:
        copy.wait()
    for group_pairs, acc in zip(pairs, accs):
        add_pairs(shard, group_pairs, hist_ref, table, acc)
    for acc, out in zip(accs, outs):
        if acc is not out:
            out[...] = acc[...].astype(out.dtype)


def run_round(shard, group, pieces, height, pair_lists, hist_t, sums, counts, dtype=jnp.float32):
    owned, excite, depth = hist_t.shape
    classes, _, panels = pieces[0][2].shape
    rows = height * (pieces_total(pieces) // height)
    places = [(mask, first, height) for mask, first, _ in pieces]
    groups = len(pair_lists)
    shapes = [(count, excite, panels) for count in counts]
    wide = [pltpu.VMEM(s, jnp.float32) for s in shapes] if dtype != jnp.float32 else []
    pair_count = sum(lists[0].shape[0] for lists in pair_lists)
    moved = classes * rows * panels * 2 + hist_t.size * 2 + sum(8 * s[0] * s[1] * s[2] for s in shapes)
    return pl.pallas_call(
        functools.partial(round_kernel, places, groups, sums is not None),
        out_shape=[jax.ShapeDtypeStruct(s, dtype) for s in shapes],
        in_specs=[SMEM] * (1 + 4 * groups)
        + [VMEM]
        + [ANY] * (len(places) + (groups if sums is not None else 0)),
        out_specs=[VMEM] * groups,
        scratch_shapes=[
            pltpu.VMEM((classes, rows, panels), jnp.bfloat16),
            pltpu.SemaphoreType.DMA((len(places),)),
            pltpu.SemaphoreType.DMA((groups,)),
        ]
        + wide,
        compiler_params=pltpu.CompilerParams(vmem_limit_bytes=40 * MIB),
        cost_estimate=pl.CostEstimate(
            flops=2 * pair_count * panels * depth * excite // 3, bytes_accessed=moved, transcendentals=0
        ),
    )(
        jnp.stack([shard, group]).astype(jnp.int32),
        *[x for lists in pair_lists for x in lists],
        hist_t,
        *[piece for _, _, piece in pieces],
        *(sums if sums is not None else []),
    )


def pieces_total(pieces):
    return sum(piece.shape[1] for _, _, piece in pieces)


def update_kernel(target_ref, near_ref, recv_ref, inverse_ref, incident_ref, out_ref, total):
    total[...] = near_ref[...]

    @pl.loop(0, target_ref.shape[0])
    def _(i):
        total[target_ref[i]] += recv_ref[i].astype(jnp.float32)

    for t in range(out_ref.shape[0]):
        residual = (incident_ref[t].astype(jnp.float32) - total[t].T).astype(jnp.bfloat16)
        out_ref[t] = jnp.dot(
            inverse_ref[t], residual, preferred_element_type=jnp.float32
        ).astype(out_ref.dtype)


def update(target, near, recv, inverse, incident):
    return pl.pallas_call(
        update_kernel,
        out_shape=jax.ShapeDtypeStruct(incident.shape, jnp.bfloat16),
        in_specs=[SMEM] + [VMEM] * 4,
        out_specs=VMEM,
        scratch_shapes=[pltpu.VMEM(near.shape, jnp.float32)],
        compiler_params=pltpu.CompilerParams(vmem_limit_bytes=32 * MIB),
    )(target, near, recv, inverse, incident)


def swap(value, bit, peers):
    return lax.ppermute(value, "grp", [(i, i ^ bit) for i in range(peers)])


def spread(piece, peers):
    held = [(0, 0, piece)]
    bit = 8
    while bit < peers:
        held += [(mask ^ bit, first, swap(value, bit, peers)) for mask, first, value in held]
        bit *= 2
    found = []
    for mask, first, value in held:
        half = value.shape[1] // 2
        across = swap(value, 2, peers)
        along = swap(value, 4, peers)
        corner_a = swap(along[:, :half], 2, peers)
        corner_b = swap(across[:, half:], 4, peers)
        found += [
            (mask, first, value),
            (mask ^ 2, first, across),
            (mask ^ 4, first, along),
            (mask ^ 6, first, corner_a),
            (mask ^ 6, first + half, corner_b),
        ]
    return found + [(mask ^ 1, first, swap(value, 1, peers)) for mask, first, value in found]


def per_device(
    weights,
    history,
    send_patch,
    send_lag,
    send_class,
    recv_target,
    local_src,
    local_lag,
    local_class,
    local_target,
    inverse_blocks,
    incident,
):
    rows = weights.shape[1]
    owned = history.shape[0]
    peers, slots = send_patch.shape
    served_count = peers * slots
    height = rows // peers
    group = lax.axis_index("grp")
    lane = lax.axis_index("lag")
    lanes = lax.axis_size("lag")

    hist_t = jnp.swapaxes(history, 1, 2)
    served_pairs = (
        send_patch.reshape(-1),
        send_lag.reshape(-1),
        send_class.reshape(-1),
        jnp.arange(served_count, dtype=jnp.int32),
    )
    local_pairs = (local_src, local_lag, local_class, local_target)
    pairs = [served_pairs, local_pairs]
    counts = [served_count, owned]

    sums = run_round(lane, group * 0, [(0, 0, weights)], rows, pairs, hist_t, None, counts)
    piece = lax.dynamic_slice_in_dim(weights, group * height, height, 1)
    for step in range(1, lanes):
        piece = lax.ppermute(piece, "lag", [(i, (i - 1) % lanes) for i in range(lanes)])
        pieces = spread(piece, peers)
        shard = lax.rem(lane + step, lanes)
        if step < lanes - 1:
            sums = run_round(shard, group, pieces, height, pairs, hist_t, sums, counts)
    served = run_round(
        shard, group, pieces, height, pairs[:1], hist_t, sums[:1], counts[:1], jnp.bfloat16
    )[0]
    recv = lax.all_to_all(
        served.reshape(peers, slots, *served.shape[1:]), "grp", split_axis=0, concat_axis=0, tiled=True
    ).reshape(served.shape)
    near = run_round(shard, group, pieces, height, pairs[1:], hist_t, sums[1:], counts[1:])[0]
    return update(recv_target.reshape(-1), near, recv, inverse_blocks, incident)


def solution(mesh):
    both = ("grp", "lag")
    return jax.shard_map(
        per_device,
        mesh=mesh,
        in_specs=(
            P(None, "lag", None),
            P(both, None, None),
            P(both, None),
            P(both, None),
            P(both, None),
            P(both, None),
            P(both),
            P(both),
            P(both),
            P(both),
            P(both, None, None),
            P(both, None, None),
        ),
        out_specs=P(both, None, None),
        check_vma=False,
    )
```

time: 319 us -> 226 us (0.71)
  waiting for transfers between devices: 231 us -> 75.6 us
  Pallas kernels: 37.6 us -> 68.3 us
  starting transfers between devices: 3.7 us -> 33.2 us
  local copies, waits for them, and re-layouts: 32.1 us -> 45.3 us
  between operations: 13.2 us -> 0.52 us
    all_gather x3 -> x0, waiting for transfers between devices: 229 us -> none  [per_device(): lax.all_gather(piece[k], ('lag', 'grp'), axis=0, tiled=True)]
    ppermute x0 -> x30, waiting for transfers between devices: none -> 70 us  [the longest x27 52.8 us: swap(): return lax.ppermute(value, 'grp', [(i, i ^ bit) for i in range(peers)])]
    pallas_call x4 -> x5, Pallas kernels: 35.1 us -> 65.9 us  [run_round(): pl.pallas_call(functools.partial(round_kernel, places, groups, sums is no...]
    ppermute x0 -> x30, starting transfers between devices: none -> 29.5 us  [the longest x27 18.7 us: swap(): return lax.ppermute(value, 'grp', [(i, i ^ bit) for i in range(peers)])]
    unnamed x41 -> x127, local copies, waits for them, and re-layouts: 29.7 us -> 40.1 us
    all_to_all x1, waiting for transfers between devices: 0.01 us -> 5.67 us  [per_device(): lax.all_to_all(served.reshape(peers, slots, *served.shape[1:]), 'grp', sp...]
  transfers between devices with their start and end apart: 4 -> 31, of which waited for: 3 -> 8; matrix products, arithmetic and copies ran while one was open for 3% -> 5% of each run, Pallas kernels for 8% -> 27%
where the time goes in v2:
time: 226 us; the launch traced here: 223 us
  waiting for transfers between devices  75.6 us (33%)
  Pallas kernels  68.3 us (30%)
  local copies, waits for them, and re-layouts  45.3 us (20%)
  starting transfers between devices  33.2 us (15%)
    pallas_call x5, Pallas kernels, run_round(): pl.pallas_call(functools.partial(round_kernel, places, groups, sums is no...  65.9 us
    ppermute x27, waiting for transfers between devices, swap(): return lax.ppermute(value, 'grp', [(i, i ^ bit) for i in range(peers)])  52.8 us
    unnamed x127, local copies, waits for them, and re-layouts  40.1 us
    ppermute x27, starting transfers between devices, swap(): return lax.ppermute(value, 'grp', [(i, i ^ bit) for i in range(peers)])  18.7 us
    ppermute x3, waiting for transfers between devices, per_device(): lax.ppermute(piece, 'lag', [(i, (i - 1) % lanes) for i in range(lanes)])  17.2 us
    ppermute x3, starting transfers between devices, per_device(): lax.ppermute(piece, 'lag', [(i, (i - 1) % lanes) for i in range(lanes)])  10.8 us
    all_to_all x1, waiting for transfers between devices, per_device(): lax.all_to_all(served.reshape(peers, slots, *served.shape[1:]), 'grp', sp...  5.67 us
  transfers between devices with their start and end apart: 31, of which 8 were waited for; matrix products, arithmetic and copies ran while one was open for 5% of the time, Pallas kernels for 27%

profile of v2, /device:TPU:0, one launch (start us, length us, event | category | flops | bytes accessed | tf_op | source)
XLA Modules:
  0.0 223.2 jit_solution(3701529959014689291)
XLA Ops:
  1.2 5.1 %collective-permute-start = (bf16[3,512,256]{2,1,0:T(8,128)(2,1)S(1)}, bf16[3,512,256]{2,1,0:T(8,128)(2,1)S(1)}, u32[]{:S(2)}, u32[]{:S(2)}) collective-permute-start(bf16[3,512,256]{2,1,0:T(8,128)(2,1)S(1)} %constant_dynamic-slice_fusion), channel_id=1, source_target_pairs={{0,3},{1,0},{2,1},{3,2},{4,7},{5,4},{6,5},{7,6},{8,11},{9,8},{10,9... | collective-permute-start | bytes 2359304 | tf_op jit(solution)/shard_map/ppermute | solution.py:203
  6.3 16.8 %collective-permute-done.refs_10_ = bf16[3,512,256]{2,1,0:T(8,128)(2,1)S(1)} collective-permute-done((bf16[3,512,256]{2,1,0:T(8,128)(2,1)S(1)}, bf16[3,512,256]{2,1,0:T(8,128)(2,1)S(1)}, u32[]{:S(2)}, u32[]{:S(2)}) %collective-permute-start) | collective-permute-done | bytes 786464 | tf_op jit(solution)/shard_map/ppermute | solution.py:203
  24.6 4.3 %collective-permute-start.1 = (bf16[3,512,256]{2,1,0:T(8,128)(2,1)S(1)}, bf16[3,512,256]{2,1,0:T(8,128)(2,1)}, u32[]{:S(2)}, u32[]{:S(2)}) collective-permute-start(bf16[3,512,256]{2,1,0:T(8,128)(2,1)S(1)} %collective-permute-done.refs_10_), channel_id=1, source_target_pairs={{0,3},{1,0},{2,1},{3,2},{4,7},{5,4},{6,5},{7,6},{8,11},{9,8},{10,9... | collective-permute-start | bytes 2359304 | tf_op jit(solution)/shard_map/ppermute | solution.py:203
  30.4 11.2 %collective-permute-done.22.refs_12_ = bf16[3,512,256]{2,1,0:T(8,128)(2,1)} collective-permute-done((bf16[3,512,256]{2,1,0:T(8,128)(2,1)S(1)}, bf16[3,512,256]{2,1,0:T(8,128)(2,1)}, u32[]{:S(2)}, u32[]{:S(2)}) %collective-permute-start.22) | collective-permute-done | bytes 786464 | tf_op jit(solution)/shard_map/ppermute | solution.py:140
  45.7 3.7 %collective-permute-done.21.refs_11_ = bf16[3,512,256]{2,1,0:T(8,128)(2,1)S(1)} collective-permute-done((bf16[3,512,256]{2,1,0:T(8,128)(2,1)S(1)}, bf16[3,512,256]{2,1,0:T(8,128)(2,1)S(1)}, u32[]{:S(2)}, u32[]{:S(2)}) %collective-permute-start.21) | collective-permute-done | bytes 786464 | tf_op jit(solution)/shard_map/ppermute | solution.py:140
  53.4 4.4 %collective-permute-done.23.refs_13_ = bf16[3,256,256]{2,1,0:T(8,128)(2,1)S(1)} collective-permute-done((bf16[3,256,256]{2,1,0:T(8,128)(2,1)S(1)}, bf16[3,256,256]{2,1,0:T(8,128)(2,1)S(1)}, u32[]{:S(2)}, u32[]{:S(2)}) %collective-permute-start.23) | collective-permute-done | bytes 393248 | tf_op jit(solution)/shard_map/ppermute | solution.py:140
  57.8 12.6 %collective-permute-done.24.refs_14_ = bf16[3,256,256]{2,1,0:T(8,128)(2,1)S(1)} collective-permute-done((bf16[3,256,256]{2,1,0:T(8,128)(2,1)S(1)}, bf16[3,256,256]{2,1,0:T(8,128)(2,1)S(1)}, u32[]{:S(2)}, u32[]{:S(2)}) %collective-permute-start.24) | collective-permute-done | bytes 393248 | tf_op jit(solution)/shard_map/ppermute | solution.py:140
  74.5 1.8 slice.26
  80.8 20.9 %collective-permute-done.14.refs_13_ = bf16[3,256,256]{2,1,0:T(8,128)(2,1)S(1)} collective-permute-done((bf16[3,256,256]{2,1,0:T(8,128)(2,1)}, bf16[3,256,256]{2,1,0:T(8,128)(2,1)S(1)}, u32[]{:S(2)}, u32[]{:S(2)}) %collective-permute-start.14) | collective-permute-done | bytes 393248 | tf_op jit(solution)/shard_map/ppermute | solution.py:140
  102.4 6.3 %copy.19 = bf16[4,2048,256]{1,2,0:T(8,128)(2,1)} copy(bf16[4,2048,256]{2,1,0:T(8,128)(2,1)} %param.13) | data formatting | bytes 8388608 | tf_op args[1]
  109.9 2.2 copy-done
  112.2 13.7 %shard_map.118 = (f32[16,256,256]{2,1,0:T(8,128)S(1)}, f32[4,256,256]{2,1,0:T(8,128)S(1)}) custom-call(s32[2]{0:T(128)S(1)} %pad_add_fusion.3.refs_0_, s32[16]{0:T(128)S(1)} %reshape.19.refs_1_, s32[16]{0:T(128)S(1)} %reshape.20.refs_2_, s32[16]{0:T(128)S(1)} %reshape.21.refs_3_, s32[16]{0:T(128)S(1)} %iota.11.refs_4_, s32[48]{0:T(128)S(1)} %copy-done.45, ...), custom_call_target="tpu_custom_call" | custom-call | flops 5726623232 | bytes 20971520 | tf_op jit(solution)/shard_map/pallas_call | solution.py:84
  125.9 2.0 copy-done.49
  128.1 4.0 %collective-permute-start.5 = (bf16[3,256,256]{2,1,0:T(8,128)(2,1)S(1)}, bf16[3,256,256]{2,1,0:T(8,128)(2,1)S(1)}, u32[]{:S(2)}, u32[]{:S(2)}) collective-permute-start(bf16[3,256,256]{2,1,0:T(8,128)(2,1)S(1)} %slice.24), channel_id=1, source_target_pairs={{0,8},{4,12},{8,0},{12,4},{16,24},{20,28},{24,16},{28,20},{1,9},{5... | collective-permute-start | bytes 1179656 | tf_op jit(solution)/shard_map/ppermute | solution.py:140
  134.0 17.9 %shard_map.119 = (f32[16,256,256]{2,1,0:T(8,128)S(1)}, f32[4,256,256]{2,1,0:T(8,128)S(1)}) custom-call(s32[2]{0:T(128)S(1)} %pad_add_fusion.2.refs_0_, s32[16]{0:T(128)S(1)} %reshape.19.refs_1_, s32[16]{0:T(128)S(1)} %reshape.20.refs_2_, s32[16]{0:T(128)S(1)} %reshape.21.refs_3_, s32[16]{0:T(128)S(1)} %iota.10.refs_4_, s32[48]{0:T(128)S(1)} %copy-done.45, ...), custom_call_target="tpu_custom_call" | custom-call | flops 5726623232 | bytes 20971520 | tf_op jit(solution)/shard_map/pallas_call | solution.py:84
  151.9 2.0 copy-done.50
  157.1 21.5 %shard_map.120 = (f32[16,256,256]{2,1,0:T(8,128)S(1)}, f32[4,256,256]{2,1,0:T(8,128)S(1)}) custom-call(s32[2]{0:T(128)S(1)} %pad_add_fusion.1.refs_0_, s32[16]{0:T(128)S(1)} %reshape.19.refs_1_, s32[16]{0:T(128)S(1)} %reshape.20.refs_2_, s32[16]{0:T(128)S(1)} %reshape.21.refs_3_, s32[16]{0:T(128)S(1)} %iota.9.refs_4_, s32[48]{0:T(128)S(1)} %copy-done.45, ...), custom_call_target="tpu_custom_call" | custom-call | flops 5726623232 | bytes 20971520 | tf_op jit(solution)/shard_map/pallas_call | solution.py:84
  178.6 2.0 copy-done.4
  180.8 6.1 %shard_map.122 = bf16[16,256,256]{2,1,0:T(8,128)(2,1)S(1)} custom-call(s32[2]{0:T(128)S(1)} %pad_add_fusion.refs_0_, s32[16]{0:T(128)S(1)} %reshape.19.refs_1_, s32[16]{0:T(128)S(1)} %reshape.20.refs_2_, s32[16]{0:T(128)S(1)} %reshape.21.refs_3_, s32[16]{0:T(128)S(1)} %iota.12.refs_4_, bf16[4,256,2048]{2,1,0:T(8,128)(2,1)S(1)} %bitcast.11, ...), custom_call_target="tpu_custom_call" | custom-call | flops 1431655808 | bytes 18874368 | tf_op jit(solution)/shard_map/pallas_call | solution.py:84
  188.3 3.7 %all-to-all-start = ((bf16[8,2,256,256]{3,2,1,0:T(8,128)(2,1)}), bf16[8,2,256,256]{3,2,1,0:T(8,128)(2,1)S(1)}, u32[]{:S(2)}, u32[]{:S(2)}) async-start(bf16[8,2,256,256]{3,2,1,0:T(8,128)(2,1)} %bitcast.14), calls=%async_computation | async-start | bytes 4194304 | tf_op jit(solution)/shard_map/all_to_all | solution.py:211
  192.2 2.2 copy-done.2
  205.3 6.7 %shard_map.121.near_ref = f32[4,256,256]{2,1,0:T(8,128)S(1)} custom-call(s32[2]{0:T(128)S(1)} %pad_add_fusion.refs_0_, s32[48]{0:T(128)S(1)} %copy-done.45, s32[48]{0:T(128)S(1)} %copy-done.46, s32[48]{0:T(128)S(1)} %copy-done.47, s32[48]{0:T(128)S(1)} %copy-done.48, bf16[4,256,2048]{2,1,0:T(8,128)(2,1)S(1)} %bitcast.12, ...), custom_call_target="tpu_custom_call" | custom-call | flops 4294967296 | bytes 12582912 | tf_op jit(solution)/shard_map/pallas_call | solution.py:84
  212.9 5.7 %all-to-all-done = bf16[8,2,256,256]{3,2,1,0:T(8,128)(2,1)S(1)} async-done(((bf16[8,2,256,256]{3,2,1,0:T(8,128)(2,1)}), bf16[8,2,256,256]{3,2,1,0:T(8,128)(2,1)S(1)}, u32[]{:S(2)}, u32[]{:S(2)}) %all-to-all-start) | async-done | bytes 2097184 | tf_op jit(solution)/shard_map/all_to_all | solution.py:211
  220.9 2.4 %shard_map.123 = bf16[4,256,256]{2,1,0:T(8,128)(2,1)} custom-call(s32[16]{0:T(128)S(1)} %reshape.18.target_ref, f32[4,256,256]{2,1,0:T(8,128)S(1)} %copy-done.8, bf16[16,256,256]{2,1,0:T(8,128)(2,1)S(1)} %bitcast.13, bf16[4,256,256]{2,1,0:T(8,128)(2,1)S(1)} %copy-done.17, bf16[4,256,256]{2,1,0:T(8,128)(2,1)S(1)} %copy-done.18), custom_call_target="tpu_custom_call" | custom-call | tf_op jit(solution)/shard_map/pallas_call | solution.py:129
  (190 shorter events, 43.6 us)
Async XLA Ops:
  1.2 21.9 %collective-permute-start = (bf16[3,512,256]{2,1,0:T(8,128)(2,1)S(1)}, bf16[3,512,256]{2,1,0:T(8,128)(2,1)S(1)}, u32[]{:S(2)}, u32[]{:S(2)}) collective-permute-start(bf16[3,512,256]{2,1,0:T(8,128)(2,1)S(1)} %constant_dynamic-slice_fusion), channel_id=1, source_target_pairs={{0,3},{1,0},{2,1},{3,2},{4,7},{5,4},{6,5},{7,6},{8,11},{9,8},{10,9... | collective-permute-start | bytes 2359304 | tf_op jit(solution)/shard_map/ppermute | solution.py:203
  24.6 19.9 %collective-permute-start.1 = (bf16[3,512,256]{2,1,0:T(8,128)(2,1)S(1)}, bf16[3,512,256]{2,1,0:T(8,128)(2,1)}, u32[]{:S(2)}, u32[]{:S(2)}) collective-permute-start(bf16[3,512,256]{2,1,0:T(8,128)(2,1)S(1)} %collective-permute-done.refs_10_), channel_id=1, source_target_pairs={{0,3},{1,0},{2,1},{3,2},{4,7},{5,4},{6,5},{7,6},{8,11},{9,8},{10,9... | collective-permute-start | bytes 2359304 | tf_op jit(solution)/shard_map/ppermute | solution.py:203
  28.9 20.5 %collective-permute-start.21 = (bf16[3,512,256]{2,1,0:T(8,128)(2,1)S(1)}, bf16[3,512,256]{2,1,0:T(8,128)(2,1)S(1)}, u32[]{:S(2)}, u32[]{:S(2)}) collective-permute-start(bf16[3,512,256]{2,1,0:T(8,128)(2,1)S(1)} %collective-permute-done.refs_10_), channel_id=1, source_target_pairs={{0,8},{4,12},{8,0},{12,4},{16,24},{20,28},{24,16},{28,20},{1,9},{5... | collective-permute-start | bytes 2359304 | tf_op jit(solution)/shard_map/ppermute | solution.py:140
  30.4 20.7 %collective-permute-start.25 = (bf16[3,512,256]{2,1,0:T(8,128)(2,1)S(1)}, bf16[3,512,256]{2,1,0:T(8,128)(2,1)S(1)}, u32[]{:S(2)}, u32[]{:S(2)}) collective-permute-start(bf16[3,512,256]{2,1,0:T(8,128)(2,1)S(1)} %collective-permute-done.refs_10_), channel_id=1, source_target_pairs={{0,4},{4,0},{8,12},{12,8},{16,20},{20,16},{24,28},{28,24},{1,5},{5... | collective-permute-start | bytes 2359304 | tf_op jit(solution)/shard_map/ppermute | solution.py:140
  44.5 27.1 %collective-permute-start.13 = (bf16[3,512,256]{2,1,0:T(8,128)(2,1)}, bf16[3,512,256]{2,1,0:T(8,128)(2,1)}, u32[]{:S(2)}, u32[]{:S(2)}) collective-permute-start(bf16[3,512,256]{2,1,0:T(8,128)(2,1)} %collective-permute-done.1.refs_10_), channel_id=1, source_target_pairs={{0,16},{4,20},{8,24},{12,28},{16,0},{20,4},{24,8},{28,12},{1,17},{... | collective-permute-start | bytes 2359304 | tf_op jit(solution)/shard_map/ppermute | solution.py:140
  49.4 21.0 %collective-permute-start.24 = (bf16[3,256,256]{2,1,0:T(8,128)(2,1)S(1)}, bf16[3,256,256]{2,1,0:T(8,128)(2,1)S(1)}, u32[]{:S(2)}, u32[]{:S(2)}) collective-permute-start(bf16[3,256,256]{2,1,0:T(8,128)(2,1)S(1)} %slice.29), channel_id=1, source_target_pairs={{0,16},{4,20},{8,24},{12,28},{16,0},{20,4},{24,8},{28,12},{1,17},{... | collective-permute-start | bytes 1179656 | tf_op jit(solution)/shard_map/ppermute | solution.py:140
  49.7 22.7 %collective-permute-start.2 = (bf16[3,512,256]{2,1,0:T(8,128)(2,1)}, bf16[3,512,256]{2,1,0:T(8,128)(2,1)S(1)}, u32[]{:S(2)}, u32[]{:S(2)}) collective-permute-start(bf16[3,512,256]{2,1,0:T(8,128)(2,1)} %collective-permute-done.1.refs_10_), channel_id=1, source_target_pairs={{0,3},{1,0},{2,1},{3,2},{4,7},{5,4},{6,5},{7,6},{8,11},{9,8},{10,9... | collective-permute-start | bytes 2359304 | tf_op jit(solution)/shard_map/ppermute | solution.py:203
  51.9 21.7 %collective-permute-start.12 = (bf16[3,512,256]{2,1,0:T(8,128)(2,1)}, bf16[3,512,256]{2,1,0:T(8,128)(2,1)S(1)}, u32[]{:S(2)}, u32[]{:S(2)}) collective-permute-start(bf16[3,512,256]{2,1,0:T(8,128)(2,1)} %collective-permute-done.1.refs_10_), channel_id=1, source_target_pairs={{0,8},{4,12},{8,0},{12,4},{16,24},{20,28},{24,16},{28,20},{1,9},{5... | collective-permute-start | bytes 2359304 | tf_op jit(solution)/shard_map/ppermute | solution.py:140
  72.4 37.0 %collective-permute-start.4 = (bf16[3,512,256]{2,1,0:T(8,128)(2,1)S(1)}, bf16[3,512,256]{2,1,0:T(8,128)(2,1)S(1)}, u32[]{:S(2)}, u32[]{:S(2)}) collective-permute-start(bf16[3,512,256]{2,1,0:T(8,128)(2,1)S(1)} %collective-permute-done.2.refs_6_), channel_id=1, source_target_pairs={{0,16},{4,20},{8,24},{12,28},{16,0},{20,4},{24,8},{28,12},{1,17},{... | collective-permute-start | bytes 2359304 | tf_op jit(solution)/shard_map/ppermute | solution.py:140
  73.6 35.9 %collective-permute-start.3 = (bf16[3,512,256]{2,1,0:T(8,128)(2,1)S(1)}, bf16[3,512,256]{2,1,0:T(8,128)(2,1)S(1)}, u32[]{:S(2)}, u32[]{:S(2)}) collective-permute-start(bf16[3,512,256]{2,1,0:T(8,128)(2,1)S(1)} %collective-permute-done.2.refs_6_), channel_id=1, source_target_pairs={{0,8},{4,12},{8,0},{12,4},{16,24},{20,28},{24,16},{28,20},{1,9},{5... | collective-permute-start | bytes 2359304 | tf_op jit(solution)/shard_map/ppermute | solution.py:140
  77.8 24.0 %collective-permute-start.14 = (bf16[3,256,256]{2,1,0:T(8,128)(2,1)}, bf16[3,256,256]{2,1,0:T(8,128)(2,1)S(1)}, u32[]{:S(2)}, u32[]{:S(2)}) collective-permute-start(bf16[3,256,256]{2,1,0:T(8,128)(2,1)} %slice.26), channel_id=1, source_target_pairs={{0,8},{4,12},{8,0},{12,4},{16,24},{20,28},{24,16},{28,20},{1,9},{5... | collective-permute-start | bytes 1179656 | tf_op jit(solution)/shard_map/ppermute | solution.py:140
  79.9 21.9 %collective-permute-start.15 = (bf16[3,256,256]{2,1,0:T(8,128)(2,1)}, bf16[3,256,256]{2,1,0:T(8,128)(2,1)}, u32[]{:S(2)}, u32[]{:S(2)}) collective-permute-start(bf16[3,256,256]{2,1,0:T(8,128)(2,1)} %slice.27), channel_id=1, source_target_pairs={{0,16},{4,20},{8,24},{12,28},{16,0},{20,4},{24,8},{28,12},{1,17},{... | collective-permute-start | bytes 1179656 | tf_op jit(solution)/shard_map/ppermute | solution.py:140
  80.8 47.2 %collective-permute-start.16 = (bf16[3,512,256]{2,1,0:T(8,128)(2,1)}, bf16[3,512,256]{2,1,0:T(8,128)(2,1)}, u32[]{:S(2)}, u32[]{:S(2)}) collective-permute-start(bf16[3,512,256]{2,1,0:T(8,128)(2,1)} %collective-permute-done.1.refs_10_), channel_id=1, source_target_pairs={{0,4},{4,0},{8,12},{12,8},{16,20},{20,16},{24,28},{28,24},{1,5},{5... | collective-permute-start | bytes 2359304 | tf_op jit(solution)/shard_map/ppermute | solution.py:140
  101.8 30.3 %collective-permute-start.17 = (bf16[3,512,256]{2,1,0:T(8,128)(2,1)}, bf16[3,512,256]{2,1,0:T(8,128)(2,1)}, u32[]{:S(2)}, u32[]{:S(2)}) collective-permute-start(bf16[3,512,256]{2,1,0:T(8,128)(2,1)} %copy-done.29), channel_id=1, source_target_pairs={{0,4},{4,0},{8,12},{12,8},{16,20},{20,16},{24,28},{28,24},{1,5},{5... | collective-permute-start | bytes 2359304 | tf_op jit(solution)/shard_map/ppermute | solution.py:140
  101.8 30.6 %collective-permute-start.18 = (bf16[3,512,256]{2,1,0:T(8,128)(2,1)}, bf16[3,512,256]{2,1,0:T(8,128)(2,1)}, u32[]{:S(2)}, u32[]{:S(2)}) collective-permute-start(bf16[3,512,256]{2,1,0:T(8,128)(2,1)} %collective-permute-done.13.refs_12_), channel_id=1, source_target_pairs={{0,4},{4,0},{8,12},{12,8},{16,20},{20,16},{24,28},{28,24},{1,5},{5... | collective-permute-start | bytes 2359304 | tf_op jit(solution)/shard_map/ppermute | solution.py:140
  109.5 22.6 %collective-permute-start.20 = (bf16[3,256,256]{2,1,0:T(8,128)(2,1)}, bf16[3,256,256]{2,1,0:T(8,128)(2,1)S(1)}, u32[]{:S(2)}, u32[]{:S(2)}) collective-permute-start(bf16[3,256,256]{2,1,0:T(8,128)(2,1)} %collective-permute-done.15.refs_14_), channel_id=1, source_target_pairs={{0,4},{4,0},{8,12},{12,8},{16,20},{20,16},{24,28},{28,24},{1,5},{5... | collective-permute-start | bytes 1179656 | tf_op jit(solution)/shard_map/ppermute | solution.py:140
  128.0 52.7 %collective-permute-start.7 = (bf16[3,512,256]{2,1,0:T(8,128)(2,1)S(1)}, bf16[3,512,256]{2,1,0:T(8,128)(2,1)S(1)}, u32[]{:S(2)}, u32[]{:S(2)}) collective-permute-start(bf16[3,512,256]{2,1,0:T(8,128)(2,1)S(1)} %collective-permute-done.2.refs_6_), channel_id=1, source_target_pairs={{0,4},{4,0},{8,12},{12,8},{16,20},{20,16},{24,28},{28,24},{1,5},{5... | collective-permute-start | bytes 2359304 | tf_op jit(solution)/shard_map/ppermute | solution.py:140
  128.1 26.8 %collective-permute-start.5 = (bf16[3,256,256]{2,1,0:T(8,128)(2,1)S(1)}, bf16[3,256,256]{2,1,0:T(8,128)(2,1)S(1)}, u32[]{:S(2)}, u32[]{:S(2)}) collective-permute-start(bf16[3,256,256]{2,1,0:T(8,128)(2,1)S(1)} %slice.24), channel_id=1, source_target_pairs={{0,8},{4,12},{8,0},{12,4},{16,24},{20,28},{24,16},{28,20},{1,9},{5... | collective-permute-start | bytes 1179656 | tf_op jit(solution)/shard_map/ppermute | solution.py:140
  132.1 23.6 %collective-permute-start.6 = (bf16[3,256,256]{2,1,0:T(8,128)(2,1)S(1)}, bf16[3,256,256]{2,1,0:T(8,128)(2,1)S(1)}, u32[]{:S(2)}, u32[]{:S(2)}) collective-permute-start(bf16[3,256,256]{2,1,0:T(8,128)(2,1)S(1)} %slice.25), channel_id=1, source_target_pairs={{0,16},{4,20},{8,24},{12,28},{16,0},{20,4},{24,8},{28,12},{1,17},{... | collective-permute-start | bytes 1179656 | tf_op jit(solution)/shard_map/ppermute | solution.py:140
  132.1 48.6 %collective-permute-start.8 = (bf16[3,512,256]{2,1,0:T(8,128)(2,1)S(1)}, bf16[3,512,256]{2,1,0:T(8,128)(2,1)S(1)}, u32[]{:S(2)}, u32[]{:S(2)}) collective-permute-start(bf16[3,512,256]{2,1,0:T(8,128)(2,1)S(1)} %collective-permute-done.3.refs_7_), channel_id=1, source_target_pairs={{0,4},{4,0},{8,12},{12,8},{16,20},{20,16},{24,28},{28,24},{1,5},{5... | collective-permute-start | bytes 2359304 | tf_op jit(solution)/shard_map/ppermute | solution.py:140
  132.3 48.4 %collective-permute-start.9 = (bf16[3,512,256]{2,1,0:T(8,128)(2,1)S(1)}, bf16[3,512,256]{2,1,0:T(8,128)(2,1)S(1)}, u32[]{:S(2)}, u32[]{:S(2)}) collective-permute-start(bf16[3,512,256]{2,1,0:T(8,128)(2,1)S(1)} %collective-permute-done.4.refs_8_), channel_id=1, source_target_pairs={{0,4},{4,0},{8,12},{12,8},{16,20},{20,16},{24,28},{28,24},{1,5},{5... | collective-permute-start | bytes 2359304 | tf_op jit(solution)/shard_map/ppermute | solution.py:140
  154.9 25.7 %collective-permute-start.10 = (bf16[3,256,256]{2,1,0:T(8,128)(2,1)S(1)}, bf16[3,256,256]{2,1,0:T(8,128)(2,1)S(1)}, u32[]{:S(2)}, u32[]{:S(2)}) collective-permute-start(bf16[3,256,256]{2,1,0:T(8,128)(2,1)S(1)} %collective-permute-done.5.refs_9_), channel_id=1, source_target_pairs={{0,4},{4,0},{8,12},{12,8},{16,20},{20,16},{24,28},{28,24},{1,5},{5... | collective-permute-start | bytes 1179656 | tf_op jit(solution)/shard_map/ppermute | solution.py:140
  155.7 25.0 %collective-permute-start.11 = (bf16[3,256,256]{2,1,0:T(8,128)(2,1)S(1)}, bf16[3,256,256]{2,1,0:T(8,128)(2,1)S(1)}, u32[]{:S(2)}, u32[]{:S(2)}) collective-permute-start(bf16[3,256,256]{2,1,0:T(8,128)(2,1)S(1)} %collective-permute-done.6.refs_10_), channel_id=1, source_target_pairs={{0,4},{4,0},{8,12},{12,8},{16,20},{20,16},{24,28},{28,24},{1,5},{5... | collective-permute-start | bytes 1179656 | tf_op jit(solution)/shard_map/ppermute | solution.py:140
  188.3 30.3 %all-to-all-start = ((bf16[8,2,256,256]{3,2,1,0:T(8,128)(2,1)}), bf16[8,2,256,256]{3,2,1,0:T(8,128)(2,1)S(1)}, u32[]{:S(2)}, u32[]{:S(2)}) async-start(bf16[8,2,256,256]{3,2,1,0:T(8,128)(2,1)} %bitcast.14), calls=%async_computation | async-start | bytes 4194304 | tf_op jit(solution)/shard_map/all_to_all | solution.py:211
  (68 other events, 738.2 us)

commit v3 on v2

v3 whole, which is shorter than its diff:
```python
import functools

import jax
import jax.numpy as jnp
from jax import lax
from jax.experimental import pallas as pl
from jax.experimental.pallas import tpu as pltpu
from jax.sharding import PartitionSpec as P

SMEM = pl.BlockSpec(memory_space=pltpu.SMEM)
VMEM = pl.BlockSpec(memory_space=pltpu.VMEM)
HBM = pl.BlockSpec(memory_space=pltpu.HBM)
MIB = 1 << 20


def add_pairs(shard, pairs, hist_ref, table, acc):
    src_ref, lag_ref, class_ref, dest_ref = pairs
    panels = table.shape[2]
    steps = hist_ref.shape[2] // panels
    lags = table.shape[1] // panels
    widths = range(min(steps, lags), 0, -1)

    @pl.loop(0, src_ref.shape[0])
    def _(i):
        offset = lag_ref[i] - shard * lags
        first = jnp.maximum(offset, 0)
        count = jnp.minimum(offset + steps, lags) - first

        @pl.when(count > 0)
        def _():
            rows = pl.multiple_of(first * panels, panels)
            columns = pl.multiple_of((first - offset) * panels, panels)
            for n in widths:
                @pl.when(count == n)
                def _():
                    acc[dest_ref[i]] += jnp.dot(
                        hist_ref[src_ref[i], :, pl.ds(columns, n * panels)],
                        table[class_ref[i], pl.ds(rows, n * panels), :],
                        preferred_element_type=jnp.float32,
                    )


def round_kernel(places, groups, begun, narrow, *refs):
    refs = list(refs)
    where = refs.pop(0)
    pairs = [[refs.pop(0) for _ in range(4)] for _ in range(groups)]
    hist_ref = refs.pop(0)
    pieces = [refs.pop(0) for _ in places]
    for _ in range(groups if begun else 0):
        refs.pop(0)
    sums = [refs.pop(0) for _ in range(groups)]
    rounded = refs.pop(0) if narrow else None
    table, sems = refs
    shard, group = where[0], where[1]

    copies = []
    for n, ((mask, height, klass), piece) in enumerate(zip(places, pieces)):
        start = pl.multiple_of((group ^ mask) * height, 16)
        count, rows, _ = piece.shape
        copies.append(
            pltpu.make_async_copy(
                piece, table.at[pl.ds(klass, count), pl.ds(start, rows), :], sems.at[n]
            )
        )
    for copy in copies:
        copy.start()
    if not begun:
        for acc in sums:
            acc[...] = jnp.zeros_like(acc)
    for copy in copies:
        copy.wait()
    for group_pairs, acc in zip(pairs, sums):
        add_pairs(shard, group_pairs, hist_ref, table, acc)
    if narrow:
        rounded[...] = sums[0][...].astype(rounded.dtype)


def run_round(shard, group, rows, pieces, pair_lists, hist_t, sums, counts, narrow=False):
    owned, excite, depth = hist_t.shape
    panels = pieces[0][2].shape[2]
    classes = max(klass + value.shape[0] for _, klass, value in pieces)
    places = [(mask, value.shape[1], klass) for mask, klass, value in pieces]
    groups = len(pair_lists)
    shapes = [(count, excite, panels) for count in counts]
    outs = [jax.ShapeDtypeStruct(s, jnp.float32) for s in shapes]
    if narrow:
        outs.append(jax.ShapeDtypeStruct(shapes[0], jnp.bfloat16))
    before = list(sums) if sums is not None else []
    first_sum = 1 + 4 * groups + 1 + len(places)
    pair_count = sum(lists[0].shape[0] for lists in pair_lists)
    return pl.pallas_call(
        functools.partial(round_kernel, places, groups, sums is not None, narrow),
        out_shape=outs,
        in_specs=[SMEM] * (1 + 4 * groups) + [VMEM] + [HBM] * len(places) + [VMEM] * len(before),
        out_specs=[VMEM] * len(outs),
        scratch_shapes=[
            pltpu.VMEM((classes, rows, panels), jnp.bfloat16),
            pltpu.SemaphoreType.DMA((len(places),)),
        ],
        input_output_aliases={first_sum + n: n for n in range(len(before))},
        compiler_params=pltpu.CompilerParams(vmem_limit_bytes=16 * MIB),
        cost_estimate=pl.CostEstimate(
            flops=2 * pair_count * panels * depth * excite,
            bytes_accessed=2 * classes * rows * panels,
            transcendentals=0,
        ),
    )(
        jnp.stack([shard, group]).astype(jnp.int32),
        *[x for lists in pair_lists for x in lists],
        hist_t,
        *[value for _, _, value in pieces],
        *before,
    )


def update_kernel(target_ref, near_ref, recv_ref, inverse_ref, incident_ref, out_ref, total):
    total[...] = near_ref[...]

    @pl.loop(0, target_ref.shape[0])
    def _(i):
        total[target_ref[i]] += recv_ref[i].astype(jnp.float32)

    for t in range(out_ref.shape[0]):
        residual = (incident_ref[t].astype(jnp.float32) - total[t].T).astype(jnp.bfloat16)
        out_ref[t] = jnp.dot(
            inverse_ref[t], residual, preferred_element_type=jnp.float32
        ).astype(out_ref.dtype)


def update(target, near, recv, inverse, incident):
    return pl.pallas_call(
        update_kernel,
        out_shape=jax.ShapeDtypeStruct(incident.shape, jnp.bfloat16),
        in_specs=[SMEM] + [VMEM] * 4,
        out_specs=VMEM,
        scratch_shapes=[pltpu.VMEM(near.shape, jnp.float32)],
        compiler_params=pltpu.CompilerParams(vmem_limit_bytes=32 * MIB),
    )(target, near, recv, inverse, incident)


def swap(value, bit, peers):
    return lax.ppermute(value, "grp", [(i, i ^ bit) for i in range(peers)])


def exchange(own, corner, peers):
    held = [(0, own, corner)]
    bit = 8
    while bit < peers:
        held += [(mask ^ bit, swap(a, bit, peers), swap(c, bit, peers)) for mask, a, c in held]
        bit *= 2
    return [(mask, a, swap(a, 2, peers), swap(a, 4, peers), c) for mask, a, c in held]


def finish(held, peers):
    found = []
    for mask, own, across, along, corner in held:
        third = corner.shape[0]
        found += [
            (mask, 0, own),
            (mask ^ 2, 0, across),
            (mask ^ 4, 0, along),
            (mask ^ 6, 0, corner),
            (mask ^ 6, third, swap(along[third : 2 * third], 2, peers)),
            (mask ^ 6, 2 * third, swap(across[2 * third :], 4, peers)),
        ]
    return found + [(mask ^ 1, klass, swap(value, 1, peers)) for mask, klass, value in found]


def per_device(
    weights,
    history,
    send_patch,
    send_lag,
    send_class,
    recv_target,
    local_src,
    local_lag,
    local_class,
    local_target,
    inverse_blocks,
    incident,
):
    classes, rows, _ = weights.shape
    owned = history.shape[0]
    peers, slots = send_patch.shape
    served_count = peers * slots
    height = rows // peers
    group = lax.axis_index("grp")
    lane = lax.axis_index("lag")
    lanes = lax.axis_size("lag")
    ring = [(i, (i - 1) % lanes) for i in range(lanes)]

    hist_t = jnp.swapaxes(history, 1, 2)
    served_pairs = (
        send_patch.reshape(-1),
        send_lag.reshape(-1),
        send_class.reshape(-1),
        jnp.arange(served_count, dtype=jnp.int32),
    )
    local_pairs = (local_src, local_lag, local_class, local_target)
    pairs = [served_pairs, local_pairs]
    counts = [served_count, owned]

    own = lax.dynamic_slice_in_dim(weights, group * height, height, 1)
    corner = lax.dynamic_slice_in_dim(
        weights[: classes // 3], (group ^ 6) * height, height, 1
    )
    sums = run_round(lane, group * 0, rows, [(0, 0, weights)], pairs, hist_t, None, counts)
    pieces = None
    for step in range(1, lanes):
        own = lax.ppermute(own, "lag", ring)
        own, corner = lax.optimization_barrier((own, corner))
        corner = lax.ppermute(corner, "lag", ring)
        if step == 1:
            own, sums = lax.optimization_barrier((own, sums))
        held = exchange(own, corner, peers)
        if step > 1:
            sums = run_round(shard, group, rows, pieces, pairs, hist_t, sums, counts)
            values, sums = lax.optimization_barrier(([h[1:] for h in held], sums))
            held = [(h[0], *v) for h, v in zip(held, values)]
        pieces = finish(held, peers)
        shard = lax.rem(lane + step, lanes)
    _, served = run_round(
        shard, group, rows, pieces, pairs[:1], hist_t, sums[:1], counts[:1], narrow=True
    )
    recv = lax.all_to_all(
        served.reshape(peers, slots, *served.shape[1:]), "grp", split_axis=0, concat_axis=0, tiled=True
    ).reshape(served.shape)
    near = run_round(shard, group, rows, pieces, pairs[1:], hist_t, sums[1:], counts[1:])[0]
    return update(recv_target.reshape(-1), near, recv, inverse_blocks, incident)


def solution(mesh):
    both = ("grp", "lag")
    return jax.shard_map(
        per_device,
        mesh=mesh,
        in_specs=(
            P(None, "lag", None),
            P(both, None, None),
            P(both, None),
            P(both, None),
            P(both, None),
            P(both, None),
            P(both),
            P(both),
            P(both),
            P(both),
            P(both, None, None),
            P(both, None, None),
        ),
        out_specs=P(both, None, None),
        check_vma=False,
    )
```

time: 226 us -> 207 us (0.916)
  waiting for transfers between devices: 75.6 us -> 55.5 us
  local copies, waits for them, and re-layouts: 45.3 us -> 59.2 us
  Pallas kernels: 68.3 us -> 55 us
    ppermute x27 -> x30, waiting for transfers between devices: 52.8 us -> 23.7 us  [swap(): return lax.ppermute(value, 'grp', [(i, i ^ bit) for i in range(peers)])]
    pallas_call x5, Pallas kernels: 65.9 us -> 52.6 us  [run_round(): pl.pallas_call(functools.partial(round_kernel, places, groups, sums is no...]
    unnamed x127 -> x93, local copies, waits for them, and re-layouts: 40.1 us -> 52.1 us
    ppermute x3 -> x6, waiting for transfers between devices: 17.2 us -> 24 us  [the longest x3 24 us: per_device(): corner = lax.ppermute(corner, 'lag', ring)]
    ppermute x3 -> x6, starting transfers between devices: 10.8 us -> 12.8 us  [the longest x3 8.34 us: per_device(): own = lax.ppermute(own, 'lag', ring)]
    slice x6 -> x8, local copies, waits for them, and re-layouts: 3.64 us -> 4.74 us  [the longest x3 3.09 us: finish(): along[third:2 * third]]
    ppermute x27 -> x30, starting transfers between devices: 18.7 us -> 18.8 us  [swap(): return lax.ppermute(value, 'grp', [(i, i ^ bit) for i in range(peers)])]
  transfers between devices with their start and end apart: 31 -> 37, of which waited for: 8 -> 12; matrix products, arithmetic and copies ran while one was open for 5% -> 4% of each run, Pallas kernels for 27% -> 23%
where the time goes in v3:
time: 207 us; the launch traced here: 206 us
  local copies, waits for them, and re-layouts  59.2 us (29%)
  waiting for transfers between devices  55.5 us (27%)
  Pallas kernels  55 us (27%)
  starting transfers between devices  35.3 us (17%)
    pallas_call x5, Pallas kernels, run_round(): pl.pallas_call(functools.partial(round_kernel, places, groups, sums is no...  52.6 us
    unnamed x93, local copies, waits for them, and re-layouts  52.1 us
    ppermute x3, waiting for transfers between devices, per_device(): corner = lax.ppermute(corner, 'lag', ring)  24 us
    ppermute x30, waiting for transfers between devices, swap(): return lax.ppermute(value, 'grp', [(i, i ^ bit) for i in range(peers)])  23.7 us
    ppermute x30, starting transfers between devices, swap(): return lax.ppermute(value, 'grp', [(i, i ^ bit) for i in range(peers)])  18.8 us
    ppermute x3, starting transfers between devices, per_device(): own = lax.ppermute(own, 'lag', ring)  8.34 us
    all_to_all x1, waiting for transfers between devices, per_device(): lax.all_to_all(served.reshape(peers, slots, *served.shape[1:]), 'grp', sp...  7.84 us
    ppermute x3, starting transfers between devices, per_device(): corner = lax.ppermute(corner, 'lag', ring)  4.47 us
  transfers between devices with their start and end apart: 37, of which 12 were waited for; matrix products, arithmetic and copies ran while one was open for 4% of the time, Pallas kernels for 23%

profile of v3, /device:TPU:0, one launch (start us, length us, event | category | flops | bytes accessed | tf_op | source)
XLA Modules:
  0.0 205.7 jit_solution(8550195792103414147)
XLA Ops:
  2.1 5.1 %collective-permute-start = (bf16[3,512,256]{2,1,0:T(8,128)(2,1)}, bf16[3,512,256]{2,1,0:T(8,128)(2,1)}, u32[]{:S(2)}, u32[]{:S(2)}) collective-permute-start(bf16[3,512,256]{2,1,0:T(8,128)(2,1)} %constant_dynamic-slice_fusion.1), channel_id=1, source_target_pairs={{0,3},{1,0},{2,1},{3,2},{4,7},{5,4},{6,5},{7,6},{8,11},{9,8},{10,9... | collective-permute-start | bytes 2359304 | tf_op jit(solution)/shard_map/ppermute | solution.py:211
  7.2 6.3 %copy.25 = bf16[4,2048,256]{1,2,0:T(8,128)(2,1)} copy(bf16[4,2048,256]{2,1,0:T(8,128)(2,1)} %param.13) | data formatting | bytes 8388608 | tf_op args[1]
  16.3 2.8 %copy-done.6 = bf16[3,4096,256]{2,1,0:T(8,128)(2,1)S(1)} copy-done((bf16[3,4096,256]{2,1,0:T(8,128)(2,1)S(1)}, bf16[3,4096,256]{2,1,0:T(8,128)(2,1)}, u32[]{:S(2)}) %copy-start.6) | copy-done | bytes 6291480
  19.1 7.4 %shard_map.118 = (f32[16,256,256]{2,1,0:T(8,128)S(1)}, f32[4,256,256]{2,1,0:T(8,128)S(1)}) custom-call(s32[2]{0:T(128)S(1)} %pad_add_fusion.1.refs_0_, s32[16]{0:T(128)S(1)} %reshape.19.refs_1_, s32[16]{0:T(128)S(1)} %reshape.20.refs_2_, s32[16]{0:T(128)S(1)} %reshape.21.refs_3_, s32[16]{0:T(128)S(1)} %iota.9.refs_4_, s32[48]{0:T(128)S(1)} %copy-done.30, ...), custom_call_target="tpu_custom_call" | custom-call | flops 17179869184 | bytes 6291456 | tf_op jit(solution)/shard_map/pallas_call | solution.py:91
  30.2 5.2 %collective-permute-start.10 = (bf16[3,512,256]{2,1,0:T(8,128)(2,1)}, bf16[3,512,256]{2,1,0:T(8,128)(2,1)S(1)}, u32[]{:S(2)}, u32[]{:S(2)}) collective-permute-start(bf16[3,512,256]{2,1,0:T(8,128)(2,1)} %collective-permute-done.refs_10_), channel_id=1, source_target_pairs={{0,8},{4,12},{8,0},{12,4},{16,24},{20,28},{24,16},{28,20},{1,9},{5... | collective-permute-start | bytes 2359304 | tf_op jit(solution)/shard_map/ppermute | solution.py:142
  35.3 2.5 %collective-permute-start.1 = (bf16[3,512,256]{2,1,0:T(8,128)(2,1)}, bf16[3,512,256]{2,1,0:T(8,128)(2,1)}, u32[]{:S(2)}, u32[]{:S(2)}) collective-permute-start(bf16[3,512,256]{2,1,0:T(8,128)(2,1)} %collective-permute-done.refs_10_), channel_id=1, source_target_pairs={{0,3},{1,0},{2,1},{3,2},{4,7},{5,4},{6,5},{7,6},{8,11},{9,8},{10,9... | collective-permute-start | bytes 2359304 | tf_op jit(solution)/shard_map/ppermute | solution.py:211
  38.9 22.6 %collective-permute-done.2.refs_13_ = bf16[1,512,256]{2,1,0:T(8,128)(2,1)S(1)} collective-permute-done((bf16[1,512,256]{2,1,0:T(8,128)(2,1)S(1)}, bf16[1,512,256]{2,1,0:T(8,128)(2,1)S(1)}, u32[]{:S(2)}, u32[]{:S(2)}) %collective-permute-start.2) | collective-permute-done | bytes 262176 | tf_op jit(solution)/shard_map/ppermute | solution.py:213
  64.6 7.2 %collective-permute-done.12.refs_14_ = bf16[1,512,256]{2,1,0:T(8,128)(2,1)S(1)} collective-permute-done((bf16[1,512,256]{2,1,0:T(8,128)(2,1)S(1)}, bf16[1,512,256]{2,1,0:T(8,128)(2,1)S(1)}, u32[]{:S(2)}, u32[]{:S(2)}) %collective-permute-start.12) | collective-permute-done | bytes 262176 | tf_op jit(solution)/shard_map/ppermute | solution.py:142
  77.9 2.2 %copy-done.1 = bf16[4,2048,256]{1,2,0:T(8,128)(2,1)S(1)} copy-done((bf16[4,2048,256]{1,2,0:T(8,128)(2,1)S(1)}, bf16[4,2048,256]{1,2,0:T(8,128)(2,1)}, u32[]{:S(2)}) %copy-start.1) | copy-done | bytes 4194328
  82.2 2.2 %copy-done.35 = f32[16,256,256]{2,1,0:T(8,128)S(1)} copy-done((f32[16,256,256]{2,1,0:T(8,128)S(1)}, f32[16,256,256]{2,1,0:T(8,128)}, u32[]{:S(2)}) %copy-start.35) | copy-done | bytes 4194328
  84.4 13.0 %shard_map.119 = (f32[16,256,256]{2,1,0:T(8,128)S(1)}, f32[4,256,256]{2,1,0:T(8,128)S(1)}) custom-call(s32[2]{0:T(128)S(1)} %pad_add_fusion.3.refs_0_, s32[16]{0:T(128)S(1)} %reshape.19.refs_1_, s32[16]{0:T(128)S(1)} %reshape.20.refs_2_, s32[16]{0:T(128)S(1)} %reshape.21.refs_3_, ...), custom_call_target="tpu_custom_call", output_to_operand_aliasing={{0}: (22, {}), {1}: (23, {})} | custom-call | flops 17179869184 | bytes 6291456 | tf_op jit(solution)/shard_map/pallas_call | solution.py:91
  103.5 3.3 %collective-permute-start.21 = (bf16[1,512,256]{2,1,0:T(8,128)(2,1)S(1)}, bf16[1,512,256]{2,1,0:T(8,128)(2,1)S(1)}, u32[]{:S(2)}, u32[]{:S(2)}) collective-permute-start(bf16[1,512,256]{2,1,0:T(8,128)(2,1)S(1)} %slice.25), channel_id=1, source_target_pairs={{0,16},{4,20},{8,24},{12,28},{16,0},{20,4},{24,8},{28,12},{1,17},{... | collective-permute-start | bytes 786440 | tf_op jit(solution)/shard_map/ppermute | solution.py:142
  106.8 3.1 %collective-permute-done.20.refs_14_ = bf16[1,512,256]{2,1,0:T(8,128)(2,1)S(1)} collective-permute-done((bf16[1,512,256]{2,1,0:T(8,128)(2,1)S(1)}, bf16[1,512,256]{2,1,0:T(8,128)(2,1)S(1)}, u32[]{:S(2)}, u32[]{:S(2)}) %collective-permute-start.20) | collective-permute-done | bytes 262176 | tf_op jit(solution)/shard_map/ppermute | solution.py:142
  110.0 3.8 %collective-permute-done.21.refs_15_ = bf16[1,512,256]{2,1,0:T(8,128)(2,1)S(1)} collective-permute-done((bf16[1,512,256]{2,1,0:T(8,128)(2,1)S(1)}, bf16[1,512,256]{2,1,0:T(8,128)(2,1)S(1)}, u32[]{:S(2)}, u32[]{:S(2)}) %collective-permute-start.21) | collective-permute-done | bytes 262176 | tf_op jit(solution)/shard_map/ppermute | solution.py:142
  125.2 2.2 %copy-done.37 = f32[16,256,256]{2,1,0:T(8,128)S(1)} copy-done((f32[16,256,256]{2,1,0:T(8,128)S(1)}, f32[16,256,256]{2,1,0:T(8,128)}, u32[]{:S(2)}) %copy-start.37) | copy-done | bytes 4194328
  127.4 15.2 %shard_map.120 = (f32[16,256,256]{2,1,0:T(8,128)S(1)}, f32[4,256,256]{2,1,0:T(8,128)S(1)}) custom-call(s32[2]{0:T(128)S(1)} %pad_add_fusion.2.refs_0_, s32[16]{0:T(128)S(1)} %reshape.19.refs_1_, s32[16]{0:T(128)S(1)} %reshape.20.refs_2_, s32[16]{0:T(128)S(1)} %reshape.21.refs_3_, ...), custom_call_target="tpu_custom_call", output_to_operand_aliasing={{0}: (22, {}), {1}: (23, {})} | custom-call | flops 17179869184 | bytes 6291456 | tf_op jit(solution)/shard_map/pallas_call | solution.py:91
  147.8 6.4 %collective-permute-done.28.refs_10_ = bf16[1,512,256]{2,1,0:T(8,128)(2,1)S(1)} collective-permute-done((bf16[1,512,256]{2,1,0:T(8,128)(2,1)S(1)}, bf16[1,512,256]{2,1,0:T(8,128)(2,1)S(1)}, u32[]{:S(2)}, u32[]{:S(2)}) %collective-permute-start.28) | collective-permute-done | bytes 262176 | tf_op jit(solution)/shard_map/ppermute | solution.py:142
  158.2 2.5 %copy-done.3 = bf16[4,2048,256]{1,2,0:T(8,128)(2,1)S(1)} copy-done((bf16[4,2048,256]{1,2,0:T(8,128)(2,1)S(1)}, bf16[4,2048,256]{1,2,0:T(8,128)(2,1)}, u32[]{:S(2)}) %copy-start.3) | copy-done | bytes 4194328
  163.8 5.8 %shard_map.122 = (f32[16,256,256]{2,1,0:T(8,128)S(1)}, bf16[16,256,256]{2,1,0:T(8,128)(2,1)S(1)}) custom-call(s32[2]{0:T(128)S(1)} %pad_add_fusion.refs_0_, s32[16]{0:T(128)S(1)} %reshape.19.refs_1_, s32[16]{0:T(128)S(1)} %reshape.20.refs_2_, s32[16]{0:T(128)S(1)} %reshape.21.refs_3_, s32[16]{0:T(128)S(1)} %iota.12.refs_4_, ...), custom_call_target="tpu_custom_call", output_to_operand_aliasing={{0}: (18, {})} | custom-call | flops 4294967296 | bytes 6291456 | tf_op jit(solution)/shard_map/pallas_call | solution.py:91
  171.0 3.7 %all-to-all-start = ((bf16[8,2,256,256]{3,2,1,0:T(8,128)(2,1)}), bf16[8,2,256,256]{3,2,1,0:T(8,128)(2,1)S(1)}, u32[]{:S(2)}, u32[]{:S(2)}) async-start(bf16[8,2,256,256]{3,2,1,0:T(8,128)(2,1)} %bitcast.14), calls=%async_computation | async-start | bytes 4194304 | tf_op jit(solution)/shard_map/all_to_all | solution.py:226
  174.9 2.2 %copy-done.4 = bf16[4,2048,256]{1,2,0:T(8,128)(2,1)S(1)} copy-done((bf16[4,2048,256]{1,2,0:T(8,128)(2,1)S(1)}, bf16[4,2048,256]{1,2,0:T(8,128)(2,1)}, u32[]{:S(2)}) %copy-start.4) | copy-done | bytes 4194328
  182.2 11.2 %shard_map.121.near_ref = f32[4,256,256]{2,1,0:T(8,128)S(1)} custom-call(s32[2]{0:T(128)S(1)} %pad_add_fusion.refs_0_, s32[48]{0:T(128)S(1)} %copy-done.30, s32[48]{0:T(128)S(1)} %copy-done.31, s32[48]{0:T(128)S(1)} %copy-done.32, s32[48]{0:T(128)S(1)} %copy-done.33, bf16[4,256,2048]{2,1,0:T(8,128)(2,1)S(1)} %bitcast.13, ...), custom_call_target="tpu_custom_call", output_to_operand_aliasing={{}: (18, {})} | custom-call | flops 12884901888 | bytes 6291456 | tf_op jit(solution)/shard_map/pallas_call | solution.py:91
  193.4 7.8 %all-to-all-done = bf16[8,2,256,256]{3,2,1,0:T(8,128)(2,1)S(1)} async-done(((bf16[8,2,256,256]{3,2,1,0:T(8,128)(2,1)}), bf16[8,2,256,256]{3,2,1,0:T(8,128)(2,1)S(1)}, u32[]{:S(2)}, u32[]{:S(2)}) %all-to-all-start) | async-done | bytes 2097184 | tf_op jit(solution)/shard_map/all_to_all | solution.py:226
  203.4 2.4 %shard_map.123 = bf16[4,256,256]{2,1,0:T(8,128)(2,1)} custom-call(s32[16]{0:T(128)S(1)} %reshape.18.target_ref, f32[4,256,256]{2,1,0:T(8,128)S(1)} %shard_map.121.near_ref, bf16[16,256,256]{2,1,0:T(8,128)(2,1)S(1)} %bitcast.8, bf16[4,256,256]{2,1,0:T(8,128)(2,1)S(1)} %copy-done.7, bf16[4,256,256]{2,1,0:T(8,128)(2,1)S(1)} %copy-done.8), custom_call_target="tpu_custom_call" | custom-call | tf_op jit(solution)/shard_map/pallas_call | solution.py:131
  (171 shorter events, 59.4 us)
Async XLA Ops:
  2.1 28.1 %collective-permute-start = (bf16[3,512,256]{2,1,0:T(8,128)(2,1)}, bf16[3,512,256]{2,1,0:T(8,128)(2,1)}, u32[]{:S(2)}, u32[]{:S(2)}) collective-permute-start(bf16[3,512,256]{2,1,0:T(8,128)(2,1)} %constant_dynamic-slice_fusion.1), channel_id=1, source_target_pairs={{0,3},{1,0},{2,1},{3,2},{4,7},{5,4},{6,5},{7,6},{8,11},{9,8},{10,9... | collective-permute-start | bytes 2359304 | tf_op jit(solution)/shard_map/ppermute | solution.py:211
  30.2 31.4 %collective-permute-start.10 = (bf16[3,512,256]{2,1,0:T(8,128)(2,1)}, bf16[3,512,256]{2,1,0:T(8,128)(2,1)S(1)}, u32[]{:S(2)}, u32[]{:S(2)}) collective-permute-start(bf16[3,512,256]{2,1,0:T(8,128)(2,1)} %collective-permute-done.refs_10_), channel_id=1, source_target_pairs={{0,8},{4,12},{8,0},{12,4},{16,24},{20,28},{24,16},{28,20},{1,9},{5... | collective-permute-start | bytes 2359304 | tf_op jit(solution)/shard_map/ppermute | solution.py:142
  35.3 26.6 %collective-permute-start.11 = (bf16[3,512,256]{2,1,0:T(8,128)(2,1)}, bf16[3,512,256]{2,1,0:T(8,128)(2,1)}, u32[]{:S(2)}, u32[]{:S(2)}) collective-permute-start(bf16[3,512,256]{2,1,0:T(8,128)(2,1)} %collective-permute-done.refs_10_), channel_id=1, source_target_pairs={{0,16},{4,20},{8,24},{12,28},{16,0},{20,4},{24,8},{28,12},{1,17},{... | collective-permute-start | bytes 2359304 | tf_op jit(solution)/shard_map/ppermute | solution.py:142
  35.3 28.9 %collective-permute-start.1 = (bf16[3,512,256]{2,1,0:T(8,128)(2,1)}, bf16[3,512,256]{2,1,0:T(8,128)(2,1)}, u32[]{:S(2)}, u32[]{:S(2)}) collective-permute-start(bf16[3,512,256]{2,1,0:T(8,128)(2,1)} %collective-permute-done.refs_10_), channel_id=1, source_target_pairs={{0,3},{1,0},{2,1},{3,2},{4,7},{5,4},{6,5},{7,6},{8,11},{9,8},{10,9... | collective-permute-start | bytes 2359304 | tf_op jit(solution)/shard_map/ppermute | solution.py:211
  37.8 23.6 %collective-permute-start.2 = (bf16[1,512,256]{2,1,0:T(8,128)(2,1)S(1)}, bf16[1,512,256]{2,1,0:T(8,128)(2,1)S(1)}, u32[]{:S(2)}, u32[]{:S(2)}) collective-permute-start(bf16[1,512,256]{2,1,0:T(8,128)(2,1)S(1)} %constant_dynamic-slice_fusion), channel_id=1, source_target_pairs={{0,3},{1,0},{2,1},{3,2},{4,7},{5,4},{6,5},{7,6},{8,11},{9,8},{10,9... | collective-permute-start | bytes 786440 | tf_op jit(solution)/shard_map/ppermute | solution.py:213
  38.9 34.2 %collective-permute-start.14 = (bf16[3,512,256]{2,1,0:T(8,128)(2,1)}, bf16[3,512,256]{2,1,0:T(8,128)(2,1)S(1)}, u32[]{:S(2)}, u32[]{:S(2)}) collective-permute-start(bf16[3,512,256]{2,1,0:T(8,128)(2,1)} %collective-permute-done.refs_10_), channel_id=1, source_target_pairs={{0,4},{4,0},{8,12},{12,8},{16,20},{20,16},{24,28},{28,24},{1,5},{5... | collective-permute-start | bytes 2359304 | tf_op jit(solution)/shard_map/ppermute | solution.py:142
  61.6 14.8 %collective-permute-start.15 = (bf16[3,512,256]{2,1,0:T(8,128)(2,1)S(1)}, bf16[3,512,256]{2,1,0:T(8,128)(2,1)}, u32[]{:S(2)}, u32[]{:S(2)}) collective-permute-start(bf16[3,512,256]{2,1,0:T(8,128)(2,1)S(1)} %collective-permute-done.10.refs_11_), channel_id=1, source_target_pairs={{0,4},{4,0},{8,12},{12,8},{16,20},{20,16},{24,28},{28,24},{1,5},{5... | collective-permute-start | bytes 2359304 | tf_op jit(solution)/shard_map/ppermute | solution.py:142
  62.0 15.9 %collective-permute-start.16 = (bf16[3,512,256]{2,1,0:T(8,128)(2,1)}, bf16[3,512,256]{2,1,0:T(8,128)(2,1)}, u32[]{:S(2)}, u32[]{:S(2)}) collective-permute-start(bf16[3,512,256]{2,1,0:T(8,128)(2,1)} %collective-permute-done.11.refs_12_), channel_id=1, source_target_pairs={{0,4},{4,0},{8,12},{12,8},{16,20},{20,16},{24,28},{28,24},{1,5},{5... | collective-permute-start | bytes 2359304 | tf_op jit(solution)/shard_map/ppermute | solution.py:142
  63.1 8.7 %collective-permute-start.12 = (bf16[1,512,256]{2,1,0:T(8,128)(2,1)S(1)}, bf16[1,512,256]{2,1,0:T(8,128)(2,1)S(1)}, u32[]{:S(2)}, u32[]{:S(2)}) collective-permute-start(bf16[1,512,256]{2,1,0:T(8,128)(2,1)S(1)} %slice.28), channel_id=1, source_target_pairs={{0,8},{4,12},{8,0},{12,4},{16,24},{20,28},{24,16},{28,20},{1,9},{5... | collective-permute-start | bytes 786440 | tf_op jit(solution)/shard_map/ppermute | solution.py:142
  74.0 26.8 %collective-permute-start.8 = (bf16[3,512,256]{2,1,0:T(8,128)(2,1)}, bf16[3,512,256]{2,1,0:T(8,128)(2,1)S(1)}, u32[]{:S(2)}, u32[]{:S(2)}) collective-permute-start(bf16[3,512,256]{2,1,0:T(8,128)(2,1)} %collective-permute-done.1.refs_10_), channel_id=1, source_target_pairs={{0,8},{4,12},{8,0},{12,4},{16,24},{20,28},{24,16},{28,20},{1,9},{5... | collective-permute-start | bytes 2359304 | tf_op jit(solution)/shard_map/ppermute | solution.py:142
  75.0 25.8 %collective-permute-start.9 = (bf16[3,512,256]{2,1,0:T(8,128)(2,1)}, bf16[3,512,256]{2,1,0:T(8,128)(2,1)}, u32[]{:S(2)}, u32[]{:S(2)}) collective-permute-start(bf16[3,512,256]{2,1,0:T(8,128)(2,1)} %collective-permute-done.1.refs_10_), channel_id=1, source_target_pairs={{0,16},{4,20},{8,24},{12,28},{16,0},{20,4},{24,8},{28,12},{1,17},{... | collective-permute-start | bytes 2359304 | tf_op jit(solution)/shard_map/ppermute | solution.py:142
  75.6 27.9 %collective-permute-start.3 = (bf16[3,512,256]{2,1,0:T(8,128)(2,1)}, bf16[3,512,256]{2,1,0:T(8,128)(2,1)}, u32[]{:S(2)}, u32[]{:S(2)}) collective-permute-start(bf16[3,512,256]{2,1,0:T(8,128)(2,1)} %collective-permute-done.1.refs_10_), channel_id=1, source_target_pairs={{0,3},{1,0},{2,1},{3,2},{4,7},{5,4},{6,5},{7,6},{8,11},{9,8},{10,9... | collective-permute-start | bytes 2359304 | tf_op jit(solution)/shard_map/ppermute | solution.py:211
  76.3 24.5 %collective-permute-start.4 = (bf16[1,512,256]{2,1,0:T(8,128)(2,1)S(1)}, bf16[1,512,256]{2,1,0:T(8,128)(2,1)S(1)}, u32[]{:S(2)}, u32[]{:S(2)}) collective-permute-start(bf16[1,512,256]{2,1,0:T(8,128)(2,1)S(1)} %collective-permute-done.2.refs_13_), channel_id=1, source_target_pairs={{0,3},{1,0},{2,1},{3,2},{4,7},{5,4},{6,5},{7,6},{8,11},{9,8},{10,9... | collective-permute-start | bytes 786440 | tf_op jit(solution)/shard_map/ppermute | solution.py:213
  102.7 15.6 %collective-permute-start.22 = (bf16[3,512,256]{2,1,0:T(8,128)(2,1)}, bf16[3,512,256]{2,1,0:T(8,128)(2,1)}, u32[]{:S(2)}, u32[]{:S(2)}) collective-permute-start(bf16[3,512,256]{2,1,0:T(8,128)(2,1)} %collective-permute-done.1.refs_10_), channel_id=1, source_target_pairs={{0,4},{4,0},{8,12},{12,8},{16,20},{20,16},{24,28},{28,24},{1,5},{5... | collective-permute-start | bytes 2359304 | tf_op jit(solution)/shard_map/ppermute | solution.py:142
  103.0 17.2 %collective-permute-start.23 = (bf16[3,512,256]{2,1,0:T(8,128)(2,1)S(1)}, bf16[3,512,256]{2,1,0:T(8,128)(2,1)}, u32[]{:S(2)}, u32[]{:S(2)}) collective-permute-start(bf16[3,512,256]{2,1,0:T(8,128)(2,1)S(1)} %collective-permute-done.8.refs_11_), channel_id=1, source_target_pairs={{0,4},{4,0},{8,12},{12,8},{16,20},{20,16},{24,28},{28,24},{1,5},{5... | collective-permute-start | bytes 2359304 | tf_op jit(solution)/shard_map/ppermute | solution.py:142
  103.2 17.0 %collective-permute-start.24 = (bf16[3,512,256]{2,1,0:T(8,128)(2,1)}, bf16[3,512,256]{2,1,0:T(8,128)(2,1)}, u32[]{:S(2)}, u32[]{:S(2)}) collective-permute-start(bf16[3,512,256]{2,1,0:T(8,128)(2,1)} %collective-permute-done.9.refs_12_), channel_id=1, source_target_pairs={{0,4},{4,0},{8,12},{12,8},{16,20},{20,16},{24,28},{28,24},{1,5},{5... | collective-permute-start | bytes 2359304 | tf_op jit(solution)/shard_map/ppermute | solution.py:142
  103.5 10.3 %collective-permute-start.21 = (bf16[1,512,256]{2,1,0:T(8,128)(2,1)S(1)}, bf16[1,512,256]{2,1,0:T(8,128)(2,1)S(1)}, u32[]{:S(2)}, u32[]{:S(2)}) collective-permute-start(bf16[1,512,256]{2,1,0:T(8,128)(2,1)S(1)} %slice.25), channel_id=1, source_target_pairs={{0,16},{4,20},{8,24},{12,28},{16,0},{20,4},{24,8},{28,12},{1,17},{... | collective-permute-start | bytes 786440 | tf_op jit(solution)/shard_map/ppermute | solution.py:142
  116.5 28.2 %collective-permute-start.5 = (bf16[3,512,256]{2,1,0:T(8,128)(2,1)}, bf16[3,512,256]{2,1,0:T(8,128)(2,1)S(1)}, u32[]{:S(2)}, u32[]{:S(2)}) collective-permute-start(bf16[3,512,256]{2,1,0:T(8,128)(2,1)} %collective-permute-done.3.refs_6_), channel_id=1, source_target_pairs={{0,8},{4,12},{8,0},{12,4},{16,24},{20,28},{24,16},{28,20},{1,9},{5... | collective-permute-start | bytes 2359304 | tf_op jit(solution)/shard_map/ppermute | solution.py:142
  116.6 28.1 %collective-permute-start.6 = (bf16[3,512,256]{2,1,0:T(8,128)(2,1)}, bf16[3,512,256]{2,1,0:T(8,128)(2,1)}, u32[]{:S(2)}, u32[]{:S(2)}) collective-permute-start(bf16[3,512,256]{2,1,0:T(8,128)(2,1)} %collective-permute-done.3.refs_6_), channel_id=1, source_target_pairs={{0,16},{4,20},{8,24},{12,28},{16,0},{20,4},{24,8},{28,12},{1,17},{... | collective-permute-start | bytes 2359304 | tf_op jit(solution)/shard_map/ppermute | solution.py:142
  118.3 26.3 %collective-permute-start.7 = (bf16[1,512,256]{2,1,0:T(8,128)(2,1)S(1)}, bf16[1,512,256]{2,1,0:T(8,128)(2,1)S(1)}, u32[]{:S(2)}, u32[]{:S(2)}) collective-permute-start(bf16[1,512,256]{2,1,0:T(8,128)(2,1)S(1)} %collective-permute-done.4.refs_13_), channel_id=1, source_target_pairs={{0,3},{1,0},{2,1},{3,2},{4,7},{5,4},{6,5},{7,6},{8,11},{9,8},{10,9... | collective-permute-start | bytes 786440 | tf_op jit(solution)/shard_map/ppermute | solution.py:213
  145.9 12.2 %collective-permute-start.30 = (bf16[3,512,256]{2,1,0:T(8,128)(2,1)}, bf16[3,512,256]{2,1,0:T(8,128)(2,1)S(1)}, u32[]{:S(2)}, u32[]{:S(2)}) collective-permute-start(bf16[3,512,256]{2,1,0:T(8,128)(2,1)} %collective-permute-done.3.refs_6_), channel_id=1, source_target_pairs={{0,4},{4,0},{8,12},{12,8},{16,20},{20,16},{24,28},{28,24},{1,5},{5... | collective-permute-start | bytes 2359304 | tf_op jit(solution)/shard_map/ppermute | solution.py:142
  146.1 12.0 %collective-permute-start.31 = (bf16[3,512,256]{2,1,0:T(8,128)(2,1)S(1)}, bf16[3,512,256]{2,1,0:T(8,128)(2,1)}, u32[]{:S(2)}, u32[]{:S(2)}) collective-permute-start(bf16[3,512,256]{2,1,0:T(8,128)(2,1)S(1)} %collective-permute-done.5.refs_7_), channel_id=1, source_target_pairs={{0,4},{4,0},{8,12},{12,8},{16,20},{20,16},{24,28},{28,24},{1,5},{5... | collective-permute-start | bytes 2359304 | tf_op jit(solution)/shard_map/ppermute | solution.py:142
  146.5 11.7 %collective-permute-start.32 = (bf16[3,512,256]{2,1,0:T(8,128)(2,1)}, bf16[3,512,256]{2,1,0:T(8,128)(2,1)}, u32[]{:S(2)}, u32[]{:S(2)}) collective-permute-start(bf16[3,512,256]{2,1,0:T(8,128)(2,1)} %collective-permute-done.6.refs_8_), channel_id=1, source_target_pairs={{0,4},{4,0},{8,12},{12,8},{16,20},{20,16},{24,28},{28,24},{1,5},{5... | collective-permute-start | bytes 2359304 | tf_op jit(solution)/shard_map/ppermute | solution.py:142
  171.0 30.3 %all-to-all-start = ((bf16[8,2,256,256]{3,2,1,0:T(8,128)(2,1)}), bf16[8,2,256,256]{3,2,1,0:T(8,128)(2,1)S(1)}, u32[]{:S(2)}, u32[]{:S(2)}) async-start(bf16[8,2,256,256]{3,2,1,0:T(8,128)(2,1)} %bitcast.14), calls=%async_computation | async-start | bytes 4194304 | tf_op jit(solution)/shard_map/all_to_all | solution.py:226
  (58 other events, 253.8 us)

commit v4 on v3

v4 whole, which is shorter than its diff:
```python
import functools

import jax
import jax.numpy as jnp
from jax import lax
from jax.experimental import pallas as pl
from jax.experimental.pallas import tpu as pltpu
from jax.sharding import PartitionSpec as P

SMEM = pl.BlockSpec(memory_space=pltpu.SMEM)
VMEM = pl.BlockSpec(memory_space=pltpu.VMEM)
HBM = pl.BlockSpec(memory_space=pltpu.HBM)
MIB = 1 << 20
CLASS_BITS, SOURCE_BITS, LAG_BITS, STEP_BITS = 4, 8, 8, 4


def widths(steps):
    return [1 << b for b in range(steps.bit_length() - 1, -1, -1)]


def list_tasks(base, span, total, steps, pair, tasks, counts):
    source, klass, lag, place = pair
    start = lax.rem(lag - base + total, total)
    inside = start < span
    first = jnp.where(inside, start, 0)
    skip = jnp.where(inside, 0, total - start)
    count = jnp.maximum(jnp.where(inside, jnp.minimum(steps, span - start), steps - skip), 0)
    for b, width in enumerate(widths(steps)):
        has = jnp.where((count & width) != 0, 1, 0)
        done = count & ~(2 * width - 1)
        packed = place
        for value, bits in (
            (skip + done, STEP_BITS),
            (first + done, LAG_BITS),
            (source, SOURCE_BITS),
            (klass, CLASS_BITS),
        ):
            packed = (packed << bits) | value
        at = counts[b]
        tasks[b, at] = packed
        counts[b] = at + has


def run_tasks(steps, spare, tasks, counts, hist, table, acc):
    panels = table.shape[2]

    def product(packed, width):
        fields = []
        for bits in (CLASS_BITS, SOURCE_BITS, LAG_BITS, STEP_BITS):
            fields.append(packed & ((1 << bits) - 1))
            packed = packed >> bits
        klass, source, lag, step = fields
        rows = pl.multiple_of(lag * panels, panels)
        columns = pl.multiple_of(step * panels, panels)
        return packed, jnp.dot(
            hist[source, :, pl.ds(columns, width * panels)],
            table[klass, pl.ds(rows, width * panels), :],
            preferred_element_type=jnp.float32,
        )

    for b, width in enumerate(widths(steps)):
        count = counts[b]
        tasks[b, count] = spare << (CLASS_BITS + SOURCE_BITS + LAG_BITS + STEP_BITS)

        @pl.loop(0, (count + 1) // 2)
        def _(j):
            one, first = product(tasks[b, 2 * j], width)
            two, second = product(tasks[b, 2 * j + 1], width)
            acc[one] += first
            acc[two] += second


def window_kernel(config, *refs):
    served, local, begun, narrow, places, total, height = config
    refs = list(refs)
    where = refs.pop(0)
    served_refs = [refs.pop(0) for _ in range(3 if served else 0)]
    local_refs = [refs.pop(0) for _ in range(4 if local else 0)]
    hist_ref = refs.pop(0)
    pieces = [refs.pop(0) for _ in places]
    before = refs.pop(0) if begun else None
    out, table, hist, acc, tasks, counts, sems, ends = refs
    base, group = where[0], where[1]
    panels = table.shape[2]
    span = table.shape[1] // panels
    steps = hist.shape[2] // panels
    number = acc.shape[0] - 1

    copies = [pltpu.make_async_copy(hist_ref, hist, ends.at[0])]
    for n, ((slot, mask, klass), piece) in enumerate(zip(places, pieces)):
        depth, rows, _ = piece.shape
        start = pl.multiple_of(slot * height + (group ^ mask) * rows, 16)
        copies.append(
            pltpu.make_async_copy(
                piece, table.at[pl.ds(klass, depth), pl.ds(start, rows), :], sems.at[n]
            )
        )
    if begun:
        first = 0 if served else before.shape[0] - number
        copies.append(
            pltpu.make_async_copy(
                before.at[pl.ds(first, number)], acc.at[pl.ds(0, number)], ends.at[1]
            )
        )
    for copy in copies:
        copy.start()
    if not begun:
        acc[...] = jnp.zeros_like(acc)

    for b in range(len(widths(steps))):
        counts[b] = 0
    if served:
        peers, slots = served_refs[0].shape

        @pl.loop(0, peers)
        def _(i):
            for c in range(slots):
                source, lag, klass = (ref[i, c] for ref in served_refs)
                pair = (source, klass, lag, i * slots + c)
                list_tasks(base, span, total, steps, pair, tasks, counts)

    if local:
        lead = number - hist.shape[0]

        @pl.loop(0, local_refs[0].shape[0])
        def _(i):
            source, lag, klass, target = (ref[i] for ref in local_refs)
            pair = (source, klass, lag, target + lead)
            list_tasks(base, span, total, steps, pair, tasks, counts)

    for copy in copies:
        copy.wait()
    run_tasks(steps, number, tasks, counts, hist, table, acc)
    if narrow:
        out[...] = acc[pl.ds(0, number)].astype(out.dtype)
    else:
        copy = pltpu.make_async_copy(acc.at[pl.ds(0, number)], out, ends.at[1])
        copy.start()
        copy.wait()


def window_sums(base, group, served, local, hist_t, pieces, sums, lanes, height, narrow=False):
    owned, excite, depth = hist_t.shape
    panels = pieces[0][3].shape[2]
    classes = max(klass + value.shape[0] for _, _, klass, value in pieces)
    rows = height * (1 + max(slot for slot, _, _, _ in pieces))
    number = (served[0].size if served else 0) + (owned if local else 0)
    pairs = (served[0].size if served else 0) + (local[0].size if local else 0)
    steps = depth // panels
    config = (
        bool(served),
        bool(local),
        sums is not None,
        narrow,
        tuple(piece[:3] for piece in pieces),
        lanes * height // panels,
        height,
    )
    operands = [jnp.stack([base * (height // panels), group]).astype(jnp.int32), *served, *local]
    wide = [hist_t, *[piece[3] for piece in pieces], *([sums] if sums is not None else [])]
    return pl.pallas_call(
        functools.partial(window_kernel, config),
        out_shape=jax.ShapeDtypeStruct(
            (number, excite, panels), jnp.bfloat16 if narrow else jnp.float32
        ),
        in_specs=[SMEM] * len(operands) + [HBM] * len(wide),
        out_specs=VMEM if narrow else HBM,
        scratch_shapes=[
            pltpu.VMEM((classes, rows, panels), jnp.bfloat16),
            pltpu.VMEM(hist_t.shape, hist_t.dtype),
            pltpu.VMEM((number + 1, excite, panels), jnp.float32),
            pltpu.SMEM((len(widths(steps)), pairs + 2), jnp.int32),
            pltpu.SMEM((len(widths(steps)),), jnp.int32),
            pltpu.SemaphoreType.DMA((len(pieces),)),
            pltpu.SemaphoreType.DMA((2,)),
        ],
        compiler_params=pltpu.CompilerParams(vmem_limit_bytes=58 * MIB),
        cost_estimate=pl.CostEstimate(
            flops=2 * pairs * panels * depth * excite,
            bytes_accessed=2 * classes * rows * panels + 2 * hist_t.size,
            transcendentals=0,
        ),
    )(*operands, *wide)


def update_kernel(target_ref, near_ref, recv_ref, inverse_ref, incident_ref, out_ref, total):
    total[...] = near_ref[...]
    peers, slots = target_ref.shape

    @pl.loop(0, peers)
    def _(i):
        for c in range(slots):
            total[target_ref[i, c]] += recv_ref[i, c].astype(jnp.float32)

    for t in range(out_ref.shape[0]):
        residual = (incident_ref[t].astype(jnp.float32) - total[t].T).astype(jnp.bfloat16)
        out_ref[t] = jnp.dot(
            inverse_ref[t], residual, preferred_element_type=jnp.float32
        ).astype(out_ref.dtype)


def update(target, near, recv, inverse, incident):
    return pl.pallas_call(
        update_kernel,
        out_shape=jax.ShapeDtypeStruct(incident.shape, jnp.bfloat16),
        in_specs=[SMEM] + [VMEM] * 4,
        out_specs=VMEM,
        scratch_shapes=[pltpu.VMEM(near.shape, jnp.float32)],
        compiler_params=pltpu.CompilerParams(vmem_limit_bytes=32 * MIB),
    )(target, near, recv, inverse, incident)


def swap(value, bit, peers):
    return lax.ppermute(value, "grp", [(i, i ^ bit) for i in range(peers)])


def exchange(own, corner, peers):
    held = [(0, own, corner)]
    bit = 8
    while bit < peers:
        held += [(mask ^ bit, swap(a, bit, peers), swap(c, bit, peers)) for mask, a, c in held]
        bit *= 2
    return [(mask, a, swap(a, 2, peers), swap(a, 4, peers), c) for mask, a, c in held]


def finish(held, slot, peers):
    found = []
    for mask, own, across, along, corner in held:
        third = corner.shape[0]
        found += [
            (slot, mask, 0, own),
            (slot, mask ^ 2, 0, across),
            (slot, mask ^ 4, 0, along),
            (slot, mask ^ 6, 0, corner),
            (slot, mask ^ 6, third, swap(along[third : 2 * third], 2, peers)),
            (slot, mask ^ 6, 2 * third, swap(across[2 * third :], 4, peers)),
        ]
    return found + [(slot, mask ^ 1, klass, swap(v, 1, peers)) for slot, mask, klass, v in found]


def per_device(
    weights,
    history,
    send_patch,
    send_lag,
    send_class,
    recv_target,
    local_src,
    local_lag,
    local_class,
    local_target,
    inverse_blocks,
    incident,
):
    classes, rows, panels = weights.shape
    peers, slots = send_patch.shape
    height = rows // peers
    group = lax.axis_index("grp")
    lane = lax.axis_index("lag")
    lanes = lax.axis_size("lag")
    ring = [(i, (i - 1) % lanes) for i in range(lanes)]
    served = (send_patch, send_lag, send_class)
    local = (local_src, local_lag, local_class, local_target)

    hist_t = jnp.swapaxes(history, 1, 2)
    own = lax.dynamic_slice(weights, (0, group * height, 0), (classes, height, panels))
    corner = lax.dynamic_slice(
        weights, (0, (group ^ 6) * height, 0), (classes // 3, height, panels)
    )
    sums = window_sums(
        lane, group * 0, served, local, hist_t, [(0, 0, 0, weights)], None, lanes, rows
    )
    pieces = []
    for step in range(1, lanes):
        own = lax.ppermute(own, "lag", ring)
        own, corner = lax.optimization_barrier((own, corner))
        corner = lax.ppermute(corner, "lag", ring)
        if step == 1:
            own, sums = lax.optimization_barrier((own, sums))
        held = exchange(own, corner, peers)
        if step == lanes - 1:
            sums = window_sums(
                lax.rem(lane + 1, lanes), group, served, local, hist_t, pieces, sums, lanes, rows
            )
            values, sums = lax.optimization_barrier(([h[1:] for h in held], sums))
            held = [(h[0], *v) for h, v in zip(held, values)]
            pieces = finish(held, 0, peers)
        else:
            pieces += finish(held, step - 1, peers)
    last = lax.rem(lane + lanes - 1, lanes)
    contribution = window_sums(
        last, group, served, (), hist_t, pieces, sums, lanes, rows, narrow=True
    )
    recv = lax.all_to_all(
        contribution.reshape(peers, slots, *contribution.shape[1:]),
        "grp",
        split_axis=0,
        concat_axis=0,
        tiled=True,
    )
    near = window_sums(last, group, (), local, hist_t, pieces, sums, lanes, rows)
    return update(recv_target, near, recv, inverse_blocks, incident)


def solution(mesh):
    both = ("grp", "lag")
    return jax.shard_map(
        per_device,
        mesh=mesh,
        in_specs=(
            P(None, "lag", None),
            P(both, None, None),
            P(both, None),
            P(both, None),
            P(both, None),
            P(both, None),
            P(both),
            P(both),
            P(both),
            P(both),
            P(both, None, None),
            P(both, None, None),
        ),
        out_specs=P(both, None, None),
        check_vma=False,
    )
```

time: 207 us -> 192 us (0.928)
  local copies, waits for them, and re-layouts: 59.2 us -> 16.4 us
  waiting for transfers between devices: 55.5 us -> 70.7 us
  Pallas kernels: 55 us -> 64.1 us
  starting transfers between devices: 35.3 us -> 37.5 us
    unnamed x93 -> x59, local copies, waits for them, and re-layouts: 52.1 us -> 12.2 us
    ppermute x30, waiting for transfers between devices: 23.7 us -> 38.9 us  [swap(): return lax.ppermute(value, 'grp', [(i, i ^ bit) for i in range(peers)])]
    pallas_call x5 -> x4, Pallas kernels: 52.6 us -> 61.7 us  [window_sums(): pl.pallas_call(functools.partial(window_kernel, config), out_shape=jax.Sh...]
    ppermute x3, waiting for transfers between devices: 24 us -> 17.1 us  [per_device(): corner = lax.ppermute(corner, 'lag', ring)]
    all_to_all x1, waiting for transfers between devices: 7.84 us -> 14.6 us  [per_device(): lax.all_to_all(contribution.reshape(peers, slots, *contribution.shape[1:]...]
    ppermute x3, starting transfers between devices: 4.47 us -> 7.43 us  [per_device(): corner = lax.ppermute(corner, 'lag', ring)]
    slice x3, local copies, waits for them, and re-layouts: 3.09 us -> 1 us  [finish(): along[third:2 * third]]
  transfers between devices with their start and end apart: 37 -> 37, of which waited for: 12 -> 13; matrix products, arithmetic and copies ran while one was open for 4% -> 7% of each run, Pallas kernels for 23% -> 27%
where the time goes in v4:
time: 192 us; the launch traced here: 191 us
  waiting for transfers between devices  70.7 us (37%)
  Pallas kernels  64.1 us (33%)
  starting transfers between devices  37.5 us (20%)
  local copies, waits for them, and re-layouts  16.4 us (9%)
    pallas_call x4, Pallas kernels, window_sums(): pl.pallas_call(functools.partial(window_kernel, config), out_shape=jax.Sh...  61.7 us
    ppermute x30, waiting for transfers between devices, swap(): return lax.ppermute(value, 'grp', [(i, i ^ bit) for i in range(peers)])  38.9 us
    ppermute x30, starting transfers between devices, swap(): return lax.ppermute(value, 'grp', [(i, i ^ bit) for i in range(peers)])  19.9 us
    ppermute x3, waiting for transfers between devices, per_device(): corner = lax.ppermute(corner, 'lag', ring)  17.1 us
    all_to_all x1, waiting for transfers between devices, per_device(): lax.all_to_all(contribution.reshape(peers, slots, *contribution.shape[1:]...  14.6 us
    unnamed x59, local copies, waits for them, and re-layouts  12.2 us
    ppermute x3, starting transfers between devices, per_device(): corner = lax.ppermute(corner, 'lag', ring)  7.43 us
    ppermute x3, starting transfers between devices, per_device(): own = lax.ppermute(own, 'lag', ring)  6.64 us
  transfers between devices with their start and end apart: 37, of which 13 were waited for; matrix products, arithmetic and copies ran while one was open for 7% of the time, Pallas kernels for 27%

profile of v4, /device:TPU:0, one launch (start us, length us, event | category | flops | bytes accessed | tf_op | source)
XLA Modules:
  0.0 190.9 jit_solution(14756851516347066519)
XLA Ops:
  1.2 5.1 %collective-permute-start = (bf16[3,512,256]{2,1,0:T(8,128)(2,1)S(1)}, bf16[3,512,256]{2,1,0:T(8,128)(2,1)S(1)}, u32[]{:S(2)}, u32[]{:S(2)}) collective-permute-start(bf16[3,512,256]{2,1,0:T(8,128)(2,1)S(1)} %constant_dynamic-slice_fusion.1), channel_id=1, source_target_pairs={{0,3},{1,0},{2,1},{3,2},{4,7},{5,4},{6,5},{7,6},{8,11},{9,8},{10,9... | collective-permute-start | bytes 2359304 | tf_op jit(solution)/shard_map/ppermute | solution.py:275
  6.3 6.3 %copy.13 = bf16[4,2048,256]{1,2,0:T(8,128)(2,1)} copy(bf16[4,2048,256]{2,1,0:T(8,128)(2,1)} %param.13) | data formatting | bytes 8388608 | tf_op args[1]
  15.2 13.6 %shard_map.118.refs_33_ = f32[20,256,256]{2,1,0:T(8,128)} custom-call(s32[2]{0:T(128)} %pad_add_fusion.1.refs_0_, s32[8,2]{1,0:T(8,128)} %copy.14.refs_1_, s32[8,2]{1,0:T(8,128)} %copy.15.refs_2_, s32[8,2]{1,0:T(8,128)} %copy.16.refs_3_, s32[48]{0:T(128)} %refs_1_.4, s32[48]{0:T(128)} %refs_2_.4, s32[48]{0:T(128)} %refs_3_.4, s32[48]{0:T(128)} %refs_4_.5, ...), custom_call_target="tpu_custom_call" | custom-call | flops 17179869184 | bytes 10485760 | tf_op jit(solution)/shard_map/pallas_call | solution.py:161
  29.8 2.7 %collective-permute-start.9 = (bf16[3,512,256]{2,1,0:T(8,128)(2,1)S(1)}, bf16[3,512,256]{2,1,0:T(8,128)(2,1)S(1)}, u32[]{:S(2)}, u32[]{:S(2)}) collective-permute-start(bf16[3,512,256]{2,1,0:T(8,128)(2,1)S(1)} %collective-permute-done.refs_9_), channel_id=1, source_target_pairs={{0,16},{4,20},{8,24},{12,28},{16,0},{20,4},{24,8},{28,12},{1,17},{... | collective-permute-start | bytes 2359304 | tf_op jit(solution)/shard_map/ppermute | solution.py:214
  34.2 3.8 %collective-permute-start.2 = (bf16[1,512,256]{2,1,0:T(8,128)(2,1)S(1)}, bf16[1,512,256]{2,1,0:T(8,128)(2,1)S(1)}, u32[]{:S(2)}, u32[]{:S(2)}) collective-permute-start(bf16[1,512,256]{2,1,0:T(8,128)(2,1)S(1)} %constant_dynamic-slice_fusion), channel_id=1, source_target_pairs={{0,3},{1,0},{2,1},{3,2},{4,7},{5,4},{6,5},{7,6},{8,11},{9,8},{10,9... | collective-permute-start | bytes 786440 | tf_op jit(solution)/shard_map/ppermute | solution.py:277
  38.1 15.2 %collective-permute-done.2.refs_12_ = bf16[1,512,256]{2,1,0:T(8,128)(2,1)S(1)} collective-permute-done((bf16[1,512,256]{2,1,0:T(8,128)(2,1)S(1)}, bf16[1,512,256]{2,1,0:T(8,128)(2,1)S(1)}, u32[]{:S(2)}, u32[]{:S(2)}) %collective-permute-start.2) | collective-permute-done | bytes 262176 | tf_op jit(solution)/shard_map/ppermute | solution.py:277
  53.3 3.6 %collective-permute-start.4 = (bf16[1,512,256]{2,1,0:T(8,128)(2,1)S(1)}, bf16[1,512,256]{2,1,0:T(8,128)(2,1)S(1)}, u32[]{:S(2)}, u32[]{:S(2)}) collective-permute-start(bf16[1,512,256]{2,1,0:T(8,128)(2,1)S(1)} %collective-permute-done.2.refs_12_), channel_id=1, source_target_pairs={{0,3},{1,0},{2,1},{3,2},{4,7},{5,4},{6,5},{7,6},{8,11},{9,8},{10,9... | collective-permute-start | bytes 786440 | tf_op jit(solution)/shard_map/ppermute | solution.py:277
  58.7 2.6 %collective-permute-start.11 = (bf16[1,512,256]{2,1,0:T(8,128)(2,1)S(1)}, bf16[1,512,256]{2,1,0:T(8,128)(2,1)S(1)}, u32[]{:S(2)}, u32[]{:S(2)}) collective-permute-start(bf16[1,512,256]{2,1,0:T(8,128)(2,1)S(1)} %slice.25), channel_id=1, source_target_pairs={{0,16},{4,20},{8,24},{12,28},{16,0},{20,4},{24,8},{28,12},{1,17},{... | collective-permute-start | bytes 786440 | tf_op jit(solution)/shard_map/ppermute | solution.py:214
  61.4 1.9 %collective-permute-done.4.refs_24_ = bf16[1,512,256]{2,1,0:T(8,128)(2,1)S(1)} collective-permute-done((bf16[1,512,256]{2,1,0:T(8,128)(2,1)S(1)}, bf16[1,512,256]{2,1,0:T(8,128)(2,1)S(1)}, u32[]{:S(2)}, u32[]{:S(2)}) %collective-permute-start.4) | collective-permute-done | bytes 262176 | tf_op jit(solution)/shard_map/ppermute | solution.py:277
  63.4 2.3 %collective-permute-done.10.refs_13_ = bf16[1,512,256]{2,1,0:T(8,128)(2,1)S(1)} collective-permute-done((bf16[1,512,256]{2,1,0:T(8,128)(2,1)S(1)}, bf16[1,512,256]{2,1,0:T(8,128)(2,1)S(1)}, u32[]{:S(2)}, u32[]{:S(2)}) %collective-permute-start.10) | collective-permute-done | bytes 262176 | tf_op jit(solution)/shard_map/ppermute | solution.py:214
  65.7 2.7 %collective-permute-done.11.refs_14_ = bf16[1,512,256]{2,1,0:T(8,128)(2,1)S(1)} collective-permute-done((bf16[1,512,256]{2,1,0:T(8,128)(2,1)S(1)}, bf16[1,512,256]{2,1,0:T(8,128)(2,1)S(1)}, u32[]{:S(2)}, u32[]{:S(2)}) %collective-permute-start.11) | collective-permute-done | bytes 262176 | tf_op jit(solution)/shard_map/ppermute | solution.py:214
  71.5 13.5 %collective-permute-done.19.refs_23_ = bf16[3,512,256]{2,1,0:T(8,128)(2,1)} collective-permute-done((bf16[3,512,256]{2,1,0:T(8,128)(2,1)S(1)}, bf16[3,512,256]{2,1,0:T(8,128)(2,1)}, u32[]{:S(2)}, u32[]{:S(2)}) %collective-permute-start.19) | collective-permute-done | bytes 786464 | tf_op jit(solution)/shard_map/ppermute | solution.py:214
  85.0 3.5 %collective-permute-done.18.refs_22_ = bf16[3,512,256]{2,1,0:T(8,128)(2,1)} collective-permute-done((bf16[3,512,256]{2,1,0:T(8,128)(2,1)S(1)}, bf16[3,512,256]{2,1,0:T(8,128)(2,1)}, u32[]{:S(2)}, u32[]{:S(2)}) %collective-permute-start.18) | collective-permute-done | bytes 786464 | tf_op jit(solution)/shard_map/ppermute | solution.py:214
  92.2 2.1 %collective-permute-start.21 = (bf16[1,512,256]{2,1,0:T(8,128)(2,1)S(1)}, bf16[1,512,256]{2,1,0:T(8,128)(2,1)}, u32[]{:S(2)}, u32[]{:S(2)}) collective-permute-start(bf16[1,512,256]{2,1,0:T(8,128)(2,1)S(1)} %slice.27), channel_id=1, source_target_pairs={{0,16},{4,20},{8,24},{12,28},{16,0},{20,4},{24,8},{28,12},{1,17},{... | collective-permute-start | bytes 786440 | tf_op jit(solution)/shard_map/ppermute | solution.py:214
  94.3 5.9 %collective-permute-done.20.refs_25_ = bf16[1,512,256]{2,1,0:T(8,128)(2,1)S(1)} collective-permute-done((bf16[1,512,256]{2,1,0:T(8,128)(2,1)S(1)}, bf16[1,512,256]{2,1,0:T(8,128)(2,1)S(1)}, u32[]{:S(2)}, u32[]{:S(2)}) %collective-permute-start.20) | collective-permute-done | bytes 262176 | tf_op jit(solution)/shard_map/ppermute | solution.py:214
  104.9 26.9 %shard_map.119.refs_18_.refs_17_ = f32[20,256,256]{2,1,0:T(8,128)} custom-call(s32[2]{0:T(128)} %pad_add_fusion.2.refs_0_, s32[8,2]{1,0:T(8,128)} %copy.14.refs_1_, s32[8,2]{1,0:T(8,128)} %copy.15.refs_2_, s32[8,2]{1,0:T(8,128)} %copy.16.refs_3_, s32[48]{0:T(128)} %refs_1_.4, s32[48]{0:T(128)} %refs_2_.4, s32[48]{0:T(128)} %refs_3_.4, s32[48]{0:T(128)} %refs_4_.5, ...), custom_call_target="tpu_custom_call" | custom-call | flops 17179869184 | bytes 16777216 | tf_op jit(solution)/shard_map/pallas_call | solution.py:161
  131.9 2.7 %collective-permute-start.28 = (bf16[1,512,256]{2,1,0:T(8,128)(2,1)S(1)}, bf16[1,512,256]{2,1,0:T(8,128)(2,1)}, u32[]{:S(2)}, u32[]{:S(2)}) collective-permute-start(bf16[1,512,256]{2,1,0:T(8,128)(2,1)S(1)} %slice.22), channel_id=1, source_target_pairs={{0,8},{4,12},{8,0},{12,4},{16,24},{20,28},{24,16},{28,20},{1,9},{5... | collective-permute-start | bytes 786440 | tf_op jit(solution)/shard_map/ppermute | solution.py:214
  135.2 5.3 %collective-permute-done.28.refs_10_.refs_9_ = bf16[1,512,256]{2,1,0:T(8,128)(2,1)} collective-permute-done((bf16[1,512,256]{2,1,0:T(8,128)(2,1)S(1)}, bf16[1,512,256]{2,1,0:T(8,128)(2,1)}, u32[]{:S(2)}, u32[]{:S(2)}) %collective-permute-start.28) | collective-permute-done | bytes 262176 | tf_op jit(solution)/shard_map/ppermute | solution.py:214
  140.6 3.5 %collective-permute-done.29.refs_11_.refs_10_ = bf16[1,512,256]{2,1,0:T(8,128)(2,1)} collective-permute-done((bf16[1,512,256]{2,1,0:T(8,128)(2,1)S(1)}, bf16[1,512,256]{2,1,0:T(8,128)(2,1)}, u32[]{:S(2)}, u32[]{:S(2)}) %collective-permute-start.29) | collective-permute-done | bytes 262176 | tf_op jit(solution)/shard_map/ppermute | solution.py:214
  147.7 9.3 %shard_map.121 = bf16[16,256,256]{2,1,0:T(8,128)(2,1)} custom-call(s32[2]{0:T(128)} %pad_add_fusion.refs_0_, s32[8,2]{1,0:T(8,128)} %copy.14.refs_1_, s32[8,2]{1,0:T(8,128)} %copy.15.refs_2_, s32[8,2]{1,0:T(8,128)} %copy.16.refs_3_, bf16[4,256,2048]{2,1,0:T(8,128)(2,1)} %bitcast.8, bf16[3,512,256]{2,1,0:T(8,128)(2,1)} %copy-done.5, ...), custom_call_target="tpu_custom_call" | custom-call | flops 4294967296 | bytes 10485760 | tf_op jit(solution)/shard_map/pallas_call | solution.py:161
  157.1 3.6 %all-to-all-start = ((bf16[8,2,256,256]{3,2,1,0:T(8,128)(2,1)}), bf16[8,2,256,256]{3,2,1,0:T(8,128)(2,1)S(1)}, u32[]{:S(2)}, u32[]{:S(2)}) async-start(bf16[8,2,256,256]{3,2,1,0:T(8,128)(2,1)} %bitcast.10), calls=%async_computation | async-start | bytes 4194304 | tf_op jit(solution)/shard_map/all_to_all | solution.py:294
  160.8 11.9 %shard_map.120.near_ref = f32[4,256,256]{2,1,0:T(8,128)} custom-call(s32[2]{0:T(128)} %pad_add_fusion.refs_0_, s32[48]{0:T(128)} %refs_1_.4, s32[48]{0:T(128)} %refs_2_.4, s32[48]{0:T(128)} %refs_3_.4, s32[48]{0:T(128)} %refs_4_.5, bf16[4,256,2048]{2,1,0:T(8,128)(2,1)} %bitcast.9, bf16[3,512,256]{2,1,0:T(8,128)(2,1)} %copy-done.5, ...), custom_call_target="tpu_custom_call" | custom-call | flops 12884901888 | bytes 10485760 | tf_op jit(solution)/shard_map/pallas_call | solution.py:161
  172.7 14.6 %all-to-all-done.recv_ref = bf16[8,2,256,256]{3,2,1,0:T(8,128)(2,1)S(1)} async-done(((bf16[8,2,256,256]{3,2,1,0:T(8,128)(2,1)}), bf16[8,2,256,256]{3,2,1,0:T(8,128)(2,1)S(1)}, u32[]{:S(2)}, u32[]{:S(2)}) %all-to-all-start) | async-done | bytes 2097184 | tf_op jit(solution)/shard_map/all_to_all | solution.py:294
  188.5 2.4 %shard_map.122 = bf16[4,256,256]{2,1,0:T(8,128)(2,1)} custom-call(s32[8,2]{1,0:T(8,128)S(1)} %copy.23.target_ref, f32[4,256,256]{2,1,0:T(8,128)S(1)} %copy-done, bf16[8,2,256,256]{3,2,1,0:T(8,128)(2,1)S(1)} %all-to-all-done.recv_ref, bf16[4,256,256]{2,1,0:T(8,128)(2,1)S(1)} %copy-done.1, bf16[4,256,256]{2,1,0:T(8,128)(2,1)S(1)} %copy-done.2), custom_call_target="tpu_custom_call" | custom-call | tf_op jit(solution)/shard_map/pallas_call | solution.py:203
  (125 shorter events, 25.4 us)
Async XLA Ops:
  1.2 28.5 %collective-permute-start = (bf16[3,512,256]{2,1,0:T(8,128)(2,1)S(1)}, bf16[3,512,256]{2,1,0:T(8,128)(2,1)S(1)}, u32[]{:S(2)}, u32[]{:S(2)}) collective-permute-start(bf16[3,512,256]{2,1,0:T(8,128)(2,1)S(1)} %constant_dynamic-slice_fusion.1), channel_id=1, source_target_pairs={{0,3},{1,0},{2,1},{3,2},{4,7},{5,4},{6,5},{7,6},{8,11},{9,8},{10,9... | collective-permute-start | bytes 2359304 | tf_op jit(solution)/shard_map/ppermute | solution.py:275
  29.8 23.5 %collective-permute-start.1 = (bf16[3,512,256]{2,1,0:T(8,128)(2,1)S(1)}, bf16[3,512,256]{2,1,0:T(8,128)(2,1)S(1)}, u32[]{:S(2)}, u32[]{:S(2)}) collective-permute-start(bf16[3,512,256]{2,1,0:T(8,128)(2,1)S(1)} %collective-permute-done.refs_9_), channel_id=1, source_target_pairs={{0,3},{1,0},{2,1},{3,2},{4,7},{5,4},{6,5},{7,6},{8,11},{9,8},{10,9... | collective-permute-start | bytes 2359304 | tf_op jit(solution)/shard_map/ppermute | solution.py:275
  29.8 27.4 %collective-permute-start.9 = (bf16[3,512,256]{2,1,0:T(8,128)(2,1)S(1)}, bf16[3,512,256]{2,1,0:T(8,128)(2,1)S(1)}, u32[]{:S(2)}, u32[]{:S(2)}) collective-permute-start(bf16[3,512,256]{2,1,0:T(8,128)(2,1)S(1)} %collective-permute-done.refs_9_), channel_id=1, source_target_pairs={{0,16},{4,20},{8,24},{12,28},{16,0},{20,4},{24,8},{28,12},{1,17},{... | collective-permute-start | bytes 2359304 | tf_op jit(solution)/shard_map/ppermute | solution.py:214
  32.6 26.2 %collective-permute-start.8 = (bf16[3,512,256]{2,1,0:T(8,128)(2,1)S(1)}, bf16[3,512,256]{2,1,0:T(8,128)(2,1)S(1)}, u32[]{:S(2)}, u32[]{:S(2)}) collective-permute-start(bf16[3,512,256]{2,1,0:T(8,128)(2,1)S(1)} %collective-permute-done.refs_9_), channel_id=1, source_target_pairs={{0,8},{4,12},{8,0},{12,4},{16,24},{20,28},{24,16},{28,20},{1,9},{5... | collective-permute-start | bytes 2359304 | tf_op jit(solution)/shard_map/ppermute | solution.py:214
  34.2 19.0 %collective-permute-start.2 = (bf16[1,512,256]{2,1,0:T(8,128)(2,1)S(1)}, bf16[1,512,256]{2,1,0:T(8,128)(2,1)S(1)}, u32[]{:S(2)}, u32[]{:S(2)}) collective-permute-start(bf16[1,512,256]{2,1,0:T(8,128)(2,1)S(1)} %constant_dynamic-slice_fusion), channel_id=1, source_target_pairs={{0,3},{1,0},{2,1},{3,2},{4,7},{5,4},{6,5},{7,6},{8,11},{9,8},{10,9... | collective-permute-start | bytes 786440 | tf_op jit(solution)/shard_map/ppermute | solution.py:277
  38.1 30.4 %collective-permute-start.12 = (bf16[3,512,256]{2,1,0:T(8,128)(2,1)S(1)}, bf16[3,512,256]{2,1,0:T(8,128)(2,1)S(1)}, u32[]{:S(2)}, u32[]{:S(2)}) collective-permute-start(bf16[3,512,256]{2,1,0:T(8,128)(2,1)S(1)} %collective-permute-done.refs_9_), channel_id=1, source_target_pairs={{0,4},{4,0},{8,12},{12,8},{16,20},{20,16},{24,28},{28,24},{1,5},{5... | collective-permute-start | bytes 2359304 | tf_op jit(solution)/shard_map/ppermute | solution.py:214
  53.3 10.0 %collective-permute-start.4 = (bf16[1,512,256]{2,1,0:T(8,128)(2,1)S(1)}, bf16[1,512,256]{2,1,0:T(8,128)(2,1)S(1)}, u32[]{:S(2)}, u32[]{:S(2)}) collective-permute-start(bf16[1,512,256]{2,1,0:T(8,128)(2,1)S(1)} %collective-permute-done.2.refs_12_), channel_id=1, source_target_pairs={{0,3},{1,0},{2,1},{3,2},{4,7},{5,4},{6,5},{7,6},{8,11},{9,8},{10,9... | collective-permute-start | bytes 786440 | tf_op jit(solution)/shard_map/ppermute | solution.py:277
  58.7 9.7 %collective-permute-start.11 = (bf16[1,512,256]{2,1,0:T(8,128)(2,1)S(1)}, bf16[1,512,256]{2,1,0:T(8,128)(2,1)S(1)}, u32[]{:S(2)}, u32[]{:S(2)}) collective-permute-start(bf16[1,512,256]{2,1,0:T(8,128)(2,1)S(1)} %slice.25), channel_id=1, source_target_pairs={{0,16},{4,20},{8,24},{12,28},{16,0},{20,4},{24,8},{28,12},{1,17},{... | collective-permute-start | bytes 786440 | tf_op jit(solution)/shard_map/ppermute | solution.py:214
  63.3 21.7 %collective-permute-start.19 = (bf16[3,512,256]{2,1,0:T(8,128)(2,1)S(1)}, bf16[3,512,256]{2,1,0:T(8,128)(2,1)}, u32[]{:S(2)}, u32[]{:S(2)}) collective-permute-start(bf16[3,512,256]{2,1,0:T(8,128)(2,1)S(1)} %collective-permute-done.1.refs_21_), channel_id=1, source_target_pairs={{0,16},{4,20},{8,24},{12,28},{16,0},{20,4},{24,8},{28,12},{1,17},{... | collective-permute-start | bytes 2359304 | tf_op jit(solution)/shard_map/ppermute | solution.py:214
  68.5 20.1 %collective-permute-start.18 = (bf16[3,512,256]{2,1,0:T(8,128)(2,1)S(1)}, bf16[3,512,256]{2,1,0:T(8,128)(2,1)}, u32[]{:S(2)}, u32[]{:S(2)}) collective-permute-start(bf16[3,512,256]{2,1,0:T(8,128)(2,1)S(1)} %collective-permute-done.1.refs_21_), channel_id=1, source_target_pairs={{0,8},{4,12},{8,0},{12,4},{16,24},{20,28},{24,16},{28,20},{1,9},{5... | collective-permute-start | bytes 2359304 | tf_op jit(solution)/shard_map/ppermute | solution.py:214
  68.7 19.8 %collective-permute-start.22 = (bf16[3,512,256]{2,1,0:T(8,128)(2,1)S(1)}, bf16[3,512,256]{2,1,0:T(8,128)(2,1)S(1)}, u32[]{:S(2)}, u32[]{:S(2)}) collective-permute-start(bf16[3,512,256]{2,1,0:T(8,128)(2,1)S(1)} %collective-permute-done.1.refs_21_), channel_id=1, source_target_pairs={{0,4},{4,0},{8,12},{12,8},{16,20},{20,16},{24,28},{28,24},{1,5},{5... | collective-permute-start | bytes 2359304 | tf_op jit(solution)/shard_map/ppermute | solution.py:214
  69.0 22.9 %collective-permute-start.13 = (bf16[3,512,256]{2,1,0:T(8,128)(2,1)S(1)}, bf16[3,512,256]{2,1,0:T(8,128)(2,1)S(1)}, u32[]{:S(2)}, u32[]{:S(2)}) collective-permute-start(bf16[3,512,256]{2,1,0:T(8,128)(2,1)S(1)} %collective-permute-done.8.refs_10_), channel_id=1, source_target_pairs={{0,4},{4,0},{8,12},{12,8},{16,20},{20,16},{24,28},{28,24},{1,5},{5... | collective-permute-start | bytes 2359304 | tf_op jit(solution)/shard_map/ppermute | solution.py:214
  70.0 22.3 %collective-permute-start.3 = (bf16[3,512,256]{2,1,0:T(8,128)(2,1)S(1)}, bf16[3,512,256]{2,1,0:T(8,128)(2,1)S(1)}, u32[]{:S(2)}, u32[]{:S(2)}) collective-permute-start(bf16[3,512,256]{2,1,0:T(8,128)(2,1)S(1)} %collective-permute-done.1.refs_21_), channel_id=1, source_target_pairs={{0,3},{1,0},{2,1},{3,2},{4,7},{5,4},{6,5},{7,6},{8,11},{9,8},{10,9... | collective-permute-start | bytes 2359304 | tf_op jit(solution)/shard_map/ppermute | solution.py:275
  85.0 16.4 %collective-permute-start.14 = (bf16[3,512,256]{2,1,0:T(8,128)(2,1)S(1)}, bf16[3,512,256]{2,1,0:T(8,128)(2,1)}, u32[]{:S(2)}, u32[]{:S(2)}) collective-permute-start(bf16[3,512,256]{2,1,0:T(8,128)(2,1)S(1)} %collective-permute-done.9.refs_11_), channel_id=1, source_target_pairs={{0,4},{4,0},{8,12},{12,8},{16,20},{20,16},{24,28},{28,24},{1,5},{5... | collective-permute-start | bytes 2359304 | tf_op jit(solution)/shard_map/ppermute | solution.py:214
  88.5 16.3 %collective-permute-start.23 = (bf16[3,512,256]{2,1,0:T(8,128)(2,1)}, bf16[3,512,256]{2,1,0:T(8,128)(2,1)}, u32[]{:S(2)}, u32[]{:S(2)}) collective-permute-start(bf16[3,512,256]{2,1,0:T(8,128)(2,1)} %collective-permute-done.18.refs_22_), channel_id=1, source_target_pairs={{0,4},{4,0},{8,12},{12,8},{16,20},{20,16},{24,28},{28,24},{1,5},{5... | collective-permute-start | bytes 2359304 | tf_op jit(solution)/shard_map/ppermute | solution.py:214
  89.4 15.4 %collective-permute-start.24 = (bf16[3,512,256]{2,1,0:T(8,128)(2,1)}, bf16[3,512,256]{2,1,0:T(8,128)(2,1)}, u32[]{:S(2)}, u32[]{:S(2)}) collective-permute-start(bf16[3,512,256]{2,1,0:T(8,128)(2,1)} %collective-permute-done.19.refs_23_), channel_id=1, source_target_pairs={{0,4},{4,0},{8,12},{12,8},{16,20},{20,16},{24,28},{28,24},{1,5},{5... | collective-permute-start | bytes 2359304 | tf_op jit(solution)/shard_map/ppermute | solution.py:214
  101.4 30.4 %collective-permute-start.5 = (bf16[3,512,256]{2,1,0:T(8,128)(2,1)S(1)}, bf16[3,512,256]{2,1,0:T(8,128)(2,1)S(1)}, u32[]{:S(2)}, u32[]{:S(2)}) collective-permute-start(bf16[3,512,256]{2,1,0:T(8,128)(2,1)S(1)} %collective-permute-done.3.refs_6_.refs_5_), channel_id=1, source_target_pairs={{0,8},{4,12},{8,0},{12,4},{16,24},{20,28},{24,16},{28,20},{1,9},{5... | collective-permute-start | bytes 2359304 | tf_op jit(solution)/shard_map/ppermute | solution.py:214
  103.1 28.8 %collective-permute-start.6 = (bf16[3,512,256]{2,1,0:T(8,128)(2,1)S(1)}, bf16[3,512,256]{2,1,0:T(8,128)(2,1)S(1)}, u32[]{:S(2)}, u32[]{:S(2)}) collective-permute-start(bf16[3,512,256]{2,1,0:T(8,128)(2,1)S(1)} %collective-permute-done.3.refs_6_.refs_5_), channel_id=1, source_target_pairs={{0,16},{4,20},{8,24},{12,28},{16,0},{20,4},{24,8},{28,12},{1,17},{... | collective-permute-start | bytes 2359304 | tf_op jit(solution)/shard_map/ppermute | solution.py:214
  104.8 27.0 %collective-permute-start.7 = (bf16[1,512,256]{2,1,0:T(8,128)(2,1)}, bf16[1,512,256]{2,1,0:T(8,128)(2,1)S(1)}, u32[]{:S(2)}, u32[]{:S(2)}) collective-permute-start(bf16[1,512,256]{2,1,0:T(8,128)(2,1)} %copy-done.20), channel_id=1, source_target_pairs={{0,3},{1,0},{2,1},{3,2},{4,7},{5,4},{6,5},{7,6},{8,11},{9,8},{10,9... | collective-permute-start | bytes 786440 | tf_op jit(solution)/shard_map/ppermute | solution.py:277
  134.6 12.2 %collective-permute-start.30 = (bf16[3,512,256]{2,1,0:T(8,128)(2,1)S(1)}, bf16[3,512,256]{2,1,0:T(8,128)(2,1)S(1)}, u32[]{:S(2)}, u32[]{:S(2)}) collective-permute-start(bf16[3,512,256]{2,1,0:T(8,128)(2,1)S(1)} %collective-permute-done.3.refs_6_.refs_5_), channel_id=1, source_target_pairs={{0,4},{4,0},{8,12},{12,8},{16,20},{20,16},{24,28},{28,24},{1,5},{5... | collective-permute-start | bytes 2359304 | tf_op jit(solution)/shard_map/ppermute | solution.py:214
  134.6 12.2 %collective-permute-start.31 = (bf16[3,512,256]{2,1,0:T(8,128)(2,1)S(1)}, bf16[3,512,256]{2,1,0:T(8,128)(2,1)}, u32[]{:S(2)}, u32[]{:S(2)}) collective-permute-start(bf16[3,512,256]{2,1,0:T(8,128)(2,1)S(1)} %collective-permute-done.5.refs_7_.refs_6_), channel_id=1, source_target_pairs={{0,4},{4,0},{8,12},{12,8},{16,20},{20,16},{24,28},{28,24},{1,5},{5... | collective-permute-start | bytes 2359304 | tf_op jit(solution)/shard_map/ppermute | solution.py:214
  135.1 11.7 %collective-permute-start.32 = (bf16[3,512,256]{2,1,0:T(8,128)(2,1)S(1)}, bf16[3,512,256]{2,1,0:T(8,128)(2,1)}, u32[]{:S(2)}, u32[]{:S(2)}) collective-permute-start(bf16[3,512,256]{2,1,0:T(8,128)(2,1)S(1)} %collective-permute-done.6.refs_8_.refs_7_), channel_id=1, source_target_pairs={{0,4},{4,0},{8,12},{12,8},{16,20},{20,16},{24,28},{28,24},{1,5},{5... | collective-permute-start | bytes 2359304 | tf_op jit(solution)/shard_map/ppermute | solution.py:214
  135.2 8.9 %collective-permute-start.29 = (bf16[1,512,256]{2,1,0:T(8,128)(2,1)S(1)}, bf16[1,512,256]{2,1,0:T(8,128)(2,1)}, u32[]{:S(2)}, u32[]{:S(2)}) collective-permute-start(bf16[1,512,256]{2,1,0:T(8,128)(2,1)S(1)} %slice.23), channel_id=1, source_target_pairs={{0,16},{4,20},{8,24},{12,28},{16,0},{20,4},{24,8},{28,12},{1,17},{... | collective-permute-start | bytes 786440 | tf_op jit(solution)/shard_map/ppermute | solution.py:214
  157.1 30.2 %all-to-all-start = ((bf16[8,2,256,256]{3,2,1,0:T(8,128)(2,1)}), bf16[8,2,256,256]{3,2,1,0:T(8,128)(2,1)S(1)}, u32[]{:S(2)}, u32[]{:S(2)}) async-start(bf16[8,2,256,256]{3,2,1,0:T(8,128)(2,1)} %bitcast.10), calls=%async_computation | async-start | bytes 4194304 | tf_op jit(solution)/shard_map/all_to_all | solution.py:294
  (40 other events, 661.7 us)

commit v5 on v4

v5 whole, which is shorter than its diff:
```python
import functools

import jax
import jax.numpy as jnp
from jax import lax
from jax.experimental import pallas as pl
from jax.experimental.pallas import tpu as pltpu
from jax.sharding import PartitionSpec as P

SMEM = pl.BlockSpec(memory_space=pltpu.SMEM)
VMEM = pl.BlockSpec(memory_space=pltpu.VMEM)
HBM = pl.BlockSpec(memory_space=pltpu.HBM)
MIB = 1 << 20
WIDTH_BITS, SOURCE_BITS, LAG_BITS, STEP_BITS = 5, 8, 8, 4
FIELDS = (WIDTH_BITS, SOURCE_BITS, LAG_BITS, STEP_BITS)
ROW_PARTS = 2


def list_task(base, span, total, steps, pair, tasks, counts):
    source, klass, lag, place = pair
    start = lax.rem(lag - base + total, total)
    inside = start < span
    first = jnp.where(inside, start, 0)
    skip = jnp.where(inside, 0, total - start)
    width = jnp.maximum(jnp.where(inside, jnp.minimum(steps, span - start), steps - skip), 0)
    packed = place
    for value, bits in ((skip, STEP_BITS), (first, LAG_BITS), (source, SOURCE_BITS), (width, WIDTH_BITS)):
        packed = (packed << bits) | value
    at = counts[klass]
    tasks[klass, at] = packed
    counts[klass] = at + jnp.where(width > 0, 1, 0)
    return width > 0


def run_width(width, low, high, run):
    if low == high:
        run(low)
        return
    middle = (low + high) // 2

    @pl.when(width <= middle)
    def _():
        run_width(width, low, middle, run)

    @pl.when(width > middle)
    def _():
        run_width(width, middle + 1, high, run)


def run_task(packed, klass, steps, hist, table, acc):
    panels = table.shape[2]
    part = hist.shape[1] // ROW_PARTS
    fields = []
    for bits in FIELDS:
        fields.append(packed & ((1 << bits) - 1))
        packed = packed >> bits
    width, source, lag, step = fields
    rows = pl.multiple_of(lag * panels, panels)
    columns = pl.multiple_of(step * panels, panels)

    def run(n):
        for p in range(ROW_PARTS):
            acc[packed, p * part : (p + 1) * part, :] += jnp.dot(
                hist[source, p * part : (p + 1) * part, pl.ds(columns, n * panels)],
                table[klass, pl.ds(rows, n * panels), :],
                preferred_element_type=jnp.float32,
            )

    run_width(width, 1, steps, run)


def window_kernel(config, *refs):
    served, local, begun, narrow, places, total, height, owned = config
    refs = list(refs)
    where = refs.pop(0)
    served_refs = [refs.pop(0) for _ in range(3 if served else 0)]
    local_refs = [refs.pop(0) for _ in range(4 if local else 0)]
    hist_ref = refs.pop(0)
    pieces = [refs.pop(0) for _ in places]
    before = [refs.pop(0) for _ in range((bool(served) + bool(local)) if begun else 0)]
    outs = [refs.pop(0) for _ in range(bool(served) + bool(local))]
    table, hist, acc, tasks, counts, used, sems, ends, served_sems = refs
    base, group = where[0], where[1]
    classes, _, panels = table.shape
    span = table.shape[1] // panels
    steps = hist.shape[2] // panels

    pltpu.make_async_copy(hist_ref, hist, ends.at[0]).start()
    near = acc.at[pl.ds(served, owned)] if local else None
    if local and begun:
        pltpu.make_async_copy(before[-1], near, ends.at[1]).start()
    for k in range(classes):
        for (mask, first), piece in zip(places, pieces):
            rows = piece.shape[1]
            start = pl.multiple_of((group ^ mask) * height + first, 16)
            pltpu.make_async_copy(
                piece.at[k], table.at[k, pl.ds(start, rows), :], sems.at[k]
            ).start()
    if not begun:
        acc[...] = jnp.zeros_like(acc)
    for k in range(classes):
        counts[k] = 0

    def served_copy(i, back):
        ends_of = (acc.at[i], outs[0].at[i]) if back else (before[0].at[i], acc.at[i])
        return pltpu.make_async_copy(*ends_of, served_sems.at[i])

    if served:
        peers, slots = served_refs[0].shape

        @pl.loop(0, peers)
        def _(i):
            for c in range(slots):
                source, lag, klass = (ref[i, c] for ref in served_refs)
                place = i * slots + c
                touched = list_task(
                    base, span, total, steps, (source, klass, lag, place), tasks, counts
                )
                needed = touched | narrow
                used[place] = jnp.where(touched, 1, 0)
                if begun:
                    @pl.when(needed)
                    def _():
                        served_copy(place, False).start()

    if local:
        @pl.loop(0, local_refs[0].shape[0])
        def _(i):
            source, lag, klass, target = (ref[i] for ref in local_refs)
            list_task(
                base, span, total, steps, (source, klass, lag, target + served), tasks, counts
            )

    pltpu.make_async_copy(hist_ref, hist, ends.at[0]).wait()
    if local and begun:
        pltpu.make_async_copy(before[-1], near, ends.at[1]).wait()
    if served and begun:
        @pl.loop(0, served)
        def _(i):
            @pl.when((used[i] != 0) | narrow)
            def _():
                served_copy(i, False).wait()

    @pl.loop(0, classes)
    def _(k):
        pltpu.make_async_copy(table.at[k], table.at[k], sems.at[k]).wait()

        @pl.loop(0, counts[k])
        def _(j):
            run_task(tasks[k, j], k, steps, hist, table, acc)

    if narrow:
        outs[0][...] = acc[...].astype(outs[0].dtype)
        return
    if local:
        pltpu.make_async_copy(near, outs[-1], ends.at[1]).start()
    if served:
        for wait in (False, True):
            @pl.loop(0, served)
            def _(i):
                @pl.when((used[i] != 0) | (not begun))
                def _():
                    copy = served_copy(i, True)
                    copy.wait() if wait else copy.start()
    if local:
        pltpu.make_async_copy(near, outs[-1], ends.at[1]).wait()


def window_sums(shard, group, served, local, hist_t, pieces, sums, lanes, rows, narrow=False):
    owned, excite, depth = hist_t.shape
    classes, _, panels = pieces[0][2].shape
    places = served[0].size if served else 0
    targets = owned if local else 0
    pairs = places + (local[0].size if local else 0)
    steps = depth // panels
    height = max(first + value.shape[1] for _, first, value in pieces)
    config = (
        places,
        bool(local),
        sums is not None,
        narrow,
        tuple(piece[:2] for piece in pieces),
        lanes * rows // panels,
        height,
        targets,
    )
    operands = [jnp.stack([shard * (rows // panels), group]).astype(jnp.int32), *served, *local]
    wide = [hist_t, *[piece[2] for piece in pieces]]
    before = list(sums) if sums is not None else []
    outs = [
        jax.ShapeDtypeStruct((n, excite, panels), jnp.bfloat16 if narrow else jnp.float32)
        for n in (places, targets)
        if n
    ]
    return pl.pallas_call(
        functools.partial(window_kernel, config),
        out_shape=outs,
        in_specs=[SMEM] * len(operands) + [HBM] * (len(wide) + len(before)),
        out_specs=[VMEM if narrow else HBM] * len(outs),
        scratch_shapes=[
            pltpu.VMEM((classes, rows, panels), jnp.bfloat16),
            pltpu.VMEM(hist_t.shape, hist_t.dtype),
            pltpu.VMEM((places + targets, excite, panels), jnp.float32),
            pltpu.SMEM((classes, pairs + 1), jnp.int32),
            pltpu.SMEM((classes,), jnp.int32),
            pltpu.SMEM((max(places, 1),), jnp.int32),
            pltpu.SemaphoreType.DMA((classes,)),
            pltpu.SemaphoreType.DMA((2,)),
            pltpu.SemaphoreType.DMA((max(places, 1),)),
        ],
        input_output_aliases={} if narrow else {
            len(operands) + len(wide) + n: n for n in range(len(before))
        },
        compiler_params=pltpu.CompilerParams(vmem_limit_bytes=58 * MIB),
        cost_estimate=pl.CostEstimate(
            flops=2 * pairs * panels * depth * excite,
            bytes_accessed=2 * classes * rows * panels + 2 * hist_t.size,
            transcendentals=0,
        ),
    )(*operands, *wide, *before)


def update_kernel(target_ref, near_ref, recv_ref, inverse_ref, incident_ref, out_ref, total):
    total[...] = near_ref[...]
    peers, slots = target_ref.shape

    @pl.loop(0, peers)
    def _(i):
        for c in range(slots):
            total[target_ref[i, c]] += recv_ref[i, c].astype(jnp.float32)

    for t in range(out_ref.shape[0]):
        residual = (incident_ref[t].astype(jnp.float32) - total[t].T).astype(jnp.bfloat16)
        out_ref[t] = jnp.dot(
            inverse_ref[t], residual, preferred_element_type=jnp.float32
        ).astype(out_ref.dtype)


def update(target, near, recv, inverse, incident):
    return pl.pallas_call(
        update_kernel,
        out_shape=jax.ShapeDtypeStruct(incident.shape, jnp.bfloat16),
        in_specs=[SMEM] + [VMEM] * 4,
        out_specs=VMEM,
        scratch_shapes=[pltpu.VMEM(near.shape, jnp.float32)],
        compiler_params=pltpu.CompilerParams(vmem_limit_bytes=32 * MIB),
    )(target, near, recv, inverse, incident)


def swap(value, bit, peers):
    return lax.ppermute(value, "grp", [(i, i ^ bit) for i in range(peers)])


def upper(value, peers):
    masks, held = [0], [value]
    bit = 8
    while bit < peers:
        masks += [mask ^ bit for mask in masks]
        held += [swap(value, bit, peers) for value in held]
        bit *= 2
    return masks, held


def with_other_core(found, peers):
    return found + [(mask ^ 1, first, swap(v, 1, peers)) for mask, first, v in found]


def per_device(
    weights,
    history,
    send_patch,
    send_lag,
    send_class,
    recv_target,
    local_src,
    local_lag,
    local_class,
    local_target,
    inverse_blocks,
    incident,
):
    classes, rows, panels = weights.shape
    peers, slots = send_patch.shape
    height = rows // peers
    group = lax.axis_index("grp")
    lane = lax.axis_index("lag")
    lanes = lax.axis_size("lag")
    ring = [(i, (i - 1) % lanes) for i in range(lanes)]
    served = (send_patch, send_lag, send_class)
    local = (local_src, local_lag, local_class, local_target)

    hist_t = jnp.swapaxes(history, 1, 2)
    half = height // 2

    def part(index):
        return lax.dynamic_slice(weights, (0, index * height, 0), (classes, height, panels))

    def add_shard(step, sums):
        shard = lax.rem(lane + step, lanes)
        return window_sums(shard, group, served, local, hist_t, rounds[step - 1], sums, lanes, rows)

    sums = window_sums(
        lane, group * 0, served, local, hist_t, [(0, 0, weights)], None, lanes, rows
    )
    own = part(group)
    corner = part(group ^ 6)
    rounds = []
    for step in range(1, lanes):
        own = lax.ppermute(own, "lag", ring)
        if step == 1:
            ready, sums = lax.optimization_barrier((own, sums))
        else:
            if step > 2:
                sums = add_shard(step - 2, sums)
            ready, corner, sums, across, along = lax.optimization_barrier(
                (own, corner, sums, across, along)
            )
            found = [(m, 0, v) for m, v in zip(masks, held)]
            found += [(m ^ 2, 0, v) for m, v in zip(masks, across)]
            found += [(m ^ 4, 0, v) for m, v in zip(masks, along)]
            found += [(m ^ 6, 0, swap(v[:, :half], 2, peers)) for m, v in zip(masks, along)]
            found += [(m ^ 6, half, swap(v[:, half:], 4, peers)) for m, v in zip(masks, across)]
            rounds.append(with_other_core(found, peers))
        masks, held = upper(ready, peers)
        across = [swap(value, 2, peers) for value in held]
        along = [swap(value, 4, peers) for value in held]
    corner = lax.ppermute(corner, "lag", [(j, i) for i, j in ring])
    if lanes > 2:
        sums = add_shard(lanes - 2, sums)
        across, along, corner, sums = lax.optimization_barrier((across, along, corner, sums))
    _, corners = upper(corner, peers)
    found = [(m, 0, v) for m, v in zip(masks, held)]
    found += [(m ^ 2, 0, v) for m, v in zip(masks, across)]
    found += [(m ^ 4, 0, v) for m, v in zip(masks, along)]
    found += [(m ^ 6, 0, v) for m, v in zip(masks, corners)]
    rounds.append(with_other_core(found, peers))
    last = lax.rem(lane + lanes - 1, lanes)
    contribution = window_sums(
        last, group, served, (), hist_t, rounds[-1], sums[:1], lanes, rows, narrow=True
    )[0]
    recv = lax.all_to_all(
        contribution.reshape(peers, slots, *contribution.shape[1:]),
        "grp",
        split_axis=0,
        concat_axis=0,
        tiled=True,
    )
    near = window_sums(last, group, (), local, hist_t, rounds[-1], sums[1:], lanes, rows)[0]
    return update(recv_target, near, recv, inverse_blocks, incident)


def solution(mesh):
    both = ("grp", "lag")
    return jax.shard_map(
        per_device,
        mesh=mesh,
        in_specs=(
            P(None, "lag", None),
            P(both, None, None),
            P(both, None),
            P(both, None),
            P(both, None),
            P(both, None),
            P(both),
            P(both),
            P(both),
            P(both),
            P(both, None, None),
            P(both, None, None),
        ),
        out_specs=P(both, None, None),
        check_vma=False,
    )
```

time: 192 us -> 177 us (0.922)
  starting transfers between devices: 37.5 us -> 25.9 us
  waiting for transfers between devices: 70.7 us -> 62.5 us
  Pallas kernels: 64.1 us -> 72.1 us
    ppermute x3 -> x1, waiting for transfers between devices: 17.1 us -> 3.28 us  [per_device(): corner = lax.ppermute(corner, 'lag', [(j, i) for i, j in ring])]
    pallas_call x4 -> x5, Pallas kernels: 61.7 us -> 69.7 us  [window_sums(): pl.pallas_call(functools.partial(window_kernel, config), out_shape=outs,...]
    ppermute x3 -> x1, starting transfers between devices: 7.43 us -> 0.01 us  [per_device(): corner = lax.ppermute(corner, 'lag', [(j, i) for i, j in ring])]
    ppermute x30 -> x24, starting transfers between devices: 19.9 us -> 12.7 us  [swap(): return lax.ppermute(value, 'grp', [(i, i ^ bit) for i in range(peers)])]
    ppermute x3, starting transfers between devices: 6.64 us -> 9.49 us  [per_device(): own = lax.ppermute(own, 'lag', ring)]
    unnamed x59 -> x39, local copies, waits for them, and re-layouts: 12.2 us -> 9.72 us
    ppermute x30 -> x24, waiting for transfers between devices: 38.9 us -> 41.1 us  [swap(): return lax.ppermute(value, 'grp', [(i, i ^ bit) for i in range(peers)])]
  transfers between devices with their start and end apart: 37 -> 29, of which waited for: 13 -> 16; matrix products, arithmetic and copies ran while one was open for 7% -> 7% of each run, Pallas kernels for 27% -> 33%
where the time goes in v5:
time: 177 us; the launch traced here: 178 us
  Pallas kernels  72.1 us (41%)
  waiting for transfers between devices  62.5 us (35%)
  starting transfers between devices  25.9 us (15%)
  local copies, waits for them, and re-layouts  14.5 us (8%)
  other arithmetic  2.49 us (1%)
    pallas_call x5, Pallas kernels, window_sums(): pl.pallas_call(functools.partial(window_kernel, config), out_shape=outs,...  69.7 us
    ppermute x24, waiting for transfers between devices, swap(): return lax.ppermute(value, 'grp', [(i, i ^ bit) for i in range(peers)])  41.1 us
    all_to_all x1, waiting for transfers between devices, per_device(): lax.all_to_all(contribution.reshape(peers, slots, *contribution.shape[1:]...  16.5 us
    ppermute x24, starting transfers between devices, swap(): return lax.ppermute(value, 'grp', [(i, i ^ bit) for i in range(peers)])  12.7 us
    unnamed x39, local copies, waits for them, and re-layouts  9.72 us
    ppermute x3, starting transfers between devices, per_device(): own = lax.ppermute(own, 'lag', ring)  9.49 us
    all_to_all x1, starting transfers between devices, per_device(): lax.all_to_all(contribution.reshape(peers, slots, *contribution.shape[1:]...  3.71 us
  transfers between devices with their start and end apart: 29, of which 16 were waited for; matrix products, arithmetic and copies ran while one was open for 7% of the time, Pallas kernels for 33%

profile of v5, /device:TPU:0, one launch (start us, length us, event | category | flops | bytes accessed | tf_op | source)
XLA Modules:
  0.0 177.7 jit_solution(3539756703688736565)
XLA Ops:
  0.0 2.4 %constant_dynamic-slice_fusion = (bf16[3,512,256]{2,1,0:T(8,128)(2,1)}, bf16[3,512,256]{2,1,0:T(8,128)(2,1)S(1)}) fusion(bf16[3,4096,256]{2,1,0:T(8,128)(2,1)} %refs_9_.1, s32[]{:T(128)S(6)} %select_n.7, s32[]{:T(128)S(6)} %select_n.6), kind=kLoop, calls=%fused_computation.4 | loop fusion | bytes 3145736 | tf_op jit(solution)/shard_map/dynamic_slice | solution.py:296
  2.4 5.0 %collective-permute-start = (bf16[3,512,256]{2,1,0:T(8,128)(2,1)S(1)}, bf16[3,512,256]{2,1,0:T(8,128)(2,1)}, u32[]{:S(2)}, u32[]{:S(2)}) collective-permute-start(bf16[3,512,256]{2,1,0:T(8,128)(2,1)S(1)} %get-tuple-element.58), channel_id=1, source_target_pairs={{0,3},{1,0},{2,1},{3,2},{4,7},{5,4},{6,5},{7,6},{8,11},{9,8},{10,9... | collective-permute-start | bytes 2359304 | tf_op jit(solution)/shard_map/ppermute | solution.py:309
  7.4 6.3 %copy.18 = bf16[4,2048,256]{1,2,0:T(8,128)(2,1)} copy(bf16[4,2048,256]{2,1,0:T(8,128)(2,1)} %param.13) | data formatting | bytes 8388608 | tf_op args[1]
  16.4 16.2 %shard_map.118 = (f32[16,256,256]{2,1,0:T(8,128)}, f32[4,256,256]{2,1,0:T(8,128)}) custom-call(s32[2]{0:T(128)} %pad_add_fusion.1.refs_0_, s32[8,2]{1,0:T(8,128)} %copy.19.refs_1_, s32[8,2]{1,0:T(8,128)} %copy.20.refs_2_, s32[8,2]{1,0:T(8,128)} %copy.21.refs_3_, s32[48]{0:T(128)} %refs_1_.5, s32[48]{0:T(128)} %refs_2_.5, s32[48]{0:T(128)} %refs_3_.5, ...), custom_call_target="tpu_custom_call" | custom-call | flops 17179869184 | bytes 10485760 | tf_op jit(solution)/shard_map/pallas_call | solution.py:195
  32.7 1.6 collective-permute-start.4
  34.5 13.9 %collective-permute-done.3.refs_10_ = bf16[3,512,256]{2,1,0:T(8,128)(2,1)S(1)} collective-permute-done((bf16[3,512,256]{2,1,0:T(8,128)(2,1)}, bf16[3,512,256]{2,1,0:T(8,128)(2,1)S(1)}, u32[]{:S(2)}, u32[]{:S(2)}) %collective-permute-start.3) | collective-permute-done | bytes 786464 | tf_op jit(solution)/shard_map/ppermute | solution.py:251
  49.8 1.7 collective-permute-done.1.refs_9_
  51.6 1.7 collective-permute-start.5
  54.2 6.7 %collective-permute-done.5.refs_12_ = bf16[3,256,256]{2,1,0:T(8,128)(2,1)S(1)} collective-permute-done((bf16[3,256,256]{2,1,0:T(8,128)(2,1)S(1)}, bf16[3,256,256]{2,1,0:T(8,128)(2,1)S(1)}, u32[]{:S(2)}, u32[]{:S(2)}) %collective-permute-start.5) | collective-permute-done | bytes 393248 | tf_op jit(solution)/shard_map/ppermute | solution.py:251
  60.9 1.5 collective-permute-done.6.refs_13_
  64.6 4.2 %collective-permute-start.2 = (bf16[3,512,256]{2,1,0:T(8,128)(2,1)S(1)}, bf16[3,512,256]{2,1,0:T(8,128)(2,1)S(1)}, u32[]{:S(2)}, u32[]{:S(2)}) collective-permute-start(bf16[3,512,256]{2,1,0:T(8,128)(2,1)S(1)} %collective-permute-done.1.refs_9_), channel_id=1, source_target_pairs={{0,3},{1,0},{2,1},{3,2},{4,7},{5,4},{6,5},{7,6},{8,11},{9,8},{10,9... | collective-permute-start | bytes 2359304 | tf_op jit(solution)/shard_map/ppermute | solution.py:309
  68.8 17.5 %shard_map.119 = (f32[16,256,256]{2,1,0:T(8,128)}, f32[4,256,256]{2,1,0:T(8,128)}) custom-call(s32[2]{0:T(128)} %pad_add_fusion.2.refs_0_, s32[8,2]{1,0:T(8,128)} %copy.19.refs_1_, s32[8,2]{1,0:T(8,128)} %copy.20.refs_2_, s32[8,2]{1,0:T(8,128)} %copy.21.refs_3_, s32[48]{0:T(128)} %refs_1_.5, ...), custom_call_target="tpu_custom_call", output_to_operand_aliasing={{0}: (19, {}), {1}: (20, {})} | custom-call | flops 17179869184 | bytes 10485760 | tf_op jit(solution)/shard_map/pallas_call | solution.py:195
  87.7 4.2 %collective-permute-start.17 = (bf16[3,256,256]{2,1,0:T(8,128)(2,1)S(1)}, bf16[3,256,256]{2,1,0:T(8,128)(2,1)S(1)}, u32[]{:S(2)}, u32[]{:S(2)}) collective-permute-start(bf16[3,256,256]{2,1,0:T(8,128)(2,1)S(1)} %slice.14), channel_id=1, source_target_pairs={{0,8},{4,12},{8,0},{12,4},{16,24},{20,28},{24,16},{28,20},{1,9},{5... | collective-permute-start | bytes 1179656 | tf_op jit(solution)/shard_map/ppermute | solution.py:251
  93.6 7.4 %collective-permute-done.17.refs_12_ = bf16[3,256,256]{2,1,0:T(8,128)(2,1)S(1)} collective-permute-done((bf16[3,256,256]{2,1,0:T(8,128)(2,1)S(1)}, bf16[3,256,256]{2,1,0:T(8,128)(2,1)S(1)}, u32[]{:S(2)}, u32[]{:S(2)}) %collective-permute-start.17) | collective-permute-done | bytes 393248 | tf_op jit(solution)/shard_map/ppermute | solution.py:251
  102.1 1.9 %collective-permute-done.18.refs_13_ = bf16[3,256,256]{2,1,0:T(8,128)(2,1)} collective-permute-done((bf16[3,256,256]{2,1,0:T(8,128)(2,1)S(1)}, bf16[3,256,256]{2,1,0:T(8,128)(2,1)}, u32[]{:S(2)}, u32[]{:S(2)}) %collective-permute-start.18) | collective-permute-done | bytes 393248 | tf_op jit(solution)/shard_map/ppermute | solution.py:251
  106.2 15.3 %shard_map.120 = (f32[16,256,256]{2,1,0:T(8,128)}, f32[4,256,256]{2,1,0:T(8,128)}) custom-call(s32[2]{0:T(128)} %pad_add_fusion.3.refs_0_, s32[8,2]{1,0:T(8,128)} %copy.19.refs_1_, s32[8,2]{1,0:T(8,128)} %copy.20.refs_2_, s32[8,2]{1,0:T(8,128)} %copy.21.refs_3_, s32[48]{0:T(128)} %refs_1_.5, ...), custom_call_target="tpu_custom_call", output_to_operand_aliasing={{0}: (19, {}), {1}: (20, {})} | custom-call | flops 17179869184 | bytes 10485760 | tf_op jit(solution)/shard_map/pallas_call | solution.py:195
  121.5 3.1 %collective-permute-done.14.refs_7_.refs_6_ = bf16[3,512,256]{2,1,0:T(8,128)(2,1)S(1)} collective-permute-done((bf16[3,512,256]{2,1,0:T(8,128)(2,1)S(1)}, bf16[3,512,256]{2,1,0:T(8,128)(2,1)S(1)}, u32[]{:S(2)}, u32[]{:S(2)}) %collective-permute-start.14) | collective-permute-done | bytes 786464 | tf_op jit(solution)/shard_map/ppermute | solution.py:251
  124.9 3.3 %collective-permute-done.16.refs_9_.refs_8_ = bf16[3,512,256]{2,1,0:T(8,128)(2,1)} collective-permute-done((bf16[3,512,256]{2,1,0:T(8,128)(2,1)}, bf16[3,512,256]{2,1,0:T(8,128)(2,1)}, u32[]{:S(2)}, u32[]{:S(2)}) %collective-permute-start.16) | collective-permute-done | bytes 786464 | tf_op jit(solution)/shard_map/ppermute | solution.py:327
  130.6 2.2 %collective-permute-done.26.refs_12_.refs_11_ = bf16[3,512,256]{2,1,0:T(8,128)(2,1)} collective-permute-done((bf16[3,512,256]{2,1,0:T(8,128)(2,1)S(1)}, bf16[3,512,256]{2,1,0:T(8,128)(2,1)}, u32[]{:S(2)}, u32[]{:S(2)}) %collective-permute-start.26) | collective-permute-done | bytes 786464 | tf_op jit(solution)/shard_map/ppermute | solution.py:251
  133.0 10.6 %shard_map.122 = bf16[16,256,256]{2,1,0:T(8,128)(2,1)} custom-call(s32[2]{0:T(128)} %pad_add_fusion.refs_0_, s32[8,2]{1,0:T(8,128)} %copy.19.refs_1_, s32[8,2]{1,0:T(8,128)} %copy.20.refs_2_, s32[8,2]{1,0:T(8,128)} %copy.21.refs_3_, bf16[4,256,2048]{2,1,0:T(8,128)(2,1)} %bitcast.10, bf16[3,512,256]{2,1,0:T(8,128)(2,1)} %copy-done.3, ...), custom_call_target="tpu_custom_call" | custom-call | flops 4294967296 | bytes 10485760 | tf_op jit(solution)/shard_map/pallas_call | solution.py:195
  143.6 3.7 %all-to-all-start = ((bf16[8,2,256,256]{3,2,1,0:T(8,128)(2,1)}), bf16[8,2,256,256]{3,2,1,0:T(8,128)(2,1)S(1)}, u32[]{:S(2)}, u32[]{:S(2)}) async-start(bf16[8,2,256,256]{3,2,1,0:T(8,128)(2,1)} %bitcast.12), calls=%async_computation | async-start | bytes 4194304 | tf_op jit(solution)/shard_map/all_to_all | solution.py:341
  147.4 10.1 %shard_map.121.near_ref = f32[4,256,256]{2,1,0:T(8,128)} custom-call(s32[2]{0:T(128)} %pad_add_fusion.refs_0_, s32[48]{0:T(128)} %refs_1_.5, s32[48]{0:T(128)} %refs_2_.5, s32[48]{0:T(128)} %refs_3_.5, s32[48]{0:T(128)} %refs_4_.7, bf16[4,256,2048]{2,1,0:T(8,128)(2,1)} %bitcast.11, bf16[3,512,256]{2,1,0:T(8,128)(2,1)} %copy-done.3, ...), custom_call_target="tpu_custom_call", output_to_operand_aliasing={{}: (14, {})} | custom-call | flops 12884901888 | bytes 10485760 | tf_op jit(solution)/shard_map/pallas_call | solution.py:195
  157.5 16.5 %all-to-all-done.recv_ref = bf16[8,2,256,256]{3,2,1,0:T(8,128)(2,1)S(1)} async-done(((bf16[8,2,256,256]{3,2,1,0:T(8,128)(2,1)}), bf16[8,2,256,256]{3,2,1,0:T(8,128)(2,1)S(1)}, u32[]{:S(2)}, u32[]{:S(2)}) %all-to-all-start) | async-done | bytes 2097184 | tf_op jit(solution)/shard_map/all_to_all | solution.py:341
  175.2 2.4 %shard_map.123 = bf16[4,256,256]{2,1,0:T(8,128)(2,1)} custom-call(s32[8,2]{1,0:T(8,128)S(1)} %copy.31.target_ref, f32[4,256,256]{2,1,0:T(8,128)S(1)} %copy-done, bf16[8,2,256,256]{3,2,1,0:T(8,128)(2,1)S(1)} %all-to-all-done.recv_ref, bf16[4,256,256]{2,1,0:T(8,128)(2,1)S(1)} %copy-done.1, bf16[4,256,256]{2,1,0:T(8,128)(2,1)S(1)} %copy-done.2), custom_call_target="tpu_custom_call" | custom-call | tf_op jit(solution)/shard_map/pallas_call | solution.py:240
  (88 shorter events, 18.1 us)
Async XLA Ops:
  2.4 30.2 %collective-permute-start = (bf16[3,512,256]{2,1,0:T(8,128)(2,1)S(1)}, bf16[3,512,256]{2,1,0:T(8,128)(2,1)}, u32[]{:S(2)}, u32[]{:S(2)}) collective-permute-start(bf16[3,512,256]{2,1,0:T(8,128)(2,1)S(1)} %get-tuple-element.58), channel_id=1, source_target_pairs={{0,3},{1,0},{2,1},{3,2},{4,7},{5,4},{6,5},{7,6},{8,11},{9,8},{10,9... | collective-permute-start | bytes 2359304 | tf_op jit(solution)/shard_map/ppermute | solution.py:309
  32.6 15.8 %collective-permute-start.3 = (bf16[3,512,256]{2,1,0:T(8,128)(2,1)}, bf16[3,512,256]{2,1,0:T(8,128)(2,1)S(1)}, u32[]{:S(2)}, u32[]{:S(2)}) collective-permute-start(bf16[3,512,256]{2,1,0:T(8,128)(2,1)} %collective-permute-done.refs_9_), channel_id=1, source_target_pairs={{0,8},{4,12},{8,0},{12,4},{16,24},{20,28},{24,16},{28,20},{1,9},{5... | collective-permute-start | bytes 2359304 | tf_op jit(solution)/shard_map/ppermute | solution.py:251
  32.7 17.2 %collective-permute-start.4 = (bf16[3,512,256]{2,1,0:T(8,128)(2,1)}, bf16[3,512,256]{2,1,0:T(8,128)(2,1)S(1)}, u32[]{:S(2)}, u32[]{:S(2)}) collective-permute-start(bf16[3,512,256]{2,1,0:T(8,128)(2,1)} %collective-permute-done.refs_9_), channel_id=1, source_target_pairs={{0,16},{4,20},{8,24},{12,28},{16,0},{20,4},{24,8},{28,12},{1,17},{... | collective-permute-start | bytes 2359304 | tf_op jit(solution)/shard_map/ppermute | solution.py:251
  34.3 17.3 %collective-permute-start.1 = (bf16[3,512,256]{2,1,0:T(8,128)(2,1)}, bf16[3,512,256]{2,1,0:T(8,128)(2,1)S(1)}, u32[]{:S(2)}, u32[]{:S(2)}) collective-permute-start(bf16[3,512,256]{2,1,0:T(8,128)(2,1)} %collective-permute-done.refs_9_), channel_id=1, source_target_pairs={{0,3},{1,0},{2,1},{3,2},{4,7},{5,4},{6,5},{7,6},{8,11},{9,8},{10,9... | collective-permute-start | bytes 2359304 | tf_op jit(solution)/shard_map/ppermute | solution.py:309
  34.5 28.5 %collective-permute-start.7 = (bf16[3,512,256]{2,1,0:T(8,128)(2,1)}, bf16[3,512,256]{2,1,0:T(8,128)(2,1)S(1)}, u32[]{:S(2)}, u32[]{:S(2)}) collective-permute-start(bf16[3,512,256]{2,1,0:T(8,128)(2,1)} %collective-permute-done.refs_9_), channel_id=1, source_target_pairs={{0,4},{4,0},{8,12},{12,8},{16,20},{20,16},{24,28},{28,24},{1,5},{5... | collective-permute-start | bytes 2359304 | tf_op jit(solution)/shard_map/ppermute | solution.py:251
  51.6 9.3 %collective-permute-start.5 = (bf16[3,256,256]{2,1,0:T(8,128)(2,1)S(1)}, bf16[3,256,256]{2,1,0:T(8,128)(2,1)S(1)}, u32[]{:S(2)}, u32[]{:S(2)}) collective-permute-start(bf16[3,256,256]{2,1,0:T(8,128)(2,1)S(1)} %slice.12), channel_id=1, source_target_pairs={{0,8},{4,12},{8,0},{12,4},{16,24},{20,28},{24,16},{28,20},{1,9},{5... | collective-permute-start | bytes 1179656 | tf_op jit(solution)/shard_map/ppermute | solution.py:251
  53.3 9.1 %collective-permute-start.6 = (bf16[3,256,256]{2,1,0:T(8,128)(2,1)S(1)}, bf16[3,256,256]{2,1,0:T(8,128)(2,1)}, u32[]{:S(2)}, u32[]{:S(2)}) collective-permute-start(bf16[3,256,256]{2,1,0:T(8,128)(2,1)S(1)} %slice.13), channel_id=1, source_target_pairs={{0,16},{4,20},{8,24},{12,28},{16,0},{20,4},{24,8},{28,12},{1,17},{... | collective-permute-start | bytes 1179656 | tf_op jit(solution)/shard_map/ppermute | solution.py:251
  53.7 10.9 %collective-permute-start.8 = (bf16[3,512,256]{2,1,0:T(8,128)(2,1)S(1)}, bf16[3,512,256]{2,1,0:T(8,128)(2,1)}, u32[]{:S(2)}, u32[]{:S(2)}) collective-permute-start(bf16[3,512,256]{2,1,0:T(8,128)(2,1)S(1)} %collective-permute-done.3.refs_10_), channel_id=1, source_target_pairs={{0,4},{4,0},{8,12},{12,8},{16,20},{20,16},{24,28},{28,24},{1,5},{5... | collective-permute-start | bytes 2359304 | tf_op jit(solution)/shard_map/ppermute | solution.py:251
  53.7 15.1 %collective-permute-start.9 = (bf16[3,512,256]{2,1,0:T(8,128)(2,1)S(1)}, bf16[3,512,256]{2,1,0:T(8,128)(2,1)}, u32[]{:S(2)}, u32[]{:S(2)}) collective-permute-start(bf16[3,512,256]{2,1,0:T(8,128)(2,1)S(1)} %collective-permute-done.4.refs_11_), channel_id=1, source_target_pairs={{0,4},{4,0},{8,12},{12,8},{16,20},{20,16},{24,28},{28,24},{1,5},{5... | collective-permute-start | bytes 2359304 | tf_op jit(solution)/shard_map/ppermute | solution.py:251
  63.0 23.4 %collective-permute-start.12 = (bf16[3,512,256]{2,1,0:T(8,128)(2,1)S(1)}, bf16[3,512,256]{2,1,0:T(8,128)(2,1)}, u32[]{:S(2)}, u32[]{:S(2)}) collective-permute-start(bf16[3,512,256]{2,1,0:T(8,128)(2,1)S(1)} %collective-permute-done.1.refs_9_), channel_id=1, source_target_pairs={{0,8},{4,12},{8,0},{12,4},{16,24},{20,28},{24,16},{28,20},{1,9},{5... | collective-permute-start | bytes 2359304 | tf_op jit(solution)/shard_map/ppermute | solution.py:251
  63.6 22.8 %collective-permute-start.13 = (bf16[3,512,256]{2,1,0:T(8,128)(2,1)S(1)}, bf16[3,512,256]{2,1,0:T(8,128)(2,1)}, u32[]{:S(2)}, u32[]{:S(2)}) collective-permute-start(bf16[3,512,256]{2,1,0:T(8,128)(2,1)S(1)} %collective-permute-done.1.refs_9_), channel_id=1, source_target_pairs={{0,16},{4,20},{8,24},{12,28},{16,0},{20,4},{24,8},{28,12},{1,17},{... | collective-permute-start | bytes 2359304 | tf_op jit(solution)/shard_map/ppermute | solution.py:251
  64.5 40.2 %collective-permute-start.19 = (bf16[3,512,256]{2,1,0:T(8,128)(2,1)S(1)}, bf16[3,512,256]{2,1,0:T(8,128)(2,1)}, u32[]{:S(2)}, u32[]{:S(2)}) collective-permute-start(bf16[3,512,256]{2,1,0:T(8,128)(2,1)S(1)} %collective-permute-done.1.refs_9_), channel_id=1, source_target_pairs={{0,4},{4,0},{8,12},{12,8},{16,20},{20,16},{24,28},{28,24},{1,5},{5... | collective-permute-start | bytes 2359304 | tf_op jit(solution)/shard_map/ppermute | solution.py:251
  64.6 21.8 %collective-permute-start.2 = (bf16[3,512,256]{2,1,0:T(8,128)(2,1)S(1)}, bf16[3,512,256]{2,1,0:T(8,128)(2,1)S(1)}, u32[]{:S(2)}, u32[]{:S(2)}) collective-permute-start(bf16[3,512,256]{2,1,0:T(8,128)(2,1)S(1)} %collective-permute-done.1.refs_9_), channel_id=1, source_target_pairs={{0,3},{1,0},{2,1},{3,2},{4,7},{5,4},{6,5},{7,6},{8,11},{9,8},{10,9... | collective-permute-start | bytes 2359304 | tf_op jit(solution)/shard_map/ppermute | solution.py:309
  87.7 13.2 %collective-permute-start.17 = (bf16[3,256,256]{2,1,0:T(8,128)(2,1)S(1)}, bf16[3,256,256]{2,1,0:T(8,128)(2,1)S(1)}, u32[]{:S(2)}, u32[]{:S(2)}) collective-permute-start(bf16[3,256,256]{2,1,0:T(8,128)(2,1)S(1)} %slice.14), channel_id=1, source_target_pairs={{0,8},{4,12},{8,0},{12,4},{16,24},{20,28},{24,16},{28,20},{1,9},{5... | collective-permute-start | bytes 1179656 | tf_op jit(solution)/shard_map/ppermute | solution.py:251
  92.9 11.1 %collective-permute-start.18 = (bf16[3,256,256]{2,1,0:T(8,128)(2,1)S(1)}, bf16[3,256,256]{2,1,0:T(8,128)(2,1)}, u32[]{:S(2)}, u32[]{:S(2)}) collective-permute-start(bf16[3,256,256]{2,1,0:T(8,128)(2,1)S(1)} %slice.15), channel_id=1, source_target_pairs={{0,16},{4,20},{8,24},{12,28},{16,0},{20,4},{24,8},{28,12},{1,17},{... | collective-permute-start | bytes 1179656 | tf_op jit(solution)/shard_map/ppermute | solution.py:251
  93.0 13.2 %collective-permute-start.20 = (bf16[3,512,256]{2,1,0:T(8,128)(2,1)}, bf16[3,512,256]{2,1,0:T(8,128)(2,1)}, u32[]{:S(2)}, u32[]{:S(2)}) collective-permute-start(bf16[3,512,256]{2,1,0:T(8,128)(2,1)} %collective-permute-done.12.refs_10_), channel_id=1, source_target_pairs={{0,4},{4,0},{8,12},{12,8},{16,20},{20,16},{24,28},{28,24},{1,5},{5... | collective-permute-start | bytes 2359304 | tf_op jit(solution)/shard_map/ppermute | solution.py:251
  93.1 13.1 %collective-permute-start.21 = (bf16[3,512,256]{2,1,0:T(8,128)(2,1)}, bf16[3,512,256]{2,1,0:T(8,128)(2,1)}, u32[]{:S(2)}, u32[]{:S(2)}) collective-permute-start(bf16[3,512,256]{2,1,0:T(8,128)(2,1)} %collective-permute-done.13.refs_11_), channel_id=1, source_target_pairs={{0,4},{4,0},{8,12},{12,8},{16,20},{20,16},{24,28},{28,24},{1,5},{5... | collective-permute-start | bytes 2359304 | tf_op jit(solution)/shard_map/ppermute | solution.py:251
  100.9 4.6 %collective-permute-start.22 = (bf16[3,256,256]{2,1,0:T(8,128)(2,1)S(1)}, bf16[3,256,256]{2,1,0:T(8,128)(2,1)}, u32[]{:S(2)}, u32[]{:S(2)}) collective-permute-start(bf16[3,256,256]{2,1,0:T(8,128)(2,1)S(1)} %collective-permute-done.17.refs_12_), channel_id=1, source_target_pairs={{0,4},{4,0},{8,12},{12,8},{16,20},{20,16},{24,28},{28,24},{1,5},{5... | collective-permute-start | bytes 1179656 | tf_op jit(solution)/shard_map/ppermute | solution.py:251
  104.7 20.0 %collective-permute-start.14 = (bf16[3,512,256]{2,1,0:T(8,128)(2,1)S(1)}, bf16[3,512,256]{2,1,0:T(8,128)(2,1)S(1)}, u32[]{:S(2)}, u32[]{:S(2)}) collective-permute-start(bf16[3,512,256]{2,1,0:T(8,128)(2,1)S(1)} %collective-permute-done.2.refs_6_.refs_5_), channel_id=1, source_target_pairs={{0,8},{4,12},{8,0},{12,4},{16,24},{20,28},{24,16},{28,20},{1,9},{5... | collective-permute-start | bytes 2359304 | tf_op jit(solution)/shard_map/ppermute | solution.py:251
  105.6 19.3 %collective-permute-start.15 = (bf16[3,512,256]{2,1,0:T(8,128)(2,1)S(1)}, bf16[3,512,256]{2,1,0:T(8,128)(2,1)S(1)}, u32[]{:S(2)}, u32[]{:S(2)}) collective-permute-start(bf16[3,512,256]{2,1,0:T(8,128)(2,1)S(1)} %collective-permute-done.2.refs_6_.refs_5_), channel_id=1, source_target_pairs={{0,16},{4,20},{8,24},{12,28},{16,0},{20,4},{24,8},{28,12},{1,17},{... | collective-permute-start | bytes 2359304 | tf_op jit(solution)/shard_map/ppermute | solution.py:251
  106.1 23.3 %collective-permute-start.24 = (bf16[3,512,256]{2,1,0:T(8,128)(2,1)S(1)}, bf16[3,512,256]{2,1,0:T(8,128)(2,1)S(1)}, u32[]{:S(2)}, u32[]{:S(2)}) collective-permute-start(bf16[3,512,256]{2,1,0:T(8,128)(2,1)S(1)} %collective-permute-done.2.refs_6_.refs_5_), channel_id=1, source_target_pairs={{0,4},{4,0},{8,12},{12,8},{16,20},{20,16},{24,28},{28,24},{1,5},{5... | collective-permute-start | bytes 2359304 | tf_op jit(solution)/shard_map/ppermute | solution.py:251
  106.2 21.9 %collective-permute-start.16 = (bf16[3,512,256]{2,1,0:T(8,128)(2,1)}, bf16[3,512,256]{2,1,0:T(8,128)(2,1)}, u32[]{:S(2)}, u32[]{:S(2)}) collective-permute-start(bf16[3,512,256]{2,1,0:T(8,128)(2,1)} %get-tuple-element.45), channel_id=1, source_target_pairs={{3,0},{0,1},{1,2},{2,3},{7,4},{4,5},{5,6},{6,7},{11,8},{8,9},{9,10... | collective-permute-start | bytes 2359304 | tf_op jit(solution)/shard_map/ppermute | solution.py:327
  128.1 4.7 %collective-permute-start.26 = (bf16[3,512,256]{2,1,0:T(8,128)(2,1)S(1)}, bf16[3,512,256]{2,1,0:T(8,128)(2,1)}, u32[]{:S(2)}, u32[]{:S(2)}) collective-permute-start(bf16[3,512,256]{2,1,0:T(8,128)(2,1)S(1)} %collective-permute-done.15.refs_8_.refs_7_), channel_id=1, source_target_pairs={{0,4},{4,0},{8,12},{12,8},{16,20},{20,16},{24,28},{28,24},{1,5},{5... | collective-permute-start | bytes 2359304 | tf_op jit(solution)/shard_map/ppermute | solution.py:251
  143.6 30.4 %all-to-all-start = ((bf16[8,2,256,256]{3,2,1,0:T(8,128)(2,1)}), bf16[8,2,256,256]{3,2,1,0:T(8,128)(2,1)S(1)}, u32[]{:S(2)}, u32[]{:S(2)}) async-start(bf16[8,2,256,256]{3,2,1,0:T(8,128)(2,1)} %bitcast.12), calls=%async_computation | async-start | bytes 4194304 | tf_op jit(solution)/shard_map/all_to_all | solution.py:341
  (22 other events, 252.3 us)

commit v6 on v5

--- a/solution.py
+++ b/solution.py
@@ -13,7 +13,7 @@
 MIB = 1 << 20
 WIDTH_BITS, SOURCE_BITS, LAG_BITS, STEP_BITS = 5, 8, 8, 4
 FIELDS = (WIDTH_BITS, SOURCE_BITS, LAG_BITS, STEP_BITS)
-ROW_PARTS = 2
+CHUNK = 4
 
 
 def list_task(base, span, total, steps, pair, tasks, counts):
@@ -32,41 +32,34 @@
     return width > 0
 
 
-def run_width(width, low, high, run):
-    if low == high:
-        run(low)
-        return
-    middle = (low + high) // 2
-
-    @pl.when(width <= middle)
-    def _():
-        run_width(width, low, middle, run)
-
-    @pl.when(width > middle)
-    def _():
-        run_width(width, middle + 1, high, run)
-
-
 def run_task(packed, klass, steps, hist, table, acc):
     panels = table.shape[2]
-    part = hist.shape[1] // ROW_PARTS
     fields = []
     for bits in FIELDS:
         fields.append(packed & ((1 << bits) - 1))
         packed = packed >> bits
     width, source, lag, step = fields
-    rows = pl.multiple_of(lag * panels, panels)
-    columns = pl.multiple_of(step * panels, panels)
-
-    def run(n):
-        for p in range(ROW_PARTS):
-            acc[packed, p * part : (p + 1) * part, :] += jnp.dot(
-                hist[source, p * part : (p + 1) * part, pl.ds(columns, n * panels)],
-                table[klass, pl.ds(rows, n * panels), :],
-                preferred_element_type=jnp.float32,
-            )
-
-    run_width(width, 1, steps, run)
+
+    def add(done, n):
+        rows = pl.multiple_of((lag + done) * panels, panels)
+        columns = pl.multiple_of((step + done) * panels, panels)
+        acc[packed] += jnp.dot(
+            hist[source, :, pl.ds(columns, n * panels)],
+            table[klass, pl.ds(rows, n * panels), :],
+            preferred_element_type=jnp.float32,
+        )
+
+    @pl.loop(0, width // CHUNK)
+    def _(j):
+        add(j * CHUNK, CHUNK)
+
+    n = CHUNK // 2
+    while n:
+        @pl.when((width & n) != 0)
+        def _(n=n):
+            add(width & ~(2 * n - 1), n)
+
+        n //= 2
 
 
 def window_kernel(config, *refs):
@@ -106,12 +99,12 @@
         return pltpu.make_async_copy(*ends_of, served_sems.at[i])
 
     if served:
-        peers, slots = served_refs[0].shape
+        slots, peers = served_refs[0].shape
 
         @pl.loop(0, peers)
         def _(i):
             for c in range(slots):
-                source, lag, klass = (ref[i, c] for ref in served_refs)
+                source, lag, klass = (ref[c, i] for ref in served_refs)
                 place = i * slots + c
                 touched = list_task(
                     base, span, total, steps, (source, klass, lag, place), tasks, counts
@@ -222,12 +215,12 @@
 
 def update_kernel(target_ref, near_ref, recv_ref, inverse_ref, incident_ref, out_ref, total):
     total[...] = near_ref[...]
-    peers, slots = target_ref.shape
+    slots, peers = target_ref.shape
 
     @pl.loop(0, peers)
     def _(i):
         for c in range(slots):
-            total[target_ref[i, c]] += recv_ref[i, c].astype(jnp.float32)
+            total[target_ref[c, i]] += recv_ref[i, c].astype(jnp.float32)
 
     for t in range(out_ref.shape[0]):
         residual = (incident_ref[t].astype(jnp.float32) - total[t].T).astype(jnp.bfloat16)
@@ -286,53 +279,77 @@
     lane = lax.axis_index("lag")
     lanes = lax.axis_size("lag")
     ring = [(i, (i - 1) % lanes) for i in range(lanes)]
-    served = (send_patch, send_lag, send_class)
+    served = (send_patch.T, send_lag.T, send_class.T)
     local = (local_src, local_lag, local_class, local_target)
 
     hist_t = jnp.swapaxes(history, 1, 2)
     half = height // 2
 
-    def part(index):
-        return lax.dynamic_slice(weights, (0, index * height, 0), (classes, height, panels))
+    def part(index, first, count):
+        return lax.dynamic_slice(weights, (0, index * height + first, 0), (classes, count, panels))
 
     def add_shard(step, sums):
         shard = lax.rem(lane + step, lanes)
         return window_sums(shard, group, served, local, hist_t, rounds[step - 1], sums, lanes, rows)
 
+    def neighbours(values):
+        return [swap(v, 2, peers) for v in values], [swap(v, 4, peers) for v in values]
+
+    low = lax.ppermute(part(group, 0, half), "lag", ring)
+    high = lax.ppermute(part(group, half, half), "lag", ring)
+    low, hist_t = lax.optimization_barrier((low, hist_t))
+    corner = part(group ^ 6, 0, height)
+    masks, lows = upper(low, peers)
+    _, highs = upper(high, peers)
+    low_x, low_y = neighbours(lows)
+    high_x, high_y = neighbours(highs)
+    own = jnp.concatenate([low, high], axis=1)
+    turned_x, turned_y = [swap(v, 2, peers) for v in low_y], [swap(v, 4, peers) for v in high_x]
     sums = window_sums(
         lane, group * 0, served, local, hist_t, [(0, 0, weights)], None, lanes, rows
     )
-    own = part(group)
-    corner = part(group ^ 6)
-    rounds = []
-    for step in range(1, lanes):
+    turned_x, turned_y, sums = lax.optimization_barrier((turned_x, turned_y, sums))
+    found = []
+    for bit, first, values in (
+        (0, 0, lows),
+        (0, half, highs),
+        (2, 0, low_x),
+        (2, half, high_x),
+        (4, 0, low_y),
+        (4, half, high_y),
+        (6, 0, turned_x),
+        (6, half, turned_y),
+    ):
+        found += [(m ^ bit, first, v) for m, v in zip(masks, values)]
+    rounds = [with_other_core(found, peers)]
+    tied = (low_x, low_y, high_x, high_y)
+
+    for step in range(2, lanes):
         own = lax.ppermute(own, "lag", ring)
-        if step == 1:
-            ready, sums = lax.optimization_barrier((own, sums))
+        if step == 2:
+            own, corner = lax.optimization_barrier((own, corner))
+            corner = lax.ppermute(corner, "lag", [(j, i) for i, j in ring])
         else:
-            if step > 2:
-                sums = add_shard(step - 2, sums)
-            ready, corner, sums, across, along = lax.optimization_barrier(
-                (own, corner, sums, across, along)
-            )
-            found = [(m, 0, v) for m, v in zip(masks, held)]
-            found += [(m ^ 2, 0, v) for m, v in zip(masks, across)]
-            found += [(m ^ 4, 0, v) for m, v in zip(masks, along)]
+            sums = add_shard(step - 2, sums)
+            corner, sums = lax.optimization_barrier((corner, sums))
+        ready, sums, tied = lax.optimization_barrier((own, sums, tied))
+        masks, held = upper(ready, peers)
+        if step > 2:
+            across, along = tied
             found += [(m ^ 6, 0, swap(v[:, :half], 2, peers)) for m, v in zip(masks, along)]
             found += [(m ^ 6, half, swap(v[:, half:], 4, peers)) for m, v in zip(masks, across)]
             rounds.append(with_other_core(found, peers))
-        masks, held = upper(ready, peers)
-        across = [swap(value, 2, peers) for value in held]
-        along = [swap(value, 4, peers) for value in held]
-    corner = lax.ppermute(corner, "lag", [(j, i) for i, j in ring])
-    if lanes > 2:
-        sums = add_shard(lanes - 2, sums)
-        across, along, corner, sums = lax.optimization_barrier((across, along, corner, sums))
+        across, along = tied = neighbours(held)
+        found = [(m, 0, v) for m, v in zip(masks, held)]
+        found += [(m ^ 2, 0, v) for m, v in zip(masks, across)]
+        found += [(m ^ 4, 0, v) for m, v in zip(masks, along)]
     _, corners = upper(corner, peers)
+    sums = add_shard(lanes - 2, sums)
+    across, along, sums = lax.optimization_barrier((across, along, sums))
     found = [(m, 0, v) for m, v in zip(masks, held)]
+    found += [(m ^ 6, 0, v) for m, v in zip(masks, corners)]
     found += [(m ^ 2, 0, v) for m, v in zip(masks, across)]
     found += [(m ^ 4, 0, v) for m, v in zip(masks, along)]
-    found += [(m ^ 6, 0, v) for m, v in zip(masks, corners)]
     rounds.append(with_other_core(found, peers))
     last = lax.rem(lane + lanes - 1, lanes)
     contribution = window_sums(
@@ -346,7 +363,7 @@
         tiled=True,
     )
     near = window_sums(last, group, (), local, hist_t, rounds[-1], sums[1:], lanes, rows)[0]
-    return update(recv_target, near, recv, inverse_blocks, incident)
+    return update(recv_target.T, near, recv, inverse_blocks, incident)
 
 
 def solution(mesh):

time: 177 us -> 205 us (1.16)
  starting transfers between devices: 25.9 us -> 43.2 us
  Pallas kernels: 72.1 us -> 85.4 us
    ppermute x24 -> x29, waiting for transfers between devices: 41.1 us -> 26.1 us  [swap(): return lax.ppermute(value, 'grp', [(i, i ^ bit) for i in range(peers)])]
    pallas_call x5, Pallas kernels: 69.7 us -> 83 us  [window_sums(): pl.pallas_call(functools.partial(window_kernel, config), out_shape=outs,...]
    ppermute x0 -> x2, waiting for transfers between devices: none -> 8.52 us  [the longest x1 5.76 us: per_device(): high = lax.ppermute(part(group, half, half), 'lag', ring)]
    ppermute x1, waiting for transfers between devices: 3.28 us -> 11.6 us  [per_device(): corner = lax.ppermute(corner, 'lag', [(j, i) for i, j in ring])]
    ppermute x24 -> x29, starting transfers between devices: 12.7 us -> 19 us  [swap(): return lax.ppermute(value, 'grp', [(i, i ^ bit) for i in range(peers)])]
    ppermute x0 -> x2, starting transfers between devices: none -> 5.55 us  [the longest x1 5.1 us: per_device(): low = lax.ppermute(part(group, 0, half), 'lag', ring)]
    all_to_all x1, starting transfers between devices: 3.71 us -> 8.29 us  [per_device(): lax.all_to_all(contribution.reshape(peers, slots, *contribution.shape[1:]...]
    ppermute x1, starting transfers between devices: 0.01 us -> 2.89 us  [per_device(): corner = lax.ppermute(corner, 'lag', [(j, i) for i, j in ring])]
  transfers between devices with their start and end apart: 29 -> 35, of which waited for: 16 -> 11; matrix products, arithmetic and copies ran while one was open for 7% -> 6% of each run, Pallas kernels for 33% -> 35%
where the time goes in v6:
time: 205 us; the launch traced here: 206 us
  Pallas kernels  85.4 us (42%)
  waiting for transfers between devices  61.3 us (30%)
  starting transfers between devices  43.2 us (21%)
  local copies, waits for them, and re-layouts  13.2 us (6%)
  other arithmetic  2.48 us (1%)
    pallas_call x5, Pallas kernels, window_sums(): pl.pallas_call(functools.partial(window_kernel, config), out_shape=outs,...  83 us
    ppermute x29, waiting for transfers between devices, swap(): return lax.ppermute(value, 'grp', [(i, i ^ bit) for i in range(peers)])  26.1 us
    ppermute x29, starting transfers between devices, swap(): return lax.ppermute(value, 'grp', [(i, i ^ bit) for i in range(peers)])  19 us
    all_to_all x1, waiting for transfers between devices, per_device(): lax.all_to_all(contribution.reshape(peers, slots, *contribution.shape[1:]...  15.1 us
    ppermute x1, waiting for transfers between devices, per_device(): corner = lax.ppermute(corner, 'lag', [(j, i) for i, j in ring])  11.6 us
    unnamed x47, local copies, waits for them, and re-layouts  8.49 us
    all_to_all x1, starting transfers between devices, per_device(): lax.all_to_all(contribution.reshape(peers, slots, *contribution.shape[1:]...  8.29 us
    ppermute x2, starting transfers between devices, per_device(): own = lax.ppermute(own, 'lag', ring)  7.46 us
  transfers between devices with their start and end apart: 35, of which 11 were waited for; matrix products, arithmetic and copies ran while one was open for 6% of the time, Pallas kernels for 35%

profile of v6, /device:TPU:0, one launch (start us, length us, event | category | flops | bytes accessed | tf_op | source)
XLA Modules:
  0.0 206.0 jit_solution(7452051714566693442)
XLA Ops:
  1.2 5.1 %collective-permute-start = (bf16[3,256,256]{2,1,0:T(8,128)(2,1)S(1)}, bf16[3,256,256]{2,1,0:T(8,128)(2,1)S(1)}, u32[]{:S(2)}, u32[]{:S(2)}) collective-permute-start(bf16[3,256,256]{2,1,0:T(8,128)(2,1)S(1)} %get-tuple-element.64), channel_id=1, source_target_pairs={{0,3},{1,0},{2,1},{3,2},{4,7},{5,4},{6,5},{7,6},{8,11},{9,8},{10,9... | collective-permute-start | bytes 1179656 | tf_op jit(solution)/shard_map/ppermute | solution.py:298
  6.7 6.3 %copy.18 = bf16[4,2048,256]{1,2,0:T(8,128)(2,1)} copy(bf16[4,2048,256]{2,1,0:T(8,128)(2,1)} %param.13) | data formatting | bytes 8388608 | tf_op args[1]
  13.0 2.8 %collective-permute-done.refs_9_ = bf16[3,256,256]{2,1,0:T(8,128)(2,1)S(1)} collective-permute-done((bf16[3,256,256]{2,1,0:T(8,128)(2,1)S(1)}, bf16[3,256,256]{2,1,0:T(8,128)(2,1)S(1)}, u32[]{:S(2)}, u32[]{:S(2)}) %collective-permute-start) | collective-permute-done | bytes 393248 | tf_op jit(solution)/shard_map/ppermute | solution.py:298
  15.8 1.5 collective-permute-start.7
  17.3 5.8 %collective-permute-done.1.refs_10_ = bf16[3,256,256]{2,1,0:T(8,128)(2,1)S(1)} collective-permute-done((bf16[3,256,256]{2,1,0:T(8,128)(2,1)S(1)}, bf16[3,256,256]{2,1,0:T(8,128)(2,1)S(1)}, u32[]{:S(2)}, u32[]{:S(2)}) %collective-permute-start.1) | collective-permute-done | bytes 393248 | tf_op jit(solution)/shard_map/ppermute | solution.py:299
  26.6 8.5 %collective-permute-done.6.refs_12_ = bf16[3,256,256]{2,1,0:T(8,128)(2,1)S(1)} collective-permute-done((bf16[3,256,256]{2,1,0:T(8,128)(2,1)S(1)}, bf16[3,256,256]{2,1,0:T(8,128)(2,1)S(1)}, u32[]{:S(2)}, u32[]{:S(2)}) %collective-permute-start.6) | collective-permute-done | bytes 393248 | tf_op jit(solution)/shard_map/ppermute | solution.py:244
  37.4 4.3 %collective-permute-start.2 = (bf16[3,512,256]{2,1,0:T(8,128)(2,1)S(1)}, bf16[3,512,256]{2,1,0:T(8,128)(2,1)S(1)}, u32[]{:S(2)}, u32[]{:S(2)}) collective-permute-start(bf16[3,512,256]{2,1,0:T(8,128)(2,1)S(1)} %pad_maximum_fusion), channel_id=1, source_target_pairs={{0,3},{1,0},{2,1},{3,2},{4,7},{5,4},{6,5},{7,6},{8,11},{9,8},{10,9... | collective-permute-start | bytes 2359304 | tf_op jit(solution)/shard_map/ppermute | solution.py:328
  41.7 1.9 collective-permute-done.5.refs_11_
  45.1 4.8 %collective-permute-done.9.refs_15_ = bf16[3,256,256]{2,1,0:T(8,128)(2,1)S(1)} collective-permute-done((bf16[3,256,256]{2,1,0:T(8,128)(2,1)S(1)}, bf16[3,256,256]{2,1,0:T(8,128)(2,1)S(1)}, u32[]{:S(2)}, u32[]{:S(2)}) %collective-permute-start.9) | collective-permute-done | bytes 393248 | tf_op jit(solution)/shard_map/ppermute | solution.py:244
  50.4 18.6 %shard_map.118 = (f32[16,256,256]{2,1,0:T(8,128)}, f32[4,256,256]{2,1,0:T(8,128)}) custom-call(s32[2]{0:T(128)} %pad_add_fusion.2.refs_0_, s32[2,8]{1,0:T(2,128)} %bitcast.18, s32[2,8]{1,0:T(2,128)} %bitcast.22, s32[2,8]{1,0:T(2,128)} %bitcast.26, s32[48]{0:T(128)} %refs_1_.1, s32[48]{0:T(128)} %refs_2_.1, s32[48]{0:T(128)} %refs_3_.1, s32[48]{0:T(128)} %refs_4_.7, ...), custom_call_target="tpu_custom_call" | custom-call | flops 17179869184 | bytes 10485760 | tf_op jit(solution)/shard_map/pallas_call | solution.py:188
  73.2 1.8 collective-permute-start.20
  75.1 3.1 %collective-permute-start.3 = (bf16[3,512,256]{2,1,0:T(8,128)(2,1)S(1)}, bf16[3,512,256]{2,1,0:T(8,128)(2,1)S(1)}, u32[]{:S(2)}, u32[]{:S(2)}) collective-permute-start(bf16[3,512,256]{2,1,0:T(8,128)(2,1)S(1)} %collective-permute-done.2.refs_9_), channel_id=1, source_target_pairs={{0,3},{1,0},{2,1},{3,2},{4,7},{5,4},{6,5},{7,6},{8,11},{9,8},{10,9... | collective-permute-start | bytes 2359304 | tf_op jit(solution)/shard_map/ppermute | solution.py:328
  78.2 2.9 %collective-permute-start.4 = (bf16[3,512,256]{2,1,0:T(8,128)(2,1)S(1)}, bf16[3,512,256]{2,1,0:T(8,128)(2,1)S(1)}, u32[]{:S(2)}, u32[]{:S(2)}) collective-permute-start(bf16[3,512,256]{2,1,0:T(8,128)(2,1)S(1)} %constant_dynamic-slice_fusion), channel_id=1, source_target_pairs={{3,0},{0,1},{1,2},{2,3},{7,4},{4,5},{5,6},{6,7},{11,8},{8,9},{9,10... | collective-permute-start | bytes 2359304 | tf_op jit(solution)/shard_map/ppermute | solution.py:331
  81.1 23.2 %shard_map.119 = (f32[16,256,256]{2,1,0:T(8,128)}, f32[4,256,256]{2,1,0:T(8,128)}) custom-call(s32[2]{0:T(128)} %pad_add_fusion.1.refs_0_, s32[2,8]{1,0:T(2,128)} %bitcast.19, s32[2,8]{1,0:T(2,128)} %bitcast.23, s32[2,8]{1,0:T(2,128)} %bitcast.27, s32[48]{0:T(128)} %refs_1_.1, s32[48]{0:T(128)} %refs_2_.1, ...), custom_call_target="tpu_custom_call", output_to_operand_aliasing={{0}: (25, {}), {1}: (26, {})} | custom-call | flops 17179869184 | bytes 10485760 | tf_op jit(solution)/shard_map/pallas_call | solution.py:188
  104.3 11.6 %collective-permute-done.4.refs_7_.refs_6_ = bf16[3,512,256]{2,1,0:T(8,128)(2,1)S(1)} collective-permute-done((bf16[3,512,256]{2,1,0:T(8,128)(2,1)S(1)}, bf16[3,512,256]{2,1,0:T(8,128)(2,1)S(1)}, u32[]{:S(2)}, u32[]{:S(2)}) %collective-permute-start.4) | collective-permute-done | bytes 786464 | tf_op jit(solution)/shard_map/ppermute | solution.py:331
  120.6 6.7 %collective-permute-done.23.refs_12_ = bf16[3,256,256]{2,1,0:T(8,128)(2,1)S(1)} collective-permute-done((bf16[3,256,256]{2,1,0:T(8,128)(2,1)S(1)}, bf16[3,256,256]{2,1,0:T(8,128)(2,1)S(1)}, u32[]{:S(2)}, u32[]{:S(2)}) %collective-permute-start.23) | collective-permute-done | bytes 393248 | tf_op jit(solution)/shard_map/ppermute | solution.py:244
  127.3 1.6 collective-permute-done.24.refs_13_
  130.8 1.6 collective-permute-start.22
  133.0 18.4 %shard_map.120 = (f32[16,256,256]{2,1,0:T(8,128)}, f32[4,256,256]{2,1,0:T(8,128)}) custom-call(s32[2]{0:T(128)} %pad_add_fusion.3.refs_0_, s32[2,8]{1,0:T(2,128)} %bitcast.20, s32[2,8]{1,0:T(2,128)} %bitcast.24, s32[2,8]{1,0:T(2,128)} %bitcast.28, s32[48]{0:T(128)} %refs_1_.1, s32[48]{0:T(128)} %refs_2_.1, ...), custom_call_target="tpu_custom_call", output_to_operand_aliasing={{0}: (19, {}), {1}: (20, {})} | custom-call | flops 17179869184 | bytes 10485760 | tf_op jit(solution)/shard_map/pallas_call | solution.py:188
  156.1 11.3 %shard_map.122 = bf16[16,256,256]{2,1,0:T(8,128)(2,1)} custom-call(s32[2]{0:T(128)} %pad_add_fusion.refs_0_, s32[2,8]{1,0:T(2,128)} %bitcast.21, s32[2,8]{1,0:T(2,128)} %bitcast.25, s32[2,8]{1,0:T(2,128)} %bitcast.29, bf16[4,256,2048]{2,1,0:T(8,128)(2,1)} %bitcast.15, bf16[3,512,256]{2,1,0:T(8,128)(2,1)} %copy-done.4, bf16[3,512,256]{2,1,0:T(8,128)(2,1)} %copy-done.5, ...), custom_call_target="tpu_custom_call" | custom-call | flops 4294967296 | bytes 10485760 | tf_op jit(solution)/shard_map/pallas_call | solution.py:188
  167.4 8.3 %all-to-all-start = ((bf16[8,2,256,256]{3,2,1,0:T(8,128)(2,1)}), bf16[8,2,256,256]{3,2,1,0:T(8,128)(2,1)S(1)}, u32[]{:S(2)}, u32[]{:S(2)}) async-start(bf16[8,2,256,256]{3,2,1,0:T(8,128)(2,1)} %bitcast.17), calls=%async_computation | async-start | bytes 4194304 | tf_op jit(solution)/shard_map/all_to_all | solution.py:358
  175.8 11.5 %shard_map.121.near_ref = f32[4,256,256]{2,1,0:T(8,128)} custom-call(s32[2]{0:T(128)} %pad_add_fusion.refs_0_, s32[48]{0:T(128)} %refs_1_.1, s32[48]{0:T(128)} %refs_2_.1, s32[48]{0:T(128)} %refs_3_.1, s32[48]{0:T(128)} %refs_4_.7, bf16[4,256,2048]{2,1,0:T(8,128)(2,1)} %bitcast.16, bf16[3,512,256]{2,1,0:T(8,128)(2,1)} %copy-done.4, ...), custom_call_target="tpu_custom_call", output_to_operand_aliasing={{}: (14, {})} | custom-call | flops 12884901888 | bytes 10485760 | tf_op jit(solution)/shard_map/pallas_call | solution.py:188
  187.3 15.1 %all-to-all-done.recv_ref = bf16[8,2,256,256]{3,2,1,0:T(8,128)(2,1)S(1)} async-done(((bf16[8,2,256,256]{3,2,1,0:T(8,128)(2,1)}), bf16[8,2,256,256]{3,2,1,0:T(8,128)(2,1)S(1)}, u32[]{:S(2)}, u32[]{:S(2)}) %all-to-all-start) | async-done | bytes 2097184 | tf_op jit(solution)/shard_map/all_to_all | solution.py:358
  203.6 2.4 %shard_map.123 = bf16[4,256,256]{2,1,0:T(8,128)(2,1)} custom-call(s32[2,8]{1,0:T(2,128)S(1)} %bitcast.11, f32[4,256,256]{2,1,0:T(8,128)S(1)} %copy-done, bf16[8,2,256,256]{3,2,1,0:T(8,128)(2,1)S(1)} %all-to-all-done.recv_ref, bf16[4,256,256]{2,1,0:T(8,128)(2,1)S(1)} %copy-done.1, bf16[4,256,256]{2,1,0:T(8,128)(2,1)S(1)} %copy-done.2), custom_call_target="tpu_custom_call" | custom-call | tf_op jit(solution)/shard_map/pallas_call | solution.py:233
  (108 shorter events, 26.4 us)
Async XLA Ops:
  1.2 14.6 %collective-permute-start = (bf16[3,256,256]{2,1,0:T(8,128)(2,1)S(1)}, bf16[3,256,256]{2,1,0:T(8,128)(2,1)S(1)}, u32[]{:S(2)}, u32[]{:S(2)}) collective-permute-start(bf16[3,256,256]{2,1,0:T(8,128)(2,1)S(1)} %get-tuple-element.64), channel_id=1, source_target_pairs={{0,3},{1,0},{2,1},{3,2},{4,7},{5,4},{6,5},{7,6},{8,11},{9,8},{10,9... | collective-permute-start | bytes 1179656 | tf_op jit(solution)/shard_map/ppermute | solution.py:298
  6.3 16.8 %collective-permute-start.1 = (bf16[3,256,256]{2,1,0:T(8,128)(2,1)S(1)}, bf16[3,256,256]{2,1,0:T(8,128)(2,1)S(1)}, u32[]{:S(2)}, u32[]{:S(2)}) collective-permute-start(bf16[3,256,256]{2,1,0:T(8,128)(2,1)S(1)} %get-tuple-element.63), channel_id=1, source_target_pairs={{0,3},{1,0},{2,1},{3,2},{4,7},{5,4},{6,5},{7,6},{8,11},{9,8},{10,9... | collective-permute-start | bytes 1179656 | tf_op jit(solution)/shard_map/ppermute | solution.py:299
  23.1 12.1 %collective-permute-start.6 = (bf16[3,256,256]{2,1,0:T(8,128)(2,1)S(1)}, bf16[3,256,256]{2,1,0:T(8,128)(2,1)S(1)}, u32[]{:S(2)}, u32[]{:S(2)}) collective-permute-start(bf16[3,256,256]{2,1,0:T(8,128)(2,1)S(1)} %collective-permute-done.1.refs_10_), channel_id=1, source_target_pairs={{0,8},{4,12},{8,0},{12,4},{16,24},{20,28},{24,16},{28,20},{1,9},{5... | collective-permute-start | bytes 1179656 | tf_op jit(solution)/shard_map/ppermute | solution.py:244
  24.6 19.0 %collective-permute-start.5 = (bf16[3,256,256]{2,1,0:T(8,128)(2,1)S(1)}, bf16[3,256,256]{2,1,0:T(8,128)(2,1)S(1)}, u32[]{:S(2)}, u32[]{:S(2)}) collective-permute-start(bf16[3,256,256]{2,1,0:T(8,128)(2,1)S(1)} %collective-permute-done.refs_9_), channel_id=1, source_target_pairs={{0,8},{4,12},{8,0},{12,4},{16,24},{20,28},{24,16},{28,20},{1,9},{5... | collective-permute-start | bytes 1179656 | tf_op jit(solution)/shard_map/ppermute | solution.py:244
  25.1 24.8 %collective-permute-start.9 = (bf16[3,256,256]{2,1,0:T(8,128)(2,1)S(1)}, bf16[3,256,256]{2,1,0:T(8,128)(2,1)S(1)}, u32[]{:S(2)}, u32[]{:S(2)}) collective-permute-start(bf16[3,256,256]{2,1,0:T(8,128)(2,1)S(1)} %collective-permute-done.7.refs_13_), channel_id=1, source_target_pairs={{0,8},{4,12},{8,0},{12,4},{16,24},{20,28},{24,16},{28,20},{1,9},{5... | collective-permute-start | bytes 1179656 | tf_op jit(solution)/shard_map/ppermute | solution.py:244
  35.1 14.8 %collective-permute-start.10 = (bf16[3,256,256]{2,1,0:T(8,128)(2,1)S(1)}, bf16[3,256,256]{2,1,0:T(8,128)(2,1)S(1)}, u32[]{:S(2)}, u32[]{:S(2)}) collective-permute-start(bf16[3,256,256]{2,1,0:T(8,128)(2,1)S(1)} %collective-permute-done.6.refs_12_), channel_id=1, source_target_pairs={{0,16},{4,20},{8,24},{12,28},{16,0},{20,4},{24,8},{28,12},{1,17},{... | collective-permute-start | bytes 1179656 | tf_op jit(solution)/shard_map/ppermute | solution.py:244
  37.3 31.9 %collective-permute-start.11 = (bf16[3,256,256]{2,1,0:T(8,128)(2,1)S(1)}, bf16[3,256,256]{2,1,0:T(8,128)(2,1)S(1)}, u32[]{:S(2)}, u32[]{:S(2)}) collective-permute-start(bf16[3,256,256]{2,1,0:T(8,128)(2,1)S(1)} %collective-permute-done.refs_9_), channel_id=1, source_target_pairs={{0,4},{4,0},{8,12},{12,8},{16,20},{20,16},{24,28},{28,24},{1,5},{5... | collective-permute-start | bytes 1179656 | tf_op jit(solution)/shard_map/ppermute | solution.py:244
  37.4 32.5 %collective-permute-start.2 = (bf16[3,512,256]{2,1,0:T(8,128)(2,1)S(1)}, bf16[3,512,256]{2,1,0:T(8,128)(2,1)S(1)}, u32[]{:S(2)}, u32[]{:S(2)}) collective-permute-start(bf16[3,512,256]{2,1,0:T(8,128)(2,1)S(1)} %pad_maximum_fusion), channel_id=1, source_target_pairs={{0,3},{1,0},{2,1},{3,2},{4,7},{5,4},{6,5},{7,6},{8,11},{9,8},{10,9... | collective-permute-start | bytes 2359304 | tf_op jit(solution)/shard_map/ppermute | solution.py:328
  43.6 25.5 %collective-permute-start.8 = (bf16[3,256,256]{2,1,0:T(8,128)(2,1)S(1)}, bf16[3,256,256]{2,1,0:T(8,128)(2,1)}, u32[]{:S(2)}, u32[]{:S(2)}) collective-permute-start(bf16[3,256,256]{2,1,0:T(8,128)(2,1)S(1)} %collective-permute-done.1.refs_10_), channel_id=1, source_target_pairs={{0,16},{4,20},{8,24},{12,28},{16,0},{20,4},{24,8},{28,12},{1,17},{... | collective-permute-start | bytes 1179656 | tf_op jit(solution)/shard_map/ppermute | solution.py:244
  49.9 19.8 %collective-permute-start.12 = (bf16[3,256,256]{2,1,0:T(8,128)(2,1)S(1)}, bf16[3,256,256]{2,1,0:T(8,128)(2,1)S(1)}, u32[]{:S(2)}, u32[]{:S(2)}) collective-permute-start(bf16[3,256,256]{2,1,0:T(8,128)(2,1)S(1)} %collective-permute-done.1.refs_10_), channel_id=1, source_target_pairs={{0,4},{4,0},{8,12},{12,8},{16,20},{20,16},{24,28},{28,24},{1,5},{5... | collective-permute-start | bytes 1179656 | tf_op jit(solution)/shard_map/ppermute | solution.py:244
  49.9 20.4 %collective-permute-start.15 = (bf16[3,256,256]{2,1,0:T(8,128)(2,1)S(1)}, bf16[3,256,256]{2,1,0:T(8,128)(2,1)S(1)}, u32[]{:S(2)}, u32[]{:S(2)}) collective-permute-start(bf16[3,256,256]{2,1,0:T(8,128)(2,1)S(1)} %collective-permute-done.7.refs_13_), channel_id=1, source_target_pairs={{0,4},{4,0},{8,12},{12,8},{16,20},{20,16},{24,28},{28,24},{1,5},{5... | collective-permute-start | bytes 1179656 | tf_op jit(solution)/shard_map/ppermute | solution.py:244
  73.1 42.8 %collective-permute-start.19 = (bf16[3,512,256]{2,1,0:T(8,128)(2,1)S(1)}, bf16[3,512,256]{2,1,0:T(8,128)(2,1)}, u32[]{:S(2)}, u32[]{:S(2)}) collective-permute-start(bf16[3,512,256]{2,1,0:T(8,128)(2,1)S(1)} %collective-permute-done.2.refs_9_), channel_id=1, source_target_pairs={{0,8},{4,12},{8,0},{12,4},{16,24},{20,28},{24,16},{28,20},{1,9},{5... | collective-permute-start | bytes 2359304 | tf_op jit(solution)/shard_map/ppermute | solution.py:244
  73.2 42.7 %collective-permute-start.20 = (bf16[3,512,256]{2,1,0:T(8,128)(2,1)S(1)}, bf16[3,512,256]{2,1,0:T(8,128)(2,1)}, u32[]{:S(2)}, u32[]{:S(2)}) collective-permute-start(bf16[3,512,256]{2,1,0:T(8,128)(2,1)S(1)} %collective-permute-done.2.refs_9_), channel_id=1, source_target_pairs={{0,16},{4,20},{8,24},{12,28},{16,0},{20,4},{24,8},{28,12},{1,17},{... | collective-permute-start | bytes 2359304 | tf_op jit(solution)/shard_map/ppermute | solution.py:244
  75.1 40.9 %collective-permute-start.3 = (bf16[3,512,256]{2,1,0:T(8,128)(2,1)S(1)}, bf16[3,512,256]{2,1,0:T(8,128)(2,1)S(1)}, u32[]{:S(2)}, u32[]{:S(2)}) collective-permute-start(bf16[3,512,256]{2,1,0:T(8,128)(2,1)S(1)} %collective-permute-done.2.refs_9_), channel_id=1, source_target_pairs={{0,3},{1,0},{2,1},{3,2},{4,7},{5,4},{6,5},{7,6},{8,11},{9,8},{10,9... | collective-permute-start | bytes 2359304 | tf_op jit(solution)/shard_map/ppermute | solution.py:328
  78.2 51.3 %collective-permute-start.25 = (bf16[3,512,256]{2,1,0:T(8,128)(2,1)S(1)}, bf16[3,512,256]{2,1,0:T(8,128)(2,1)}, u32[]{:S(2)}, u32[]{:S(2)}) collective-permute-start(bf16[3,512,256]{2,1,0:T(8,128)(2,1)S(1)} %collective-permute-done.2.refs_9_), channel_id=1, source_target_pairs={{0,4},{4,0},{8,12},{12,8},{16,20},{20,16},{24,28},{28,24},{1,5},{5... | collective-permute-start | bytes 2359304 | tf_op jit(solution)/shard_map/ppermute | solution.py:244
  78.2 37.7 %collective-permute-start.4 = (bf16[3,512,256]{2,1,0:T(8,128)(2,1)S(1)}, bf16[3,512,256]{2,1,0:T(8,128)(2,1)S(1)}, u32[]{:S(2)}, u32[]{:S(2)}) collective-permute-start(bf16[3,512,256]{2,1,0:T(8,128)(2,1)S(1)} %constant_dynamic-slice_fusion), channel_id=1, source_target_pairs={{3,0},{0,1},{1,2},{2,3},{7,4},{4,5},{5,6},{6,7},{11,8},{8,9},{9,10... | collective-permute-start | bytes 2359304 | tf_op jit(solution)/shard_map/ppermute | solution.py:331
  117.3 10.0 %collective-permute-start.23 = (bf16[3,256,256]{2,1,0:T(8,128)(2,1)S(1)}, bf16[3,256,256]{2,1,0:T(8,128)(2,1)S(1)}, u32[]{:S(2)}, u32[]{:S(2)}) collective-permute-start(bf16[3,256,256]{2,1,0:T(8,128)(2,1)S(1)} %slice.6), channel_id=1, source_target_pairs={{0,8},{4,12},{8,0},{12,4},{16,24},{20,28},{24,16},{28,20},{1,9},{5... | collective-permute-start | bytes 1179656 | tf_op jit(solution)/shard_map/ppermute | solution.py:244
  120.0 12.4 %collective-permute-start.26 = (bf16[3,512,256]{2,1,0:T(8,128)(2,1)}, bf16[3,512,256]{2,1,0:T(8,128)(2,1)}, u32[]{:S(2)}, u32[]{:S(2)}) collective-permute-start(bf16[3,512,256]{2,1,0:T(8,128)(2,1)} %collective-permute-done.19.refs_10_), channel_id=1, source_target_pairs={{0,4},{4,0},{8,12},{12,8},{16,20},{20,16},{24,28},{28,24},{1,5},{5... | collective-permute-start | bytes 2359304 | tf_op jit(solution)/shard_map/ppermute | solution.py:244
  120.0 12.9 %collective-permute-start.27 = (bf16[3,512,256]{2,1,0:T(8,128)(2,1)}, bf16[3,512,256]{2,1,0:T(8,128)(2,1)}, u32[]{:S(2)}, u32[]{:S(2)}) collective-permute-start(bf16[3,512,256]{2,1,0:T(8,128)(2,1)} %collective-permute-done.20.refs_11_), channel_id=1, source_target_pairs={{0,4},{4,0},{8,12},{12,8},{16,20},{20,16},{24,28},{28,24},{1,5},{5... | collective-permute-start | bytes 2359304 | tf_op jit(solution)/shard_map/ppermute | solution.py:244
  129.5 21.9 %collective-permute-start.21 = (bf16[3,512,256]{2,1,0:T(8,128)(2,1)S(1)}, bf16[3,512,256]{2,1,0:T(8,128)(2,1)S(1)}, u32[]{:S(2)}, u32[]{:S(2)}) collective-permute-start(bf16[3,512,256]{2,1,0:T(8,128)(2,1)S(1)} %collective-permute-done.3.refs_6_.refs_5_), channel_id=1, source_target_pairs={{0,8},{4,12},{8,0},{12,4},{16,24},{20,28},{24,16},{28,20},{1,9},{5... | collective-permute-start | bytes 2359304 | tf_op jit(solution)/shard_map/ppermute | solution.py:244
  130.8 20.6 %collective-permute-start.22 = (bf16[3,512,256]{2,1,0:T(8,128)(2,1)S(1)}, bf16[3,512,256]{2,1,0:T(8,128)(2,1)S(1)}, u32[]{:S(2)}, u32[]{:S(2)}) collective-permute-start(bf16[3,512,256]{2,1,0:T(8,128)(2,1)S(1)} %collective-permute-done.3.refs_6_.refs_5_), channel_id=1, source_target_pairs={{0,16},{4,20},{8,24},{12,28},{16,0},{20,4},{24,8},{28,12},{1,17},{... | collective-permute-start | bytes 2359304 | tf_op jit(solution)/shard_map/ppermute | solution.py:244
  132.4 21.2 %collective-permute-start.30 = (bf16[3,512,256]{2,1,0:T(8,128)(2,1)S(1)}, bf16[3,512,256]{2,1,0:T(8,128)(2,1)}, u32[]{:S(2)}, u32[]{:S(2)}) collective-permute-start(bf16[3,512,256]{2,1,0:T(8,128)(2,1)S(1)} %collective-permute-done.3.refs_6_.refs_5_), channel_id=1, source_target_pairs={{0,4},{4,0},{8,12},{12,8},{16,20},{20,16},{24,28},{28,24},{1,5},{5... | collective-permute-start | bytes 2359304 | tf_op jit(solution)/shard_map/ppermute | solution.py:244
  132.4 21.2 %collective-permute-start.31 = (bf16[3,512,256]{2,1,0:T(8,128)(2,1)S(1)}, bf16[3,512,256]{2,1,0:T(8,128)(2,1)}, u32[]{:S(2)}, u32[]{:S(2)}) collective-permute-start(bf16[3,512,256]{2,1,0:T(8,128)(2,1)S(1)} %collective-permute-done.4.refs_7_.refs_6_), channel_id=1, source_target_pairs={{0,4},{4,0},{8,12},{12,8},{16,20},{20,16},{24,28},{28,24},{1,5},{5... | collective-permute-start | bytes 2359304 | tf_op jit(solution)/shard_map/ppermute | solution.py:244
  167.4 34.9 %all-to-all-start = ((bf16[8,2,256,256]{3,2,1,0:T(8,128)(2,1)}), bf16[8,2,256,256]{3,2,1,0:T(8,128)(2,1)S(1)}, u32[]{:S(2)}, u32[]{:S(2)}) async-start(bf16[8,2,256,256]{3,2,1,0:T(8,128)(2,1)} %bitcast.17), calls=%async_computation | async-start | bytes 4194304 | tf_op jit(solution)/shard_map/all_to_all | solution.py:358
  (34 other events, 525.8 us)

commit v7 on v5

--- a/solution.py
+++ b/solution.py
@@ -11,66 +11,55 @@
 VMEM = pl.BlockSpec(memory_space=pltpu.VMEM)
 HBM = pl.BlockSpec(memory_space=pltpu.HBM)
 MIB = 1 << 20
-WIDTH_BITS, SOURCE_BITS, LAG_BITS, STEP_BITS = 5, 8, 8, 4
-FIELDS = (WIDTH_BITS, SOURCE_BITS, LAG_BITS, STEP_BITS)
-ROW_PARTS = 2
-
-
-def list_task(base, span, total, steps, pair, tasks, counts):
+STEP_BITS, SOURCE_BITS, LAG_BITS = 4, 8, 8
+FIELDS = (STEP_BITS, SOURCE_BITS, LAG_BITS)
+CHUNK = 4
+
+
+def pack(step, source, lag, place):
+    packed = place
+    for value, bits in ((lag, LAG_BITS), (source, SOURCE_BITS), (step, STEP_BITS)):
+        packed = (packed << bits) | value
+    return packed
+
+
+def list_tasks(base, span, total, steps, pair, tasks, counts):
     source, klass, lag, place = pair
-    start = lax.rem(lag - base + total, total)
-    inside = start < span
-    first = jnp.where(inside, start, 0)
-    skip = jnp.where(inside, 0, total - start)
-    width = jnp.maximum(jnp.where(inside, jnp.minimum(steps, span - start), steps - skip), 0)
-    packed = place
-    for value, bits in ((skip, STEP_BITS), (first, LAG_BITS), (source, SOURCE_BITS), (width, WIDTH_BITS)):
-        packed = (packed << bits) | value
-    at = counts[klass]
-    tasks[klass, at] = packed
-    counts[klass] = at + jnp.where(width > 0, 1, 0)
-    return width > 0
-
-
-def run_width(width, low, high, run):
-    if low == high:
-        run(low)
-        return
-    middle = (low + high) // 2
-
-    @pl.when(width <= middle)
-    def _():
-        run_width(width, low, middle, run)
-
-    @pl.when(width > middle)
-    def _():
-        run_width(width, middle + 1, high, run)
-
-
-def run_task(packed, klass, steps, hist, table, acc):
+    touched = None
+    for step in range(steps // CHUNK):
+        start = lax.rem(lag + step * CHUNK - base + total, total)
+        first = jnp.where(start < span, start, start - total) + CHUNK - 1
+        active = first >= 0
+        at = counts[klass]
+        tasks[klass, at] = pack(step, source, jnp.maximum(first, 0), place)
+        counts[klass] = at + jnp.where(active, 1, 0)
+        touched = active if touched is None else touched | active
+    return touched
+
+
+def run_tasks(number, klass, tasks, hist, table, acc):
     panels = table.shape[2]
-    part = hist.shape[1] // ROW_PARTS
-    fields = []
-    for bits in FIELDS:
-        fields.append(packed & ((1 << bits) - 1))
-        packed = packed >> bits
-    width, source, lag, step = fields
-    rows = pl.multiple_of(lag * panels, panels)
-    columns = pl.multiple_of(step * panels, panels)
-
-    def run(n):
-        for p in range(ROW_PARTS):
-            acc[packed, p * part : (p + 1) * part, :] += jnp.dot(
-                hist[source, p * part : (p + 1) * part, pl.ds(columns, n * panels)],
-                table[klass, pl.ds(rows, n * panels), :],
-                preferred_element_type=jnp.float32,
-            )
-
-    run_width(width, 1, steps, run)
+    products = []
+    for n in range(number):
+        packed = tasks[n]
+        fields = []
+        for bits in FIELDS:
+            fields.append(packed & ((1 << bits) - 1))
+            packed = packed >> bits
+        step, source, lag = fields
+        columns = pl.multiple_of(step * (CHUNK * panels), CHUNK * panels)
+        rows = pl.multiple_of(lag * panels, panels)
+        products.append((packed, jnp.dot(
+            hist[source, :, pl.ds(columns, CHUNK * panels)],
+            table[klass, pl.ds(rows, CHUNK * panels), :],
+            preferred_element_type=jnp.float32,
+        )))
+    for place, product in products:
+        acc[place] += product
 
 
 def window_kernel(config, *refs):
-    served, local, begun, narrow, places, total, height, owned = config
+    served, local, begun, narrow, places, total, height, owned, unroll = config
     refs = list(refs)
     where = refs.pop(0)
     served_refs = [refs.pop(0) for _ in range(3 if served else 0)]
@@ -82,7 +71,8 @@
     table, hist, acc, tasks, counts, used, sems, ends, served_sems = refs
     base, group = where[0], where[1]
     classes, _, panels = table.shape
-    span = table.shape[1] // panels
+    margin = (CHUNK - 1) * panels
+    span = (table.shape[1] - 2 * margin) // panels
     steps = hist.shape[2] // panels
 
     pltpu.make_async_copy(hist_ref, hist, ends.at[0]).start()
@@ -92,28 +82,31 @@
     for k in range(classes):
         for (mask, first), piece in zip(places, pieces):
             rows = piece.shape[1]
-            start = pl.multiple_of((group ^ mask) * height + first, 16)
+            start = pl.multiple_of(margin + (group ^ mask) * height + first, 16)
             pltpu.make_async_copy(
                 piece.at[k], table.at[k, pl.ds(start, rows), :], sems.at[k]
             ).start()
     if not begun:
         acc[...] = jnp.zeros_like(acc)
+    ends_of_table = jnp.zeros((margin, panels), table.dtype)
     for k in range(classes):
         counts[k] = 0
+        table[k, pl.ds(0, margin), :] = ends_of_table
+        table[k, pl.ds(margin + span * panels, margin), :] = ends_of_table
 
     def served_copy(i, back):
         ends_of = (acc.at[i], outs[0].at[i]) if back else (before[0].at[i], acc.at[i])
         return pltpu.make_async_copy(*ends_of, served_sems.at[i])
 
     if served:
-        peers, slots = served_refs[0].shape
+        slots, peers = served_refs[0].shape
 
         @pl.loop(0, peers)
         def _(i):
             for c in range(slots):
-                source, lag, klass = (ref[i, c] for ref in served_refs)
+                source, lag, klass = (ref[c, i] for ref in served_refs)
                 place = i * slots + c
-                touched = list_task(
+                touched = list_tasks(
                     base, span, total, steps, (source, klass, lag, place), tasks, counts
                 )
                 needed = touched | narrow
@@ -127,7 +120,7 @@
         @pl.loop(0, local_refs[0].shape[0])
         def _(i):
             source, lag, klass, target = (ref[i] for ref in local_refs)
-            list_task(
+            list_tasks(
                 base, span, total, steps, (source, klass, lag, target + served), tasks, counts
             )
 
@@ -141,16 +134,23 @@
             def _():
                 served_copy(i, False).wait()
 
+    spare = acc.shape[0] - 1
+
     @pl.loop(0, classes)
     def _(k):
-        pltpu.make_async_copy(table.at[k], table.at[k], sems.at[k]).wait()
-
-        @pl.loop(0, counts[k])
+        count = counts[k]
+        for n in range(unroll - 1):
+            tasks[k, count + n] = pack(0, 0, 0, spare)
+        inner = table.at[k, pl.ds(margin, span * panels), :]
+        pltpu.make_async_copy(inner, inner, sems.at[k]).wait()
+
+        @pl.loop(0, (count + unroll - 1) // unroll)
         def _(j):
-            run_task(tasks[k, j], k, steps, hist, table, acc)
+            first = j * unroll
+            run_tasks(unroll, k, [tasks[k, first + n] for n in range(unroll)], hist, table, acc)
 
     if narrow:
-        outs[0][...] = acc[...].astype(outs[0].dtype)
+        outs[0][...] = acc[pl.ds(0, served)].astype(outs[0].dtype)
         return
     if local:
         pltpu.make_async_copy(near, outs[-1], ends.at[1]).start()
@@ -183,6 +183,7 @@
         lanes * rows // panels,
         height,
         targets,
+        4 if local else 2,
     )
     operands = [jnp.stack([shard * (rows // panels), group]).astype(jnp.int32), *served, *local]
     wide = [hist_t, *[piece[2] for piece in pieces]]
@@ -198,10 +199,10 @@
         in_specs=[SMEM] * len(operands) + [HBM] * (len(wide) + len(before)),
         out_specs=[VMEM if narrow else HBM] * len(outs),
         scratch_shapes=[
-            pltpu.VMEM((classes, rows, panels), jnp.bfloat16),
+            pltpu.VMEM((classes, rows + 2 * (CHUNK - 1) * panels, panels), jnp.bfloat16),
             pltpu.VMEM(hist_t.shape, hist_t.dtype),
-            pltpu.VMEM((places + targets, excite, panels), jnp.float32),
-            pltpu.SMEM((classes, pairs + 1), jnp.int32),
+            pltpu.VMEM((places + targets + 1, excite, panels), jnp.float32),
+            pltpu.SMEM((classes, pairs * (steps // CHUNK) + 4), jnp.int32),
             pltpu.SMEM((classes,), jnp.int32),
             pltpu.SMEM((max(places, 1),), jnp.int32),
             pltpu.SemaphoreType.DMA((classes,)),
@@ -222,12 +223,12 @@
 
 def update_kernel(target_ref, near_ref, recv_ref, inverse_ref, incident_ref, out_ref, total):
     total[...] = near_ref[...]
-    peers, slots = target_ref.shape
+    slots, peers = target_ref.shape
 
     @pl.loop(0, peers)
     def _(i):
         for c in range(slots):
-            total[target_ref[i, c]] += recv_ref[i, c].astype(jnp.float32)
+            total[target_ref[c, i]] += recv_ref[i, c].astype(jnp.float32)
 
     for t in range(out_ref.shape[0]):
         residual = (incident_ref[t].astype(jnp.float32) - total[t].T).astype(jnp.bfloat16)
@@ -286,7 +287,7 @@
     lane = lax.axis_index("lag")
     lanes = lax.axis_size("lag")
     ring = [(i, (i - 1) % lanes) for i in range(lanes)]
-    served = (send_patch, send_lag, send_class)
+    served = (send_patch.T, send_lag.T, send_class.T)
     local = (local_src, local_lag, local_class, local_target)
 
     hist_t = jnp.swapaxes(history, 1, 2)
@@ -346,7 +347,7 @@
         tiled=True,
     )
     near = window_sums(last, group, (), local, hist_t, rounds[-1], sums[1:], lanes, rows)[0]
-    return update(recv_target, near, recv, inverse_blocks, incident)
+    return update(recv_target.T, near, recv, inverse_blocks, incident)
 
 
 def solution(mesh):

time: 177 us -> 172 us (0.972); the launches traced: 178 us -> 170 us
  Pallas kernels: 72.1 us -> 66.6 us
  local copies, waits for them, and re-layouts: 14.5 us -> 11.4 us
    pallas_call x5, Pallas kernels: 69.7 us -> 64.3 us  [window_sums(): pl.pallas_call(functools.partial(window_kernel, config), out_shape=outs,...]
    unnamed x39 -> x27, local copies, waits for them, and re-layouts: 9.72 us -> 7.62 us
  transfers between devices with their start and end apart: 29 -> 29, of which waited for: 16 -> 17; matrix products, arithmetic and copies ran while one was open for 7% -> 7% of each run, Pallas kernels for 33% -> 32%
where the time goes in v7:
time: 172 us; the launch traced here: 170 us
  Pallas kernels  66.6 us (39%)
  waiting for transfers between devices  64.1 us (37%)
  starting transfers between devices  25.5 us (15%)
  local copies, waits for them, and re-layouts  11.4 us (7%)
  other arithmetic  2.55 us (1%)
    pallas_call x5, Pallas kernels, window_sums(): pl.pallas_call(functools.partial(window_kernel, config), out_shape=outs,...  64.3 us
    ppermute x24, waiting for transfers between devices, swap(): return lax.ppermute(value, 'grp', [(i, i ^ bit) for i in range(peers)])  41.4 us
    all_to_all x1, waiting for transfers between devices, per_device(): lax.all_to_all(contribution.reshape(peers, slots, *contribution.shape[1:]...  16.6 us
    ppermute x24, starting transfers between devices, swap(): return lax.ppermute(value, 'grp', [(i, i ^ bit) for i in range(peers)])  11.8 us
    ppermute x3, starting transfers between devices, per_device(): own = lax.ppermute(own, 'lag', ring)  8.37 us
    unnamed x27, local copies, waits for them, and re-layouts  7.62 us
    all_to_all x1, starting transfers between devices, per_device(): lax.all_to_all(contribution.reshape(peers, slots, *contribution.shape[1:]...  4.01 us
    ppermute x1, waiting for transfers between devices, per_device(): corner = lax.ppermute(corner, 'lag', [(j, i) for i, j in ring])  3.59 us
  transfers between devices with their start and end apart: 29, of which 17 were waited for; matrix products, arithmetic and copies ran while one was open for 7% of the time, Pallas kernels for 32%

profile of v7, /device:TPU:0, one launch (start us, length us, event | category | flops | bytes accessed | tf_op | source)
XLA Modules:
  0.0 170.5 jit_solution(10234732073239749149)
XLA Ops:
  0.0 1.5 constant_dynamic-slice_fusion
  1.5 5.1 %collective-permute-start = (bf16[3,512,256]{2,1,0:T(8,128)(2,1)S(1)}, bf16[3,512,256]{2,1,0:T(8,128)(2,1)}, u32[]{:S(2)}, u32[]{:S(2)}) collective-permute-start(bf16[3,512,256]{2,1,0:T(8,128)(2,1)S(1)} %get-tuple-element.58), channel_id=1, source_target_pairs={{0,3},{1,0},{2,1},{3,2},{4,7},{5,4},{6,5},{7,6},{8,11},{9,8},{10,9... | collective-permute-start | bytes 2359304 | tf_op jit(solution)/shard_map/ppermute | solution.py:310
  6.6 6.4 %copy.18 = bf16[4,2048,256]{1,2,0:T(8,128)(2,1)} copy(bf16[4,2048,256]{2,1,0:T(8,128)(2,1)} %param.13) | data formatting | bytes 8388608 | tf_op args[1]
  13.6 12.9 %shard_map.118 = (f32[16,256,256]{2,1,0:T(8,128)}, f32[4,256,256]{2,1,0:T(8,128)}) custom-call(s32[2]{0:T(128)} %pad_add_fusion.1.refs_0_, s32[2,8]{1,0:T(2,128)} %bitcast.18, s32[2,8]{1,0:T(2,128)} %bitcast.22, s32[2,8]{1,0:T(2,128)} %bitcast.26, s32[48]{0:T(128)} %refs_1_.1, s32[48]{0:T(128)} %refs_2_.1, s32[48]{0:T(128)} %refs_3_.1, s32[48]{0:T(128)} %refs_4_.7, ...), custom_call_target="tpu_custom_call" | custom-call | flops 17179869184 | bytes 10485760 | tf_op jit(solution)/shard_map/pallas_call | solution.py:196
  26.5 1.5 collective-permute-start.3
  28.8 2.0 %collective-permute-start.1 = (bf16[3,512,256]{2,1,0:T(8,128)(2,1)}, bf16[3,512,256]{2,1,0:T(8,128)(2,1)}, u32[]{:S(2)}, u32[]{:S(2)}) collective-permute-start(bf16[3,512,256]{2,1,0:T(8,128)(2,1)} %collective-permute-done.refs_9_), channel_id=1, source_target_pairs={{0,3},{1,0},{2,1},{3,2},{4,7},{5,4},{6,5},{7,6},{8,11},{9,8},{10,9... | collective-permute-start | bytes 2359304 | tf_op jit(solution)/shard_map/ppermute | solution.py:310
  30.8 14.2 %collective-permute-done.3.refs_10_ = bf16[3,512,256]{2,1,0:T(8,128)(2,1)S(1)} collective-permute-done((bf16[3,512,256]{2,1,0:T(8,128)(2,1)}, bf16[3,512,256]{2,1,0:T(8,128)(2,1)S(1)}, u32[]{:S(2)}, u32[]{:S(2)}) %collective-permute-start.3) | collective-permute-done | bytes 786464 | tf_op jit(solution)/shard_map/ppermute | solution.py:252
  45.0 2.5 %collective-permute-done.4.refs_11_ = bf16[3,512,256]{2,1,0:T(8,128)(2,1)S(1)} collective-permute-done((bf16[3,512,256]{2,1,0:T(8,128)(2,1)}, bf16[3,512,256]{2,1,0:T(8,128)(2,1)S(1)}, u32[]{:S(2)}, u32[]{:S(2)}) %collective-permute-start.4) | collective-permute-done | bytes 786464 | tf_op jit(solution)/shard_map/ppermute | solution.py:252
  47.5 1.5 collective-permute-done.1.refs_9_
  51.3 8.5 %collective-permute-done.5.refs_12_ = bf16[3,256,256]{2,1,0:T(8,128)(2,1)S(1)} collective-permute-done((bf16[3,256,256]{2,1,0:T(8,128)(2,1)S(1)}, bf16[3,256,256]{2,1,0:T(8,128)(2,1)S(1)}, u32[]{:S(2)}, u32[]{:S(2)}) %collective-permute-start.5) | collective-permute-done | bytes 393248 | tf_op jit(solution)/shard_map/ppermute | solution.py:252
  64.7 15.9 %shard_map.119 = (f32[16,256,256]{2,1,0:T(8,128)}, f32[4,256,256]{2,1,0:T(8,128)}) custom-call(s32[2]{0:T(128)} %pad_add_fusion.2.refs_0_, s32[2,8]{1,0:T(2,128)} %bitcast.19, s32[2,8]{1,0:T(2,128)} %bitcast.23, s32[2,8]{1,0:T(2,128)} %bitcast.27, s32[48]{0:T(128)} %refs_1_.1, s32[48]{0:T(128)} %refs_2_.1, ...), custom_call_target="tpu_custom_call", output_to_operand_aliasing={{0}: (19, {}), {1}: (20, {})} | custom-call | flops 17179869184 | bytes 10485760 | tf_op jit(solution)/shard_map/pallas_call | solution.py:196
  80.5 1.5 collective-permute-done.12.refs_10_
  86.9 1.6 collective-permute-start.18
  89.0 6.3 %collective-permute-done.17.refs_12_ = bf16[3,256,256]{2,1,0:T(8,128)(2,1)S(1)} collective-permute-done((bf16[3,256,256]{2,1,0:T(8,128)(2,1)S(1)}, bf16[3,256,256]{2,1,0:T(8,128)(2,1)S(1)}, u32[]{:S(2)}, u32[]{:S(2)}) %collective-permute-start.17) | collective-permute-done | bytes 393248 | tf_op jit(solution)/shard_map/ppermute | solution.py:252
  95.3 2.2 %collective-permute-done.18.refs_13_ = bf16[3,256,256]{2,1,0:T(8,128)(2,1)} collective-permute-done((bf16[3,256,256]{2,1,0:T(8,128)(2,1)S(1)}, bf16[3,256,256]{2,1,0:T(8,128)(2,1)}, u32[]{:S(2)}, u32[]{:S(2)}) %collective-permute-start.18) | collective-permute-done | bytes 393248 | tf_op jit(solution)/shard_map/ppermute | solution.py:252
  98.9 1.4 collective-permute-start.15
  101.7 16.4 %shard_map.120 = (f32[16,256,256]{2,1,0:T(8,128)}, f32[4,256,256]{2,1,0:T(8,128)}) custom-call(s32[2]{0:T(128)} %pad_add_fusion.3.refs_0_, s32[2,8]{1,0:T(2,128)} %bitcast.20, s32[2,8]{1,0:T(2,128)} %bitcast.24, s32[2,8]{1,0:T(2,128)} %bitcast.28, s32[48]{0:T(128)} %refs_1_.1, s32[48]{0:T(128)} %refs_2_.1, ...), custom_call_target="tpu_custom_call", output_to_operand_aliasing={{0}: (19, {}), {1}: (20, {})} | custom-call | flops 17179869184 | bytes 10485760 | tf_op jit(solution)/shard_map/pallas_call | solution.py:196
  118.6 3.6 %collective-permute-done.16.refs_9_.refs_8_ = bf16[3,512,256]{2,1,0:T(8,128)(2,1)} collective-permute-done((bf16[3,512,256]{2,1,0:T(8,128)(2,1)S(1)}, bf16[3,512,256]{2,1,0:T(8,128)(2,1)}, u32[]{:S(2)}, u32[]{:S(2)}) %collective-permute-start.16) | collective-permute-done | bytes 786464 | tf_op jit(solution)/shard_map/ppermute | solution.py:328
  123.3 2.2 %collective-permute-done.25.refs_11_.refs_10_ = bf16[3,512,256]{2,1,0:T(8,128)(2,1)S(1)} collective-permute-done((bf16[3,512,256]{2,1,0:T(8,128)(2,1)S(1)}, bf16[3,512,256]{2,1,0:T(8,128)(2,1)S(1)}, u32[]{:S(2)}, u32[]{:S(2)}) %collective-permute-start.25) | collective-permute-done | bytes 786464 | tf_op jit(solution)/shard_map/ppermute | solution.py:252
  127.1 9.1 %shard_map.122 = bf16[16,256,256]{2,1,0:T(8,128)(2,1)} custom-call(s32[2]{0:T(128)} %pad_add_fusion.refs_0_, s32[2,8]{1,0:T(2,128)} %bitcast.21, s32[2,8]{1,0:T(2,128)} %bitcast.25, s32[2,8]{1,0:T(2,128)} %bitcast.29, bf16[4,256,2048]{2,1,0:T(8,128)(2,1)} %bitcast.15, bf16[3,512,256]{2,1,0:T(8,128)(2,1)} %copy-done.4, bf16[3,512,256]{2,1,0:T(8,128)(2,1)} %copy-done.5, ...), custom_call_target="tpu_custom_call" | custom-call | flops 4294967296 | bytes 10485760 | tf_op jit(solution)/shard_map/pallas_call | solution.py:196
  136.2 4.0 %all-to-all-start = ((bf16[8,2,256,256]{3,2,1,0:T(8,128)(2,1)}), bf16[8,2,256,256]{3,2,1,0:T(8,128)(2,1)S(1)}, u32[]{:S(2)}, u32[]{:S(2)}) async-start(bf16[8,2,256,256]{3,2,1,0:T(8,128)(2,1)} %bitcast.17), calls=%async_computation | async-start | bytes 4194304 | tf_op jit(solution)/shard_map/all_to_all | solution.py:342
  140.2 10.0 %shard_map.121.near_ref = f32[4,256,256]{2,1,0:T(8,128)} custom-call(s32[2]{0:T(128)} %pad_add_fusion.refs_0_, s32[48]{0:T(128)} %refs_1_.1, s32[48]{0:T(128)} %refs_2_.1, s32[48]{0:T(128)} %refs_3_.1, s32[48]{0:T(128)} %refs_4_.7, bf16[4,256,2048]{2,1,0:T(8,128)(2,1)} %bitcast.16, bf16[3,512,256]{2,1,0:T(8,128)(2,1)} %copy-done.4, ...), custom_call_target="tpu_custom_call", output_to_operand_aliasing={{}: (14, {})} | custom-call | flops 12884901888 | bytes 10485760 | tf_op jit(solution)/shard_map/pallas_call | solution.py:196
  150.2 16.6 %all-to-all-done.recv_ref = bf16[8,2,256,256]{3,2,1,0:T(8,128)(2,1)S(1)} async-done(((bf16[8,2,256,256]{3,2,1,0:T(8,128)(2,1)}), bf16[8,2,256,256]{3,2,1,0:T(8,128)(2,1)S(1)}, u32[]{:S(2)}, u32[]{:S(2)}) %all-to-all-start) | async-done | bytes 2097184 | tf_op jit(solution)/shard_map/all_to_all | solution.py:342
  168.1 2.4 %shard_map.123 = bf16[4,256,256]{2,1,0:T(8,128)(2,1)} custom-call(s32[2,8]{1,0:T(2,128)S(1)} %bitcast.11, f32[4,256,256]{2,1,0:T(8,128)S(1)} %copy-done, bf16[8,2,256,256]{3,2,1,0:T(8,128)(2,1)S(1)} %all-to-all-done.recv_ref, bf16[4,256,256]{2,1,0:T(8,128)(2,1)S(1)} %copy-done.1, bf16[4,256,256]{2,1,0:T(8,128)(2,1)S(1)} %copy-done.2), custom_call_target="tpu_custom_call" | custom-call | tf_op jit(solution)/shard_map/pallas_call | solution.py:241
  (76 shorter events, 20.9 us)
Async XLA Ops:
  1.5 25.0 %collective-permute-start = (bf16[3,512,256]{2,1,0:T(8,128)(2,1)S(1)}, bf16[3,512,256]{2,1,0:T(8,128)(2,1)}, u32[]{:S(2)}, u32[]{:S(2)}) collective-permute-start(bf16[3,512,256]{2,1,0:T(8,128)(2,1)S(1)} %get-tuple-element.58), channel_id=1, source_target_pairs={{0,3},{1,0},{2,1},{3,2},{4,7},{5,4},{6,5},{7,6},{8,11},{9,8},{10,9... | collective-permute-start | bytes 2359304 | tf_op jit(solution)/shard_map/ppermute | solution.py:310
  26.5 18.5 %collective-permute-start.3 = (bf16[3,512,256]{2,1,0:T(8,128)(2,1)}, bf16[3,512,256]{2,1,0:T(8,128)(2,1)S(1)}, u32[]{:S(2)}, u32[]{:S(2)}) collective-permute-start(bf16[3,512,256]{2,1,0:T(8,128)(2,1)} %collective-permute-done.refs_9_), channel_id=1, source_target_pairs={{0,8},{4,12},{8,0},{12,4},{16,24},{20,28},{24,16},{28,20},{1,9},{5... | collective-permute-start | bytes 2359304 | tf_op jit(solution)/shard_map/ppermute | solution.py:252
  28.0 19.5 %collective-permute-start.4 = (bf16[3,512,256]{2,1,0:T(8,128)(2,1)}, bf16[3,512,256]{2,1,0:T(8,128)(2,1)S(1)}, u32[]{:S(2)}, u32[]{:S(2)}) collective-permute-start(bf16[3,512,256]{2,1,0:T(8,128)(2,1)} %collective-permute-done.refs_9_), channel_id=1, source_target_pairs={{0,16},{4,20},{8,24},{12,28},{16,0},{20,4},{24,8},{28,12},{1,17},{... | collective-permute-start | bytes 2359304 | tf_op jit(solution)/shard_map/ppermute | solution.py:252
  28.8 20.3 %collective-permute-start.1 = (bf16[3,512,256]{2,1,0:T(8,128)(2,1)}, bf16[3,512,256]{2,1,0:T(8,128)(2,1)}, u32[]{:S(2)}, u32[]{:S(2)}) collective-permute-start(bf16[3,512,256]{2,1,0:T(8,128)(2,1)} %collective-permute-done.refs_9_), channel_id=1, source_target_pairs={{0,3},{1,0},{2,1},{3,2},{4,7},{5,4},{6,5},{7,6},{8,11},{9,8},{10,9... | collective-permute-start | bytes 2359304 | tf_op jit(solution)/shard_map/ppermute | solution.py:310
  30.8 31.0 %collective-permute-start.7 = (bf16[3,512,256]{2,1,0:T(8,128)(2,1)}, bf16[3,512,256]{2,1,0:T(8,128)(2,1)S(1)}, u32[]{:S(2)}, u32[]{:S(2)}) collective-permute-start(bf16[3,512,256]{2,1,0:T(8,128)(2,1)} %collective-permute-done.refs_9_), channel_id=1, source_target_pairs={{0,4},{4,0},{8,12},{12,8},{16,20},{20,16},{24,28},{28,24},{1,5},{5... | collective-permute-start | bytes 2359304 | tf_op jit(solution)/shard_map/ppermute | solution.py:252
  49.1 10.8 %collective-permute-start.5 = (bf16[3,256,256]{2,1,0:T(8,128)(2,1)S(1)}, bf16[3,256,256]{2,1,0:T(8,128)(2,1)S(1)}, u32[]{:S(2)}, u32[]{:S(2)}) collective-permute-start(bf16[3,256,256]{2,1,0:T(8,128)(2,1)S(1)} %slice.12), channel_id=1, source_target_pairs={{0,8},{4,12},{8,0},{12,4},{16,24},{20,28},{24,16},{28,20},{1,9},{5... | collective-permute-start | bytes 1179656 | tf_op jit(solution)/shard_map/ppermute | solution.py:252
  50.5 10.7 %collective-permute-start.6 = (bf16[3,256,256]{2,1,0:T(8,128)(2,1)S(1)}, bf16[3,256,256]{2,1,0:T(8,128)(2,1)}, u32[]{:S(2)}, u32[]{:S(2)}) collective-permute-start(bf16[3,256,256]{2,1,0:T(8,128)(2,1)S(1)} %slice.13), channel_id=1, source_target_pairs={{0,16},{4,20},{8,24},{12,28},{16,0},{20,4},{24,8},{28,12},{1,17},{... | collective-permute-start | bytes 1179656 | tf_op jit(solution)/shard_map/ppermute | solution.py:252
  50.8 12.5 %collective-permute-start.8 = (bf16[3,512,256]{2,1,0:T(8,128)(2,1)S(1)}, bf16[3,512,256]{2,1,0:T(8,128)(2,1)}, u32[]{:S(2)}, u32[]{:S(2)}) collective-permute-start(bf16[3,512,256]{2,1,0:T(8,128)(2,1)S(1)} %collective-permute-done.3.refs_10_), channel_id=1, source_target_pairs={{0,4},{4,0},{8,12},{12,8},{16,20},{20,16},{24,28},{28,24},{1,5},{5... | collective-permute-start | bytes 2359304 | tf_op jit(solution)/shard_map/ppermute | solution.py:252
  50.8 13.8 %collective-permute-start.9 = (bf16[3,512,256]{2,1,0:T(8,128)(2,1)S(1)}, bf16[3,512,256]{2,1,0:T(8,128)(2,1)}, u32[]{:S(2)}, u32[]{:S(2)}) collective-permute-start(bf16[3,512,256]{2,1,0:T(8,128)(2,1)S(1)} %collective-permute-done.4.refs_11_), channel_id=1, source_target_pairs={{0,4},{4,0},{8,12},{12,8},{16,20},{20,16},{24,28},{28,24},{1,5},{5... | collective-permute-start | bytes 2359304 | tf_op jit(solution)/shard_map/ppermute | solution.py:252
  61.8 20.3 %collective-permute-start.12 = (bf16[3,512,256]{2,1,0:T(8,128)(2,1)}, bf16[3,512,256]{2,1,0:T(8,128)(2,1)}, u32[]{:S(2)}, u32[]{:S(2)}) collective-permute-start(bf16[3,512,256]{2,1,0:T(8,128)(2,1)} %collective-permute-done.1.refs_9_), channel_id=1, source_target_pairs={{0,8},{4,12},{8,0},{12,4},{16,24},{20,28},{24,16},{28,20},{1,9},{5... | collective-permute-start | bytes 2359304 | tf_op jit(solution)/shard_map/ppermute | solution.py:252
  62.5 20.0 %collective-permute-start.13 = (bf16[3,512,256]{2,1,0:T(8,128)(2,1)}, bf16[3,512,256]{2,1,0:T(8,128)(2,1)}, u32[]{:S(2)}, u32[]{:S(2)}) collective-permute-start(bf16[3,512,256]{2,1,0:T(8,128)(2,1)} %collective-permute-done.1.refs_9_), channel_id=1, source_target_pairs={{0,16},{4,20},{8,24},{12,28},{16,0},{20,4},{24,8},{28,12},{1,17},{... | collective-permute-start | bytes 2359304 | tf_op jit(solution)/shard_map/ppermute | solution.py:252
  63.2 34.9 %collective-permute-start.19 = (bf16[3,512,256]{2,1,0:T(8,128)(2,1)}, bf16[3,512,256]{2,1,0:T(8,128)(2,1)}, u32[]{:S(2)}, u32[]{:S(2)}) collective-permute-start(bf16[3,512,256]{2,1,0:T(8,128)(2,1)} %collective-permute-done.1.refs_9_), channel_id=1, source_target_pairs={{0,4},{4,0},{8,12},{12,8},{16,20},{20,16},{24,28},{28,24},{1,5},{5... | collective-permute-start | bytes 2359304 | tf_op jit(solution)/shard_map/ppermute | solution.py:252
  63.4 20.0 %collective-permute-start.2 = (bf16[3,512,256]{2,1,0:T(8,128)(2,1)}, bf16[3,512,256]{2,1,0:T(8,128)(2,1)S(1)}, u32[]{:S(2)}, u32[]{:S(2)}) collective-permute-start(bf16[3,512,256]{2,1,0:T(8,128)(2,1)} %collective-permute-done.1.refs_9_), channel_id=1, source_target_pairs={{0,3},{1,0},{2,1},{3,2},{4,7},{5,4},{6,5},{7,6},{8,11},{9,8},{10,9... | collective-permute-start | bytes 2359304 | tf_op jit(solution)/shard_map/ppermute | solution.py:310
  84.7 10.6 %collective-permute-start.17 = (bf16[3,256,256]{2,1,0:T(8,128)(2,1)S(1)}, bf16[3,256,256]{2,1,0:T(8,128)(2,1)S(1)}, u32[]{:S(2)}, u32[]{:S(2)}) collective-permute-start(bf16[3,256,256]{2,1,0:T(8,128)(2,1)S(1)} %slice.14), channel_id=1, source_target_pairs={{0,8},{4,12},{8,0},{12,4},{16,24},{20,28},{24,16},{28,20},{1,9},{5... | collective-permute-start | bytes 1179656 | tf_op jit(solution)/shard_map/ppermute | solution.py:252
  86.9 10.6 %collective-permute-start.18 = (bf16[3,256,256]{2,1,0:T(8,128)(2,1)S(1)}, bf16[3,256,256]{2,1,0:T(8,128)(2,1)}, u32[]{:S(2)}, u32[]{:S(2)}) collective-permute-start(bf16[3,256,256]{2,1,0:T(8,128)(2,1)S(1)} %slice.15), channel_id=1, source_target_pairs={{0,16},{4,20},{8,24},{12,28},{16,0},{20,4},{24,8},{28,12},{1,17},{... | collective-permute-start | bytes 1179656 | tf_op jit(solution)/shard_map/ppermute | solution.py:252
  88.5 11.8 %collective-permute-start.20 = (bf16[3,512,256]{2,1,0:T(8,128)(2,1)}, bf16[3,512,256]{2,1,0:T(8,128)(2,1)}, u32[]{:S(2)}, u32[]{:S(2)}) collective-permute-start(bf16[3,512,256]{2,1,0:T(8,128)(2,1)} %collective-permute-done.12.refs_10_), channel_id=1, source_target_pairs={{0,4},{4,0},{8,12},{12,8},{16,20},{20,16},{24,28},{28,24},{1,5},{5... | collective-permute-start | bytes 2359304 | tf_op jit(solution)/shard_map/ppermute | solution.py:252
  88.5 13.2 %collective-permute-start.21 = (bf16[3,512,256]{2,1,0:T(8,128)(2,1)}, bf16[3,512,256]{2,1,0:T(8,128)(2,1)}, u32[]{:S(2)}, u32[]{:S(2)}) collective-permute-start(bf16[3,512,256]{2,1,0:T(8,128)(2,1)} %collective-permute-done.13.refs_11_), channel_id=1, source_target_pairs={{0,4},{4,0},{8,12},{12,8},{16,20},{20,16},{24,28},{28,24},{1,5},{5... | collective-permute-start | bytes 2359304 | tf_op jit(solution)/shard_map/ppermute | solution.py:252
  98.2 20.0 %collective-permute-start.14 = (bf16[3,512,256]{2,1,0:T(8,128)(2,1)S(1)}, bf16[3,512,256]{2,1,0:T(8,128)(2,1)S(1)}, u32[]{:S(2)}, u32[]{:S(2)}) collective-permute-start(bf16[3,512,256]{2,1,0:T(8,128)(2,1)S(1)} %collective-permute-done.2.refs_6_.refs_5_), channel_id=1, source_target_pairs={{0,8},{4,12},{8,0},{12,4},{16,24},{20,28},{24,16},{28,20},{1,9},{5... | collective-permute-start | bytes 2359304 | tf_op jit(solution)/shard_map/ppermute | solution.py:252
  98.9 19.7 %collective-permute-start.15 = (bf16[3,512,256]{2,1,0:T(8,128)(2,1)S(1)}, bf16[3,512,256]{2,1,0:T(8,128)(2,1)S(1)}, u32[]{:S(2)}, u32[]{:S(2)}) collective-permute-start(bf16[3,512,256]{2,1,0:T(8,128)(2,1)S(1)} %collective-permute-done.2.refs_6_.refs_5_), channel_id=1, source_target_pairs={{0,16},{4,20},{8,24},{12,28},{16,0},{20,4},{24,8},{28,12},{1,17},{... | collective-permute-start | bytes 2359304 | tf_op jit(solution)/shard_map/ppermute | solution.py:252
  100.3 23.0 %collective-permute-start.24 = (bf16[3,512,256]{2,1,0:T(8,128)(2,1)S(1)}, bf16[3,512,256]{2,1,0:T(8,128)(2,1)}, u32[]{:S(2)}, u32[]{:S(2)}) collective-permute-start(bf16[3,512,256]{2,1,0:T(8,128)(2,1)S(1)} %collective-permute-done.2.refs_6_.refs_5_), channel_id=1, source_target_pairs={{0,4},{4,0},{8,12},{12,8},{16,20},{20,16},{24,28},{28,24},{1,5},{5... | collective-permute-start | bytes 2359304 | tf_op jit(solution)/shard_map/ppermute | solution.py:252
  100.3 21.9 %collective-permute-start.16 = (bf16[3,512,256]{2,1,0:T(8,128)(2,1)S(1)}, bf16[3,512,256]{2,1,0:T(8,128)(2,1)}, u32[]{:S(2)}, u32[]{:S(2)}) collective-permute-start(bf16[3,512,256]{2,1,0:T(8,128)(2,1)S(1)} %get-tuple-element.45), channel_id=1, source_target_pairs={{3,0},{0,1},{1,2},{2,3},{7,4},{4,5},{5,6},{6,7},{11,8},{8,9},{9,10... | collective-permute-start | bytes 2359304 | tf_op jit(solution)/shard_map/ppermute | solution.py:328
  122.2 4.3 %collective-permute-start.26 = (bf16[3,512,256]{2,1,0:T(8,128)(2,1)S(1)}, bf16[3,512,256]{2,1,0:T(8,128)(2,1)}, u32[]{:S(2)}, u32[]{:S(2)}) collective-permute-start(bf16[3,512,256]{2,1,0:T(8,128)(2,1)S(1)} %collective-permute-done.15.refs_8_.refs_7_), channel_id=1, source_target_pairs={{0,4},{4,0},{8,12},{12,8},{16,20},{20,16},{24,28},{28,24},{1,5},{5... | collective-permute-start | bytes 2359304 | tf_op jit(solution)/shard_map/ppermute | solution.py:252
  122.7 4.4 %collective-permute-start.27 = (bf16[3,512,256]{2,1,0:T(8,128)(2,1)}, bf16[3,512,256]{2,1,0:T(8,128)(2,1)}, u32[]{:S(2)}, u32[]{:S(2)}) collective-permute-start(bf16[3,512,256]{2,1,0:T(8,128)(2,1)} %collective-permute-done.16.refs_9_.refs_8_), channel_id=1, source_target_pairs={{0,4},{4,0},{8,12},{12,8},{16,20},{20,16},{24,28},{28,24},{1,5},{5... | collective-permute-start | bytes 2359304 | tf_op jit(solution)/shard_map/ppermute | solution.py:252
  136.2 30.7 %all-to-all-start = ((bf16[8,2,256,256]{3,2,1,0:T(8,128)(2,1)}), bf16[8,2,256,256]{3,2,1,0:T(8,128)(2,1)S(1)}, u32[]{:S(2)}, u32[]{:S(2)}) async-start(bf16[8,2,256,256]{3,2,1,0:T(8,128)(2,1)} %bitcast.17), calls=%async_computation | async-start | bytes 4194304 | tf_op jit(solution)/shard_map/all_to_all | solution.py:342
  (18 other events, 198.7 us)

commit v8 on v7

--- a/solution.py
+++ b/solution.py
@@ -305,36 +305,57 @@
     )
     own = part(group)
     corner = part(group ^ 6)
-    rounds = []
-    for step in range(1, lanes):
+
+    def neighbours(value):
+        masks, held = upper(value, peers)
+        return (
+            [(m, 0, v) for m, v in zip(masks, held)],
+            [(m ^ 2, 0, swap(v, 2, peers)) for m, v in zip(masks, held)],
+            [(m ^ 4, 0, swap(v, 4, peers)) for m, v in zip(masks, held)],
+        )
+
+    def tie(*values):
+        leaves, tree = jax.tree.flatten(values)
+        arrays = lax.optimization_barrier([v for v in leaves if not isinstance(v, int)])
+        return jax.tree.unflatten(
+            tree, [v if isinstance(v, int) else arrays.pop(0) for v in leaves]
+        )
+
+    def corners(value):
+        masks, held = upper(value, peers)
+        return [(m ^ 6, 0, v) for m, v in zip(masks, held)]
+
+    own = lax.ppermute(own, "lag", ring)
+    own, sums = tie(own, sums)
+    trio = neighbours(own)
+    own = lax.ppermute(own, "lag", ring)
+    trio, own, corner = tie(trio, own, corner)
+    found = with_other_core(sum(trio, []), peers)
+    held, across, along = neighbours(own)
+    diagonal = lax.ppermute(corner, "lag", ring)
+    held = with_other_core(held, peers)
+    across, along, own, diagonal, found, held = tie(across, along, own, diagonal, found, held)
+    diagonal = with_other_core(corners(diagonal), peers)
+    rounds = [found + diagonal]
+    for step in range(2, lanes - 1):
         own = lax.ppermute(own, "lag", ring)
-        if step == 1:
-            ready, sums = lax.optimization_barrier((own, sums))
-        else:
-            if step > 2:
-                sums = add_shard(step - 2, sums)
-            ready, corner, sums, across, along = lax.optimization_barrier(
-                (own, corner, sums, across, along)
-            )
-            found = [(m, 0, v) for m, v in zip(masks, held)]
-            found += [(m ^ 2, 0, v) for m, v in zip(masks, across)]
-            found += [(m ^ 4, 0, v) for m, v in zip(masks, along)]
-            found += [(m ^ 6, 0, swap(v[:, :half], 2, peers)) for m, v in zip(masks, along)]
-            found += [(m ^ 6, half, swap(v[:, half:], 4, peers)) for m, v in zip(masks, across)]
-            rounds.append(with_other_core(found, peers))
-        masks, held = upper(ready, peers)
-        across = [swap(value, 2, peers) for value in held]
-        along = [swap(value, 4, peers) for value in held]
-    corner = lax.ppermute(corner, "lag", [(j, i) for i, j in ring])
-    if lanes > 2:
-        sums = add_shard(lanes - 2, sums)
-        across, along, corner, sums = lax.optimization_barrier((across, along, corner, sums))
-    _, corners = upper(corner, peers)
-    found = [(m, 0, v) for m, v in zip(masks, held)]
-    found += [(m ^ 2, 0, v) for m, v in zip(masks, across)]
-    found += [(m ^ 4, 0, v) for m, v in zip(masks, along)]
-    found += [(m ^ 6, 0, v) for m, v in zip(masks, corners)]
-    rounds.append(with_other_core(found, peers))
+        turned = [(m ^ 2, 0, swap(v[:, :half], 2, peers)) for m, _, v in along]
+        turned += [(m ^ 4, half, swap(v[:, half:], 4, peers)) for m, _, v in across]
+        if step == 2:
+            rounds[0], across, along = tie(rounds[0], across, along)
+        found = held + with_other_core(across + along, peers)
+        sums = add_shard(step - 1, sums)
+        own, turned, sums, corner, found = tie(own, turned, sums, corner, found)
+        held, across, along = neighbours(own)
+        found, held = tie(found + with_other_core(turned, peers), held)
+        rounds.append(found)
+        held = with_other_core(held, peers)
+        if step < lanes - 2:
+            across, along, own = tie(across, along, own)
+    diagonal = lax.ppermute(corner, "lag", [(j, i) for i, j in ring])
+    sums = add_shard(lanes - 2, sums)
+    across, along, diagonal, sums = tie(across, along, diagonal, sums)
+    rounds.append(held + with_other_core(across + along + corners(diagonal), peers))
     last = lax.rem(lane + lanes - 1, lanes)
     contribution = window_sums(
         last, group, served, (), hist_t, rounds[-1], sums[:1], lanes, rows, narrow=True

time: 172 us -> 170 us (0.988); the launches traced: 170 us -> 171 us
  waiting for transfers between devices: 64.1 us -> 56.6 us
  Pallas kernels: 66.6 us -> 70.7 us
  starting transfers between devices: 25.5 us -> 29.4 us
    ppermute x24 -> x21, waiting for transfers between devices: 41.4 us -> 36.5 us  [swap(): return lax.ppermute(value, 'grp', [(i, i ^ bit) for i in range(peers)])]
    pallas_call x5, Pallas kernels: 64.3 us -> 68.4 us  [window_sums(): pl.pallas_call(functools.partial(window_kernel, config), out_shape=outs,...]
    unnamed x27 -> x47, local copies, waits for them, and re-layouts: 7.62 us -> 10.2 us
    ppermute x3, waiting for transfers between devices: 2.45 us -> 0.01 us  [per_device(): own = lax.ppermute(own, 'lag', ring)]
    slice x4 -> x2, local copies, waits for them, and re-layouts: 2.36 us -> 0.05 us  [the longest x1 0.03 us: per_device(): turned = [(m ^ 2, 0, swap(v[:, :half], 2, peers)) for m, _, v in along]]
    ppermute x3, starting transfers between devices: 8.37 us -> 10.2 us  [per_device(): own = lax.ppermute(own, 'lag', ring)]
    all_to_all x1, starting transfers between devices: 4.01 us -> 5.81 us  [per_device(): lax.all_to_all(contribution.reshape(peers, slots, *contribution.shape[1:]...]
    ppermute x1 -> x2, waiting for transfers between devices: 3.59 us -> 4.84 us  [the longest x1 3.35 us: per_device(): diagonal = lax.ppermute(corner, 'lag', [(j, i) for i, j in ring])]
  transfers between devices with their start and end apart: 29 -> 27, of which waited for: 17 -> 10; matrix products, arithmetic and copies ran while one was open for 7% -> 5% of each run, Pallas kernels for 32% -> 35%
where the time goes in v8:
time: 170 us; the launch traced here: 171 us
  Pallas kernels  70.7 us (42%)
  waiting for transfers between devices  56.6 us (33%)
  starting transfers between devices  29.4 us (17%)
  local copies, waits for them, and re-layouts  11.7 us (7%)
  other arithmetic  1.86 us (1%)
    pallas_call x5, Pallas kernels, window_sums(): pl.pallas_call(functools.partial(window_kernel, config), out_shape=outs,...  68.4 us
    ppermute x21, waiting for transfers between devices, swap(): return lax.ppermute(value, 'grp', [(i, i ^ bit) for i in range(peers)])  36.5 us
    all_to_all x1, waiting for transfers between devices, per_device(): lax.all_to_all(contribution.reshape(peers, slots, *contribution.shape[1:]...  15.2 us
    ppermute x21, starting transfers between devices, swap(): return lax.ppermute(value, 'grp', [(i, i ^ bit) for i in range(peers)])  11.3 us
    ppermute x3, starting transfers between devices, per_device(): own = lax.ppermute(own, 'lag', ring)  10.2 us
    unnamed x47, local copies, waits for them, and re-layouts  10.2 us
    all_to_all x1, starting transfers between devices, per_device(): lax.all_to_all(contribution.reshape(peers, slots, *contribution.shape[1:]...  5.81 us
  transfers between devices with their start and end apart: 27, of which 10 were waited for; matrix products, arithmetic and copies ran while one was open for 5% of the time, Pallas kernels for 35%

profile of v8, /device:TPU:0, one launch (start us, length us, event | category | flops | bytes accessed | tf_op | source)
XLA Modules:
  0.0 170.6 jit_solution(3522846127161905970)
XLA Ops:
  0.0 1.5 constant_dynamic-slice_fusion
  1.5 5.1 %collective-permute-start = (bf16[3,512,256]{2,1,0:T(8,128)(2,1)S(1)}, bf16[3,512,256]{2,1,0:T(8,128)(2,1)S(1)}, u32[]{:S(2)}, u32[]{:S(2)}) collective-permute-start(bf16[3,512,256]{2,1,0:T(8,128)(2,1)S(1)} %get-tuple-element.134), channel_id=1, source_target_pairs={{0,3},{1,0},{2,1},{3,2},{4,7},{5,4},{6,5},{7,6},{8,11},{9,8},{10,9... | collective-permute-start | bytes 2359304 | tf_op jit(solution)/shard_map/ppermute | solution.py:328
  6.6 6.2 %copy.18 = bf16[4,2048,256]{1,2,0:T(8,128)(2,1)} copy(bf16[4,2048,256]{2,1,0:T(8,128)(2,1)} %param.13) | data formatting | bytes 8388608 | tf_op args[1]
  13.4 14.4 %shard_map.118 = (f32[16,256,256]{2,1,0:T(8,128)}, f32[4,256,256]{2,1,0:T(8,128)}) custom-call(s32[2]{0:T(128)} %pad_add_fusion.1.refs_0_, s32[2,8]{1,0:T(2,128)} %bitcast.18, s32[2,8]{1,0:T(2,128)} %bitcast.22, s32[2,8]{1,0:T(2,128)} %bitcast.26, s32[48]{0:T(128)} %refs_1_.1, s32[48]{0:T(128)} %refs_2_.1, s32[48]{0:T(128)} %refs_3_.1, s32[48]{0:T(128)} %refs_4_.7, ...), custom_call_target="tpu_custom_call" | custom-call | flops 17179869184 | bytes 10485760 | tf_op jit(solution)/shard_map/pallas_call | solution.py:196
  27.8 1.6 collective-permute-start.2
  29.4 1.2 collective-permute-start.3
  30.7 16.9 %collective-permute-done.1.refs_10_ = bf16[3,512,256]{2,1,0:T(8,128)(2,1)S(1)} collective-permute-done((bf16[3,512,256]{2,1,0:T(8,128)(2,1)S(1)}, bf16[3,512,256]{2,1,0:T(8,128)(2,1)S(1)}, u32[]{:S(2)}, u32[]{:S(2)}) %collective-permute-start.1) | collective-permute-done | bytes 786464 | tf_op jit(solution)/shard_map/ppermute | solution.py:252
  48.1 1.4 collective-permute-start.4
  49.5 1.6 collective-permute-start.5
  51.1 2.1 %collective-permute-start.6 = (bf16[3,512,256]{2,1,0:T(8,128)(2,1)S(1)}, bf16[3,512,256]{2,1,0:T(8,128)(2,1)}, u32[]{:S(2)}, u32[]{:S(2)}) collective-permute-start(bf16[3,512,256]{2,1,0:T(8,128)(2,1)S(1)} %get-tuple-element.113), channel_id=1, source_target_pairs={{0,3},{1,0},{2,1},{3,2},{4,7},{5,4},{6,5},{7,6},{8,11},{9,8},{10,9... | collective-permute-start | bytes 2359304 | tf_op jit(solution)/shard_map/ppermute | solution.py:335
  53.7 14.4 %collective-permute-done.4.refs_11_ = bf16[3,512,256]{2,1,0:T(8,128)(2,1)S(1)} collective-permute-done((bf16[3,512,256]{2,1,0:T(8,128)(2,1)S(1)}, bf16[3,512,256]{2,1,0:T(8,128)(2,1)S(1)}, u32[]{:S(2)}, u32[]{:S(2)}) %collective-permute-start.4) | collective-permute-done | bytes 786464 | tf_op jit(solution)/shard_map/ppermute | solution.py:252
  69.1 1.5 collective-permute-done.6.refs_15_
  73.3 3.9 %collective-permute-start.11 = (bf16[3,512,256]{2,1,0:T(8,128)(2,1)}, bf16[3,512,256]{2,1,0:T(8,128)(2,1)S(1)}, u32[]{:S(2)}, u32[]{:S(2)}) collective-permute-start(bf16[3,512,256]{2,1,0:T(8,128)(2,1)} %copy-done.10), channel_id=1, source_target_pairs={{0,3},{1,0},{2,1},{3,2},{4,7},{5,4},{6,5},{7,6},{8,11},{9,8},{10,9... | collective-permute-start | bytes 2359304 | tf_op jit(solution)/shard_map/ppermute | solution.py:341
  79.2 16.7 %shard_map.119 = (f32[16,256,256]{2,1,0:T(8,128)}, f32[4,256,256]{2,1,0:T(8,128)}) custom-call(s32[2]{0:T(128)} %get-tuple-element.135.refs_0_, s32[2,8]{1,0:T(2,128)} %bitcast.19, s32[2,8]{1,0:T(2,128)} %bitcast.23, s32[2,8]{1,0:T(2,128)} %bitcast.27, s32[48]{0:T(128)} %refs_1_.1, s32[48]{0:T(128)} %refs_2_.1, ...), custom_call_target="tpu_custom_call", output_to_operand_aliasing={{0}: (17, {}), {1}: (18, {})} | custom-call | flops 17179869184 | bytes 10485760 | tf_op jit(solution)/shard_map/pallas_call | solution.py:196
  96.8 2.7 %collective-permute-start.21 = (bf16[3,512,256]{2,1,0:T(8,128)(2,1)S(1)}, bf16[3,512,256]{2,1,0:T(8,128)(2,1)S(1)}, u32[]{:S(2)}, u32[]{:S(2)}) collective-permute-start(bf16[3,512,256]{2,1,0:T(8,128)(2,1)S(1)} %collective-permute-done.11.refs_6_.refs_5_), channel_id=1, source_target_pairs={{0,16},{4,20},{8,24},{12,28},{16,0},{20,4},{24,8},{28,12},{1,17},{... | collective-permute-start | bytes 2359304 | tf_op jit(solution)/shard_map/ppermute | solution.py:252
  100.4 17.2 %shard_map.120 = (f32[16,256,256]{2,1,0:T(8,128)}, f32[4,256,256]{2,1,0:T(8,128)}) custom-call(s32[2]{0:T(128)} %get-tuple-element.136.refs_0_, s32[2,8]{1,0:T(2,128)} %bitcast.20, s32[2,8]{1,0:T(2,128)} %bitcast.24, s32[2,8]{1,0:T(2,128)} %bitcast.28, s32[48]{0:T(128)} %refs_1_.1, s32[48]{0:T(128)} %refs_2_.1, ...), custom_call_target="tpu_custom_call", output_to_operand_aliasing={{0}: (19, {}), {1}: (20, {})} | custom-call | flops 17179869184 | bytes 10485760 | tf_op jit(solution)/shard_map/pallas_call | solution.py:196
  117.6 3.4 %collective-permute-done.22.refs_10_.refs_9_ = bf16[3,512,256]{2,1,0:T(8,128)(2,1)} collective-permute-done((bf16[3,512,256]{2,1,0:T(8,128)(2,1)S(1)}, bf16[3,512,256]{2,1,0:T(8,128)(2,1)}, u32[]{:S(2)}, u32[]{:S(2)}) %collective-permute-start.22) | collective-permute-done | bytes 786464 | tf_op jit(solution)/shard_map/ppermute | solution.py:355
  122.2 2.2 %collective-permute-done.23.refs_11_.refs_10_ = bf16[3,512,256]{2,1,0:T(8,128)(2,1)S(1)} collective-permute-done((bf16[3,512,256]{2,1,0:T(8,128)(2,1)S(1)}, bf16[3,512,256]{2,1,0:T(8,128)(2,1)S(1)}, u32[]{:S(2)}, u32[]{:S(2)}) %collective-permute-start.23) | collective-permute-done | bytes 786464 | tf_op jit(solution)/shard_map/ppermute | solution.py:252
  125.9 8.7 %shard_map.122 = bf16[16,256,256]{2,1,0:T(8,128)(2,1)} custom-call(s32[2]{0:T(128)} %pad_add_fusion.refs_0_, s32[2,8]{1,0:T(2,128)} %bitcast.21, s32[2,8]{1,0:T(2,128)} %bitcast.25, s32[2,8]{1,0:T(2,128)} %bitcast.29, bf16[4,256,2048]{2,1,0:T(8,128)(2,1)} %bitcast.15, bf16[3,512,256]{2,1,0:T(8,128)(2,1)} %copy-done.4, ...), custom_call_target="tpu_custom_call" | custom-call | flops 4294967296 | bytes 10485760 | tf_op jit(solution)/shard_map/pallas_call | solution.py:196
  134.6 5.8 %all-to-all-start = ((bf16[8,2,256,256]{3,2,1,0:T(8,128)(2,1)}), bf16[8,2,256,256]{3,2,1,0:T(8,128)(2,1)S(1)}, u32[]{:S(2)}, u32[]{:S(2)}) async-start(bf16[8,2,256,256]{3,2,1,0:T(8,128)(2,1)} %bitcast.17), calls=%async_computation | async-start | bytes 4194304 | tf_op jit(solution)/shard_map/all_to_all | solution.py:363
  140.4 11.4 %shard_map.121.near_ref = f32[4,256,256]{2,1,0:T(8,128)} custom-call(s32[2]{0:T(128)} %pad_add_fusion.refs_0_, s32[48]{0:T(128)} %refs_1_.1, s32[48]{0:T(128)} %refs_2_.1, s32[48]{0:T(128)} %refs_3_.1, s32[48]{0:T(128)} %refs_4_.7, bf16[4,256,2048]{2,1,0:T(8,128)(2,1)} %bitcast.16, bf16[3,512,256]{2,1,0:T(8,128)(2,1)} %copy-done.4, ...), custom_call_target="tpu_custom_call", output_to_operand_aliasing={{}: (14, {})} | custom-call | flops 12884901888 | bytes 10485760 | tf_op jit(solution)/shard_map/pallas_call | solution.py:196
  151.8 15.2 %all-to-all-done.recv_ref = bf16[8,2,256,256]{3,2,1,0:T(8,128)(2,1)S(1)} async-done(((bf16[8,2,256,256]{3,2,1,0:T(8,128)(2,1)}), bf16[8,2,256,256]{3,2,1,0:T(8,128)(2,1)S(1)}, u32[]{:S(2)}, u32[]{:S(2)}) %all-to-all-start) | async-done | bytes 2097184 | tf_op jit(solution)/shard_map/all_to_all | solution.py:363
  167.0 1.2 copy-done
  168.2 2.4 %shard_map.123 = bf16[4,256,256]{2,1,0:T(8,128)(2,1)} custom-call(s32[2,8]{1,0:T(2,128)S(1)} %bitcast.11, f32[4,256,256]{2,1,0:T(8,128)S(1)} %copy-done, bf16[8,2,256,256]{3,2,1,0:T(8,128)(2,1)S(1)} %all-to-all-done.recv_ref, bf16[4,256,256]{2,1,0:T(8,128)(2,1)S(1)} %copy-done.1, bf16[4,256,256]{2,1,0:T(8,128)(2,1)S(1)} %copy-done.2), custom_call_target="tpu_custom_call" | custom-call | tf_op jit(solution)/shard_map/pallas_call | solution.py:241
  (89 shorter events, 11.7 us)
Async XLA Ops:
  1.5 26.3 %collective-permute-start = (bf16[3,512,256]{2,1,0:T(8,128)(2,1)S(1)}, bf16[3,512,256]{2,1,0:T(8,128)(2,1)S(1)}, u32[]{:S(2)}, u32[]{:S(2)}) collective-permute-start(bf16[3,512,256]{2,1,0:T(8,128)(2,1)S(1)} %get-tuple-element.134), channel_id=1, source_target_pairs={{0,3},{1,0},{2,1},{3,2},{4,7},{5,4},{6,5},{7,6},{8,11},{9,8},{10,9... | collective-permute-start | bytes 2359304 | tf_op jit(solution)/shard_map/ppermute | solution.py:328
  27.8 19.8 %collective-permute-start.1 = (bf16[3,512,256]{2,1,0:T(8,128)(2,1)S(1)}, bf16[3,512,256]{2,1,0:T(8,128)(2,1)S(1)}, u32[]{:S(2)}, u32[]{:S(2)}) collective-permute-start(bf16[3,512,256]{2,1,0:T(8,128)(2,1)S(1)} %collective-permute-done.refs_9_), channel_id=1, source_target_pairs={{0,8},{4,12},{8,0},{12,4},{16,24},{20,28},{24,16},{28,20},{1,9},{5... | collective-permute-start | bytes 2359304 | tf_op jit(solution)/shard_map/ppermute | solution.py:252
  27.8 20.2 %collective-permute-start.2 = (bf16[3,512,256]{2,1,0:T(8,128)(2,1)S(1)}, bf16[3,512,256]{2,1,0:T(8,128)(2,1)S(1)}, u32[]{:S(2)}, u32[]{:S(2)}) collective-permute-start(bf16[3,512,256]{2,1,0:T(8,128)(2,1)S(1)} %collective-permute-done.refs_9_), channel_id=1, source_target_pairs={{0,16},{4,20},{8,24},{12,28},{16,0},{20,4},{24,8},{28,12},{1,17},{... | collective-permute-start | bytes 2359304 | tf_op jit(solution)/shard_map/ppermute | solution.py:252
  29.4 18.6 %collective-permute-start.3 = (bf16[3,512,256]{2,1,0:T(8,128)(2,1)S(1)}, bf16[3,512,256]{2,1,0:T(8,128)(2,1)S(1)}, u32[]{:S(2)}, u32[]{:S(2)}) collective-permute-start(bf16[3,512,256]{2,1,0:T(8,128)(2,1)S(1)} %collective-permute-done.refs_9_), channel_id=1, source_target_pairs={{0,3},{1,0},{2,1},{3,2},{4,7},{5,4},{6,5},{7,6},{8,11},{9,8},{10,9... | collective-permute-start | bytes 2359304 | tf_op jit(solution)/shard_map/ppermute | solution.py:331
  48.1 5.1 %collective-permute-start.10 = (bf16[3,512,256]{2,1,0:T(8,128)(2,1)S(1)}, bf16[3,512,256]{2,1,0:T(8,128)(2,1)S(1)}, u32[]{:S(2)}, u32[]{:S(2)}) collective-permute-start(bf16[3,512,256]{2,1,0:T(8,128)(2,1)S(1)} %collective-permute-done.3.refs_9_), channel_id=1, source_target_pairs={{0,4},{4,0},{8,12},{12,8},{16,20},{20,16},{24,28},{28,24},{1,5},{5... | collective-permute-start | bytes 2359304 | tf_op jit(solution)/shard_map/ppermute | solution.py:252
  48.1 20.0 %collective-permute-start.4 = (bf16[3,512,256]{2,1,0:T(8,128)(2,1)S(1)}, bf16[3,512,256]{2,1,0:T(8,128)(2,1)S(1)}, u32[]{:S(2)}, u32[]{:S(2)}) collective-permute-start(bf16[3,512,256]{2,1,0:T(8,128)(2,1)S(1)} %collective-permute-done.3.refs_9_), channel_id=1, source_target_pairs={{0,8},{4,12},{8,0},{12,4},{16,24},{20,28},{24,16},{28,20},{1,9},{5... | collective-permute-start | bytes 2359304 | tf_op jit(solution)/shard_map/ppermute | solution.py:252
  49.5 19.6 %collective-permute-start.5 = (bf16[3,512,256]{2,1,0:T(8,128)(2,1)S(1)}, bf16[3,512,256]{2,1,0:T(8,128)(2,1)S(1)}, u32[]{:S(2)}, u32[]{:S(2)}) collective-permute-start(bf16[3,512,256]{2,1,0:T(8,128)(2,1)S(1)} %collective-permute-done.3.refs_9_), channel_id=1, source_target_pairs={{0,16},{4,20},{8,24},{12,28},{16,0},{20,4},{24,8},{28,12},{1,17},{... | collective-permute-start | bytes 2359304 | tf_op jit(solution)/shard_map/ppermute | solution.py:252
  51.1 19.5 %collective-permute-start.6 = (bf16[3,512,256]{2,1,0:T(8,128)(2,1)S(1)}, bf16[3,512,256]{2,1,0:T(8,128)(2,1)}, u32[]{:S(2)}, u32[]{:S(2)}) collective-permute-start(bf16[3,512,256]{2,1,0:T(8,128)(2,1)S(1)} %get-tuple-element.113), channel_id=1, source_target_pairs={{0,3},{1,0},{2,1},{3,2},{4,7},{5,4},{6,5},{7,6},{8,11},{9,8},{10,9... | collective-permute-start | bytes 2359304 | tf_op jit(solution)/shard_map/ppermute | solution.py:335
  53.2 17.4 %collective-permute-start.7 = (bf16[3,512,256]{2,1,0:T(8,128)(2,1)S(1)}, bf16[3,512,256]{2,1,0:T(8,128)(2,1)S(1)}, u32[]{:S(2)}, u32[]{:S(2)}) collective-permute-start(bf16[3,512,256]{2,1,0:T(8,128)(2,1)S(1)} %collective-permute-done.refs_9_), channel_id=1, source_target_pairs={{0,4},{4,0},{8,12},{12,8},{16,20},{20,16},{24,28},{28,24},{1,5},{5... | collective-permute-start | bytes 2359304 | tf_op jit(solution)/shard_map/ppermute | solution.py:252
  53.2 17.4 %collective-permute-start.8 = (bf16[3,512,256]{2,1,0:T(8,128)(2,1)S(1)}, bf16[3,512,256]{2,1,0:T(8,128)(2,1)S(1)}, u32[]{:S(2)}, u32[]{:S(2)}) collective-permute-start(bf16[3,512,256]{2,1,0:T(8,128)(2,1)S(1)} %collective-permute-done.1.refs_10_), channel_id=1, source_target_pairs={{0,4},{4,0},{8,12},{12,8},{16,20},{20,16},{24,28},{28,24},{1,5},{5... | collective-permute-start | bytes 2359304 | tf_op jit(solution)/shard_map/ppermute | solution.py:252
  72.7 6.0 %collective-permute-start.14 = (bf16[3,512,256]{2,1,0:T(8,128)(2,1)}, bf16[3,512,256]{2,1,0:T(8,128)(2,1)}, u32[]{:S(2)}, u32[]{:S(2)}) collective-permute-start(bf16[3,512,256]{2,1,0:T(8,128)(2,1)} %collective-permute-done.6.refs_15_), channel_id=1, source_target_pairs={{0,4},{4,0},{8,12},{12,8},{16,20},{20,16},{24,28},{28,24},{1,5},{5... | collective-permute-start | bytes 2359304 | tf_op jit(solution)/shard_map/ppermute | solution.py:252
  73.3 22.7 %collective-permute-start.11 = (bf16[3,512,256]{2,1,0:T(8,128)(2,1)}, bf16[3,512,256]{2,1,0:T(8,128)(2,1)S(1)}, u32[]{:S(2)}, u32[]{:S(2)}) collective-permute-start(bf16[3,512,256]{2,1,0:T(8,128)(2,1)} %copy-done.10), channel_id=1, source_target_pairs={{0,3},{1,0},{2,1},{3,2},{4,7},{5,4},{6,5},{7,6},{8,11},{9,8},{10,9... | collective-permute-start | bytes 2359304 | tf_op jit(solution)/shard_map/ppermute | solution.py:341
  77.2 18.7 %collective-permute-start.12 = (bf16[3,256,256]{2,1,0:T(8,128)(2,1)S(1)}, bf16[3,256,256]{2,1,0:T(8,128)(2,1)S(1)}, u32[]{:S(2)}, u32[]{:S(2)}) collective-permute-start(bf16[3,256,256]{2,1,0:T(8,128)(2,1)S(1)} %slice.6), channel_id=1, source_target_pairs={{0,8},{4,12},{8,0},{12,4},{16,24},{20,28},{24,16},{28,20},{1,9},{5... | collective-permute-start | bytes 1179656 | tf_op jit(solution)/shard_map/ppermute | solution.py:252
  78.1 17.9 %collective-permute-start.13 = (bf16[3,256,256]{2,1,0:T(8,128)(2,1)S(1)}, bf16[3,256,256]{2,1,0:T(8,128)(2,1)}, u32[]{:S(2)}, u32[]{:S(2)}) collective-permute-start(bf16[3,256,256]{2,1,0:T(8,128)(2,1)S(1)} %slice.7), channel_id=1, source_target_pairs={{0,16},{4,20},{8,24},{12,28},{16,0},{20,4},{24,8},{28,12},{1,17},{... | collective-permute-start | bytes 1179656 | tf_op jit(solution)/shard_map/ppermute | solution.py:252
  78.7 17.3 %collective-permute-start.15 = (bf16[3,512,256]{2,1,0:T(8,128)(2,1)S(1)}, bf16[3,512,256]{2,1,0:T(8,128)(2,1)S(1)}, u32[]{:S(2)}, u32[]{:S(2)}) collective-permute-start(bf16[3,512,256]{2,1,0:T(8,128)(2,1)S(1)} %collective-permute-done.4.refs_11_), channel_id=1, source_target_pairs={{0,4},{4,0},{8,12},{12,8},{16,20},{20,16},{24,28},{28,24},{1,5},{5... | collective-permute-start | bytes 2359304 | tf_op jit(solution)/shard_map/ppermute | solution.py:252
  78.7 17.3 %collective-permute-start.16 = (bf16[3,512,256]{2,1,0:T(8,128)(2,1)S(1)}, bf16[3,512,256]{2,1,0:T(8,128)(2,1)S(1)}, u32[]{:S(2)}, u32[]{:S(2)}) collective-permute-start(bf16[3,512,256]{2,1,0:T(8,128)(2,1)S(1)} %collective-permute-done.5.refs_12_), channel_id=1, source_target_pairs={{0,4},{4,0},{8,12},{12,8},{16,20},{20,16},{24,28},{28,24},{1,5},{5... | collective-permute-start | bytes 2359304 | tf_op jit(solution)/shard_map/ppermute | solution.py:252
  96.1 3.4 %collective-permute-start.17 = (bf16[3,256,256]{2,1,0:T(8,128)(2,1)S(1)}, bf16[3,256,256]{2,1,0:T(8,128)(2,1)S(1)}, u32[]{:S(2)}, u32[]{:S(2)}) collective-permute-start(bf16[3,256,256]{2,1,0:T(8,128)(2,1)S(1)} %collective-permute-done.12.refs_15_), channel_id=1, source_target_pairs={{0,4},{4,0},{8,12},{12,8},{16,20},{20,16},{24,28},{28,24},{1,5},{5... | collective-permute-start | bytes 1179656 | tf_op jit(solution)/shard_map/ppermute | solution.py:252
  96.6 21.0 %collective-permute-start.20 = (bf16[3,512,256]{2,1,0:T(8,128)(2,1)S(1)}, bf16[3,512,256]{2,1,0:T(8,128)(2,1)S(1)}, u32[]{:S(2)}, u32[]{:S(2)}) collective-permute-start(bf16[3,512,256]{2,1,0:T(8,128)(2,1)S(1)} %collective-permute-done.11.refs_6_.refs_5_), channel_id=1, source_target_pairs={{0,8},{4,12},{8,0},{12,4},{16,24},{20,28},{24,16},{28,20},{1,9},{5... | collective-permute-start | bytes 2359304 | tf_op jit(solution)/shard_map/ppermute | solution.py:252
  96.8 20.9 %collective-permute-start.21 = (bf16[3,512,256]{2,1,0:T(8,128)(2,1)S(1)}, bf16[3,512,256]{2,1,0:T(8,128)(2,1)S(1)}, u32[]{:S(2)}, u32[]{:S(2)}) collective-permute-start(bf16[3,512,256]{2,1,0:T(8,128)(2,1)S(1)} %collective-permute-done.11.refs_6_.refs_5_), channel_id=1, source_target_pairs={{0,16},{4,20},{8,24},{12,28},{16,0},{20,4},{24,8},{28,12},{1,17},{... | collective-permute-start | bytes 2359304 | tf_op jit(solution)/shard_map/ppermute | solution.py:252
  99.5 21.5 %collective-permute-start.22 = (bf16[3,512,256]{2,1,0:T(8,128)(2,1)S(1)}, bf16[3,512,256]{2,1,0:T(8,128)(2,1)}, u32[]{:S(2)}, u32[]{:S(2)}) collective-permute-start(bf16[3,512,256]{2,1,0:T(8,128)(2,1)S(1)} %get-tuple-element.113), channel_id=1, source_target_pairs={{3,0},{0,1},{1,2},{2,3},{7,4},{4,5},{5,6},{6,7},{11,8},{8,9},{9,10... | collective-permute-start | bytes 2359304 | tf_op jit(solution)/shard_map/ppermute | solution.py:355
  99.5 22.6 %collective-permute-start.19 = (bf16[3,512,256]{2,1,0:T(8,128)(2,1)S(1)}, bf16[3,512,256]{2,1,0:T(8,128)(2,1)}, u32[]{:S(2)}, u32[]{:S(2)}) collective-permute-start(bf16[3,512,256]{2,1,0:T(8,128)(2,1)S(1)} %collective-permute-done.11.refs_6_.refs_5_), channel_id=1, source_target_pairs={{0,4},{4,0},{8,12},{12,8},{16,20},{20,16},{24,28},{28,24},{1,5},{5... | collective-permute-start | bytes 2359304 | tf_op jit(solution)/shard_map/ppermute | solution.py:252
  121.0 4.3 %collective-permute-start.24 = (bf16[3,512,256]{2,1,0:T(8,128)(2,1)S(1)}, bf16[3,512,256]{2,1,0:T(8,128)(2,1)}, u32[]{:S(2)}, u32[]{:S(2)}) collective-permute-start(bf16[3,512,256]{2,1,0:T(8,128)(2,1)S(1)} %collective-permute-done.21.refs_9_.refs_8_), channel_id=1, source_target_pairs={{0,4},{4,0},{8,12},{12,8},{16,20},{20,16},{24,28},{28,24},{1,5},{5... | collective-permute-start | bytes 2359304 | tf_op jit(solution)/shard_map/ppermute | solution.py:252
  121.5 4.4 %collective-permute-start.25 = (bf16[3,512,256]{2,1,0:T(8,128)(2,1)}, bf16[3,512,256]{2,1,0:T(8,128)(2,1)}, u32[]{:S(2)}, u32[]{:S(2)}) collective-permute-start(bf16[3,512,256]{2,1,0:T(8,128)(2,1)} %collective-permute-done.22.refs_10_.refs_9_), channel_id=1, source_target_pairs={{0,4},{4,0},{8,12},{12,8},{16,20},{20,16},{24,28},{28,24},{1,5},{5... | collective-permute-start | bytes 2359304 | tf_op jit(solution)/shard_map/ppermute | solution.py:252
  134.6 32.5 %all-to-all-start = ((bf16[8,2,256,256]{3,2,1,0:T(8,128)(2,1)}), bf16[8,2,256,256]{3,2,1,0:T(8,128)(2,1)S(1)}, u32[]{:S(2)}, u32[]{:S(2)}) async-start(bf16[8,2,256,256]{3,2,1,0:T(8,128)(2,1)} %bitcast.17), calls=%async_computation | async-start | bytes 4194304 | tf_op jit(solution)/shard_map/all_to_all | solution.py:363
  (26 other events, 330.7 us)

commit v9 on v8

--- a/solution.py
+++ b/solution.py
@@ -11,55 +11,65 @@
 VMEM = pl.BlockSpec(memory_space=pltpu.VMEM)
 HBM = pl.BlockSpec(memory_space=pltpu.HBM)
 MIB = 1 << 20
-STEP_BITS, SOURCE_BITS, LAG_BITS = 4, 8, 8
-FIELDS = (STEP_BITS, SOURCE_BITS, LAG_BITS)
-CHUNK = 4
-
-
-def pack(step, source, lag, place):
+HALF_BITS, SOURCE_BITS, CLASS_BITS, LAG_BITS = 1, 8, 4, 8
+FIELDS = (HALF_BITS, SOURCE_BITS, CLASS_BITS, LAG_BITS)
+UNROLL = 2
+
+
+def pack(half, source, klass, lag, place):
     packed = place
-    for value, bits in ((lag, LAG_BITS), (source, SOURCE_BITS), (step, STEP_BITS)):
+    for value, bits in ((lag, LAG_BITS), (klass, CLASS_BITS), (source, SOURCE_BITS), (half, HALF_BITS)):
         packed = (packed << bits) | value
     return packed
 
 
-def list_tasks(base, span, total, steps, pair, tasks, counts):
+def list_task(base, span, total, steps, phased, pair, tasks, counts):
     source, klass, lag, place = pair
-    touched = None
-    for step in range(steps // CHUNK):
-        start = lax.rem(lag + step * CHUNK - base + total, total)
-        first = jnp.where(start < span, start, start - total) + CHUNK - 1
-        active = first >= 0
-        at = counts[klass]
-        tasks[klass, at] = pack(step, source, jnp.maximum(first, 0), place)
-        counts[klass] = at + jnp.where(active, 1, 0)
-        touched = active if touched is None else touched | active
-    return touched
-
-
-def run_tasks(number, klass, tasks, hist, table, acc):
+    half = steps // 2
+    start = lax.rem(lag - base + total, total)
+    first = jnp.where(start < span, start, start - total)
+    whole = (first > -half) & (first < span - half)
+    lower = (first >= span - half) & (first < span)
+    upper_half = (first > -steps) & (first <= -half)
+    row = jnp.maximum(first + half - 1, 0)
+    number = 2 * klass if phased else 0
+    at = counts[number]
+    tasks[number, at] = pack(0, source, klass, row, place)
+    counts[number] = at + jnp.where(whole, 1, 0)
+    at = counts[number + 1]
+    second = jnp.where(upper_half, 1, 0)
+    row = jnp.maximum(first + half - 1 + half * second, 0)
+    tasks[number + 1, at] = pack(second, source, klass, row, place)
+    counts[number + 1] = at + jnp.where(lower | upper_half, 1, 0)
+    return whole | lower | upper_half
+
+
+def run_list(number, width, spare, tasks, counts, hist, table, acc):
     panels = table.shape[2]
-    products = []
-    for n in range(number):
-        packed = tasks[n]
-        fields = []
-        for bits in FIELDS:
-            fields.append(packed & ((1 << bits) - 1))
-            packed = packed >> bits
-        step, source, lag = fields
-        columns = pl.multiple_of(step * (CHUNK * panels), CHUNK * panels)
-        rows = pl.multiple_of(lag * panels, panels)
-        products.append((packed, jnp.dot(
-            hist[source, :, pl.ds(columns, CHUNK * panels)],
-            table[klass, pl.ds(rows, CHUNK * panels), :],
-            preferred_element_type=jnp.float32,
-        )))
-    for place, product in products:
-        acc[place] += product
+    count = counts[number]
+    for n in range(UNROLL - 1):
+        tasks[number, count + n] = pack(0, 0, 0, 0, spare)
+
+    @pl.loop(0, (count + UNROLL - 1) // UNROLL)
+    def _(j):
+        for n in range(UNROLL):
+            packed = tasks[number, j * UNROLL + n]
+            fields = []
+            for bits in FIELDS:
+                fields.append(packed & ((1 << bits) - 1))
+                packed = packed >> bits
+            half, source, klass, lag = fields
+            columns = pl.multiple_of(half * (width * panels), width * panels)
+            rows = pl.multiple_of(lag * panels, panels)
+            acc[packed] += jnp.dot(
+                hist[source, :, pl.ds(columns, width * panels)],
+                table[klass, pl.ds(rows, width * panels), :],
+                preferred_element_type=jnp.float32,
+            )
 
 
 def window_kernel(config, *refs):
-    served, local, begun, narrow, places, total, height, owned, unroll = config
+    served, local, begun, narrow, places, total, rows, height, owned = config
     refs = list(refs)
     where = refs.pop(0)
     served_refs = [refs.pop(0) for _ in range(3 if served else 0)]
@@ -71,26 +81,27 @@
     table, hist, acc, tasks, counts, used, sems, ends, served_sems = refs
     base, group = where[0], where[1]
     classes, _, panels = table.shape
-    margin = (CHUNK - 1) * panels
+    steps = hist.shape[2] // panels
+    margin = (steps // 2 - 1) * panels
     span = (table.shape[1] - 2 * margin) // panels
-    steps = hist.shape[2] // panels
+    phased = bool(local)
 
     pltpu.make_async_copy(hist_ref, hist, ends.at[0]).start()
     near = acc.at[pl.ds(served, owned)] if local else None
     if local and begun:
         pltpu.make_async_copy(before[-1], near, ends.at[1]).start()
     for k in range(classes):
-        for (mask, first), piece in zip(places, pieces):
-            rows = piece.shape[1]
-            start = pl.multiple_of(margin + (group ^ mask) * height + first, 16)
+        for (slot, mask, first), piece in zip(places, pieces):
+            start = pl.multiple_of(margin + slot * rows + (group ^ mask) * height + first, 16)
             pltpu.make_async_copy(
-                piece.at[k], table.at[k, pl.ds(start, rows), :], sems.at[k]
+                piece.at[k], table.at[k, pl.ds(start, piece.shape[1]), :], sems.at[k]
             ).start()
     if not begun:
         acc[...] = jnp.zeros_like(acc)
     ends_of_table = jnp.zeros((margin, panels), table.dtype)
     for k in range(classes):
-        counts[k] = 0
+        counts[2 * k] = 0
+        counts[2 * k + 1] = 0
         table[k, pl.ds(0, margin), :] = ends_of_table
         table[k, pl.ds(margin + span * panels, margin), :] = ends_of_table
 
@@ -106,9 +117,8 @@
             for c in range(slots):
                 source, lag, klass = (ref[c, i] for ref in served_refs)
                 place = i * slots + c
-                touched = list_tasks(
-                    base, span, total, steps, (source, klass, lag, place), tasks, counts
-                )
+                pair = (source, klass, lag, place)
+                touched = list_task(base, span, total, steps, phased, pair, tasks, counts)
                 needed = touched | narrow
                 used[place] = jnp.where(touched, 1, 0)
                 if begun:
@@ -120,9 +130,8 @@
         @pl.loop(0, local_refs[0].shape[0])
         def _(i):
             source, lag, klass, target = (ref[i] for ref in local_refs)
-            list_tasks(
-                base, span, total, steps, (source, klass, lag, target + served), tasks, counts
-            )
+            pair = (source, klass, lag, target + served)
+            list_task(base, span, total, steps, phased, pair, tasks, counts)
 
     pltpu.make_async_copy(hist_ref, hist, ends.at[0]).wait()
     if local and begun:
@@ -136,18 +145,23 @@
 
     spare = acc.shape[0] - 1
 
-    @pl.loop(0, classes)
-    def _(k):
-        count = counts[k]
-        for n in range(unroll - 1):
-            tasks[k, count + n] = pack(0, 0, 0, spare)
+    def wait_class(k):
         inner = table.at[k, pl.ds(margin, span * panels), :]
         pltpu.make_async_copy(inner, inner, sems.at[k]).wait()
 
-        @pl.loop(0, (count + unroll - 1) // unroll)
-        def _(j):
-            first = j * unroll
-            run_tasks(unroll, k, [tasks[k, first + n] for n in range(unroll)], hist, table, acc)
+    def run_lists(number):
+        run_list(number, steps, spare, tasks, counts, hist, table, acc)
+        run_list(number + 1, steps // 2, spare, tasks, counts, hist, table, acc)
+
+    if phased:
+        @pl.loop(0, classes)
+        def _(k):
+            wait_class(k)
+            run_lists(2 * k)
+    else:
+        for k in range(classes):
+            wait_class(k)
+        run_lists(0)
 
     if narrow:
         outs[0][...] = acc[pl.ds(0, served)].astype(outs[0].dtype)
@@ -166,44 +180,45 @@
         pltpu.make_async_copy(near, outs[-1], ends.at[1]).wait()
 
 
-def window_sums(shard, group, served, local, hist_t, pieces, sums, lanes, rows, narrow=False):
+def window_sums(shard, group, served, local, hist_t, shards, sums, lanes, rows, narrow=False):
     owned, excite, depth = hist_t.shape
-    classes, _, panels = pieces[0][2].shape
+    pieces = [(slot, *piece) for slot, found in enumerate(shards) for piece in found]
+    classes, _, panels = pieces[0][3].shape
     places = served[0].size if served else 0
     targets = owned if local else 0
     pairs = places + (local[0].size if local else 0)
     steps = depth // panels
-    height = max(first + value.shape[1] for _, first, value in pieces)
     config = (
         places,
         bool(local),
         sums is not None,
         narrow,
-        tuple(piece[:2] for piece in pieces),
+        tuple(piece[:3] for piece in pieces),
         lanes * rows // panels,
-        height,
+        rows,
+        max(first + value.shape[1] for _, _, first, value in pieces),
         targets,
-        4 if local else 2,
     )
     operands = [jnp.stack([shard * (rows // panels), group]).astype(jnp.int32), *served, *local]
-    wide = [hist_t, *[piece[2] for piece in pieces]]
+    wide = [hist_t, *[piece[3] for piece in pieces]]
     before = list(sums) if sums is not None else []
     outs = [
         jax.ShapeDtypeStruct((n, excite, panels), jnp.bfloat16 if narrow else jnp.float32)
         for n in (places, targets)
         if n
     ]
+    depth_of_table = len(shards) * rows + 2 * (steps // 2 - 1) * panels
     return pl.pallas_call(
         functools.partial(window_kernel, config),
         out_shape=outs,
         in_specs=[SMEM] * len(operands) + [HBM] * (len(wide) + len(before)),
         out_specs=[VMEM if narrow else HBM] * len(outs),
         scratch_shapes=[
-            pltpu.VMEM((classes, rows + 2 * (CHUNK - 1) * panels, panels), jnp.bfloat16),
+            pltpu.VMEM((classes, depth_of_table, panels), jnp.bfloat16),
             pltpu.VMEM(hist_t.shape, hist_t.dtype),
             pltpu.VMEM((places + targets + 1, excite, panels), jnp.float32),
-            pltpu.SMEM((classes, pairs * (steps // CHUNK) + 4), jnp.int32),
-            pltpu.SMEM((classes,), jnp.int32),
+            pltpu.SMEM((2 * classes, pairs + UNROLL), jnp.int32),
+            pltpu.SMEM((2 * classes,), jnp.int32),
             pltpu.SMEM((max(places, 1),), jnp.int32),
             pltpu.SemaphoreType.DMA((classes,)),
             pltpu.SemaphoreType.DMA((2,)),
@@ -215,7 +230,7 @@
         compiler_params=pltpu.CompilerParams(vmem_limit_bytes=58 * MIB),
         cost_estimate=pl.CostEstimate(
             flops=2 * pairs * panels * depth * excite,
-            bytes_accessed=2 * classes * rows * panels + 2 * hist_t.size,
+            bytes_accessed=2 * classes * len(shards) * rows * panels + 2 * hist_t.size,
             transcendentals=0,
         ),
     )(*operands, *wide, *before)
@@ -296,12 +311,15 @@
     def part(index):
         return lax.dynamic_slice(weights, (0, index * height, 0), (classes, height, panels))
 
-    def add_shard(step, sums):
+    def add_shard(step, sums, served=served, local=local, **options):
         shard = lax.rem(lane + step, lanes)
-        return window_sums(shard, group, served, local, hist_t, rounds[step - 1], sums, lanes, rows)
+        shards = rounds[step - 1 : step] if served else rounds[step - 1 :]
+        return window_sums(
+            shard, group, served, local, hist_t, shards, sums, lanes, rows, **options
+        )
 
     sums = window_sums(
-        lane, group * 0, served, local, hist_t, [(0, 0, weights)], None, lanes, rows
+        lane, group * 0, served, local, hist_t, [[(0, 0, weights)]], None, lanes, rows
     )
     own = part(group)
     corner = part(group ^ 6)
@@ -353,13 +371,11 @@
         if step < lanes - 2:
             across, along, own = tie(across, along, own)
     diagonal = lax.ppermute(corner, "lag", [(j, i) for i, j in ring])
-    sums = add_shard(lanes - 2, sums)
-    across, along, diagonal, sums = tie(across, along, diagonal, sums)
+    served_sums, near = sums
+    served_sums = add_shard(lanes - 2, [served_sums], local=())[0]
+    across, along, diagonal, served_sums = tie(across, along, diagonal, served_sums)
     rounds.append(held + with_other_core(across + along + corners(diagonal), peers))
-    last = lax.rem(lane + lanes - 1, lanes)
-    contribution = window_sums(
-        last, group, served, (), hist_t, rounds[-1], sums[:1], lanes, rows, narrow=True
-    )[0]
+    contribution = add_shard(lanes - 1, [served_sums], local=(), narrow=True)[0]
     recv = lax.all_to_all(
         contribution.reshape(peers, slots, *contribution.shape[1:]),
         "grp",
@@ -367,7 +383,7 @@
         concat_axis=0,
         tiled=True,
     )
-    near = window_sums(last, group, (), local, hist_t, rounds[-1], sums[1:], lanes, rows)[0]
+    near = add_shard(lanes - 2, [near], served=())[0]
     return update(recv_target.T, near, recv, inverse_blocks, incident)
 
 

time: 170 us -> 174 us (1.024)
  waiting for transfers between devices: 56.6 us -> 60.6 us
  Pallas kernels: 70.7 us -> 68.1 us
  local copies, waits for them, and re-layouts: 11.7 us -> 13.5 us
    ppermute x21, waiting for transfers between devices: 36.5 us -> 48.5 us  [swap(): return lax.ppermute(value, 'grp', [(i, i ^ bit) for i in range(peers)])]
    all_to_all x1, waiting for transfers between devices: 15.2 us -> 8.63 us  [per_device(): lax.all_to_all(contribution.reshape(peers, slots, *contribution.shape[1:]...]
    ppermute x21, starting transfers between devices: 11.3 us -> 14.6 us  [swap(): return lax.ppermute(value, 'grp', [(i, i ^ bit) for i in range(peers)])]
    pallas_call x5, Pallas kernels: 68.4 us -> 65.7 us  [window_sums(): pl.pallas_call(functools.partial(window_kernel, config), out_shape=outs,...]
    all_to_all x1, starting transfers between devices: 5.81 us -> 3.61 us  [per_device(): lax.all_to_all(contribution.reshape(peers, slots, *contribution.shape[1:]...]
    unnamed x47 -> x45, local copies, waits for them, and re-layouts: 10.2 us -> 11.1 us
  transfers between devices with their start and end apart: 27 -> 27, of which waited for: 10 -> 14; matrix products, arithmetic and copies ran while one was open for 5% -> 5% of each run, Pallas kernels for 35% -> 32%
where the time goes in v9:
time: 174 us
  Pallas kernels  68.1 us (39%)
  waiting for transfers between devices  60.6 us (35%)
  starting transfers between devices  29.4 us (17%)
  local copies, waits for them, and re-layouts  13.5 us (8%)
  other arithmetic  2.59 us (1%)
    pallas_call x5, Pallas kernels, window_sums(): pl.pallas_call(functools.partial(window_kernel, config), out_shape=outs,...  65.7 us
    ppermute x21, waiting for transfers between devices, swap(): return lax.ppermute(value, 'grp', [(i, i ^ bit) for i in range(peers)])  48.5 us
    ppermute x21, starting transfers between devices, swap(): return lax.ppermute(value, 'grp', [(i, i ^ bit) for i in range(peers)])  14.6 us
    unnamed x45, local copies, waits for them, and re-layouts  11.1 us
    ppermute x3, starting transfers between devices, per_device(): own = lax.ppermute(own, 'lag', ring)  9.04 us
    all_to_all x1, waiting for transfers between devices, per_device(): lax.all_to_all(contribution.reshape(peers, slots, *contribution.shape[1:]...  8.63 us
    all_to_all x1, starting transfers between devices, per_device(): lax.all_to_all(contribution.reshape(peers, slots, *contribution.shape[1:]...  3.61 us
  transfers between devices with their start and end apart: 27, of which 14 were waited for; matrix products, arithmetic and copies ran while one was open for 5% of the time, Pallas kernels for 32%

profile of v9, /device:TPU:0, one launch (start us, length us, event | category | flops | bytes accessed | tf_op | source)
XLA Modules:
  0.0 174.4 jit_solution(14022894012537907533)
XLA Ops:
  0.0 2.3 %constant_dynamic-slice_fusion = (bf16[3,512,256]{2,1,0:T(8,128)(2,1)}, bf16[3,512,256]{2,1,0:T(8,128)(2,1)S(1)}) fusion(bf16[3,4096,256]{2,1,0:T(8,128)(2,1)} %refs_9_.1, s32[]{:T(128)S(6)} %select_n.7, s32[]{:T(128)S(6)} %select_n.6), kind=kLoop, calls=%fused_computation.4 | loop fusion | bytes 3145736 | tf_op jit(solution)/shard_map/dynamic_slice | solution.py:312
  2.3 5.0 %collective-permute-start = (bf16[3,512,256]{2,1,0:T(8,128)(2,1)S(1)}, bf16[3,512,256]{2,1,0:T(8,128)(2,1)S(1)}, u32[]{:S(2)}, u32[]{:S(2)}) collective-permute-start(bf16[3,512,256]{2,1,0:T(8,128)(2,1)S(1)} %get-tuple-element.128), channel_id=1, source_target_pairs={{0,3},{1,0},{2,1},{3,2},{4,7},{5,4},{6,5},{7,6},{8,11},{9,8},{10,9... | collective-permute-start | bytes 2359304 | tf_op jit(solution)/shard_map/ppermute | solution.py:346
  7.4 6.3 %copy.17 = bf16[4,2048,256]{1,2,0:T(8,128)(2,1)} copy(bf16[4,2048,256]{2,1,0:T(8,128)(2,1)} %param.13) | data formatting | bytes 8388608 | tf_op args[1]
  14.4 13.1 %shard_map.118 = (f32[16,256,256]{2,1,0:T(8,128)}, f32[4,256,256]{2,1,0:T(8,128)}) custom-call(s32[2]{0:T(128)} %pad_add_fusion.1.refs_0_, s32[2,8]{1,0:T(2,128)} %bitcast.18, s32[2,8]{1,0:T(2,128)} %bitcast.22, s32[2,8]{1,0:T(2,128)} %bitcast.26, s32[48]{0:T(128)} %refs_1_.1, s32[48]{0:T(128)} %refs_2_.1, s32[48]{0:T(128)} %refs_3_.1, s32[48]{0:T(128)} %refs_4_.5, ...), custom_call_target="tpu_custom_call" | custom-call | flops 17179869184 | bytes 10485760 | tf_op jit(solution)/shard_map/pallas_call | solution.py:211
  27.8 3.7 %collective-permute-start.2 = (bf16[3,512,256]{2,1,0:T(8,128)(2,1)S(1)}, bf16[3,512,256]{2,1,0:T(8,128)(2,1)S(1)}, u32[]{:S(2)}, u32[]{:S(2)}) collective-permute-start(bf16[3,512,256]{2,1,0:T(8,128)(2,1)S(1)} %collective-permute-done.refs_9_), channel_id=1, source_target_pairs={{0,16},{4,20},{8,24},{12,28},{16,0},{20,4},{24,8},{28,12},{1,17},{... | collective-permute-start | bytes 2359304 | tf_op jit(solution)/shard_map/ppermute | solution.py:267
  32.2 15.6 %collective-permute-done.1.refs_10_ = bf16[3,512,256]{2,1,0:T(8,128)(2,1)S(1)} collective-permute-done((bf16[3,512,256]{2,1,0:T(8,128)(2,1)S(1)}, bf16[3,512,256]{2,1,0:T(8,128)(2,1)S(1)}, u32[]{:S(2)}, u32[]{:S(2)}) %collective-permute-start.1) | collective-permute-done | bytes 786464 | tf_op jit(solution)/shard_map/ppermute | solution.py:267
  47.9 1.6 collective-permute-done.2.refs_11_
  51.7 2.1 %collective-permute-start.6 = (bf16[3,512,256]{2,1,0:T(8,128)(2,1)}, bf16[3,512,256]{2,1,0:T(8,128)(2,1)}, u32[]{:S(2)}, u32[]{:S(2)}) collective-permute-start(bf16[3,512,256]{2,1,0:T(8,128)(2,1)} %get-tuple-element.120), channel_id=1, source_target_pairs={{0,3},{1,0},{2,1},{3,2},{4,7},{5,4},{6,5},{7,6},{8,11},{9,8},{10,9... | collective-permute-start | bytes 2359304 | tf_op jit(solution)/shard_map/ppermute | solution.py:353
  54.3 16.4 %collective-permute-done.4.refs_7_.refs_8_ = bf16[3,512,256]{2,1,0:T(8,128)(2,1)S(1)} collective-permute-done((bf16[3,512,256]{2,1,0:T(8,128)(2,1)S(1)}, bf16[3,512,256]{2,1,0:T(8,128)(2,1)S(1)}, u32[]{:S(2)}, u32[]{:S(2)}) %collective-permute-start.4) | collective-permute-done | bytes 786464 | tf_op jit(solution)/shard_map/ppermute | solution.py:267
  71.4 1.6 collective-permute-done.9.refs_14_
  74.7 3.3 %collective-permute-start.11 = (bf16[3,512,256]{2,1,0:T(8,128)(2,1)S(1)}, bf16[3,512,256]{2,1,0:T(8,128)(2,1)}, u32[]{:S(2)}, u32[]{:S(2)}) collective-permute-start(bf16[3,512,256]{2,1,0:T(8,128)(2,1)S(1)} %collective-permute-done.3.refs_5_.refs_6_), channel_id=1, source_target_pairs={{0,3},{1,0},{2,1},{3,2},{4,7},{5,4},{6,5},{7,6},{8,11},{9,8},{10,9... | collective-permute-start | bytes 2359304 | tf_op jit(solution)/shard_map/ppermute | solution.py:359
  78.0 1.7 collective-permute-start.12
  79.8 1.5 collective-permute-start.13
  81.8 15.9 %shard_map.119 = (f32[16,256,256]{2,1,0:T(8,128)}, f32[4,256,256]{2,1,0:T(8,128)}) custom-call(s32[2]{0:T(128)} %pad_add_fusion.2.refs_0_, s32[2,8]{1,0:T(2,128)} %bitcast.19, s32[2,8]{1,0:T(2,128)} %bitcast.23, s32[2,8]{1,0:T(2,128)} %bitcast.27, s32[48]{0:T(128)} %refs_1_.1, s32[48]{0:T(128)} %refs_2_.1, ...), custom_call_target="tpu_custom_call", output_to_operand_aliasing={{0}: (17, {}), {1}: (18, {})} | custom-call | flops 17179869184 | bytes 10485760 | tf_op jit(solution)/shard_map/pallas_call | solution.py:211
  100.1 4.2 %collective-permute-start.20 = (bf16[3,512,256]{2,1,0:T(8,128)(2,1)}, bf16[3,512,256]{2,1,0:T(8,128)(2,1)S(1)}, u32[]{:S(2)}, u32[]{:S(2)}) collective-permute-start(bf16[3,512,256]{2,1,0:T(8,128)(2,1)} %collective-permute-done.11.refs_16_.refs_5_), channel_id=1, source_target_pairs={{0,8},{4,12},{8,0},{12,4},{16,24},{20,28},{24,16},{28,20},{1,9},{5... | collective-permute-start | bytes 2359304 | tf_op jit(solution)/shard_map/ppermute | solution.py:267
  105.7 8.5 %shard_map.120.refs_13_ = f32[16,256,256]{2,1,0:T(8,128)} custom-call(s32[2]{0:T(128)} %pad_add_fusion.refs_0_, s32[2,8]{1,0:T(2,128)} %bitcast.20, s32[2,8]{1,0:T(2,128)} %bitcast.24, s32[2,8]{1,0:T(2,128)} %bitcast.28, bf16[4,256,2048]{2,1,0:T(8,128)(2,1)} %bitcast.14, bf16[3,512,256]{2,1,0:T(8,128)(2,1)} %copy-done.6, ...), custom_call_target="tpu_custom_call", output_to_operand_aliasing={{}: (15, {})} | custom-call | flops 4294967296 | bytes 10485760 | tf_op jit(solution)/shard_map/pallas_call | solution.py:211
  114.1 8.0 %collective-permute-done.20.refs_18_.refs_7_ = bf16[3,512,256]{2,1,0:T(8,128)(2,1)S(1)} collective-permute-done((bf16[3,512,256]{2,1,0:T(8,128)(2,1)}, bf16[3,512,256]{2,1,0:T(8,128)(2,1)S(1)}, u32[]{:S(2)}, u32[]{:S(2)}) %collective-permute-start.20) | collective-permute-done | bytes 786464 | tf_op jit(solution)/shard_map/ppermute | solution.py:267
  122.2 1.5 collective-permute-done.21.refs_19_.refs_8_
  123.6 1.8 %collective-permute-done.22.refs_20_.refs_9_ = bf16[3,512,256]{2,1,0:T(8,128)(2,1)S(1)} collective-permute-done((bf16[3,512,256]{2,1,0:T(8,128)(2,1)}, bf16[3,512,256]{2,1,0:T(8,128)(2,1)S(1)}, u32[]{:S(2)}, u32[]{:S(2)}) %collective-permute-start.22) | collective-permute-done | bytes 786464 | tf_op jit(solution)/shard_map/ppermute | solution.py:373
  130.1 10.4 %shard_map.122 = bf16[16,256,256]{2,1,0:T(8,128)(2,1)} custom-call(s32[2]{0:T(128)} %pad_add_fusion.3.refs_0_, s32[2,8]{1,0:T(2,128)} %bitcast.21, s32[2,8]{1,0:T(2,128)} %bitcast.25, s32[2,8]{1,0:T(2,128)} %bitcast.29, bf16[4,256,2048]{2,1,0:T(8,128)(2,1)} %bitcast.15, bf16[3,512,256]{2,1,0:T(8,128)(2,1)} %collective-permute-done.11.refs_16_.refs_5_, ...), custom_call_target="tpu_custom_call" | custom-call | flops 4294967296 | bytes 10485760 | tf_op jit(solution)/shard_map/pallas_call | solution.py:211
  140.5 3.6 %all-to-all-start = ((bf16[8,2,256,256]{3,2,1,0:T(8,128)(2,1)}), bf16[8,2,256,256]{3,2,1,0:T(8,128)(2,1)S(1)}, u32[]{:S(2)}, u32[]{:S(2)}) async-start(bf16[8,2,256,256]{3,2,1,0:T(8,128)(2,1)} %bitcast.17), calls=%async_computation | async-start | bytes 4194304 | tf_op jit(solution)/shard_map/all_to_all | solution.py:379
  144.2 17.9 %shard_map.121.near_ref = f32[4,256,256]{2,1,0:T(8,128)} custom-call(s32[2]{0:T(128)} %pad_add_fusion.refs_0_, s32[48]{0:T(128)} %refs_1_.1, s32[48]{0:T(128)} %refs_2_.1, s32[48]{0:T(128)} %refs_3_.1, s32[48]{0:T(128)} %refs_4_.5, bf16[4,256,2048]{2,1,0:T(8,128)(2,1)} %bitcast.16, bf16[3,512,256]{2,1,0:T(8,128)(2,1)} %copy-done.6, ...), custom_call_target="tpu_custom_call", output_to_operand_aliasing={{}: (24, {})} | custom-call | flops 12884901888 | bytes 16777216 | tf_op jit(solution)/shard_map/pallas_call | solution.py:211
  162.1 8.6 %all-to-all-done.recv_ref = bf16[8,2,256,256]{3,2,1,0:T(8,128)(2,1)S(1)} async-done(((bf16[8,2,256,256]{3,2,1,0:T(8,128)(2,1)}), bf16[8,2,256,256]{3,2,1,0:T(8,128)(2,1)S(1)}, u32[]{:S(2)}, u32[]{:S(2)}) %all-to-all-start) | async-done | bytes 2097184 | tf_op jit(solution)/shard_map/all_to_all | solution.py:379
  172.0 2.4 %shard_map.123 = bf16[4,256,256]{2,1,0:T(8,128)(2,1)} custom-call(s32[2,8]{1,0:T(2,128)S(1)} %bitcast.11, f32[4,256,256]{2,1,0:T(8,128)S(1)} %copy-done, bf16[8,2,256,256]{3,2,1,0:T(8,128)(2,1)S(1)} %all-to-all-done.recv_ref, bf16[4,256,256]{2,1,0:T(8,128)(2,1)S(1)} %copy-done.1, bf16[4,256,256]{2,1,0:T(8,128)(2,1)S(1)} %copy-done.2), custom_call_target="tpu_custom_call" | custom-call | tf_op jit(solution)/shard_map/pallas_call | solution.py:256
  (88 shorter events, 17.0 us)
Async XLA Ops:
  2.3 25.1 %collective-permute-start = (bf16[3,512,256]{2,1,0:T(8,128)(2,1)S(1)}, bf16[3,512,256]{2,1,0:T(8,128)(2,1)S(1)}, u32[]{:S(2)}, u32[]{:S(2)}) collective-permute-start(bf16[3,512,256]{2,1,0:T(8,128)(2,1)S(1)} %get-tuple-element.128), channel_id=1, source_target_pairs={{0,3},{1,0},{2,1},{3,2},{4,7},{5,4},{6,5},{7,6},{8,11},{9,8},{10,9... | collective-permute-start | bytes 2359304 | tf_op jit(solution)/shard_map/ppermute | solution.py:346
  27.5 20.4 %collective-permute-start.1 = (bf16[3,512,256]{2,1,0:T(8,128)(2,1)S(1)}, bf16[3,512,256]{2,1,0:T(8,128)(2,1)S(1)}, u32[]{:S(2)}, u32[]{:S(2)}) collective-permute-start(bf16[3,512,256]{2,1,0:T(8,128)(2,1)S(1)} %collective-permute-done.refs_9_), channel_id=1, source_target_pairs={{0,8},{4,12},{8,0},{12,4},{16,24},{20,28},{24,16},{28,20},{1,9},{5... | collective-permute-start | bytes 2359304 | tf_op jit(solution)/shard_map/ppermute | solution.py:267
  27.8 21.7 %collective-permute-start.2 = (bf16[3,512,256]{2,1,0:T(8,128)(2,1)S(1)}, bf16[3,512,256]{2,1,0:T(8,128)(2,1)S(1)}, u32[]{:S(2)}, u32[]{:S(2)}) collective-permute-start(bf16[3,512,256]{2,1,0:T(8,128)(2,1)S(1)} %collective-permute-done.refs_9_), channel_id=1, source_target_pairs={{0,16},{4,20},{8,24},{12,28},{16,0},{20,4},{24,8},{28,12},{1,17},{... | collective-permute-start | bytes 2359304 | tf_op jit(solution)/shard_map/ppermute | solution.py:267
  31.5 19.2 %collective-permute-start.3 = (bf16[3,512,256]{2,1,0:T(8,128)(2,1)S(1)}, bf16[3,512,256]{2,1,0:T(8,128)(2,1)S(1)}, u32[]{:S(2)}, u32[]{:S(2)}) collective-permute-start(bf16[3,512,256]{2,1,0:T(8,128)(2,1)S(1)} %collective-permute-done.refs_9_), channel_id=1, source_target_pairs={{0,3},{1,0},{2,1},{3,2},{4,7},{5,4},{6,5},{7,6},{8,11},{9,8},{10,9... | collective-permute-start | bytes 2359304 | tf_op jit(solution)/shard_map/ppermute | solution.py:349
  50.7 20.0 %collective-permute-start.4 = (bf16[3,512,256]{2,1,0:T(8,128)(2,1)S(1)}, bf16[3,512,256]{2,1,0:T(8,128)(2,1)S(1)}, u32[]{:S(2)}, u32[]{:S(2)}) collective-permute-start(bf16[3,512,256]{2,1,0:T(8,128)(2,1)S(1)} %collective-permute-done.3.refs_5_.refs_6_), channel_id=1, source_target_pairs={{0,8},{4,12},{8,0},{12,4},{16,24},{20,28},{24,16},{28,20},{1,9},{5... | collective-permute-start | bytes 2359304 | tf_op jit(solution)/shard_map/ppermute | solution.py:267
  51.3 19.6 %collective-permute-start.5 = (bf16[3,512,256]{2,1,0:T(8,128)(2,1)S(1)}, bf16[3,512,256]{2,1,0:T(8,128)(2,1)S(1)}, u32[]{:S(2)}, u32[]{:S(2)}) collective-permute-start(bf16[3,512,256]{2,1,0:T(8,128)(2,1)S(1)} %collective-permute-done.3.refs_5_.refs_6_), channel_id=1, source_target_pairs={{0,16},{4,20},{8,24},{12,28},{16,0},{20,4},{24,8},{28,12},{1,17},{... | collective-permute-start | bytes 2359304 | tf_op jit(solution)/shard_map/ppermute | solution.py:267
  51.7 19.6 %collective-permute-start.6 = (bf16[3,512,256]{2,1,0:T(8,128)(2,1)}, bf16[3,512,256]{2,1,0:T(8,128)(2,1)}, u32[]{:S(2)}, u32[]{:S(2)}) collective-permute-start(bf16[3,512,256]{2,1,0:T(8,128)(2,1)} %get-tuple-element.120), channel_id=1, source_target_pairs={{0,3},{1,0},{2,1},{3,2},{4,7},{5,4},{6,5},{7,6},{8,11},{9,8},{10,9... | collective-permute-start | bytes 2359304 | tf_op jit(solution)/shard_map/ppermute | solution.py:353
  53.8 17.6 %collective-permute-start.7 = (bf16[3,512,256]{2,1,0:T(8,128)(2,1)}, bf16[3,512,256]{2,1,0:T(8,128)(2,1)S(1)}, u32[]{:S(2)}, u32[]{:S(2)}) collective-permute-start(bf16[3,512,256]{2,1,0:T(8,128)(2,1)} %copy-done.16), channel_id=1, source_target_pairs={{0,4},{4,0},{8,12},{12,8},{16,20},{20,16},{24,28},{28,24},{1,5},{5... | collective-permute-start | bytes 2359304 | tf_op jit(solution)/shard_map/ppermute | solution.py:267
  53.8 17.6 %collective-permute-start.8 = (bf16[3,512,256]{2,1,0:T(8,128)(2,1)S(1)}, bf16[3,512,256]{2,1,0:T(8,128)(2,1)S(1)}, u32[]{:S(2)}, u32[]{:S(2)}) collective-permute-start(bf16[3,512,256]{2,1,0:T(8,128)(2,1)S(1)} %collective-permute-done.1.refs_10_), channel_id=1, source_target_pairs={{0,4},{4,0},{8,12},{12,8},{16,20},{20,16},{24,28},{28,24},{1,5},{5... | collective-permute-start | bytes 2359304 | tf_op jit(solution)/shard_map/ppermute | solution.py:267
  73.9 7.4 %collective-permute-start.14 = (bf16[3,512,256]{2,1,0:T(8,128)(2,1)}, bf16[3,512,256]{2,1,0:T(8,128)(2,1)}, u32[]{:S(2)}, u32[]{:S(2)}) collective-permute-start(bf16[3,512,256]{2,1,0:T(8,128)(2,1)} %collective-permute-done.6.refs_15_), channel_id=1, source_target_pairs={{0,4},{4,0},{8,12},{12,8},{16,20},{20,16},{24,28},{28,24},{1,5},{5... | collective-permute-start | bytes 2359304 | tf_op jit(solution)/shard_map/ppermute | solution.py:267
  74.7 23.1 %collective-permute-start.11 = (bf16[3,512,256]{2,1,0:T(8,128)(2,1)S(1)}, bf16[3,512,256]{2,1,0:T(8,128)(2,1)}, u32[]{:S(2)}, u32[]{:S(2)}) collective-permute-start(bf16[3,512,256]{2,1,0:T(8,128)(2,1)S(1)} %collective-permute-done.3.refs_5_.refs_6_), channel_id=1, source_target_pairs={{0,3},{1,0},{2,1},{3,2},{4,7},{5,4},{6,5},{7,6},{8,11},{9,8},{10,9... | collective-permute-start | bytes 2359304 | tf_op jit(solution)/shard_map/ppermute | solution.py:359
  78.0 19.7 %collective-permute-start.12 = (bf16[3,256,256]{2,1,0:T(8,128)(2,1)S(1)}, bf16[3,256,256]{2,1,0:T(8,128)(2,1)S(1)}, u32[]{:S(2)}, u32[]{:S(2)}) collective-permute-start(bf16[3,256,256]{2,1,0:T(8,128)(2,1)S(1)} %slice.6), channel_id=1, source_target_pairs={{0,8},{4,12},{8,0},{12,4},{16,24},{20,28},{24,16},{28,20},{1,9},{5... | collective-permute-start | bytes 1179656 | tf_op jit(solution)/shard_map/ppermute | solution.py:267
  79.8 18.0 %collective-permute-start.13 = (bf16[3,256,256]{2,1,0:T(8,128)(2,1)S(1)}, bf16[3,256,256]{2,1,0:T(8,128)(2,1)}, u32[]{:S(2)}, u32[]{:S(2)}) collective-permute-start(bf16[3,256,256]{2,1,0:T(8,128)(2,1)S(1)} %slice.7), channel_id=1, source_target_pairs={{0,16},{4,20},{8,24},{12,28},{16,0},{20,4},{24,8},{28,12},{1,17},{... | collective-permute-start | bytes 1179656 | tf_op jit(solution)/shard_map/ppermute | solution.py:267
  81.3 16.5 %collective-permute-start.15 = (bf16[3,512,256]{2,1,0:T(8,128)(2,1)S(1)}, bf16[3,512,256]{2,1,0:T(8,128)(2,1)S(1)}, u32[]{:S(2)}, u32[]{:S(2)}) collective-permute-start(bf16[3,512,256]{2,1,0:T(8,128)(2,1)S(1)} %collective-permute-done.4.refs_7_.refs_8_), channel_id=1, source_target_pairs={{0,4},{4,0},{8,12},{12,8},{16,20},{20,16},{24,28},{28,24},{1,5},{5... | collective-permute-start | bytes 2359304 | tf_op jit(solution)/shard_map/ppermute | solution.py:267
  81.3 16.5 %collective-permute-start.16 = (bf16[3,512,256]{2,1,0:T(8,128)(2,1)S(1)}, bf16[3,512,256]{2,1,0:T(8,128)(2,1)S(1)}, u32[]{:S(2)}, u32[]{:S(2)}) collective-permute-start(bf16[3,512,256]{2,1,0:T(8,128)(2,1)S(1)} %collective-permute-done.5.refs_8_.refs_9_), channel_id=1, source_target_pairs={{0,4},{4,0},{8,12},{12,8},{16,20},{20,16},{24,28},{28,24},{1,5},{5... | collective-permute-start | bytes 2359304 | tf_op jit(solution)/shard_map/ppermute | solution.py:267
  99.6 5.3 %collective-permute-start.17 = (bf16[3,256,256]{2,1,0:T(8,128)(2,1)S(1)}, bf16[3,256,256]{2,1,0:T(8,128)(2,1)S(1)}, u32[]{:S(2)}, u32[]{:S(2)}) collective-permute-start(bf16[3,256,256]{2,1,0:T(8,128)(2,1)S(1)} %collective-permute-done.12.refs_11_.refs_12_), channel_id=1, source_target_pairs={{0,4},{4,0},{8,12},{12,8},{16,20},{20,16},{24,28},{28,24},{1,5},{5... | collective-permute-start | bytes 1179656 | tf_op jit(solution)/shard_map/ppermute | solution.py:267
  99.6 6.1 %collective-permute-start.18 = (bf16[3,256,256]{2,1,0:T(8,128)(2,1)}, bf16[3,256,256]{2,1,0:T(8,128)(2,1)}, u32[]{:S(2)}, u32[]{:S(2)}) collective-permute-start(bf16[3,256,256]{2,1,0:T(8,128)(2,1)} %collective-permute-done.13.refs_12_.refs_13_), channel_id=1, source_target_pairs={{0,4},{4,0},{8,12},{12,8},{16,20},{20,16},{24,28},{28,24},{1,5},{5... | collective-permute-start | bytes 1179656 | tf_op jit(solution)/shard_map/ppermute | solution.py:267
  100.1 22.1 %collective-permute-start.20 = (bf16[3,512,256]{2,1,0:T(8,128)(2,1)}, bf16[3,512,256]{2,1,0:T(8,128)(2,1)S(1)}, u32[]{:S(2)}, u32[]{:S(2)}) collective-permute-start(bf16[3,512,256]{2,1,0:T(8,128)(2,1)} %collective-permute-done.11.refs_16_.refs_5_), channel_id=1, source_target_pairs={{0,8},{4,12},{8,0},{12,4},{16,24},{20,28},{24,16},{28,20},{1,9},{5... | collective-permute-start | bytes 2359304 | tf_op jit(solution)/shard_map/ppermute | solution.py:267
  104.2 19.4 %collective-permute-start.21 = (bf16[3,512,256]{2,1,0:T(8,128)(2,1)}, bf16[3,512,256]{2,1,0:T(8,128)(2,1)S(1)}, u32[]{:S(2)}, u32[]{:S(2)}) collective-permute-start(bf16[3,512,256]{2,1,0:T(8,128)(2,1)} %collective-permute-done.11.refs_16_.refs_5_), channel_id=1, source_target_pairs={{0,16},{4,20},{8,24},{12,28},{16,0},{20,4},{24,8},{28,12},{1,17},{... | collective-permute-start | bytes 2359304 | tf_op jit(solution)/shard_map/ppermute | solution.py:267
  104.2 21.2 %collective-permute-start.22 = (bf16[3,512,256]{2,1,0:T(8,128)(2,1)}, bf16[3,512,256]{2,1,0:T(8,128)(2,1)S(1)}, u32[]{:S(2)}, u32[]{:S(2)}) collective-permute-start(bf16[3,512,256]{2,1,0:T(8,128)(2,1)} %get-tuple-element.120), channel_id=1, source_target_pairs={{3,0},{0,1},{1,2},{2,3},{7,4},{4,5},{5,6},{6,7},{11,8},{8,9},{9,10... | collective-permute-start | bytes 2359304 | tf_op jit(solution)/shard_map/ppermute | solution.py:373
  105.7 20.9 %collective-permute-start.19 = (bf16[3,512,256]{2,1,0:T(8,128)(2,1)}, bf16[3,512,256]{2,1,0:T(8,128)(2,1)S(1)}, u32[]{:S(2)}, u32[]{:S(2)}) collective-permute-start(bf16[3,512,256]{2,1,0:T(8,128)(2,1)} %collective-permute-done.11.refs_16_.refs_5_), channel_id=1, source_target_pairs={{0,4},{4,0},{8,12},{12,8},{16,20},{20,16},{24,28},{28,24},{1,5},{5... | collective-permute-start | bytes 2359304 | tf_op jit(solution)/shard_map/ppermute | solution.py:267
  125.4 3.5 %collective-permute-start.24 = (bf16[3,512,256]{2,1,0:T(8,128)(2,1)S(1)}, bf16[3,512,256]{2,1,0:T(8,128)(2,1)}, u32[]{:S(2)}, u32[]{:S(2)}) collective-permute-start(bf16[3,512,256]{2,1,0:T(8,128)(2,1)S(1)} %collective-permute-done.21.refs_19_.refs_8_), channel_id=1, source_target_pairs={{0,4},{4,0},{8,12},{12,8},{16,20},{20,16},{24,28},{28,24},{1,5},{5... | collective-permute-start | bytes 2359304 | tf_op jit(solution)/shard_map/ppermute | solution.py:267
  125.9 4.2 %collective-permute-start.25 = (bf16[3,512,256]{2,1,0:T(8,128)(2,1)S(1)}, bf16[3,512,256]{2,1,0:T(8,128)(2,1)}, u32[]{:S(2)}, u32[]{:S(2)}) collective-permute-start(bf16[3,512,256]{2,1,0:T(8,128)(2,1)S(1)} %collective-permute-done.22.refs_20_.refs_9_), channel_id=1, source_target_pairs={{0,4},{4,0},{8,12},{12,8},{16,20},{20,16},{24,28},{28,24},{1,5},{5... | collective-permute-start | bytes 2359304 | tf_op jit(solution)/shard_map/ppermute | solution.py:267
  140.5 30.2 %all-to-all-start = ((bf16[8,2,256,256]{3,2,1,0:T(8,128)(2,1)}), bf16[8,2,256,256]{3,2,1,0:T(8,128)(2,1)S(1)}, u32[]{:S(2)}, u32[]{:S(2)}) async-start(bf16[8,2,256,256]{3,2,1,0:T(8,128)(2,1)} %bitcast.17), calls=%async_computation | async-start | bytes 4194304 | tf_op jit(solution)/shard_map/all_to_all | solution.py:379
  (25 other events, 338.7 us)

commit v10 on v9

--- a/solution.py
+++ b/solution.py
@@ -11,61 +11,54 @@
 VMEM = pl.BlockSpec(memory_space=pltpu.VMEM)
 HBM = pl.BlockSpec(memory_space=pltpu.HBM)
 MIB = 1 << 20
-HALF_BITS, SOURCE_BITS, CLASS_BITS, LAG_BITS = 1, 8, 4, 8
-FIELDS = (HALF_BITS, SOURCE_BITS, CLASS_BITS, LAG_BITS)
-UNROLL = 2
-
-
-def pack(half, source, klass, lag, place):
-    packed = place
-    for value, bits in ((lag, LAG_BITS), (klass, CLASS_BITS), (source, SOURCE_BITS), (half, HALF_BITS)):
-        packed = (packed << bits) | value
-    return packed
-
-
-def list_task(base, span, total, steps, phased, pair, tasks, counts):
+CLASS_BITS, LAG_BITS = 4, 8
+BESIDE = 2
+
+
+def pack(klass, lag, place):
+    return (((place << LAG_BITS) | lag) << CLASS_BITS) | klass
+
+
+def list_task(base, span, total, steps, pair, tasks, counts):
     source, klass, lag, place = pair
     half = steps // 2
     start = lax.rem(lag - base + total, total)
     first = jnp.where(start < span, start, start - total)
     whole = (first > -half) & (first < span - half)
     lower = (first >= span - half) & (first < span)
-    upper_half = (first > -steps) & (first <= -half)
-    row = jnp.maximum(first + half - 1, 0)
-    number = 2 * klass if phased else 0
+    higher = (first > -steps) & (first <= -half)
+    row = jnp.maximum(first + half - 1 + jnp.where(higher, half, 0), 0)
+    number = 3 * source + jnp.where(lower, 1, 0) + jnp.where(higher, 2, 0)
+    active = whole | lower | higher
     at = counts[number]
-    tasks[number, at] = pack(0, source, klass, row, place)
-    counts[number] = at + jnp.where(whole, 1, 0)
-    at = counts[number + 1]
-    second = jnp.where(upper_half, 1, 0)
-    row = jnp.maximum(first + half - 1 + half * second, 0)
-    tasks[number + 1, at] = pack(second, source, klass, row, place)
-    counts[number + 1] = at + jnp.where(lower | upper_half, 1, 0)
-    return whole | lower | upper_half
-
-
-def run_list(number, width, spare, tasks, counts, hist, table, acc):
+    tasks[number, at] = pack(klass, row, place)
+    counts[number] = at + jnp.where(active, 1, 0)
+    return active
+
+
+def run_list(number, source, column, width, spare, tasks, counts, hist, table, acc):
     panels = table.shape[2]
     count = counts[number]
-    for n in range(UNROLL - 1):
-        tasks[number, count + n] = pack(0, 0, 0, 0, spare)
-
-    @pl.loop(0, (count + UNROLL - 1) // UNROLL)
+    for n in range(BESIDE - 1):
+        tasks[number, count + n] = pack(0, 0, spare)
+
+    @pl.loop(0, (count + BESIDE - 1) // BESIDE)
     def _(j):
-        for n in range(UNROLL):
-            packed = tasks[number, j * UNROLL + n]
-            fields = []
-            for bits in FIELDS:
-                fields.append(packed & ((1 << bits) - 1))
-                packed = packed >> bits
-            half, source, klass, lag = fields
-            columns = pl.multiple_of(half * (width * panels), width * panels)
+        windows, places = [], []
+        for n in range(BESIDE):
+            packed = tasks[number, j * BESIDE + n]
+            klass = packed & ((1 << CLASS_BITS) - 1)
+            lag = (packed >> CLASS_BITS) & ((1 << LAG_BITS) - 1)
+            places.append(packed >> (CLASS_BITS + LAG_BITS))
             rows = pl.multiple_of(lag * panels, panels)
-            acc[packed] += jnp.dot(
-                hist[source, :, pl.ds(columns, width * panels)],
-                table[klass, pl.ds(rows, width * panels), :],
-                preferred_element_type=jnp.float32,
-            )
+            windows.append(table[klass, pl.ds(rows, width * panels), :])
+        product = jnp.dot(
+            hist[source, :, pl.ds(pl.multiple_of(column, panels), width * panels)],
+            jnp.concatenate(windows, axis=1),
+            preferred_element_type=jnp.float32,
+        )
+        for n, place in enumerate(places):
+            acc[place] += product[:, n * panels : (n + 1) * panels]
 
 
 def window_kernel(config, *refs):
@@ -78,30 +71,35 @@
     pieces = [refs.pop(0) for _ in places]
     before = [refs.pop(0) for _ in range((bool(served) + bool(local)) if begun else 0)]
     outs = [refs.pop(0) for _ in range(bool(served) + bool(local))]
-    table, hist, acc, tasks, counts, used, sems, ends, served_sems = refs
+    table, hist, acc, tasks, counts, used, sems, hist_sems, ends, served_sems = refs
     base, group = where[0], where[1]
     classes, _, panels = table.shape
     steps = hist.shape[2] // panels
     margin = (steps // 2 - 1) * panels
     span = (table.shape[1] - 2 * margin) // panels
-    phased = bool(local)
-
-    pltpu.make_async_copy(hist_ref, hist, ends.at[0]).start()
+    sources = hist.shape[0]
+
     near = acc.at[pl.ds(served, owned)] if local else None
     if local and begun:
-        pltpu.make_async_copy(before[-1], near, ends.at[1]).start()
+        pltpu.make_async_copy(before[-1], near, ends).start()
     for k in range(classes):
         for (slot, mask, first), piece in zip(places, pieces):
             start = pl.multiple_of(margin + slot * rows + (group ^ mask) * height + first, 16)
             pltpu.make_async_copy(
                 piece.at[k], table.at[k, pl.ds(start, piece.shape[1]), :], sems.at[k]
             ).start()
+
+    def history_copy(i):
+        return pltpu.make_async_copy(hist_ref.at[i], hist.at[i], hist_sems.at[i])
+
+    for i in range(sources):
+        history_copy(i).start()
     if not begun:
         acc[...] = jnp.zeros_like(acc)
     ends_of_table = jnp.zeros((margin, panels), table.dtype)
+    for n in range(3 * sources):
+        counts[n] = 0
     for k in range(classes):
-        counts[2 * k] = 0
-        counts[2 * k + 1] = 0
         table[k, pl.ds(0, margin), :] = ends_of_table
         table[k, pl.ds(margin + span * panels, margin), :] = ends_of_table
 
@@ -118,7 +116,7 @@
                 source, lag, klass = (ref[c, i] for ref in served_refs)
                 place = i * slots + c
                 pair = (source, klass, lag, place)
-                touched = list_task(base, span, total, steps, phased, pair, tasks, counts)
+                touched = list_task(base, span, total, steps, pair, tasks, counts)
                 needed = touched | narrow
                 used[place] = jnp.where(touched, 1, 0)
                 if begun:
@@ -131,11 +129,10 @@
         def _(i):
             source, lag, klass, target = (ref[i] for ref in local_refs)
             pair = (source, klass, lag, target + served)
-            list_task(base, span, total, steps, phased, pair, tasks, counts)
-
-    pltpu.make_async_copy(hist_ref, hist, ends.at[0]).wait()
+            list_task(base, span, total, steps, pair, tasks, counts)
+
     if local and begun:
-        pltpu.make_async_copy(before[-1], near, ends.at[1]).wait()
+        pltpu.make_async_copy(before[-1], near, ends).wait()
     if served and begun:
         @pl.loop(0, served)
         def _(i):
@@ -145,29 +142,26 @@
 
     spare = acc.shape[0] - 1
 
-    def wait_class(k):
+    for k in range(classes):
         inner = table.at[k, pl.ds(margin, span * panels), :]
         pltpu.make_async_copy(inner, inner, sems.at[k]).wait()
 
-    def run_lists(number):
-        run_list(number, steps, spare, tasks, counts, hist, table, acc)
-        run_list(number + 1, steps // 2, spare, tasks, counts, hist, table, acc)
-
-    if phased:
-        @pl.loop(0, classes)
-        def _(k):
-            wait_class(k)
-            run_lists(2 * k)
-    else:
-        for k in range(classes):
-            wait_class(k)
-        run_lists(0)
+    @pl.loop(0, sources)
+    def _(i):
+        history_copy(i).wait()
+        half = steps // 2
+        run_list(3 * i, i, 0, steps, spare, tasks, counts, hist, table, acc)
+
+        @pl.loop(0, 2)
+        def _(h):
+            column = h * (half * panels)
+            run_list(3 * i + 1 + h, i, column, half, spare, tasks, counts, hist, table, acc)
 
     if narrow:
         outs[0][...] = acc[pl.ds(0, served)].astype(outs[0].dtype)
         return
     if local:
-        pltpu.make_async_copy(near, outs[-1], ends.at[1]).start()
+        pltpu.make_async_copy(near, outs[-1], ends).start()
     if served:
         for wait in (False, True):
             @pl.loop(0, served)
@@ -177,7 +171,7 @@
                     copy = served_copy(i, True)
                     copy.wait() if wait else copy.start()
     if local:
-        pltpu.make_async_copy(near, outs[-1], ends.at[1]).wait()
+        pltpu.make_async_copy(near, outs[-1], ends).wait()
 
 
 def window_sums(shard, group, served, local, hist_t, shards, sums, lanes, rows, narrow=False):
@@ -217,11 +211,12 @@
             pltpu.VMEM((classes, depth_of_table, panels), jnp.bfloat16),
             pltpu.VMEM(hist_t.shape, hist_t.dtype),
             pltpu.VMEM((places + targets + 1, excite, panels), jnp.float32),
-            pltpu.SMEM((2 * classes, pairs + UNROLL), jnp.int32),
-            pltpu.SMEM((2 * classes,), jnp.int32),
+            pltpu.SMEM((3 * owned, pairs + BESIDE), jnp.int32),
+            pltpu.SMEM((3 * owned,), jnp.int32),
             pltpu.SMEM((max(places, 1),), jnp.int32),
             pltpu.SemaphoreType.DMA((classes,)),
-            pltpu.SemaphoreType.DMA((2,)),
+            pltpu.SemaphoreType.DMA((owned,)),
+            pltpu.SemaphoreType.DMA,
             pltpu.SemaphoreType.DMA((max(places, 1),)),
         ],
         input_output_aliases={} if narrow else {

time: 174 us -> 176 us (1.011); the launches traced: 174 us -> 174 us
  waiting for transfers between devices: 60.6 us -> 54 us
  Pallas kernels: 68.1 us -> 71.9 us
  starting transfers between devices: 29.4 us -> 31.3 us
    ppermute x21, waiting for transfers between devices: 48.5 us -> 43.7 us  [swap(): return lax.ppermute(value, 'grp', [(i, i ^ bit) for i in range(peers)])]
    pallas_call x5, Pallas kernels: 65.7 us -> 69.5 us  [window_sums(): pl.pallas_call(functools.partial(window_kernel, config), out_shape=outs,...]
    all_to_all x1, starting transfers between devices: 3.61 us -> 6.17 us  [per_device(): lax.all_to_all(contribution.reshape(peers, slots, *contribution.shape[1:]...]
    all_to_all x1, waiting for transfers between devices: 8.63 us -> 6.42 us  [per_device(): lax.all_to_all(contribution.reshape(peers, slots, *contribution.shape[1:]...]
    ppermute x21, starting transfers between devices: 14.6 us -> 12.6 us  [swap(): return lax.ppermute(value, 'grp', [(i, i ^ bit) for i in range(peers)])]
  transfers between devices with their start and end apart: 27 -> 27, of which waited for: 14 -> 13; matrix products, arithmetic and copies ran while one was open for 5% -> 5% of each run, Pallas kernels for 32% -> 35%
where the time goes in v10:
time: 176 us; the launch traced here: 174 us
  Pallas kernels  71.9 us (41%)
  waiting for transfers between devices  54 us (31%)
  starting transfers between devices  31.3 us (18%)
  local copies, waits for them, and re-layouts  14.2 us (8%)
  other arithmetic  2.59 us (1%)
    pallas_call x5, Pallas kernels, window_sums(): pl.pallas_call(functools.partial(window_kernel, config), out_shape=outs,...  69.5 us
    ppermute x21, waiting for transfers between devices, swap(): return lax.ppermute(value, 'grp', [(i, i ^ bit) for i in range(peers)])  43.7 us
    ppermute x21, starting transfers between devices, swap(): return lax.ppermute(value, 'grp', [(i, i ^ bit) for i in range(peers)])  12.6 us
    unnamed x45, local copies, waits for them, and re-layouts  11.8 us
    ppermute x3, starting transfers between devices, per_device(): own = lax.ppermute(own, 'lag', ring)  9.09 us
    all_to_all x1, waiting for transfers between devices, per_device(): lax.all_to_all(contribution.reshape(peers, slots, *contribution.shape[1:]...  6.42 us
    all_to_all x1, starting transfers between devices, per_device(): lax.all_to_all(contribution.reshape(peers, slots, *contribution.shape[1:]...  6.17 us
  transfers between devices with their start and end apart: 27, of which 13 were waited for; matrix products, arithmetic and copies ran while one was open for 5% of the time, Pallas kernels for 35%

profile of v10, /device:TPU:0, one launch (start us, length us, event | category | flops | bytes accessed | tf_op | source)
XLA Modules:
  0.0 174.2 jit_solution(10754950313105045029)
XLA Ops:
  0.0 2.3 %constant_dynamic-slice_fusion = (bf16[3,512,256]{2,1,0:T(8,128)(2,1)}, bf16[3,512,256]{2,1,0:T(8,128)(2,1)S(1)}) fusion(bf16[3,4096,256]{2,1,0:T(8,128)(2,1)} %refs_9_.1, s32[]{:T(128)S(6)} %select_n.7, s32[]{:T(128)S(6)} %select_n.6), kind=kLoop, calls=%fused_computation.4 | loop fusion | bytes 3145736 | tf_op jit(solution)/shard_map/dynamic_slice | solution.py:307
  2.3 5.0 %collective-permute-start = (bf16[3,512,256]{2,1,0:T(8,128)(2,1)S(1)}, bf16[3,512,256]{2,1,0:T(8,128)(2,1)S(1)}, u32[]{:S(2)}, u32[]{:S(2)}) collective-permute-start(bf16[3,512,256]{2,1,0:T(8,128)(2,1)S(1)} %get-tuple-element.128), channel_id=1, source_target_pairs={{0,3},{1,0},{2,1},{3,2},{4,7},{5,4},{6,5},{7,6},{8,11},{9,8},{10,9... | collective-permute-start | bytes 2359304 | tf_op jit(solution)/shard_map/ppermute | solution.py:341
  7.4 6.3 %copy.17 = bf16[4,2048,256]{1,2,0:T(8,128)(2,1)} copy(bf16[4,2048,256]{2,1,0:T(8,128)(2,1)} %param.13) | data formatting | bytes 8388608 | tf_op args[1]
  14.4 14.3 %shard_map.118 = (f32[16,256,256]{2,1,0:T(8,128)}, f32[4,256,256]{2,1,0:T(8,128)}) custom-call(s32[2]{0:T(128)} %pad_add_fusion.1.refs_0_, s32[2,8]{1,0:T(2,128)} %bitcast.18, s32[2,8]{1,0:T(2,128)} %bitcast.22, s32[2,8]{1,0:T(2,128)} %bitcast.26, s32[48]{0:T(128)} %refs_1_.1, s32[48]{0:T(128)} %refs_2_.1, s32[48]{0:T(128)} %refs_3_.1, s32[48]{0:T(128)} %refs_4_.5, ...), custom_call_target="tpu_custom_call" | custom-call | flops 17179869184 | bytes 10485760 | tf_op jit(solution)/shard_map/pallas_call | solution.py:205
  28.8 2.5 %collective-permute-start.2 = (bf16[3,512,256]{2,1,0:T(8,128)(2,1)S(1)}, bf16[3,512,256]{2,1,0:T(8,128)(2,1)S(1)}, u32[]{:S(2)}, u32[]{:S(2)}) collective-permute-start(bf16[3,512,256]{2,1,0:T(8,128)(2,1)S(1)} %collective-permute-done.refs_9_), channel_id=1, source_target_pairs={{0,16},{4,20},{8,24},{12,28},{16,0},{20,4},{24,8},{28,12},{1,17},{... | collective-permute-start | bytes 2359304 | tf_op jit(solution)/shard_map/ppermute | solution.py:262
  31.5 17.0 %collective-permute-done.1.refs_10_ = bf16[3,512,256]{2,1,0:T(8,128)(2,1)S(1)} collective-permute-done((bf16[3,512,256]{2,1,0:T(8,128)(2,1)S(1)}, bf16[3,512,256]{2,1,0:T(8,128)(2,1)S(1)}, u32[]{:S(2)}, u32[]{:S(2)}) %collective-permute-start.1) | collective-permute-done | bytes 786464 | tf_op jit(solution)/shard_map/ppermute | solution.py:262
  52.1 2.3 %collective-permute-start.6 = (bf16[3,512,256]{2,1,0:T(8,128)(2,1)}, bf16[3,512,256]{2,1,0:T(8,128)(2,1)}, u32[]{:S(2)}, u32[]{:S(2)}) collective-permute-start(bf16[3,512,256]{2,1,0:T(8,128)(2,1)} %get-tuple-element.120), channel_id=1, source_target_pairs={{0,3},{1,0},{2,1},{3,2},{4,7},{5,4},{6,5},{7,6},{8,11},{9,8},{10,9... | collective-permute-start | bytes 2359304 | tf_op jit(solution)/shard_map/ppermute | solution.py:348
  55.0 15.2 %collective-permute-done.4.refs_7_.refs_8_ = bf16[3,512,256]{2,1,0:T(8,128)(2,1)S(1)} collective-permute-done((bf16[3,512,256]{2,1,0:T(8,128)(2,1)S(1)}, bf16[3,512,256]{2,1,0:T(8,128)(2,1)S(1)}, u32[]{:S(2)}, u32[]{:S(2)}) %collective-permute-start.4) | collective-permute-done | bytes 786464 | tf_op jit(solution)/shard_map/ppermute | solution.py:262
  74.8 3.8 %collective-permute-start.11 = (bf16[3,512,256]{2,1,0:T(8,128)(2,1)S(1)}, bf16[3,512,256]{2,1,0:T(8,128)(2,1)}, u32[]{:S(2)}, u32[]{:S(2)}) collective-permute-start(bf16[3,512,256]{2,1,0:T(8,128)(2,1)S(1)} %collective-permute-done.3.refs_5_.refs_6_), channel_id=1, source_target_pairs={{0,3},{1,0},{2,1},{3,2},{4,7},{5,4},{6,5},{7,6},{8,11},{9,8},{10,9... | collective-permute-start | bytes 2359304 | tf_op jit(solution)/shard_map/ppermute | solution.py:354
  78.6 1.7 collective-permute-start.12
  80.3 1.8 %collective-permute-start.13 = (bf16[3,256,256]{2,1,0:T(8,128)(2,1)S(1)}, bf16[3,256,256]{2,1,0:T(8,128)(2,1)}, u32[]{:S(2)}, u32[]{:S(2)}) collective-permute-start(bf16[3,256,256]{2,1,0:T(8,128)(2,1)S(1)} %slice.7), channel_id=1, source_target_pairs={{0,16},{4,20},{8,24},{12,28},{16,0},{20,4},{24,8},{28,12},{1,17},{... | collective-permute-start | bytes 1179656 | tf_op jit(solution)/shard_map/ppermute | solution.py:262
  82.7 16.0 %shard_map.119 = (f32[16,256,256]{2,1,0:T(8,128)}, f32[4,256,256]{2,1,0:T(8,128)}) custom-call(s32[2]{0:T(128)} %pad_add_fusion.2.refs_0_, s32[2,8]{1,0:T(2,128)} %bitcast.19, s32[2,8]{1,0:T(2,128)} %bitcast.23, s32[2,8]{1,0:T(2,128)} %bitcast.27, s32[48]{0:T(128)} %refs_1_.1, s32[48]{0:T(128)} %refs_2_.1, ...), custom_call_target="tpu_custom_call", output_to_operand_aliasing={{0}: (17, {}), {1}: (18, {})} | custom-call | flops 17179869184 | bytes 10485760 | tf_op jit(solution)/shard_map/pallas_call | solution.py:205
  100.6 1.8 %collective-permute-start.17 = (bf16[3,256,256]{2,1,0:T(8,128)(2,1)S(1)}, bf16[3,256,256]{2,1,0:T(8,128)(2,1)S(1)}, u32[]{:S(2)}, u32[]{:S(2)}) collective-permute-start(bf16[3,256,256]{2,1,0:T(8,128)(2,1)S(1)} %collective-permute-done.12.refs_11_.refs_12_), channel_id=1, source_target_pairs={{0,4},{4,0},{8,12},{12,8},{16,20},{20,16},{24,28},{28,24},{1,5},{5... | collective-permute-start | bytes 1179656 | tf_op jit(solution)/shard_map/ppermute | solution.py:262
  102.4 1.2 collective-permute-start.21
  106.2 10.5 %shard_map.120.refs_13_ = f32[16,256,256]{2,1,0:T(8,128)} custom-call(s32[2]{0:T(128)} %pad_add_fusion.refs_0_, s32[2,8]{1,0:T(2,128)} %bitcast.20, s32[2,8]{1,0:T(2,128)} %bitcast.24, s32[2,8]{1,0:T(2,128)} %bitcast.28, bf16[4,256,2048]{2,1,0:T(8,128)(2,1)} %bitcast.14, bf16[3,512,256]{2,1,0:T(8,128)(2,1)} %copy-done.6, ...), custom_call_target="tpu_custom_call", output_to_operand_aliasing={{}: (15, {})} | custom-call | flops 4294967296 | bytes 10485760 | tf_op jit(solution)/shard_map/pallas_call | solution.py:205
  116.7 5.9 %collective-permute-done.20.refs_18_.refs_7_ = bf16[3,512,256]{2,1,0:T(8,128)(2,1)S(1)} collective-permute-done((bf16[3,512,256]{2,1,0:T(8,128)(2,1)}, bf16[3,512,256]{2,1,0:T(8,128)(2,1)S(1)}, u32[]{:S(2)}, u32[]{:S(2)}) %collective-permute-start.20) | collective-permute-done | bytes 786464 | tf_op jit(solution)/shard_map/ppermute | solution.py:262
  122.6 2.0 %collective-permute-done.22.refs_20_.refs_9_ = bf16[3,512,256]{2,1,0:T(8,128)(2,1)S(1)} collective-permute-done((bf16[3,512,256]{2,1,0:T(8,128)(2,1)}, bf16[3,512,256]{2,1,0:T(8,128)(2,1)S(1)}, u32[]{:S(2)}, u32[]{:S(2)}) %collective-permute-start.22) | collective-permute-done | bytes 786464 | tf_op jit(solution)/shard_map/ppermute | solution.py:368
  125.7 1.3 collective-permute-done.23.refs_21_.refs_10_
  129.3 8.5 %shard_map.122 = bf16[16,256,256]{2,1,0:T(8,128)(2,1)} custom-call(s32[2]{0:T(128)} %pad_add_fusion.3.refs_0_, s32[2,8]{1,0:T(2,128)} %bitcast.21, s32[2,8]{1,0:T(2,128)} %bitcast.25, s32[2,8]{1,0:T(2,128)} %bitcast.29, bf16[4,256,2048]{2,1,0:T(8,128)(2,1)} %bitcast.15, bf16[3,512,256]{2,1,0:T(8,128)(2,1)} %collective-permute-done.11.refs_16_.refs_5_, ...), custom_call_target="tpu_custom_call" | custom-call | flops 4294967296 | bytes 10485760 | tf_op jit(solution)/shard_map/pallas_call | solution.py:205
  137.8 6.2 %all-to-all-start = ((bf16[8,2,256,256]{3,2,1,0:T(8,128)(2,1)}), bf16[8,2,256,256]{3,2,1,0:T(8,128)(2,1)S(1)}, u32[]{:S(2)}, u32[]{:S(2)}) async-start(bf16[8,2,256,256]{3,2,1,0:T(8,128)(2,1)} %bitcast.17), calls=%async_computation | async-start | bytes 4194304 | tf_op jit(solution)/shard_map/all_to_all | solution.py:374
  144.0 20.2 %shard_map.121.near_ref = f32[4,256,256]{2,1,0:T(8,128)} custom-call(s32[2]{0:T(128)} %pad_add_fusion.refs_0_, s32[48]{0:T(128)} %refs_1_.1, s32[48]{0:T(128)} %refs_2_.1, s32[48]{0:T(128)} %refs_3_.1, s32[48]{0:T(128)} %refs_4_.5, bf16[4,256,2048]{2,1,0:T(8,128)(2,1)} %bitcast.16, bf16[3,512,256]{2,1,0:T(8,128)(2,1)} %copy-done.6, ...), custom_call_target="tpu_custom_call", output_to_operand_aliasing={{}: (24, {})} | custom-call | flops 12884901888 | bytes 16777216 | tf_op jit(solution)/shard_map/pallas_call | solution.py:205
  164.2 6.4 %all-to-all-done.recv_ref = bf16[8,2,256,256]{3,2,1,0:T(8,128)(2,1)S(1)} async-done(((bf16[8,2,256,256]{3,2,1,0:T(8,128)(2,1)}), bf16[8,2,256,256]{3,2,1,0:T(8,128)(2,1)S(1)}, u32[]{:S(2)}, u32[]{:S(2)}) %all-to-all-start) | async-done | bytes 2097184 | tf_op jit(solution)/shard_map/all_to_all | solution.py:374
  170.6 1.2 copy-done
  171.8 2.4 %shard_map.123 = bf16[4,256,256]{2,1,0:T(8,128)(2,1)} custom-call(s32[2,8]{1,0:T(2,128)S(1)} %bitcast.11, f32[4,256,256]{2,1,0:T(8,128)S(1)} %copy-done, bf16[8,2,256,256]{3,2,1,0:T(8,128)(2,1)S(1)} %all-to-all-done.recv_ref, bf16[4,256,256]{2,1,0:T(8,128)(2,1)S(1)} %copy-done.1, bf16[4,256,256]{2,1,0:T(8,128)(2,1)S(1)} %copy-done.2), custom_call_target="tpu_custom_call" | custom-call | tf_op jit(solution)/shard_map/pallas_call | solution.py:251
  (88 shorter events, 18.0 us)
Async XLA Ops:
  2.3 26.3 %collective-permute-start = (bf16[3,512,256]{2,1,0:T(8,128)(2,1)S(1)}, bf16[3,512,256]{2,1,0:T(8,128)(2,1)S(1)}, u32[]{:S(2)}, u32[]{:S(2)}) collective-permute-start(bf16[3,512,256]{2,1,0:T(8,128)(2,1)S(1)} %get-tuple-element.128), channel_id=1, source_target_pairs={{0,3},{1,0},{2,1},{3,2},{4,7},{5,4},{6,5},{7,6},{8,11},{9,8},{10,9... | collective-permute-start | bytes 2359304 | tf_op jit(solution)/shard_map/ppermute | solution.py:341
  28.7 19.8 %collective-permute-start.1 = (bf16[3,512,256]{2,1,0:T(8,128)(2,1)S(1)}, bf16[3,512,256]{2,1,0:T(8,128)(2,1)S(1)}, u32[]{:S(2)}, u32[]{:S(2)}) collective-permute-start(bf16[3,512,256]{2,1,0:T(8,128)(2,1)S(1)} %collective-permute-done.refs_9_), channel_id=1, source_target_pairs={{0,8},{4,12},{8,0},{12,4},{16,24},{20,28},{24,16},{28,20},{1,9},{5... | collective-permute-start | bytes 2359304 | tf_op jit(solution)/shard_map/ppermute | solution.py:262
  28.8 20.6 %collective-permute-start.2 = (bf16[3,512,256]{2,1,0:T(8,128)(2,1)S(1)}, bf16[3,512,256]{2,1,0:T(8,128)(2,1)S(1)}, u32[]{:S(2)}, u32[]{:S(2)}) collective-permute-start(bf16[3,512,256]{2,1,0:T(8,128)(2,1)S(1)} %collective-permute-done.refs_9_), channel_id=1, source_target_pairs={{0,16},{4,20},{8,24},{12,28},{16,0},{20,4},{24,8},{28,12},{1,17},{... | collective-permute-start | bytes 2359304 | tf_op jit(solution)/shard_map/ppermute | solution.py:262
  31.3 18.9 %collective-permute-start.3 = (bf16[3,512,256]{2,1,0:T(8,128)(2,1)S(1)}, bf16[3,512,256]{2,1,0:T(8,128)(2,1)S(1)}, u32[]{:S(2)}, u32[]{:S(2)}) collective-permute-start(bf16[3,512,256]{2,1,0:T(8,128)(2,1)S(1)} %collective-permute-done.refs_9_), channel_id=1, source_target_pairs={{0,3},{1,0},{2,1},{3,2},{4,7},{5,4},{6,5},{7,6},{8,11},{9,8},{10,9... | collective-permute-start | bytes 2359304 | tf_op jit(solution)/shard_map/ppermute | solution.py:344
  50.2 4.3 %collective-permute-start.10 = (bf16[3,512,256]{2,1,0:T(8,128)(2,1)S(1)}, bf16[3,512,256]{2,1,0:T(8,128)(2,1)S(1)}, u32[]{:S(2)}, u32[]{:S(2)}) collective-permute-start(bf16[3,512,256]{2,1,0:T(8,128)(2,1)S(1)} %collective-permute-done.3.refs_5_.refs_6_), channel_id=1, source_target_pairs={{0,4},{4,0},{8,12},{12,8},{16,20},{20,16},{24,28},{28,24},{1,5},{5... | collective-permute-start | bytes 2359304 | tf_op jit(solution)/shard_map/ppermute | solution.py:262
  50.2 20.0 %collective-permute-start.4 = (bf16[3,512,256]{2,1,0:T(8,128)(2,1)S(1)}, bf16[3,512,256]{2,1,0:T(8,128)(2,1)S(1)}, u32[]{:S(2)}, u32[]{:S(2)}) collective-permute-start(bf16[3,512,256]{2,1,0:T(8,128)(2,1)S(1)} %collective-permute-done.3.refs_5_.refs_6_), channel_id=1, source_target_pairs={{0,8},{4,12},{8,0},{12,4},{16,24},{20,28},{24,16},{28,20},{1,9},{5... | collective-permute-start | bytes 2359304 | tf_op jit(solution)/shard_map/ppermute | solution.py:262
  51.3 19.6 %collective-permute-start.5 = (bf16[3,512,256]{2,1,0:T(8,128)(2,1)S(1)}, bf16[3,512,256]{2,1,0:T(8,128)(2,1)S(1)}, u32[]{:S(2)}, u32[]{:S(2)}) collective-permute-start(bf16[3,512,256]{2,1,0:T(8,128)(2,1)S(1)} %collective-permute-done.3.refs_5_.refs_6_), channel_id=1, source_target_pairs={{0,16},{4,20},{8,24},{12,28},{16,0},{20,4},{24,8},{28,12},{1,17},{... | collective-permute-start | bytes 2359304 | tf_op jit(solution)/shard_map/ppermute | solution.py:262
  52.1 19.9 %collective-permute-start.6 = (bf16[3,512,256]{2,1,0:T(8,128)(2,1)}, bf16[3,512,256]{2,1,0:T(8,128)(2,1)}, u32[]{:S(2)}, u32[]{:S(2)}) collective-permute-start(bf16[3,512,256]{2,1,0:T(8,128)(2,1)} %get-tuple-element.120), channel_id=1, source_target_pairs={{0,3},{1,0},{2,1},{3,2},{4,7},{5,4},{6,5},{7,6},{8,11},{9,8},{10,9... | collective-permute-start | bytes 2359304 | tf_op jit(solution)/shard_map/ppermute | solution.py:348
  54.4 17.6 %collective-permute-start.7 = (bf16[3,512,256]{2,1,0:T(8,128)(2,1)}, bf16[3,512,256]{2,1,0:T(8,128)(2,1)S(1)}, u32[]{:S(2)}, u32[]{:S(2)}) collective-permute-start(bf16[3,512,256]{2,1,0:T(8,128)(2,1)} %copy-done.16), channel_id=1, source_target_pairs={{0,4},{4,0},{8,12},{12,8},{16,20},{20,16},{24,28},{28,24},{1,5},{5... | collective-permute-start | bytes 2359304 | tf_op jit(solution)/shard_map/ppermute | solution.py:262
  54.5 17.6 %collective-permute-start.8 = (bf16[3,512,256]{2,1,0:T(8,128)(2,1)S(1)}, bf16[3,512,256]{2,1,0:T(8,128)(2,1)S(1)}, u32[]{:S(2)}, u32[]{:S(2)}) collective-permute-start(bf16[3,512,256]{2,1,0:T(8,128)(2,1)S(1)} %collective-permute-done.1.refs_10_), channel_id=1, source_target_pairs={{0,4},{4,0},{8,12},{12,8},{16,20},{20,16},{24,28},{28,24},{1,5},{5... | collective-permute-start | bytes 2359304 | tf_op jit(solution)/shard_map/ppermute | solution.py:262
  74.1 8.0 %collective-permute-start.14 = (bf16[3,512,256]{2,1,0:T(8,128)(2,1)}, bf16[3,512,256]{2,1,0:T(8,128)(2,1)}, u32[]{:S(2)}, u32[]{:S(2)}) collective-permute-start(bf16[3,512,256]{2,1,0:T(8,128)(2,1)} %collective-permute-done.6.refs_15_), channel_id=1, source_target_pairs={{0,4},{4,0},{8,12},{12,8},{16,20},{20,16},{24,28},{28,24},{1,5},{5... | collective-permute-start | bytes 2359304 | tf_op jit(solution)/shard_map/ppermute | solution.py:262
  74.8 24.0 %collective-permute-start.11 = (bf16[3,512,256]{2,1,0:T(8,128)(2,1)S(1)}, bf16[3,512,256]{2,1,0:T(8,128)(2,1)}, u32[]{:S(2)}, u32[]{:S(2)}) collective-permute-start(bf16[3,512,256]{2,1,0:T(8,128)(2,1)S(1)} %collective-permute-done.3.refs_5_.refs_6_), channel_id=1, source_target_pairs={{0,3},{1,0},{2,1},{3,2},{4,7},{5,4},{6,5},{7,6},{8,11},{9,8},{10,9... | collective-permute-start | bytes 2359304 | tf_op jit(solution)/shard_map/ppermute | solution.py:354
  78.6 20.1 %collective-permute-start.12 = (bf16[3,256,256]{2,1,0:T(8,128)(2,1)S(1)}, bf16[3,256,256]{2,1,0:T(8,128)(2,1)S(1)}, u32[]{:S(2)}, u32[]{:S(2)}) collective-permute-start(bf16[3,256,256]{2,1,0:T(8,128)(2,1)S(1)} %slice.6), channel_id=1, source_target_pairs={{0,8},{4,12},{8,0},{12,4},{16,24},{20,28},{24,16},{28,20},{1,9},{5... | collective-permute-start | bytes 1179656 | tf_op jit(solution)/shard_map/ppermute | solution.py:262
  80.3 18.4 %collective-permute-start.13 = (bf16[3,256,256]{2,1,0:T(8,128)(2,1)S(1)}, bf16[3,256,256]{2,1,0:T(8,128)(2,1)}, u32[]{:S(2)}, u32[]{:S(2)}) collective-permute-start(bf16[3,256,256]{2,1,0:T(8,128)(2,1)S(1)} %slice.7), channel_id=1, source_target_pairs={{0,16},{4,20},{8,24},{12,28},{16,0},{20,4},{24,8},{28,12},{1,17},{... | collective-permute-start | bytes 1179656 | tf_op jit(solution)/shard_map/ppermute | solution.py:262
  82.1 16.6 %collective-permute-start.15 = (bf16[3,512,256]{2,1,0:T(8,128)(2,1)S(1)}, bf16[3,512,256]{2,1,0:T(8,128)(2,1)S(1)}, u32[]{:S(2)}, u32[]{:S(2)}) collective-permute-start(bf16[3,512,256]{2,1,0:T(8,128)(2,1)S(1)} %collective-permute-done.4.refs_7_.refs_8_), channel_id=1, source_target_pairs={{0,4},{4,0},{8,12},{12,8},{16,20},{20,16},{24,28},{28,24},{1,5},{5... | collective-permute-start | bytes 2359304 | tf_op jit(solution)/shard_map/ppermute | solution.py:262
  82.1 16.7 %collective-permute-start.16 = (bf16[3,512,256]{2,1,0:T(8,128)(2,1)S(1)}, bf16[3,512,256]{2,1,0:T(8,128)(2,1)S(1)}, u32[]{:S(2)}, u32[]{:S(2)}) collective-permute-start(bf16[3,512,256]{2,1,0:T(8,128)(2,1)S(1)} %collective-permute-done.5.refs_8_.refs_9_), channel_id=1, source_target_pairs={{0,4},{4,0},{8,12},{12,8},{16,20},{20,16},{24,28},{28,24},{1,5},{5... | collective-permute-start | bytes 2359304 | tf_op jit(solution)/shard_map/ppermute | solution.py:262
  100.6 4.9 %collective-permute-start.17 = (bf16[3,256,256]{2,1,0:T(8,128)(2,1)S(1)}, bf16[3,256,256]{2,1,0:T(8,128)(2,1)S(1)}, u32[]{:S(2)}, u32[]{:S(2)}) collective-permute-start(bf16[3,256,256]{2,1,0:T(8,128)(2,1)S(1)} %collective-permute-done.12.refs_11_.refs_12_), channel_id=1, source_target_pairs={{0,4},{4,0},{8,12},{12,8},{16,20},{20,16},{24,28},{28,24},{1,5},{5... | collective-permute-start | bytes 1179656 | tf_op jit(solution)/shard_map/ppermute | solution.py:262
  102.4 3.8 %collective-permute-start.18 = (bf16[3,256,256]{2,1,0:T(8,128)(2,1)}, bf16[3,256,256]{2,1,0:T(8,128)(2,1)}, u32[]{:S(2)}, u32[]{:S(2)}) collective-permute-start(bf16[3,256,256]{2,1,0:T(8,128)(2,1)} %collective-permute-done.13.refs_12_.refs_13_), channel_id=1, source_target_pairs={{0,4},{4,0},{8,12},{12,8},{16,20},{20,16},{24,28},{28,24},{1,5},{5... | collective-permute-start | bytes 1179656 | tf_op jit(solution)/shard_map/ppermute | solution.py:262
  102.4 20.2 %collective-permute-start.20 = (bf16[3,512,256]{2,1,0:T(8,128)(2,1)}, bf16[3,512,256]{2,1,0:T(8,128)(2,1)S(1)}, u32[]{:S(2)}, u32[]{:S(2)}) collective-permute-start(bf16[3,512,256]{2,1,0:T(8,128)(2,1)} %collective-permute-done.11.refs_16_.refs_5_), channel_id=1, source_target_pairs={{0,8},{4,12},{8,0},{12,4},{16,24},{20,28},{24,16},{28,20},{1,9},{5... | collective-permute-start | bytes 2359304 | tf_op jit(solution)/shard_map/ppermute | solution.py:262
  102.4 20.2 %collective-permute-start.21 = (bf16[3,512,256]{2,1,0:T(8,128)(2,1)}, bf16[3,512,256]{2,1,0:T(8,128)(2,1)S(1)}, u32[]{:S(2)}, u32[]{:S(2)}) collective-permute-start(bf16[3,512,256]{2,1,0:T(8,128)(2,1)} %collective-permute-done.11.refs_16_.refs_5_), channel_id=1, source_target_pairs={{0,16},{4,20},{8,24},{12,28},{16,0},{20,4},{24,8},{28,12},{1,17},{... | collective-permute-start | bytes 2359304 | tf_op jit(solution)/shard_map/ppermute | solution.py:262
  103.7 20.9 %collective-permute-start.22 = (bf16[3,512,256]{2,1,0:T(8,128)(2,1)}, bf16[3,512,256]{2,1,0:T(8,128)(2,1)S(1)}, u32[]{:S(2)}, u32[]{:S(2)}) collective-permute-start(bf16[3,512,256]{2,1,0:T(8,128)(2,1)} %get-tuple-element.120), channel_id=1, source_target_pairs={{3,0},{0,1},{1,2},{2,3},{7,4},{4,5},{5,6},{6,7},{11,8},{8,9},{9,10... | collective-permute-start | bytes 2359304 | tf_op jit(solution)/shard_map/ppermute | solution.py:368
  106.2 19.5 %collective-permute-start.19 = (bf16[3,512,256]{2,1,0:T(8,128)(2,1)}, bf16[3,512,256]{2,1,0:T(8,128)(2,1)S(1)}, u32[]{:S(2)}, u32[]{:S(2)}) collective-permute-start(bf16[3,512,256]{2,1,0:T(8,128)(2,1)} %collective-permute-done.11.refs_16_.refs_5_), channel_id=1, source_target_pairs={{0,4},{4,0},{8,12},{12,8},{16,20},{20,16},{24,28},{28,24},{1,5},{5... | collective-permute-start | bytes 2359304 | tf_op jit(solution)/shard_map/ppermute | solution.py:262
  125.1 4.2 %collective-permute-start.25 = (bf16[3,512,256]{2,1,0:T(8,128)(2,1)S(1)}, bf16[3,512,256]{2,1,0:T(8,128)(2,1)}, u32[]{:S(2)}, u32[]{:S(2)}) collective-permute-start(bf16[3,512,256]{2,1,0:T(8,128)(2,1)S(1)} %collective-permute-done.22.refs_20_.refs_9_), channel_id=1, source_target_pairs={{0,4},{4,0},{8,12},{12,8},{16,20},{20,16},{24,28},{28,24},{1,5},{5... | collective-permute-start | bytes 2359304 | tf_op jit(solution)/shard_map/ppermute | solution.py:262
  137.8 32.8 %all-to-all-start = ((bf16[8,2,256,256]{3,2,1,0:T(8,128)(2,1)}), bf16[8,2,256,256]{3,2,1,0:T(8,128)(2,1)S(1)}, u32[]{:S(2)}, u32[]{:S(2)}) async-start(bf16[8,2,256,256]{3,2,1,0:T(8,128)(2,1)} %bitcast.17), calls=%async_computation | async-start | bytes 4194304 | tf_op jit(solution)/shard_map/all_to_all | solution.py:374
  (25 other events, 339.6 us)

commit v11 on v9

--- a/solution.py
+++ b/solution.py
@@ -84,7 +84,7 @@
     steps = hist.shape[2] // panels
     margin = (steps // 2 - 1) * panels
     span = (table.shape[1] - 2 * margin) // panels
-    phased = bool(local)
+    phased = bool(local) or span * panels > rows
 
     pltpu.make_async_copy(hist_ref, hist, ends.at[0]).start()
     near = acc.at[pl.ds(served, owned)] if local else None
@@ -236,8 +236,10 @@
     )(*operands, *wide, *before)
 
 
-def update_kernel(target_ref, near_ref, recv_ref, inverse_ref, incident_ref, out_ref, total):
-    total[...] = near_ref[...]
+def update_kernel(target_ref, near_ref, recv_ref, inverse_ref, incident_ref, out_ref, total, sem):
+    copy = pltpu.make_async_copy(near_ref, total, sem)
+    copy.start()
+    copy.wait()
     slots, peers = target_ref.shape
 
     @pl.loop(0, peers)
@@ -256,9 +258,9 @@
     return pl.pallas_call(
         update_kernel,
         out_shape=jax.ShapeDtypeStruct(incident.shape, jnp.bfloat16),
-        in_specs=[SMEM] + [VMEM] * 4,
+        in_specs=[SMEM, HBM] + [VMEM] * 3,
         out_specs=VMEM,
-        scratch_shapes=[pltpu.VMEM(near.shape, jnp.float32)],
+        scratch_shapes=[pltpu.VMEM(near.shape, jnp.float32), pltpu.SemaphoreType.DMA],
         compiler_params=pltpu.CompilerParams(vmem_limit_bytes=32 * MIB),
     )(target, near, recv, inverse, incident)
 
@@ -311,16 +313,13 @@
     def part(index):
         return lax.dynamic_slice(weights, (0, index * height, 0), (classes, height, panels))
 
-    def add_shard(step, sums, served=served, local=local, **options):
-        shard = lax.rem(lane + step, lanes)
-        shards = rounds[step - 1 : step] if served else rounds[step - 1 :]
+    def add_shards(first, end, served, local, sums, **options):
+        shard = lax.rem(lane + first, lanes)
+        shards = rounds[first - 1 : end - 1]
         return window_sums(
-            shard, group, served, local, hist_t, shards, sums, lanes, rows, **options
-        )
-
-    sums = window_sums(
-        lane, group * 0, served, local, hist_t, [[(0, 0, weights)]], None, lanes, rows
-    )
+            shard, group, served, local, hist_t, shards, [sums], lanes, rows, **options
+        )[0]
+
     own = part(group)
     corner = part(group ^ 6)
 
@@ -344,12 +343,20 @@
         return [(m ^ 6, 0, v) for m, v in zip(masks, held)]
 
     own = lax.ppermute(own, "lag", ring)
-    own, sums = tie(own, sums)
+    own, hist_t = tie(own, hist_t)
     trio = neighbours(own)
     own = lax.ppermute(own, "lag", ring)
-    trio, own, corner = tie(trio, own, corner)
-    found = with_other_core(sum(trio, []), peers)
+    served_sums, near = window_sums(
+        lane, group * 0, served, local, hist_t, [[(0, 0, weights)]], None, lanes, rows
+    )
+    trio, own, corner, served_sums, near = tie(trio, own, corner, served_sums, near)
+    held, across, along = trio
+    found, across = tie(with_other_core(held, peers), across)
+    found += with_other_core(across, peers)
+    more = with_other_core(along, peers)
     held, across, along = neighbours(own)
+    more, held = tie(more, held)
+    found += more
     diagonal = lax.ppermute(corner, "lag", ring)
     held = with_other_core(held, peers)
     across, along, own, diagonal, found, held = tie(across, along, own, diagonal, found, held)
@@ -362,8 +369,8 @@
         if step == 2:
             rounds[0], across, along = tie(rounds[0], across, along)
         found = held + with_other_core(across + along, peers)
-        sums = add_shard(step - 1, sums)
-        own, turned, sums, corner, found = tie(own, turned, sums, corner, found)
+        near = add_shards(step - 1, step, (), local, near)
+        own, turned, near, corner, found = tie(own, turned, near, corner, found)
         held, across, along = neighbours(own)
         found, held = tie(found + with_other_core(turned, peers), held)
         rounds.append(found)
@@ -371,11 +378,10 @@
         if step < lanes - 2:
             across, along, own = tie(across, along, own)
     diagonal = lax.ppermute(corner, "lag", [(j, i) for i, j in ring])
-    served_sums, near = sums
-    served_sums = add_shard(lanes - 2, [served_sums], local=())[0]
+    served_sums = add_shards(1, lanes - 1, served, (), served_sums)
     across, along, diagonal, served_sums = tie(across, along, diagonal, served_sums)
     rounds.append(held + with_other_core(across + along + corners(diagonal), peers))
-    contribution = add_shard(lanes - 1, [served_sums], local=(), narrow=True)[0]
+    contribution = add_shards(lanes - 1, lanes, served, (), served_sums, narrow=True)
     recv = lax.all_to_all(
         contribution.reshape(peers, slots, *contribution.shape[1:]),
         "grp",
@@ -383,7 +389,7 @@
         concat_axis=0,
         tiled=True,
     )
-    near = add_shard(lanes - 2, [near], served=())[0]
+    near = add_shards(lanes - 2, lanes, (), local, near)
     return update(recv_target.T, near, recv, inverse_blocks, incident)
 
 

time: 174 us -> 165 us (0.948)
  waiting for transfers between devices: 60.6 us -> 47.2 us
  Pallas kernels: 68.1 us -> 71.8 us
    ppermute x21, waiting for transfers between devices: 48.5 us -> 6.86 us  [swap(): return lax.ppermute(value, 'grp', [(i, i ^ bit) for i in range(peers)])]
    ppermute x1, waiting for transfers between devices: 0.42 us -> 16.8 us  [per_device(): diagonal = lax.ppermute(corner, 'lag', ring)]
    ppermute x3, waiting for transfers between devices: 1.18 us -> 12.8 us  [per_device(): own = lax.ppermute(own, 'lag', ring)]
    pallas_call x5, Pallas kernels: 65.7 us -> 69.4 us  [window_sums(): pl.pallas_call(functools.partial(window_kernel, config), out_shape=outs,...]
    ppermute x3, starting transfers between devices: 9.04 us -> 12.1 us  [per_device(): own = lax.ppermute(own, 'lag', ring)]
    ppermute x1, waiting for transfers between devices: 1.8 us -> 3.83 us  [per_device(): diagonal = lax.ppermute(corner, 'lag', [(j, i) for i, j in ring])]
    unnamed x45, local copies, waits for them, and re-layouts: 11.1 us -> 9.1 us
    all_to_all x1, waiting for transfers between devices: 8.63 us -> 6.87 us  [per_device(): lax.all_to_all(contribution.reshape(peers, slots, *contribution.shape[1:]...]
  transfers between devices with their start and end apart: 27 -> 27, of which waited for: 14 -> 11; matrix products, arithmetic and copies ran while one was open for 5% -> 6% of each run, Pallas kernels for 32% -> 36%
where the time goes in v11:
time: 165 us
  Pallas kernels  71.8 us (44%)
  waiting for transfers between devices  47.2 us (29%)
  starting transfers between devices  30.7 us (19%)
  local copies, waits for them, and re-layouts  12.3 us (7%)
  other arithmetic  2.59 us (2%)
    pallas_call x5, Pallas kernels, window_sums(): pl.pallas_call(functools.partial(window_kernel, config), out_shape=outs,...  69.4 us
    ppermute x1, waiting for transfers between devices, per_device(): diagonal = lax.ppermute(corner, 'lag', ring)  16.8 us
    ppermute x21, starting transfers between devices, swap(): return lax.ppermute(value, 'grp', [(i, i ^ bit) for i in range(peers)])  12.9 us
    ppermute x3, waiting for transfers between devices, per_device(): own = lax.ppermute(own, 'lag', ring)  12.8 us
    ppermute x3, starting transfers between devices, per_device(): own = lax.ppermute(own, 'lag', ring)  12.1 us
    unnamed x45, local copies, waits for them, and re-layouts  9.1 us
    all_to_all x1, waiting for transfers between devices, per_device(): lax.all_to_all(contribution.reshape(peers, slots, *contribution.shape[1:]...  6.87 us
    ppermute x21, waiting for transfers between devices, swap(): return lax.ppermute(value, 'grp', [(i, i ^ bit) for i in range(peers)])  6.86 us
  transfers between devices with their start and end apart: 27, of which 11 were waited for; matrix products, arithmetic and copies ran while one was open for 6% of the time, Pallas kernels for 36%

profile of v11, /device:TPU:0, one launch (start us, length us, event | category | flops | bytes accessed | tf_op | source)
XLA Modules:
  0.0 164.8 jit_solution(4394602228823803319)
XLA Ops:
  0.0 2.4 %constant_dynamic-slice_fusion = (bf16[3,512,256]{2,1,0:T(8,128)(2,1)}, bf16[3,512,256]{2,1,0:T(8,128)(2,1)S(1)}) fusion(bf16[3,4096,256]{2,1,0:T(8,128)(2,1)} %refs_9_.1, s32[]{:T(128)S(6)} %select_n.7, s32[]{:T(128)S(6)} %select_n.6), kind=kLoop, calls=%fused_computation.4 | loop fusion | bytes 3145736 | tf_op jit(solution)/shard_map/dynamic_slice | solution.py:314
  2.4 5.0 %collective-permute-start = (bf16[3,512,256]{2,1,0:T(8,128)(2,1)S(1)}, bf16[3,512,256]{2,1,0:T(8,128)(2,1)S(1)}, u32[]{:S(2)}, u32[]{:S(2)}) collective-permute-start(bf16[3,512,256]{2,1,0:T(8,128)(2,1)S(1)} %get-tuple-element.136), channel_id=1, source_target_pairs={{0,3},{1,0},{2,1},{3,2},{4,7},{5,4},{6,5},{7,6},{8,11},{9,8},{10,9... | collective-permute-start | bytes 2359304 | tf_op jit(solution)/shard_map/ppermute | solution.py:345
  7.4 6.3 %copy.16 = bf16[4,2048,256]{1,2,0:T(8,128)(2,1)} copy(bf16[4,2048,256]{2,1,0:T(8,128)(2,1)} %param.13) | data formatting | bytes 8388608 | tf_op args[1]
  14.3 9.9 %collective-permute-done.refs_6_.refs_5_ = bf16[3,512,256]{2,1,0:T(8,128)(2,1)S(1)} collective-permute-done((bf16[3,512,256]{2,1,0:T(8,128)(2,1)S(1)}, bf16[3,512,256]{2,1,0:T(8,128)(2,1)S(1)}, u32[]{:S(2)}, u32[]{:S(2)}) %collective-permute-start) | collective-permute-done | bytes 786464 | tf_op jit(solution)/shard_map/ppermute | solution.py:345
  24.2 4.3 %collective-permute-start.3 = (bf16[3,512,256]{2,1,0:T(8,128)(2,1)S(1)}, bf16[3,512,256]{2,1,0:T(8,128)(2,1)S(1)}, u32[]{:S(2)}, u32[]{:S(2)}) collective-permute-start(bf16[3,512,256]{2,1,0:T(8,128)(2,1)S(1)} %collective-permute-done.refs_6_.refs_5_), channel_id=1, source_target_pairs={{0,3},{1,0},{2,1},{3,2},{4,7},{5,4},{6,5},{7,6},{8,11},{9,8},{10,9... | collective-permute-start | bytes 2359304 | tf_op jit(solution)/shard_map/ppermute | solution.py:348
  28.5 1.5 collective-permute-start.2
  30.0 1.5 collective-permute-start.1
  31.5 11.6 %shard_map.118 = (f32[16,256,256]{2,1,0:T(8,128)}, f32[4,256,256]{2,1,0:T(8,128)}) custom-call(s32[2]{0:T(128)} %pad_add_fusion.1.refs_0_, s32[2,8]{1,0:T(2,128)} %bitcast.18, s32[2,8]{1,0:T(2,128)} %bitcast.21, s32[2,8]{1,0:T(2,128)} %bitcast.24, s32[48]{0:T(128)} %refs_1_.3, s32[48]{0:T(128)} %refs_2_.3, s32[48]{0:T(128)} %refs_3_.3, s32[48]{0:T(128)} %refs_4_.5, ...), custom_call_target="tpu_custom_call" | custom-call | flops 17179869184 | bytes 10485760 | tf_op jit(solution)/shard_map/pallas_call | solution.py:211
  44.4 2.2 %collective-permute-done.2.refs_10_.refs_9_ = bf16[3,512,256]{2,1,0:T(8,128)(2,1)S(1)} collective-permute-done((bf16[3,512,256]{2,1,0:T(8,128)(2,1)S(1)}, bf16[3,512,256]{2,1,0:T(8,128)(2,1)S(1)}, u32[]{:S(2)}, u32[]{:S(2)}) %collective-permute-start.2) | collective-permute-done | bytes 786464 | tf_op jit(solution)/shard_map/ppermute | solution.py:269
  48.9 1.5 collective-permute-start.4
  50.4 1.9 %collective-permute-start.6 = (bf16[3,512,256]{2,1,0:T(8,128)(2,1)}, bf16[3,512,256]{2,1,0:T(8,128)(2,1)}, u32[]{:S(2)}, u32[]{:S(2)}) collective-permute-start(bf16[3,512,256]{2,1,0:T(8,128)(2,1)} %get-tuple-element.128), channel_id=1, source_target_pairs={{0,3},{1,0},{2,1},{3,2},{4,7},{5,4},{6,5},{7,6},{8,11},{9,8},{10,9... | collective-permute-start | bytes 2359304 | tf_op jit(solution)/shard_map/ppermute | solution.py:360
  52.8 16.8 %collective-permute-done.6.refs_12_.refs_11_ = bf16[3,512,256]{2,1,0:T(8,128)(2,1)} collective-permute-done((bf16[3,512,256]{2,1,0:T(8,128)(2,1)}, bf16[3,512,256]{2,1,0:T(8,128)(2,1)}, u32[]{:S(2)}, u32[]{:S(2)}) %collective-permute-start.6) | collective-permute-done | bytes 786464 | tf_op jit(solution)/shard_map/ppermute | solution.py:360
  72.1 1.5 collective-permute-start.13
  74.2 2.7 %collective-permute-start.11 = (bf16[3,512,256]{2,1,0:T(8,128)(2,1)S(1)}, bf16[3,512,256]{2,1,0:T(8,128)(2,1)}, u32[]{:S(2)}, u32[]{:S(2)}) collective-permute-start(bf16[3,512,256]{2,1,0:T(8,128)(2,1)S(1)} %collective-permute-done.3.refs_13_.refs_6_), channel_id=1, source_target_pairs={{0,3},{1,0},{2,1},{3,2},{4,7},{5,4},{6,5},{7,6},{8,11},{9,8},{10,9... | collective-permute-start | bytes 2359304 | tf_op jit(solution)/shard_map/ppermute | solution.py:366
  77.4 14.7 %shard_map.119.refs_24_ = f32[4,256,256]{2,1,0:T(8,128)} custom-call(s32[2]{0:T(128)} %pad_add_fusion.2.refs_0_, s32[48]{0:T(128)} %refs_1_.3, s32[48]{0:T(128)} %refs_2_.3, s32[48]{0:T(128)} %refs_3_.3, s32[48]{0:T(128)} %refs_4_.5, bf16[4,256,2048]{2,1,0:T(8,128)(2,1)} %bitcast.13, ...), custom_call_target="tpu_custom_call", output_to_operand_aliasing={{}: (14, {})} | custom-call | flops 12884901888 | bytes 10485760 | tf_op jit(solution)/shard_map/pallas_call | solution.py:211
  92.2 1.6 collective-permute-done.11.refs_16_.refs_5_
  94.3 1.5 collective-permute-start.21
  98.1 14.6 %shard_map.120.refs_13_ = f32[16,256,256]{2,1,0:T(8,128)} custom-call(s32[2]{0:T(128)} %pad_add_fusion.2.refs_0_, s32[2,8]{1,0:T(2,128)} %bitcast.19, s32[2,8]{1,0:T(2,128)} %bitcast.22, s32[2,8]{1,0:T(2,128)} %bitcast.25, bf16[4,256,2048]{2,1,0:T(8,128)(2,1)} %bitcast.14, bf16[3,512,256]{2,1,0:T(8,128)(2,1)} %copy-done.8, ...), custom_call_target="tpu_custom_call", output_to_operand_aliasing={{}: (23, {})} | custom-call | flops 4294967296 | bytes 16777216 | tf_op jit(solution)/shard_map/pallas_call | solution.py:211
  112.7 3.8 %collective-permute-done.22.refs_20_.refs_9_ = bf16[3,512,256]{2,1,0:T(8,128)(2,1)S(1)} collective-permute-done((bf16[3,512,256]{2,1,0:T(8,128)(2,1)S(1)}, bf16[3,512,256]{2,1,0:T(8,128)(2,1)S(1)}, u32[]{:S(2)}, u32[]{:S(2)}) %collective-permute-start.22) | collective-permute-done | bytes 786464 | tf_op jit(solution)/shard_map/ppermute | solution.py:380
  121.3 9.4 %shard_map.122 = bf16[16,256,256]{2,1,0:T(8,128)(2,1)} custom-call(s32[2]{0:T(128)} %pad_add_fusion.3.refs_0_, s32[2,8]{1,0:T(2,128)} %bitcast.20, s32[2,8]{1,0:T(2,128)} %bitcast.23, s32[2,8]{1,0:T(2,128)} %bitcast.26, bf16[4,256,2048]{2,1,0:T(8,128)(2,1)} %bitcast.15, bf16[3,512,256]{2,1,0:T(8,128)(2,1)} %collective-permute-done.11.refs_16_.refs_5_, ...), custom_call_target="tpu_custom_call" | custom-call | flops 4294967296 | bytes 10485760 | tf_op jit(solution)/shard_map/pallas_call | solution.py:211
  130.7 3.8 %all-to-all-start = ((bf16[8,2,256,256]{3,2,1,0:T(8,128)(2,1)}), bf16[8,2,256,256]{3,2,1,0:T(8,128)(2,1)S(1)}, u32[]{:S(2)}, u32[]{:S(2)}) async-start(bf16[8,2,256,256]{3,2,1,0:T(8,128)(2,1)} %bitcast.17), calls=%async_computation | async-start | bytes 4194304 | tf_op jit(solution)/shard_map/all_to_all | solution.py:385
  135.2 19.1 %shard_map.121.near_ref = f32[4,256,256]{2,1,0:T(8,128)} custom-call(s32[2]{0:T(128)} %pad_add_fusion.refs_0_, s32[48]{0:T(128)} %refs_1_.3, s32[48]{0:T(128)} %refs_2_.3, s32[48]{0:T(128)} %refs_3_.3, s32[48]{0:T(128)} %refs_4_.5, bf16[4,256,2048]{2,1,0:T(8,128)(2,1)} %bitcast.16, bf16[3,512,256]{2,1,0:T(8,128)(2,1)} %copy-done.6, ...), custom_call_target="tpu_custom_call", output_to_operand_aliasing={{}: (24, {})} | custom-call | flops 12884901888 | bytes 16777216 | tf_op jit(solution)/shard_map/pallas_call | solution.py:211
  154.3 6.9 %all-to-all-done.recv_ref = bf16[8,2,256,256]{3,2,1,0:T(8,128)(2,1)S(1)} async-done(((bf16[8,2,256,256]{3,2,1,0:T(8,128)(2,1)}), bf16[8,2,256,256]{3,2,1,0:T(8,128)(2,1)S(1)}, u32[]{:S(2)}, u32[]{:S(2)}) %all-to-all-start) | async-done | bytes 2097184 | tf_op jit(solution)/shard_map/all_to_all | solution.py:385
  162.4 2.4 %shard_map.123 = bf16[4,256,256]{2,1,0:T(8,128)(2,1)} custom-call(s32[2,8]{1,0:T(2,128)S(1)} %bitcast.11, f32[4,256,256]{2,1,0:T(8,128)S(1)} %copy-done, bf16[8,2,256,256]{3,2,1,0:T(8,128)(2,1)S(1)} %all-to-all-done.recv_ref, bf16[4,256,256]{2,1,0:T(8,128)(2,1)S(1)} %copy-done.1, bf16[4,256,256]{2,1,0:T(8,128)(2,1)S(1)} %copy-done.2), custom_call_target="tpu_custom_call" | custom-call | tf_op jit(solution)/shard_map/pallas_call | solution.py:258
  (88 shorter events, 17.5 us)
Async XLA Ops:
  2.4 21.8 %collective-permute-start = (bf16[3,512,256]{2,1,0:T(8,128)(2,1)S(1)}, bf16[3,512,256]{2,1,0:T(8,128)(2,1)S(1)}, u32[]{:S(2)}, u32[]{:S(2)}) collective-permute-start(bf16[3,512,256]{2,1,0:T(8,128)(2,1)S(1)} %get-tuple-element.136), channel_id=1, source_target_pairs={{0,3},{1,0},{2,1},{3,2},{4,7},{5,4},{6,5},{7,6},{8,11},{9,8},{10,9... | collective-permute-start | bytes 2359304 | tf_op jit(solution)/shard_map/ppermute | solution.py:345
  24.2 20.2 %collective-permute-start.3 = (bf16[3,512,256]{2,1,0:T(8,128)(2,1)S(1)}, bf16[3,512,256]{2,1,0:T(8,128)(2,1)S(1)}, u32[]{:S(2)}, u32[]{:S(2)}) collective-permute-start(bf16[3,512,256]{2,1,0:T(8,128)(2,1)S(1)} %collective-permute-done.refs_6_.refs_5_), channel_id=1, source_target_pairs={{0,3},{1,0},{2,1},{3,2},{4,7},{5,4},{6,5},{7,6},{8,11},{9,8},{10,9... | collective-permute-start | bytes 2359304 | tf_op jit(solution)/shard_map/ppermute | solution.py:348
  28.5 18.1 %collective-permute-start.2 = (bf16[3,512,256]{2,1,0:T(8,128)(2,1)S(1)}, bf16[3,512,256]{2,1,0:T(8,128)(2,1)S(1)}, u32[]{:S(2)}, u32[]{:S(2)}) collective-permute-start(bf16[3,512,256]{2,1,0:T(8,128)(2,1)S(1)} %collective-permute-done.refs_6_.refs_5_), channel_id=1, source_target_pairs={{0,16},{4,20},{8,24},{12,28},{16,0},{20,4},{24,8},{28,12},{1,17},{... | collective-permute-start | bytes 2359304 | tf_op jit(solution)/shard_map/ppermute | solution.py:269
  30.0 17.8 %collective-permute-start.1 = (bf16[3,512,256]{2,1,0:T(8,128)(2,1)S(1)}, bf16[3,512,256]{2,1,0:T(8,128)(2,1)S(1)}, u32[]{:S(2)}, u32[]{:S(2)}) collective-permute-start(bf16[3,512,256]{2,1,0:T(8,128)(2,1)S(1)} %collective-permute-done.refs_6_.refs_5_), channel_id=1, source_target_pairs={{0,8},{4,12},{8,0},{12,4},{16,24},{20,28},{24,16},{28,20},{1,9},{5... | collective-permute-start | bytes 2359304 | tf_op jit(solution)/shard_map/ppermute | solution.py:269
  47.9 4.5 %collective-permute-start.7 = (bf16[3,512,256]{2,1,0:T(8,128)(2,1)S(1)}, bf16[3,512,256]{2,1,0:T(8,128)(2,1)S(1)}, u32[]{:S(2)}, u32[]{:S(2)}) collective-permute-start(bf16[3,512,256]{2,1,0:T(8,128)(2,1)S(1)} %collective-permute-done.refs_6_.refs_5_), channel_id=1, source_target_pairs={{0,4},{4,0},{8,12},{12,8},{16,20},{20,16},{24,28},{28,24},{1,5},{5... | collective-permute-start | bytes 2359304 | tf_op jit(solution)/shard_map/ppermute | solution.py:269
  47.9 4.5 %collective-permute-start.9 = (bf16[3,512,256]{2,1,0:T(8,128)(2,1)S(1)}, bf16[3,512,256]{2,1,0:T(8,128)(2,1)S(1)}, u32[]{:S(2)}, u32[]{:S(2)}) collective-permute-start(bf16[3,512,256]{2,1,0:T(8,128)(2,1)S(1)} %collective-permute-done.2.refs_10_.refs_9_), channel_id=1, source_target_pairs={{0,4},{4,0},{8,12},{12,8},{16,20},{20,16},{24,28},{28,24},{1,5},{5... | collective-permute-start | bytes 2359304 | tf_op jit(solution)/shard_map/ppermute | solution.py:269
  48.4 21.3 %collective-permute-start.5 = (bf16[3,512,256]{2,1,0:T(8,128)(2,1)S(1)}, bf16[3,512,256]{2,1,0:T(8,128)(2,1)S(1)}, u32[]{:S(2)}, u32[]{:S(2)}) collective-permute-start(bf16[3,512,256]{2,1,0:T(8,128)(2,1)S(1)} %collective-permute-done.3.refs_13_.refs_6_), channel_id=1, source_target_pairs={{0,16},{4,20},{8,24},{12,28},{16,0},{20,4},{24,8},{28,12},{1,17},{... | collective-permute-start | bytes 2359304 | tf_op jit(solution)/shard_map/ppermute | solution.py:269
  48.9 20.8 %collective-permute-start.4 = (bf16[3,512,256]{2,1,0:T(8,128)(2,1)S(1)}, bf16[3,512,256]{2,1,0:T(8,128)(2,1)S(1)}, u32[]{:S(2)}, u32[]{:S(2)}) collective-permute-start(bf16[3,512,256]{2,1,0:T(8,128)(2,1)S(1)} %collective-permute-done.3.refs_13_.refs_6_), channel_id=1, source_target_pairs={{0,8},{4,12},{8,0},{12,4},{16,24},{20,28},{24,16},{28,20},{1,9},{5... | collective-permute-start | bytes 2359304 | tf_op jit(solution)/shard_map/ppermute | solution.py:269
  50.4 19.3 %collective-permute-start.6 = (bf16[3,512,256]{2,1,0:T(8,128)(2,1)}, bf16[3,512,256]{2,1,0:T(8,128)(2,1)}, u32[]{:S(2)}, u32[]{:S(2)}) collective-permute-start(bf16[3,512,256]{2,1,0:T(8,128)(2,1)} %get-tuple-element.128), channel_id=1, source_target_pairs={{0,3},{1,0},{2,1},{3,2},{4,7},{5,4},{6,5},{7,6},{8,11},{9,8},{10,9... | collective-permute-start | bytes 2359304 | tf_op jit(solution)/shard_map/ppermute | solution.py:360
  52.3 17.3 %collective-permute-start.8 = (bf16[3,512,256]{2,1,0:T(8,128)(2,1)S(1)}, bf16[3,512,256]{2,1,0:T(8,128)(2,1)S(1)}, u32[]{:S(2)}, u32[]{:S(2)}) collective-permute-start(bf16[3,512,256]{2,1,0:T(8,128)(2,1)S(1)} %collective-permute-done.1.refs_8_.refs_7_), channel_id=1, source_target_pairs={{0,4},{4,0},{8,12},{12,8},{16,20},{20,16},{24,28},{28,24},{1,5},{5... | collective-permute-start | bytes 2359304 | tf_op jit(solution)/shard_map/ppermute | solution.py:269
  52.4 17.3 %collective-permute-start.10 = (bf16[3,512,256]{2,1,0:T(8,128)(2,1)S(1)}, bf16[3,512,256]{2,1,0:T(8,128)(2,1)S(1)}, u32[]{:S(2)}, u32[]{:S(2)}) collective-permute-start(bf16[3,512,256]{2,1,0:T(8,128)(2,1)S(1)} %collective-permute-done.3.refs_13_.refs_6_), channel_id=1, source_target_pairs={{0,4},{4,0},{8,12},{12,8},{16,20},{20,16},{24,28},{28,24},{1,5},{5... | collective-permute-start | bytes 2359304 | tf_op jit(solution)/shard_map/ppermute | solution.py:269
  70.6 6.3 %collective-permute-start.14 = (bf16[3,512,256]{2,1,0:T(8,128)(2,1)}, bf16[3,512,256]{2,1,0:T(8,128)(2,1)}, u32[]{:S(2)}, u32[]{:S(2)}) collective-permute-start(bf16[3,512,256]{2,1,0:T(8,128)(2,1)} %collective-permute-done.6.refs_12_.refs_11_), channel_id=1, source_target_pairs={{0,4},{4,0},{8,12},{12,8},{16,20},{20,16},{24,28},{28,24},{1,5},{5... | collective-permute-start | bytes 2359304 | tf_op jit(solution)/shard_map/ppermute | solution.py:269
  72.1 20.0 %collective-permute-start.13 = (bf16[3,256,256]{2,1,0:T(8,128)(2,1)}, bf16[3,256,256]{2,1,0:T(8,128)(2,1)}, u32[]{:S(2)}, u32[]{:S(2)}) collective-permute-start(bf16[3,256,256]{2,1,0:T(8,128)(2,1)} %slice.7), channel_id=1, source_target_pairs={{0,16},{4,20},{8,24},{12,28},{16,0},{20,4},{24,8},{28,12},{1,17},{... | collective-permute-start | bytes 1179656 | tf_op jit(solution)/shard_map/ppermute | solution.py:269
  73.6 18.5 %collective-permute-start.12 = (bf16[3,256,256]{2,1,0:T(8,128)(2,1)S(1)}, bf16[3,256,256]{2,1,0:T(8,128)(2,1)}, u32[]{:S(2)}, u32[]{:S(2)}) collective-permute-start(bf16[3,256,256]{2,1,0:T(8,128)(2,1)S(1)} %slice.6), channel_id=1, source_target_pairs={{0,8},{4,12},{8,0},{12,4},{16,24},{20,28},{24,16},{28,20},{1,9},{5... | collective-permute-start | bytes 1179656 | tf_op jit(solution)/shard_map/ppermute | solution.py:269
  74.2 19.6 %collective-permute-start.11 = (bf16[3,512,256]{2,1,0:T(8,128)(2,1)S(1)}, bf16[3,512,256]{2,1,0:T(8,128)(2,1)}, u32[]{:S(2)}, u32[]{:S(2)}) collective-permute-start(bf16[3,512,256]{2,1,0:T(8,128)(2,1)S(1)} %collective-permute-done.3.refs_13_.refs_6_), channel_id=1, source_target_pairs={{0,3},{1,0},{2,1},{3,2},{4,7},{5,4},{6,5},{7,6},{8,11},{9,8},{10,9... | collective-permute-start | bytes 2359304 | tf_op jit(solution)/shard_map/ppermute | solution.py:366
  76.9 16.9 %collective-permute-start.15 = (bf16[3,512,256]{2,1,0:T(8,128)(2,1)S(1)}, bf16[3,512,256]{2,1,0:T(8,128)(2,1)S(1)}, u32[]{:S(2)}, u32[]{:S(2)}) collective-permute-start(bf16[3,512,256]{2,1,0:T(8,128)(2,1)S(1)} %collective-permute-done.4.refs_15_.refs_8_), channel_id=1, source_target_pairs={{0,4},{4,0},{8,12},{12,8},{16,20},{20,16},{24,28},{28,24},{1,5},{5... | collective-permute-start | bytes 2359304 | tf_op jit(solution)/shard_map/ppermute | solution.py:269
  76.9 16.9 %collective-permute-start.16 = (bf16[3,512,256]{2,1,0:T(8,128)(2,1)S(1)}, bf16[3,512,256]{2,1,0:T(8,128)(2,1)S(1)}, u32[]{:S(2)}, u32[]{:S(2)}) collective-permute-start(bf16[3,512,256]{2,1,0:T(8,128)(2,1)S(1)} %collective-permute-done.5.refs_16_.refs_9_), channel_id=1, source_target_pairs={{0,4},{4,0},{8,12},{12,8},{16,20},{20,16},{24,28},{28,24},{1,5},{5... | collective-permute-start | bytes 2359304 | tf_op jit(solution)/shard_map/ppermute | solution.py:269
  93.8 3.6 %collective-permute-start.17 = (bf16[3,256,256]{2,1,0:T(8,128)(2,1)}, bf16[3,256,256]{2,1,0:T(8,128)(2,1)S(1)}, u32[]{:S(2)}, u32[]{:S(2)}) collective-permute-start(bf16[3,256,256]{2,1,0:T(8,128)(2,1)} %collective-permute-done.12.refs_19_.refs_12_), channel_id=1, source_target_pairs={{0,4},{4,0},{8,12},{12,8},{16,20},{20,16},{24,28},{28,24},{1,5},{5... | collective-permute-start | bytes 1179656 | tf_op jit(solution)/shard_map/ppermute | solution.py:269
  94.3 22.2 %collective-permute-start.22 = (bf16[3,512,256]{2,1,0:T(8,128)(2,1)S(1)}, bf16[3,512,256]{2,1,0:T(8,128)(2,1)S(1)}, u32[]{:S(2)}, u32[]{:S(2)}) collective-permute-start(bf16[3,512,256]{2,1,0:T(8,128)(2,1)S(1)} %copy-done.16), channel_id=1, source_target_pairs={{3,0},{0,1},{1,2},{2,3},{7,4},{4,5},{5,6},{6,7},{11,8},{8,9},{9,10... | collective-permute-start | bytes 2359304 | tf_op jit(solution)/shard_map/ppermute | solution.py:380
  94.3 22.2 %collective-permute-start.21 = (bf16[3,512,256]{2,1,0:T(8,128)(2,1)}, bf16[3,512,256]{2,1,0:T(8,128)(2,1)S(1)}, u32[]{:S(2)}, u32[]{:S(2)}) collective-permute-start(bf16[3,512,256]{2,1,0:T(8,128)(2,1)} %collective-permute-done.11.refs_16_.refs_5_), channel_id=1, source_target_pairs={{0,16},{4,20},{8,24},{12,28},{16,0},{20,4},{24,8},{28,12},{1,17},{... | collective-permute-start | bytes 2359304 | tf_op jit(solution)/shard_map/ppermute | solution.py:269
  95.9 20.7 %collective-permute-start.20 = (bf16[3,512,256]{2,1,0:T(8,128)(2,1)}, bf16[3,512,256]{2,1,0:T(8,128)(2,1)S(1)}, u32[]{:S(2)}, u32[]{:S(2)}) collective-permute-start(bf16[3,512,256]{2,1,0:T(8,128)(2,1)} %collective-permute-done.11.refs_16_.refs_5_), channel_id=1, source_target_pairs={{0,8},{4,12},{8,0},{12,4},{16,24},{20,28},{24,16},{28,20},{1,9},{5... | collective-permute-start | bytes 2359304 | tf_op jit(solution)/shard_map/ppermute | solution.py:269
  97.4 20.5 %collective-permute-start.19 = (bf16[3,512,256]{2,1,0:T(8,128)(2,1)}, bf16[3,512,256]{2,1,0:T(8,128)(2,1)S(1)}, u32[]{:S(2)}, u32[]{:S(2)}) collective-permute-start(bf16[3,512,256]{2,1,0:T(8,128)(2,1)} %collective-permute-done.11.refs_16_.refs_5_), channel_id=1, source_target_pairs={{0,4},{4,0},{8,12},{12,8},{16,20},{20,16},{24,28},{28,24},{1,5},{5... | collective-permute-start | bytes 2359304 | tf_op jit(solution)/shard_map/ppermute | solution.py:269
  117.1 4.2 %collective-permute-start.25 = (bf16[3,512,256]{2,1,0:T(8,128)(2,1)S(1)}, bf16[3,512,256]{2,1,0:T(8,128)(2,1)}, u32[]{:S(2)}, u32[]{:S(2)}) collective-permute-start(bf16[3,512,256]{2,1,0:T(8,128)(2,1)S(1)} %collective-permute-done.22.refs_20_.refs_9_), channel_id=1, source_target_pairs={{0,4},{4,0},{8,12},{12,8},{16,20},{20,16},{24,28},{28,24},{1,5},{5... | collective-permute-start | bytes 2359304 | tf_op jit(solution)/shard_map/ppermute | solution.py:269
  130.7 30.4 %all-to-all-start = ((bf16[8,2,256,256]{3,2,1,0:T(8,128)(2,1)}), bf16[8,2,256,256]{3,2,1,0:T(8,128)(2,1)S(1)}, u32[]{:S(2)}, u32[]{:S(2)}) async-start(bf16[8,2,256,256]{3,2,1,0:T(8,128)(2,1)} %bitcast.17), calls=%async_computation | async-start | bytes 4194304 | tf_op jit(solution)/shard_map/all_to_all | solution.py:385
  (25 other events, 354.8 us)

commit v12 on v11

--- a/solution.py
+++ b/solution.py
@@ -78,7 +78,7 @@
     pieces = [refs.pop(0) for _ in places]
     before = [refs.pop(0) for _ in range((bool(served) + bool(local)) if begun else 0)]
     outs = [refs.pop(0) for _ in range(bool(served) + bool(local))]
-    table, hist, acc, tasks, counts, used, sems, ends, served_sems = refs
+    table, hist, acc, prior, tasks, counts, used, sems, ends, served_sems = refs
     base, group = where[0], where[1]
     classes, _, panels = table.shape
     steps = hist.shape[2] // panels
@@ -96,7 +96,7 @@
             pltpu.make_async_copy(
                 piece.at[k], table.at[k, pl.ds(start, piece.shape[1]), :], sems.at[k]
             ).start()
-    if not begun:
+    if not begun or narrow:
         acc[...] = jnp.zeros_like(acc)
     ends_of_table = jnp.zeros((margin, panels), table.dtype)
     for k in range(classes):
@@ -109,6 +109,10 @@
         ends_of = (acc.at[i], outs[0].at[i]) if back else (before[0].at[i], acc.at[i])
         return pltpu.make_async_copy(*ends_of, served_sems.at[i])
 
+    prior_copy = pltpu.make_async_copy(before[0], prior, ends.at[1]) if narrow else None
+    if narrow:
+        prior_copy.start()
+
     if served:
         slots, peers = served_refs[0].shape
 
@@ -119,10 +123,9 @@
                 place = i * slots + c
                 pair = (source, klass, lag, place)
                 touched = list_task(base, span, total, steps, phased, pair, tasks, counts)
-                needed = touched | narrow
                 used[place] = jnp.where(touched, 1, 0)
-                if begun:
-                    @pl.when(needed)
+                if begun and not narrow:
+                    @pl.when(touched)
                     def _():
                         served_copy(place, False).start()
 
@@ -136,10 +139,10 @@
     pltpu.make_async_copy(hist_ref, hist, ends.at[0]).wait()
     if local and begun:
         pltpu.make_async_copy(before[-1], near, ends.at[1]).wait()
-    if served and begun:
+    if served and begun and not narrow:
         @pl.loop(0, served)
         def _(i):
-            @pl.when((used[i] != 0) | narrow)
+            @pl.when(used[i] != 0)
             def _():
                 served_copy(i, False).wait()
 
@@ -164,7 +167,8 @@
         run_lists(0)
 
     if narrow:
-        outs[0][...] = acc[pl.ds(0, served)].astype(outs[0].dtype)
+        prior_copy.wait()
+        outs[0][...] = (prior[...] + acc[pl.ds(0, served)]).astype(outs[0].dtype)
         return
     if local:
         pltpu.make_async_copy(near, outs[-1], ends.at[1]).start()
@@ -217,6 +221,7 @@
             pltpu.VMEM((classes, depth_of_table, panels), jnp.bfloat16),
             pltpu.VMEM(hist_t.shape, hist_t.dtype),
             pltpu.VMEM((places + targets + 1, excite, panels), jnp.float32),
+            pltpu.VMEM((places if narrow else 1, excite, panels), jnp.float32),
             pltpu.SMEM((2 * classes, pairs + UNROLL), jnp.int32),
             pltpu.SMEM((2 * classes,), jnp.int32),
             pltpu.SMEM((max(places, 1),), jnp.int32),
@@ -236,10 +241,8 @@
     )(*operands, *wide, *before)
 
 
-def update_kernel(target_ref, near_ref, recv_ref, inverse_ref, incident_ref, out_ref, total, sem):
-    copy = pltpu.make_async_copy(near_ref, total, sem)
-    copy.start()
-    copy.wait()
+def update_kernel(target_ref, near_ref, recv_ref, inverse_ref, incident_ref, out_ref, total):
+    total[...] = near_ref[...]
     slots, peers = target_ref.shape
 
     @pl.loop(0, peers)
@@ -258,10 +261,10 @@
     return pl.pallas_call(
         update_kernel,
         out_shape=jax.ShapeDtypeStruct(incident.shape, jnp.bfloat16),
-        in_specs=[SMEM, HBM] + [VMEM] * 3,
+        in_specs=[SMEM] + [VMEM] * 4,
         out_specs=VMEM,
-        scratch_shapes=[pltpu.VMEM(near.shape, jnp.float32), pltpu.SemaphoreType.DMA],
-        compiler_params=pltpu.CompilerParams(vmem_limit_bytes=32 * MIB),
+        scratch_shapes=[pltpu.VMEM(near.shape, jnp.float32)],
+        compiler_params=pltpu.CompilerParams(vmem_limit_bytes=58 * MIB),
     )(target, near, recv, inverse, incident)
 
 
@@ -321,7 +324,6 @@
         )[0]
 
     own = part(group)
-    corner = part(group ^ 6)
 
     def neighbours(value):
         masks, held = upper(value, peers)
@@ -343,7 +345,8 @@
         return [(m ^ 6, 0, v) for m, v in zip(masks, held)]
 
     own = lax.ppermute(own, "lag", ring)
-    own, hist_t = tie(own, hist_t)
+    own, hist_t, opposite = tie(own, hist_t, group ^ 6)
+    corner = part(opposite)
     trio = neighbours(own)
     own = lax.ppermute(own, "lag", ring)
     served_sums, near = window_sums(
@@ -364,10 +367,10 @@
     rounds = [found + diagonal]
     for step in range(2, lanes - 1):
         own = lax.ppermute(own, "lag", ring)
+        if step == 2:
+            rounds[0], across, along = tie(rounds[0], across, along)
         turned = [(m ^ 2, 0, swap(v[:, :half], 2, peers)) for m, _, v in along]
         turned += [(m ^ 4, half, swap(v[:, half:], 4, peers)) for m, _, v in across]
-        if step == 2:
-            rounds[0], across, along = tie(rounds[0], across, along)
         found = held + with_other_core(across + along, peers)
         near = add_shards(step - 1, step, (), local, near)
         own, turned, near, corner, found = tie(own, turned, near, corner, found)

time: 165 us -> 165 us (level)
  starting transfers between devices: 30.7 us -> 28.4 us
  waiting for transfers between devices: 47.2 us -> 45 us
  local copies, waits for them, and re-layouts: 12.3 us -> 14.2 us
    ppermute x21, starting transfers between devices: 12.9 us -> 9.54 us  [swap(): return lax.ppermute(value, 'grp', [(i, i ^ bit) for i in range(peers)])]
    ppermute x3, waiting for transfers between devices: 12.8 us -> 10.2 us  [per_device(): own = lax.ppermute(own, 'lag', ring)]
    unnamed x45 -> x37, local copies, waits for them, and re-layouts: 9.1 us -> 11 us
  transfers between devices with their start and end apart: 27 -> 27, of which waited for: 11 -> 12; matrix products, arithmetic and copies ran while one was open for 6% -> 7% of each run, Pallas kernels for 36% -> 37%
where the time goes in v12:
time: 165 us; the launch traced here: 163 us
  Pallas kernels  73 us (44%)
  waiting for transfers between devices  45 us (27%)
  starting transfers between devices  28.4 us (17%)
  local copies, waits for them, and re-layouts  14.2 us (9%)
  other arithmetic  2.5 us (2%)
    pallas_call x5, Pallas kernels, window_sums(): pl.pallas_call(functools.partial(window_kernel, config), out_shape=outs,...  69 us
    ppermute x1, waiting for transfers between devices, per_device(): diagonal = lax.ppermute(corner, 'lag', ring)  16.2 us
    ppermute x3, starting transfers between devices, per_device(): own = lax.ppermute(own, 'lag', ring)  13.3 us
    unnamed x37, local copies, waits for them, and re-layouts  11 us
    ppermute x3, waiting for transfers between devices, per_device(): own = lax.ppermute(own, 'lag', ring)  10.2 us
    ppermute x21, starting transfers between devices, swap(): return lax.ppermute(value, 'grp', [(i, i ^ bit) for i in range(peers)])  9.54 us
    all_to_all x1, waiting for transfers between devices, per_device(): lax.all_to_all(contribution.reshape(peers, slots, *contribution.shape[1:]...  7.66 us
    ppermute x21, waiting for transfers between devices, swap(): return lax.ppermute(value, 'grp', [(i, i ^ bit) for i in range(peers)])  5.68 us
  transfers between devices with their start and end apart: 27, of which 12 were waited for; matrix products, arithmetic and copies ran while one was open for 7% of the time, Pallas kernels for 37%

profile of v12, /device:TPU:0, one launch (start us, length us, event | category | flops | bytes accessed | tf_op | source)
XLA Modules:
  0.0 163.3 jit_solution(6788555233404898194)
XLA Ops:
  0.0 1.2 constant_dynamic-slice_fusion.1
  1.2 5.1 %collective-permute-start = (bf16[3,512,256]{2,1,0:T(8,128)(2,1)S(1)}, bf16[3,512,256]{2,1,0:T(8,128)(2,1)}, u32[]{:S(2)}, u32[]{:S(2)}) collective-permute-start(bf16[3,512,256]{2,1,0:T(8,128)(2,1)S(1)} %constant_dynamic-slice_fusion.1), channel_id=1, source_target_pairs={{0,3},{1,0},{2,1},{3,2},{4,7},{5,4},{6,5},{7,6},{8,11},{9,8},{10,9... | collective-permute-start | bytes 2359304 | tf_op jit(solution)/shard_map/ppermute | solution.py:347
  6.3 6.3 %copy.16 = bf16[4,2048,256]{1,2,0:T(8,128)(2,1)} copy(bf16[4,2048,256]{2,1,0:T(8,128)(2,1)} %param.13) | data formatting | bytes 8388608 | tf_op args[1]
  13.2 9.9 %collective-permute-done.refs_6_.refs_5_ = bf16[3,512,256]{2,1,0:T(8,128)(2,1)} collective-permute-done((bf16[3,512,256]{2,1,0:T(8,128)(2,1)S(1)}, bf16[3,512,256]{2,1,0:T(8,128)(2,1)}, u32[]{:S(2)}, u32[]{:S(2)}) %collective-permute-start) | collective-permute-done | bytes 786464 | tf_op jit(solution)/shard_map/ppermute | solution.py:347
  23.1 4.4 %collective-permute-start.3 = (bf16[3,512,256]{2,1,0:T(8,128)(2,1)}, bf16[3,512,256]{2,1,0:T(8,128)(2,1)S(1)}, u32[]{:S(2)}, u32[]{:S(2)}) collective-permute-start(bf16[3,512,256]{2,1,0:T(8,128)(2,1)} %collective-permute-done.refs_6_.refs_5_), channel_id=1, source_target_pairs={{0,3},{1,0},{2,1},{3,2},{4,7},{5,4},{6,5},{7,6},{8,11},{9,8},{10,9... | collective-permute-start | bytes 2359304 | tf_op jit(solution)/shard_map/ppermute | solution.py:351
  27.5 1.5 collective-permute-start.2
  29.0 1.5 collective-permute-start.1
  30.5 14.0 %shard_map.118 = (f32[16,256,256]{2,1,0:T(8,128)}, f32[4,256,256]{2,1,0:T(8,128)}) custom-call(s32[2]{0:T(128)} %pad_add_fusion.1.refs_0_, s32[2,8]{1,0:T(2,128)} %bitcast.17, s32[2,8]{1,0:T(2,128)} %bitcast.20, s32[2,8]{1,0:T(2,128)} %bitcast.23, s32[48]{0:T(128)} %refs_1_.3, s32[48]{0:T(128)} %refs_2_.3, s32[48]{0:T(128)} %refs_3_.3, s32[48]{0:T(128)} %refs_4_.5, ...), custom_call_target="tpu_custom_call" | custom-call | flops 17179869184 | bytes 10485760 | tf_op jit(solution)/shard_map/pallas_call | solution.py:215
  44.5 1.2 constant_dynamic-slice_fusion
  45.9 1.1 collective-permute-done.1.refs_8_.refs_7_
  48.1 1.5 collective-permute-start.4
  49.6 1.9 %collective-permute-start.6 = (bf16[3,512,256]{2,1,0:T(8,128)(2,1)S(1)}, bf16[3,512,256]{2,1,0:T(8,128)(2,1)}, u32[]{:S(2)}, u32[]{:S(2)}) collective-permute-start(bf16[3,512,256]{2,1,0:T(8,128)(2,1)S(1)} %constant_dynamic-slice_fusion), channel_id=1, source_target_pairs={{0,3},{1,0},{2,1},{3,2},{4,7},{5,4},{6,5},{7,6},{8,11},{9,8},{10,9... | collective-permute-start | bytes 2359304 | tf_op jit(solution)/shard_map/ppermute | solution.py:363
  52.4 16.2 %collective-permute-done.6.refs_12_.refs_11_ = bf16[3,512,256]{2,1,0:T(8,128)(2,1)} collective-permute-done((bf16[3,512,256]{2,1,0:T(8,128)(2,1)S(1)}, bf16[3,512,256]{2,1,0:T(8,128)(2,1)}, u32[]{:S(2)}, u32[]{:S(2)}) %collective-permute-start.6) | collective-permute-done | bytes 786464 | tf_op jit(solution)/shard_map/ppermute | solution.py:363
  71.0 3.8 %collective-permute-start.11 = (bf16[3,512,256]{2,1,0:T(8,128)(2,1)S(1)}, bf16[3,512,256]{2,1,0:T(8,128)(2,1)}, u32[]{:S(2)}, u32[]{:S(2)}) collective-permute-start(bf16[3,512,256]{2,1,0:T(8,128)(2,1)S(1)} %collective-permute-done.3.refs_13_.refs_6_), channel_id=1, source_target_pairs={{0,3},{1,0},{2,1},{3,2},{4,7},{5,4},{6,5},{7,6},{8,11},{9,8},{10,9... | collective-permute-start | bytes 2359304 | tf_op jit(solution)/shard_map/ppermute | solution.py:369
  77.3 14.7 %shard_map.119.refs_24_ = f32[4,256,256]{2,1,0:T(8,128)} custom-call(s32[2]{0:T(128)} %pad_add_fusion.2.refs_0_, s32[48]{0:T(128)} %refs_1_.3, s32[48]{0:T(128)} %refs_2_.3, s32[48]{0:T(128)} %refs_3_.3, s32[48]{0:T(128)} %refs_4_.5, bf16[4,256,2048]{2,1,0:T(8,128)(2,1)} %bitcast.12, ...), custom_call_target="tpu_custom_call", output_to_operand_aliasing={{}: (14, {})} | custom-call | flops 12884901888 | bytes 10485760 | tf_op jit(solution)/shard_map/pallas_call | solution.py:215
  95.7 14.1 %shard_map.120.refs_13_ = f32[16,256,256]{2,1,0:T(8,128)} custom-call(s32[2]{0:T(128)} %pad_add_fusion.2.refs_0_, s32[2,8]{1,0:T(2,128)} %bitcast.18, s32[2,8]{1,0:T(2,128)} %bitcast.21, s32[2,8]{1,0:T(2,128)} %bitcast.24, bf16[4,256,2048]{2,1,0:T(8,128)(2,1)} %bitcast.13, ...), custom_call_target="tpu_custom_call", output_to_operand_aliasing={{}: (23, {})} | custom-call | flops 4294967296 | bytes 16777216 | tf_op jit(solution)/shard_map/pallas_call | solution.py:215
  109.8 5.3 %collective-permute-done.22.refs_20_.refs_9_ = bf16[3,512,256]{2,1,0:T(8,128)(2,1)S(1)} collective-permute-done((bf16[3,512,256]{2,1,0:T(8,128)(2,1)S(1)}, bf16[3,512,256]{2,1,0:T(8,128)(2,1)S(1)}, u32[]{:S(2)}, u32[]{:S(2)}) %collective-permute-start.22) | collective-permute-done | bytes 786464 | tf_op jit(solution)/shard_map/ppermute | solution.py:383
  116.4 1.2 collective-permute-done.23.refs_21_.refs_10_
  119.9 7.9 %shard_map.122 = bf16[16,256,256]{2,1,0:T(8,128)(2,1)} custom-call(s32[2]{0:T(128)} %pad_add_fusion.3.refs_0_, s32[2,8]{1,0:T(2,128)} %bitcast.19, s32[2,8]{1,0:T(2,128)} %bitcast.22, s32[2,8]{1,0:T(2,128)} %bitcast.25, bf16[4,256,2048]{2,1,0:T(8,128)(2,1)} %bitcast.14, bf16[3,512,256]{2,1,0:T(8,128)(2,1)} %collective-permute-done.11.refs_16_.refs_5_, ...), custom_call_target="tpu_custom_call" | custom-call | flops 4294967296 | bytes 10485760 | tf_op jit(solution)/shard_map/pallas_call | solution.py:215
  127.8 3.6 %all-to-all-start = ((bf16[8,2,256,256]{3,2,1,0:T(8,128)(2,1)}), bf16[8,2,256,256]{3,2,1,0:T(8,128)(2,1)S(1)}, u32[]{:S(2)}, u32[]{:S(2)}) async-start(bf16[8,2,256,256]{3,2,1,0:T(8,128)(2,1)} %bitcast.16), calls=%async_computation | async-start | bytes 4194304 | tf_op jit(solution)/shard_map/all_to_all | solution.py:388
  132.1 18.3 %shard_map.121.near_ref = f32[4,256,256]{2,1,0:T(8,128)} custom-call(s32[2]{0:T(128)} %pad_add_fusion.refs_0_, s32[48]{0:T(128)} %refs_1_.3, s32[48]{0:T(128)} %refs_2_.3, s32[48]{0:T(128)} %refs_3_.3, s32[48]{0:T(128)} %refs_4_.5, bf16[4,256,2048]{2,1,0:T(8,128)(2,1)} %bitcast.15, bf16[3,512,256]{2,1,0:T(8,128)(2,1)} %copy-done.3, ...), custom_call_target="tpu_custom_call", output_to_operand_aliasing={{}: (24, {})} | custom-call | flops 12884901888 | bytes 16777216 | tf_op jit(solution)/shard_map/pallas_call | solution.py:215
  150.3 7.7 %all-to-all-done.recv_ref = bf16[8,2,256,256]{3,2,1,0:T(8,128)(2,1)S(1)} async-done(((bf16[8,2,256,256]{3,2,1,0:T(8,128)(2,1)}), bf16[8,2,256,256]{3,2,1,0:T(8,128)(2,1)S(1)}, u32[]{:S(2)}, u32[]{:S(2)}) %all-to-all-start) | async-done | bytes 2097184 | tf_op jit(solution)/shard_map/all_to_all | solution.py:388
  158.0 1.3 copy-done
  159.3 4.0 %shard_map.123 = bf16[4,256,256]{2,1,0:T(8,128)(2,1)} custom-call(s32[2,8]{1,0:T(2,128)} %bitcast.26, f32[4,256,256]{2,1,0:T(8,128)} %shard_map.121.near_ref, bf16[8,2,256,256]{3,2,1,0:T(8,128)(2,1)} %copy-done, bf16[4,256,256]{2,1,0:T(8,128)(2,1)} %inverse_ref.1, bf16[4,256,256]{2,1,0:T(8,128)(2,1)} %incident_ref.1), custom_call_target="tpu_custom_call" | custom-call | tf_op jit(solution)/shard_map/pallas_call | solution.py:261
  (81 shorter events, 15.4 us)
Async XLA Ops:
  1.2 21.9 %collective-permute-start = (bf16[3,512,256]{2,1,0:T(8,128)(2,1)S(1)}, bf16[3,512,256]{2,1,0:T(8,128)(2,1)}, u32[]{:S(2)}, u32[]{:S(2)}) collective-permute-start(bf16[3,512,256]{2,1,0:T(8,128)(2,1)S(1)} %constant_dynamic-slice_fusion.1), channel_id=1, source_target_pairs={{0,3},{1,0},{2,1},{3,2},{4,7},{5,4},{6,5},{7,6},{8,11},{9,8},{10,9... | collective-permute-start | bytes 2359304 | tf_op jit(solution)/shard_map/ppermute | solution.py:347
  23.1 22.7 %collective-permute-start.3 = (bf16[3,512,256]{2,1,0:T(8,128)(2,1)}, bf16[3,512,256]{2,1,0:T(8,128)(2,1)S(1)}, u32[]{:S(2)}, u32[]{:S(2)}) collective-permute-start(bf16[3,512,256]{2,1,0:T(8,128)(2,1)} %collective-permute-done.refs_6_.refs_5_), channel_id=1, source_target_pairs={{0,3},{1,0},{2,1},{3,2},{4,7},{5,4},{6,5},{7,6},{8,11},{9,8},{10,9... | collective-permute-start | bytes 2359304 | tf_op jit(solution)/shard_map/ppermute | solution.py:351
  27.5 18.4 %collective-permute-start.2 = (bf16[3,512,256]{2,1,0:T(8,128)(2,1)}, bf16[3,512,256]{2,1,0:T(8,128)(2,1)}, u32[]{:S(2)}, u32[]{:S(2)}) collective-permute-start(bf16[3,512,256]{2,1,0:T(8,128)(2,1)} %collective-permute-done.refs_6_.refs_5_), channel_id=1, source_target_pairs={{0,16},{4,20},{8,24},{12,28},{16,0},{20,4},{24,8},{28,12},{1,17},{... | collective-permute-start | bytes 2359304 | tf_op jit(solution)/shard_map/ppermute | solution.py:272
  29.0 18.1 %collective-permute-start.1 = (bf16[3,512,256]{2,1,0:T(8,128)(2,1)}, bf16[3,512,256]{2,1,0:T(8,128)(2,1)S(1)}, u32[]{:S(2)}, u32[]{:S(2)}) collective-permute-start(bf16[3,512,256]{2,1,0:T(8,128)(2,1)} %collective-permute-done.refs_6_.refs_5_), channel_id=1, source_target_pairs={{0,8},{4,12},{8,0},{12,4},{16,24},{20,28},{24,16},{28,20},{1,9},{5... | collective-permute-start | bytes 2359304 | tf_op jit(solution)/shard_map/ppermute | solution.py:272
  47.1 4.4 %collective-permute-start.7 = (bf16[3,512,256]{2,1,0:T(8,128)(2,1)}, bf16[3,512,256]{2,1,0:T(8,128)(2,1)S(1)}, u32[]{:S(2)}, u32[]{:S(2)}) collective-permute-start(bf16[3,512,256]{2,1,0:T(8,128)(2,1)} %collective-permute-done.refs_6_.refs_5_), channel_id=1, source_target_pairs={{0,4},{4,0},{8,12},{12,8},{16,20},{20,16},{24,28},{28,24},{1,5},{5... | collective-permute-start | bytes 2359304 | tf_op jit(solution)/shard_map/ppermute | solution.py:272
  47.1 5.3 %collective-permute-start.9 = (bf16[3,512,256]{2,1,0:T(8,128)(2,1)}, bf16[3,512,256]{2,1,0:T(8,128)(2,1)S(1)}, u32[]{:S(2)}, u32[]{:S(2)}) collective-permute-start(bf16[3,512,256]{2,1,0:T(8,128)(2,1)} %collective-permute-done.2.refs_10_.refs_9_), channel_id=1, source_target_pairs={{0,4},{4,0},{8,12},{12,8},{16,20},{20,16},{24,28},{28,24},{1,5},{5... | collective-permute-start | bytes 2359304 | tf_op jit(solution)/shard_map/ppermute | solution.py:272
  47.6 21.0 %collective-permute-start.5 = (bf16[3,512,256]{2,1,0:T(8,128)(2,1)S(1)}, bf16[3,512,256]{2,1,0:T(8,128)(2,1)S(1)}, u32[]{:S(2)}, u32[]{:S(2)}) collective-permute-start(bf16[3,512,256]{2,1,0:T(8,128)(2,1)S(1)} %collective-permute-done.3.refs_13_.refs_6_), channel_id=1, source_target_pairs={{0,16},{4,20},{8,24},{12,28},{16,0},{20,4},{24,8},{28,12},{1,17},{... | collective-permute-start | bytes 2359304 | tf_op jit(solution)/shard_map/ppermute | solution.py:272
  48.1 20.5 %collective-permute-start.4 = (bf16[3,512,256]{2,1,0:T(8,128)(2,1)S(1)}, bf16[3,512,256]{2,1,0:T(8,128)(2,1)S(1)}, u32[]{:S(2)}, u32[]{:S(2)}) collective-permute-start(bf16[3,512,256]{2,1,0:T(8,128)(2,1)S(1)} %collective-permute-done.3.refs_13_.refs_6_), channel_id=1, source_target_pairs={{0,8},{4,12},{8,0},{12,4},{16,24},{20,28},{24,16},{28,20},{1,9},{5... | collective-permute-start | bytes 2359304 | tf_op jit(solution)/shard_map/ppermute | solution.py:272
  49.6 19.0 %collective-permute-start.6 = (bf16[3,512,256]{2,1,0:T(8,128)(2,1)S(1)}, bf16[3,512,256]{2,1,0:T(8,128)(2,1)}, u32[]{:S(2)}, u32[]{:S(2)}) collective-permute-start(bf16[3,512,256]{2,1,0:T(8,128)(2,1)S(1)} %constant_dynamic-slice_fusion), channel_id=1, source_target_pairs={{0,3},{1,0},{2,1},{3,2},{4,7},{5,4},{6,5},{7,6},{8,11},{9,8},{10,9... | collective-permute-start | bytes 2359304 | tf_op jit(solution)/shard_map/ppermute | solution.py:363
  51.5 17.1 %collective-permute-start.8 = (bf16[3,512,256]{2,1,0:T(8,128)(2,1)S(1)}, bf16[3,512,256]{2,1,0:T(8,128)(2,1)S(1)}, u32[]{:S(2)}, u32[]{:S(2)}) collective-permute-start(bf16[3,512,256]{2,1,0:T(8,128)(2,1)S(1)} %collective-permute-done.1.refs_8_.refs_7_), channel_id=1, source_target_pairs={{0,4},{4,0},{8,12},{12,8},{16,20},{20,16},{24,28},{28,24},{1,5},{5... | collective-permute-start | bytes 2359304 | tf_op jit(solution)/shard_map/ppermute | solution.py:272
  52.4 16.2 %collective-permute-start.10 = (bf16[3,512,256]{2,1,0:T(8,128)(2,1)S(1)}, bf16[3,512,256]{2,1,0:T(8,128)(2,1)S(1)}, u32[]{:S(2)}, u32[]{:S(2)}) collective-permute-start(bf16[3,512,256]{2,1,0:T(8,128)(2,1)S(1)} %collective-permute-done.3.refs_13_.refs_6_), channel_id=1, source_target_pairs={{0,4},{4,0},{8,12},{12,8},{16,20},{20,16},{24,28},{28,24},{1,5},{5... | collective-permute-start | bytes 2359304 | tf_op jit(solution)/shard_map/ppermute | solution.py:272
  70.4 4.4 %collective-permute-start.12 = (bf16[3,512,256]{2,1,0:T(8,128)(2,1)}, bf16[3,512,256]{2,1,0:T(8,128)(2,1)}, u32[]{:S(2)}, u32[]{:S(2)}) collective-permute-start(bf16[3,512,256]{2,1,0:T(8,128)(2,1)} %collective-permute-done.6.refs_12_.refs_11_), channel_id=1, source_target_pairs={{0,4},{4,0},{8,12},{12,8},{16,20},{20,16},{24,28},{28,24},{1,5},{5... | collective-permute-start | bytes 2359304 | tf_op jit(solution)/shard_map/ppermute | solution.py:272
  71.0 21.3 %collective-permute-start.11 = (bf16[3,512,256]{2,1,0:T(8,128)(2,1)S(1)}, bf16[3,512,256]{2,1,0:T(8,128)(2,1)}, u32[]{:S(2)}, u32[]{:S(2)}) collective-permute-start(bf16[3,512,256]{2,1,0:T(8,128)(2,1)S(1)} %collective-permute-done.3.refs_13_.refs_6_), channel_id=1, source_target_pairs={{0,3},{1,0},{2,1},{3,2},{4,7},{5,4},{6,5},{7,6},{8,11},{9,8},{10,9... | collective-permute-start | bytes 2359304 | tf_op jit(solution)/shard_map/ppermute | solution.py:369
  74.9 17.4 %collective-permute-start.16 = (bf16[3,512,256]{2,1,0:T(8,128)(2,1)S(1)}, bf16[3,512,256]{2,1,0:T(8,128)(2,1)S(1)}, u32[]{:S(2)}, u32[]{:S(2)}) collective-permute-start(bf16[3,512,256]{2,1,0:T(8,128)(2,1)S(1)} %collective-permute-done.5.refs_16_.refs_9_), channel_id=1, source_target_pairs={{0,4},{4,0},{8,12},{12,8},{16,20},{20,16},{24,28},{28,24},{1,5},{5... | collective-permute-start | bytes 2359304 | tf_op jit(solution)/shard_map/ppermute | solution.py:272
  75.9 16.4 %collective-permute-start.15 = (bf16[3,512,256]{2,1,0:T(8,128)(2,1)S(1)}, bf16[3,512,256]{2,1,0:T(8,128)(2,1)S(1)}, u32[]{:S(2)}, u32[]{:S(2)}) collective-permute-start(bf16[3,512,256]{2,1,0:T(8,128)(2,1)S(1)} %collective-permute-done.4.refs_15_.refs_8_), channel_id=1, source_target_pairs={{0,4},{4,0},{8,12},{12,8},{16,20},{20,16},{24,28},{28,24},{1,5},{5... | collective-permute-start | bytes 2359304 | tf_op jit(solution)/shard_map/ppermute | solution.py:272
  76.2 16.1 %collective-permute-start.14 = (bf16[3,256,256]{2,1,0:T(8,128)(2,1)}, bf16[3,256,256]{2,1,0:T(8,128)(2,1)}, u32[]{:S(2)}, u32[]{:S(2)}) collective-permute-start(bf16[3,256,256]{2,1,0:T(8,128)(2,1)} %slice.7), channel_id=1, source_target_pairs={{0,16},{4,20},{8,24},{12,28},{16,0},{20,4},{24,8},{28,12},{1,17},{... | collective-permute-start | bytes 1179656 | tf_op jit(solution)/shard_map/ppermute | solution.py:272
  76.7 15.6 %collective-permute-start.13 = (bf16[3,256,256]{2,1,0:T(8,128)(2,1)S(1)}, bf16[3,256,256]{2,1,0:T(8,128)(2,1)}, u32[]{:S(2)}, u32[]{:S(2)}) collective-permute-start(bf16[3,256,256]{2,1,0:T(8,128)(2,1)S(1)} %slice.6), channel_id=1, source_target_pairs={{0,8},{4,12},{8,0},{12,4},{16,24},{20,28},{24,16},{28,20},{1,9},{5... | collective-permute-start | bytes 1179656 | tf_op jit(solution)/shard_map/ppermute | solution.py:272
  92.9 22.2 %collective-permute-start.22 = (bf16[3,512,256]{2,1,0:T(8,128)(2,1)S(1)}, bf16[3,512,256]{2,1,0:T(8,128)(2,1)S(1)}, u32[]{:S(2)}, u32[]{:S(2)}) collective-permute-start(bf16[3,512,256]{2,1,0:T(8,128)(2,1)S(1)} %copy-done.12), channel_id=1, source_target_pairs={{3,0},{0,1},{1,2},{2,3},{7,4},{4,5},{5,6},{6,7},{11,8},{8,9},{9,10... | collective-permute-start | bytes 2359304 | tf_op jit(solution)/shard_map/ppermute | solution.py:383
  92.9 22.2 %collective-permute-start.21 = (bf16[3,512,256]{2,1,0:T(8,128)(2,1)}, bf16[3,512,256]{2,1,0:T(8,128)(2,1)S(1)}, u32[]{:S(2)}, u32[]{:S(2)}) collective-permute-start(bf16[3,512,256]{2,1,0:T(8,128)(2,1)} %collective-permute-done.11.refs_16_.refs_5_), channel_id=1, source_target_pairs={{0,16},{4,20},{8,24},{12,28},{16,0},{20,4},{24,8},{28,12},{1,17},{... | collective-permute-start | bytes 2359304 | tf_op jit(solution)/shard_map/ppermute | solution.py:272
  93.4 21.7 %collective-permute-start.20 = (bf16[3,512,256]{2,1,0:T(8,128)(2,1)}, bf16[3,512,256]{2,1,0:T(8,128)(2,1)S(1)}, u32[]{:S(2)}, u32[]{:S(2)}) collective-permute-start(bf16[3,512,256]{2,1,0:T(8,128)(2,1)} %collective-permute-done.11.refs_16_.refs_5_), channel_id=1, source_target_pairs={{0,8},{4,12},{8,0},{12,4},{16,24},{20,28},{24,16},{28,20},{1,9},{5... | collective-permute-start | bytes 2359304 | tf_op jit(solution)/shard_map/ppermute | solution.py:272
  94.9 21.5 %collective-permute-start.19 = (bf16[3,512,256]{2,1,0:T(8,128)(2,1)}, bf16[3,512,256]{2,1,0:T(8,128)(2,1)}, u32[]{:S(2)}, u32[]{:S(2)}) collective-permute-start(bf16[3,512,256]{2,1,0:T(8,128)(2,1)} %collective-permute-done.11.refs_16_.refs_5_), channel_id=1, source_target_pairs={{0,4},{4,0},{8,12},{12,8},{16,20},{20,16},{24,28},{28,24},{1,5},{5... | collective-permute-start | bytes 2359304 | tf_op jit(solution)/shard_map/ppermute | solution.py:272
  115.2 3.5 %collective-permute-start.24 = (bf16[3,512,256]{2,1,0:T(8,128)(2,1)S(1)}, bf16[3,512,256]{2,1,0:T(8,128)(2,1)}, u32[]{:S(2)}, u32[]{:S(2)}) collective-permute-start(bf16[3,512,256]{2,1,0:T(8,128)(2,1)S(1)} %collective-permute-done.21.refs_19_.refs_8_), channel_id=1, source_target_pairs={{0,4},{4,0},{8,12},{12,8},{16,20},{20,16},{24,28},{28,24},{1,5},{5... | collective-permute-start | bytes 2359304 | tf_op jit(solution)/shard_map/ppermute | solution.py:272
  115.7 4.2 %collective-permute-start.25 = (bf16[3,512,256]{2,1,0:T(8,128)(2,1)S(1)}, bf16[3,512,256]{2,1,0:T(8,128)(2,1)}, u32[]{:S(2)}, u32[]{:S(2)}) collective-permute-start(bf16[3,512,256]{2,1,0:T(8,128)(2,1)S(1)} %collective-permute-done.22.refs_20_.refs_9_), channel_id=1, source_target_pairs={{0,4},{4,0},{8,12},{12,8},{16,20},{20,16},{24,28},{28,24},{1,5},{5... | collective-permute-start | bytes 2359304 | tf_op jit(solution)/shard_map/ppermute | solution.py:272
  127.8 30.2 %all-to-all-start = ((bf16[8,2,256,256]{3,2,1,0:T(8,128)(2,1)}), bf16[8,2,256,256]{3,2,1,0:T(8,128)(2,1)S(1)}, u32[]{:S(2)}, u32[]{:S(2)}) async-start(bf16[8,2,256,256]{3,2,1,0:T(8,128)(2,1)} %bitcast.16), calls=%async_computation | async-start | bytes 4194304 | tf_op jit(solution)/shard_map/all_to_all | solution.py:388
  (21 other events, 211.6 us)

commit v13 on v12

--- a/solution.py
+++ b/solution.py
@@ -44,28 +44,34 @@
     return whole | lower | upper_half
 
 
-def run_list(number, width, spare, tasks, counts, hist, table, acc):
+def run_list(number, width, tasks, counts, hist, table, acc):
     panels = table.shape[2]
+
+    def run(n):
+        packed = tasks[number, n]
+        fields = []
+        for bits in FIELDS:
+            fields.append(packed & ((1 << bits) - 1))
+            packed = packed >> bits
+        half, source, klass, lag = fields
+        columns = pl.multiple_of(half * (width * panels), width * panels)
+        rows = pl.multiple_of(lag * panels, panels)
+        acc[packed] += jnp.dot(
+            hist[source, :, pl.ds(columns, width * panels)],
+            table[klass, pl.ds(rows, width * panels), :],
+            preferred_element_type=jnp.float32,
+        )
+
     count = counts[number]
-    for n in range(UNROLL - 1):
-        tasks[number, count + n] = pack(0, 0, 0, 0, spare)
-
-    @pl.loop(0, (count + UNROLL - 1) // UNROLL)
+
+    @pl.loop(0, count // UNROLL)
     def _(j):
         for n in range(UNROLL):
-            packed = tasks[number, j * UNROLL + n]
-            fields = []
-            for bits in FIELDS:
-                fields.append(packed & ((1 << bits) - 1))
-                packed = packed >> bits
-            half, source, klass, lag = fields
-            columns = pl.multiple_of(half * (width * panels), width * panels)
-            rows = pl.multiple_of(lag * panels, panels)
-            acc[packed] += jnp.dot(
-                hist[source, :, pl.ds(columns, width * panels)],
-                table[klass, pl.ds(rows, width * panels), :],
-                preferred_element_type=jnp.float32,
-            )
+            run(j * UNROLL + n)
+
+    @pl.loop(count // UNROLL * UNROLL, count)
+    def _(j):
+        run(j)
 
 
 def window_kernel(config, *refs):
@@ -146,15 +152,13 @@
             def _():
                 served_copy(i, False).wait()
 
-    spare = acc.shape[0] - 1
-
     def wait_class(k):
         inner = table.at[k, pl.ds(margin, span * panels), :]
         pltpu.make_async_copy(inner, inner, sems.at[k]).wait()
 
     def run_lists(number):
-        run_list(number, steps, spare, tasks, counts, hist, table, acc)
-        run_list(number + 1, steps // 2, spare, tasks, counts, hist, table, acc)
+        run_list(number, steps, tasks, counts, hist, table, acc)
+        run_list(number + 1, steps // 2, tasks, counts, hist, table, acc)
 
     if phased:
         @pl.loop(0, classes)
@@ -220,9 +224,9 @@
         scratch_shapes=[
             pltpu.VMEM((classes, depth_of_table, panels), jnp.bfloat16),
             pltpu.VMEM(hist_t.shape, hist_t.dtype),
-            pltpu.VMEM((places + targets + 1, excite, panels), jnp.float32),
+            pltpu.VMEM((places + targets, excite, panels), jnp.float32),
             pltpu.VMEM((places if narrow else 1, excite, panels), jnp.float32),
-            pltpu.SMEM((2 * classes, pairs + UNROLL), jnp.int32),
+            pltpu.SMEM((2 * classes, pairs + 1), jnp.int32),
             pltpu.SMEM((2 * classes,), jnp.int32),
             pltpu.SMEM((max(places, 1),), jnp.int32),
             pltpu.SemaphoreType.DMA((classes,)),
@@ -241,8 +245,10 @@
     )(*operands, *wide, *before)
 
 
-def update_kernel(target_ref, near_ref, recv_ref, inverse_ref, incident_ref, out_ref, total):
-    total[...] = near_ref[...]
+def update_kernel(target_ref, near_ref, recv_ref, inverse_ref, incident_ref, out_ref, total, sem):
+    copy = pltpu.make_async_copy(near_ref, total, sem)
+    copy.start()
+    copy.wait()
     slots, peers = target_ref.shape
 
     @pl.loop(0, peers)
@@ -261,10 +267,10 @@
     return pl.pallas_call(
         update_kernel,
         out_shape=jax.ShapeDtypeStruct(incident.shape, jnp.bfloat16),
-        in_specs=[SMEM] + [VMEM] * 4,
+        in_specs=[SMEM, HBM] + [VMEM] * 3,
         out_specs=VMEM,
-        scratch_shapes=[pltpu.VMEM(near.shape, jnp.float32)],
-        compiler_params=pltpu.CompilerParams(vmem_limit_bytes=58 * MIB),
+        scratch_shapes=[pltpu.VMEM(near.shape, jnp.float32), pltpu.SemaphoreType.DMA],
+        compiler_params=pltpu.CompilerParams(vmem_limit_bytes=32 * MIB),
     )(target, near, recv, inverse, incident)
 
 
@@ -348,6 +354,7 @@
     own, hist_t, opposite = tie(own, hist_t, group ^ 6)
     corner = part(opposite)
     trio = neighbours(own)
+    own, corner = tie(own, corner)
     own = lax.ppermute(own, "lag", ring)
     served_sums, near = window_sums(
         lane, group * 0, served, local, hist_t, [[(0, 0, weights)]], None, lanes, rows

time: 165 us -> 164 us (level); the launches traced: 163 us -> 164 us
  starting transfers between devices: 28.4 us -> 34.8 us
  Pallas kernels: 73 us -> 67 us
    pallas_call x5, Pallas kernels: 69 us -> 64.6 us  [window_sums(): pl.pallas_call(functools.partial(window_kernel, config), out_shape=outs,...]
    ppermute x21, starting transfers between devices: 9.54 us -> 12.4 us  [swap(): return lax.ppermute(value, 'grp', [(i, i ^ bit) for i in range(peers)])]
    ppermute x3, waiting for transfers between devices: 10.2 us -> 12.9 us  [per_device(): own = lax.ppermute(own, 'lag', ring)]
    ppermute x1, starting transfers between devices: 1.93 us -> 4.28 us  [per_device(): diagonal = lax.ppermute(corner, 'lag', ring)]
    ppermute x21, waiting for transfers between devices: 5.68 us -> 3.54 us  [swap(): return lax.ppermute(value, 'grp', [(i, i ^ bit) for i in range(peers)])]
    unnamed x37 -> x45, local copies, waits for them, and re-layouts: 11 us -> 10 us
  transfers between devices with their start and end apart: 27 -> 27, of which waited for: 12 -> 8; matrix products, arithmetic and copies ran while one was open for 7% -> 7% of each run, Pallas kernels for 37% -> 34%
where the time goes in v13:
time: 164 us
  Pallas kernels  67 us (41%)
  waiting for transfers between devices  46.4 us (28%)
  starting transfers between devices  34.8 us (21%)
  local copies, waits for them, and re-layouts  13.2 us (8%)
  other arithmetic  2.5 us (2%)
    pallas_call x5, Pallas kernels, window_sums(): pl.pallas_call(functools.partial(window_kernel, config), out_shape=outs,...  64.6 us
    ppermute x1, waiting for transfers between devices, per_device(): diagonal = lax.ppermute(corner, 'lag', ring)  16.4 us
    ppermute x3, starting transfers between devices, per_device(): own = lax.ppermute(own, 'lag', ring)  13.8 us
    ppermute x3, waiting for transfers between devices, per_device(): own = lax.ppermute(own, 'lag', ring)  12.9 us
    ppermute x21, starting transfers between devices, swap(): return lax.ppermute(value, 'grp', [(i, i ^ bit) for i in range(peers)])  12.4 us
    unnamed x45, local copies, waits for them, and re-layouts  10 us
    all_to_all x1, waiting for transfers between devices, per_device(): lax.all_to_all(contribution.reshape(peers, slots, *contribution.shape[1:]...  8.59 us
    ppermute x1, waiting for transfers between devices, per_device(): diagonal = lax.ppermute(corner, 'lag', [(j, i) for i, j in ring])  4.99 us
  transfers between devices with their start and end apart: 27, of which 8 were waited for; matrix products, arithmetic and copies ran while one was open for 7% of the time, Pallas kernels for 34%

profile of v13, /device:TPU:0, one launch (start us, length us, event | category | flops | bytes accessed | tf_op | source)
XLA Modules:
  0.0 164.2 jit_solution(3892190091339924408)
XLA Ops:
  1.2 5.1 %collective-permute-start = (bf16[3,512,256]{2,1,0:T(8,128)(2,1)S(1)}, bf16[3,512,256]{2,1,0:T(8,128)(2,1)S(1)}, u32[]{:S(2)}, u32[]{:S(2)}) collective-permute-start(bf16[3,512,256]{2,1,0:T(8,128)(2,1)S(1)} %constant_dynamic-slice_fusion.1), channel_id=1, source_target_pairs={{0,3},{1,0},{2,1},{3,2},{4,7},{5,4},{6,5},{7,6},{8,11},{9,8},{10,9... | collective-permute-start | bytes 2359304 | tf_op jit(solution)/shard_map/ppermute | solution.py:353
  6.3 6.3 %copy.16 = bf16[4,2048,256]{1,2,0:T(8,128)(2,1)} copy(bf16[4,2048,256]{2,1,0:T(8,128)(2,1)} %param.13) | data formatting | bytes 8388608 | tf_op args[1]
  13.2 9.8 %collective-permute-done.refs_6_.refs_5_ = bf16[3,512,256]{2,1,0:T(8,128)(2,1)S(1)} collective-permute-done((bf16[3,512,256]{2,1,0:T(8,128)(2,1)S(1)}, bf16[3,512,256]{2,1,0:T(8,128)(2,1)S(1)}, u32[]{:S(2)}, u32[]{:S(2)}) %collective-permute-start) | collective-permute-done | bytes 786464 | tf_op jit(solution)/shard_map/ppermute | solution.py:353
  23.1 1.5 collective-permute-start.2
  24.6 1.5 collective-permute-start.1
  27.3 4.3 %collective-permute-start.3 = (bf16[3,512,256]{2,1,0:T(8,128)(2,1)S(1)}, bf16[3,512,256]{2,1,0:T(8,128)(2,1)S(1)}, u32[]{:S(2)}, u32[]{:S(2)}) collective-permute-start(bf16[3,512,256]{2,1,0:T(8,128)(2,1)S(1)} %collective-permute-done.refs_6_.refs_5_), channel_id=1, source_target_pairs={{0,3},{1,0},{2,1},{3,2},{4,7},{5,4},{6,5},{7,6},{8,11},{9,8},{10,9... | collective-permute-start | bytes 2359304 | tf_op jit(solution)/shard_map/ppermute | solution.py:358
  31.6 12.3 %shard_map.118 = (f32[16,256,256]{2,1,0:T(8,128)}, f32[4,256,256]{2,1,0:T(8,128)}) custom-call(s32[2]{0:T(128)} %pad_add_fusion.1.refs_0_, s32[2,8]{1,0:T(2,128)} %bitcast.18, s32[2,8]{1,0:T(2,128)} %bitcast.21, s32[2,8]{1,0:T(2,128)} %bitcast.24, s32[48]{0:T(128)} %refs_1_.3, s32[48]{0:T(128)} %refs_2_.3, s32[48]{0:T(128)} %refs_3_.3, s32[48]{0:T(128)} %refs_4_.5, ...), custom_call_target="tpu_custom_call" | custom-call | flops 17179869184 | bytes 10485760 | tf_op jit(solution)/shard_map/pallas_call | solution.py:219
  44.0 3.0 %collective-permute-done.3.refs_13_.refs_6_ = bf16[3,512,256]{2,1,0:T(8,128)(2,1)S(1)} collective-permute-done((bf16[3,512,256]{2,1,0:T(8,128)(2,1)S(1)}, bf16[3,512,256]{2,1,0:T(8,128)(2,1)S(1)}, u32[]{:S(2)}, u32[]{:S(2)}) %collective-permute-start.3) | collective-permute-done | bytes 786464 | tf_op jit(solution)/shard_map/ppermute | solution.py:358
  49.0 4.3 %collective-permute-start.6 = (bf16[3,512,256]{2,1,0:T(8,128)(2,1)S(1)}, bf16[3,512,256]{2,1,0:T(8,128)(2,1)}, u32[]{:S(2)}, u32[]{:S(2)}) collective-permute-start(bf16[3,512,256]{2,1,0:T(8,128)(2,1)S(1)} %constant_dynamic-slice_fusion), channel_id=1, source_target_pairs={{0,3},{1,0},{2,1},{3,2},{4,7},{5,4},{6,5},{7,6},{8,11},{9,8},{10,9... | collective-permute-start | bytes 2359304 | tf_op jit(solution)/shard_map/ppermute | solution.py:370
  53.8 16.4 %collective-permute-done.6.refs_12_.refs_11_ = bf16[3,512,256]{2,1,0:T(8,128)(2,1)} collective-permute-done((bf16[3,512,256]{2,1,0:T(8,128)(2,1)S(1)}, bf16[3,512,256]{2,1,0:T(8,128)(2,1)}, u32[]{:S(2)}, u32[]{:S(2)}) %collective-permute-start.6) | collective-permute-done | bytes 786464 | tf_op jit(solution)/shard_map/ppermute | solution.py:370
  71.9 4.4 %collective-permute-start.11 = (bf16[3,512,256]{2,1,0:T(8,128)(2,1)S(1)}, bf16[3,512,256]{2,1,0:T(8,128)(2,1)}, u32[]{:S(2)}, u32[]{:S(2)}) collective-permute-start(bf16[3,512,256]{2,1,0:T(8,128)(2,1)S(1)} %collective-permute-done.3.refs_13_.refs_6_), channel_id=1, source_target_pairs={{0,3},{1,0},{2,1},{3,2},{4,7},{5,4},{6,5},{7,6},{8,11},{9,8},{10,9... | collective-permute-start | bytes 2359304 | tf_op jit(solution)/shard_map/ppermute | solution.py:376
  77.6 1.5 collective-permute-start.14
  79.2 1.5 collective-permute-start.13
  80.7 13.1 %shard_map.119.refs_24_ = f32[4,256,256]{2,1,0:T(8,128)} custom-call(s32[2]{0:T(128)} %pad_add_fusion.2.refs_0_, s32[48]{0:T(128)} %refs_1_.3, s32[48]{0:T(128)} %refs_2_.3, s32[48]{0:T(128)} %refs_3_.3, s32[48]{0:T(128)} %refs_4_.5, bf16[4,256,2048]{2,1,0:T(8,128)(2,1)} %bitcast.13, ...), custom_call_target="tpu_custom_call", output_to_operand_aliasing={{}: (14, {})} | custom-call | flops 12884901888 | bytes 10485760 | tf_op jit(solution)/shard_map/pallas_call | solution.py:219
  94.4 1.4 collective-permute-start.21
  95.8 1.5 collective-permute-start.20
  98.0 13.4 %shard_map.120.refs_13_ = f32[16,256,256]{2,1,0:T(8,128)} custom-call(s32[2]{0:T(128)} %pad_add_fusion.2.refs_0_, s32[2,8]{1,0:T(2,128)} %bitcast.19, s32[2,8]{1,0:T(2,128)} %bitcast.22, s32[2,8]{1,0:T(2,128)} %bitcast.25, bf16[4,256,2048]{2,1,0:T(8,128)(2,1)} %bitcast.14, bf16[3,512,256]{2,1,0:T(8,128)(2,1)} %copy-done.8, ...), custom_call_target="tpu_custom_call", output_to_operand_aliasing={{}: (23, {})} | custom-call | flops 4294967296 | bytes 16777216 | tf_op jit(solution)/shard_map/pallas_call | solution.py:219
  111.5 5.0 %collective-permute-done.22.refs_20_.refs_9_ = bf16[3,512,256]{2,1,0:T(8,128)(2,1)S(1)} collective-permute-done((bf16[3,512,256]{2,1,0:T(8,128)(2,1)S(1)}, bf16[3,512,256]{2,1,0:T(8,128)(2,1)S(1)}, u32[]{:S(2)}, u32[]{:S(2)}) %collective-permute-start.22) | collective-permute-done | bytes 786464 | tf_op jit(solution)/shard_map/ppermute | solution.py:390
  117.7 1.2 collective-permute-done.23.refs_21_.refs_10_
  121.2 8.4 %shard_map.122 = bf16[16,256,256]{2,1,0:T(8,128)(2,1)} custom-call(s32[2]{0:T(128)} %pad_add_fusion.3.refs_0_, s32[2,8]{1,0:T(2,128)} %bitcast.20, s32[2,8]{1,0:T(2,128)} %bitcast.23, s32[2,8]{1,0:T(2,128)} %bitcast.26, bf16[4,256,2048]{2,1,0:T(8,128)(2,1)} %bitcast.15, bf16[3,512,256]{2,1,0:T(8,128)(2,1)} %collective-permute-done.11.refs_16_.refs_5_, ...), custom_call_target="tpu_custom_call" | custom-call | flops 4294967296 | bytes 10485760 | tf_op jit(solution)/shard_map/pallas_call | solution.py:219
  129.6 4.4 %all-to-all-start = ((bf16[8,2,256,256]{3,2,1,0:T(8,128)(2,1)}), bf16[8,2,256,256]{3,2,1,0:T(8,128)(2,1)S(1)}, u32[]{:S(2)}, u32[]{:S(2)}) async-start(bf16[8,2,256,256]{3,2,1,0:T(8,128)(2,1)} %bitcast.17), calls=%async_computation | async-start | bytes 4194304 | tf_op jit(solution)/shard_map/all_to_all | solution.py:395
  134.6 17.5 %shard_map.121.near_ref = f32[4,256,256]{2,1,0:T(8,128)} custom-call(s32[2]{0:T(128)} %pad_add_fusion.refs_0_, s32[48]{0:T(128)} %refs_1_.3, s32[48]{0:T(128)} %refs_2_.3, s32[48]{0:T(128)} %refs_3_.3, s32[48]{0:T(128)} %refs_4_.5, bf16[4,256,2048]{2,1,0:T(8,128)(2,1)} %bitcast.16, bf16[3,512,256]{2,1,0:T(8,128)(2,1)} %copy-done.6, ...), custom_call_target="tpu_custom_call", output_to_operand_aliasing={{}: (24, {})} | custom-call | flops 12884901888 | bytes 16777216 | tf_op jit(solution)/shard_map/pallas_call | solution.py:219
  152.0 8.6 %all-to-all-done.recv_ref = bf16[8,2,256,256]{3,2,1,0:T(8,128)(2,1)S(1)} async-done(((bf16[8,2,256,256]{3,2,1,0:T(8,128)(2,1)}), bf16[8,2,256,256]{3,2,1,0:T(8,128)(2,1)S(1)}, u32[]{:S(2)}, u32[]{:S(2)}) %all-to-all-start) | async-done | bytes 2097184 | tf_op jit(solution)/shard_map/all_to_all | solution.py:395
  161.9 2.4 %shard_map.123 = bf16[4,256,256]{2,1,0:T(8,128)(2,1)} custom-call(s32[2,8]{1,0:T(2,128)S(1)} %bitcast.11, f32[4,256,256]{2,1,0:T(8,128)S(1)} %copy-done, bf16[8,2,256,256]{3,2,1,0:T(8,128)(2,1)S(1)} %all-to-all-done.recv_ref, bf16[4,256,256]{2,1,0:T(8,128)(2,1)S(1)} %copy-done.1, bf16[4,256,256]{2,1,0:T(8,128)(2,1)S(1)} %copy-done.2), custom_call_target="tpu_custom_call" | custom-call | tf_op jit(solution)/shard_map/pallas_call | solution.py:267
  (89 shorter events, 15.1 us)
Async XLA Ops:
  1.2 21.9 %collective-permute-start = (bf16[3,512,256]{2,1,0:T(8,128)(2,1)S(1)}, bf16[3,512,256]{2,1,0:T(8,128)(2,1)S(1)}, u32[]{:S(2)}, u32[]{:S(2)}) collective-permute-start(bf16[3,512,256]{2,1,0:T(8,128)(2,1)S(1)} %constant_dynamic-slice_fusion.1), channel_id=1, source_target_pairs={{0,3},{1,0},{2,1},{3,2},{4,7},{5,4},{6,5},{7,6},{8,11},{9,8},{10,9... | collective-permute-start | bytes 2359304 | tf_op jit(solution)/shard_map/ppermute | solution.py:353
  23.1 23.9 %collective-permute-start.2 = (bf16[3,512,256]{2,1,0:T(8,128)(2,1)S(1)}, bf16[3,512,256]{2,1,0:T(8,128)(2,1)}, u32[]{:S(2)}, u32[]{:S(2)}) collective-permute-start(bf16[3,512,256]{2,1,0:T(8,128)(2,1)S(1)} %collective-permute-done.refs_6_.refs_5_), channel_id=1, source_target_pairs={{0,16},{4,20},{8,24},{12,28},{16,0},{20,4},{24,8},{28,12},{1,17},{... | collective-permute-start | bytes 2359304 | tf_op jit(solution)/shard_map/ppermute | solution.py:278
  24.6 22.4 %collective-permute-start.1 = (bf16[3,512,256]{2,1,0:T(8,128)(2,1)S(1)}, bf16[3,512,256]{2,1,0:T(8,128)(2,1)S(1)}, u32[]{:S(2)}, u32[]{:S(2)}) collective-permute-start(bf16[3,512,256]{2,1,0:T(8,128)(2,1)S(1)} %collective-permute-done.refs_6_.refs_5_), channel_id=1, source_target_pairs={{0,8},{4,12},{8,0},{12,4},{16,24},{20,28},{24,16},{28,20},{1,9},{5... | collective-permute-start | bytes 2359304 | tf_op jit(solution)/shard_map/ppermute | solution.py:278
  27.3 19.7 %collective-permute-start.3 = (bf16[3,512,256]{2,1,0:T(8,128)(2,1)S(1)}, bf16[3,512,256]{2,1,0:T(8,128)(2,1)S(1)}, u32[]{:S(2)}, u32[]{:S(2)}) collective-permute-start(bf16[3,512,256]{2,1,0:T(8,128)(2,1)S(1)} %collective-permute-done.refs_6_.refs_5_), channel_id=1, source_target_pairs={{0,3},{1,0},{2,1},{3,2},{4,7},{5,4},{6,5},{7,6},{8,11},{9,8},{10,9... | collective-permute-start | bytes 2359304 | tf_op jit(solution)/shard_map/ppermute | solution.py:358
  47.0 6.2 %collective-permute-start.7 = (bf16[3,512,256]{2,1,0:T(8,128)(2,1)S(1)}, bf16[3,512,256]{2,1,0:T(8,128)(2,1)S(1)}, u32[]{:S(2)}, u32[]{:S(2)}) collective-permute-start(bf16[3,512,256]{2,1,0:T(8,128)(2,1)S(1)} %collective-permute-done.refs_6_.refs_5_), channel_id=1, source_target_pairs={{0,4},{4,0},{8,12},{12,8},{16,20},{20,16},{24,28},{28,24},{1,5},{5... | collective-permute-start | bytes 2359304 | tf_op jit(solution)/shard_map/ppermute | solution.py:278
  47.9 5.3 %collective-permute-start.9 = (bf16[3,512,256]{2,1,0:T(8,128)(2,1)}, bf16[3,512,256]{2,1,0:T(8,128)(2,1)S(1)}, u32[]{:S(2)}, u32[]{:S(2)}) collective-permute-start(bf16[3,512,256]{2,1,0:T(8,128)(2,1)} %collective-permute-done.2.refs_10_.refs_9_), channel_id=1, source_target_pairs={{0,4},{4,0},{8,12},{12,8},{16,20},{20,16},{24,28},{28,24},{1,5},{5... | collective-permute-start | bytes 2359304 | tf_op jit(solution)/shard_map/ppermute | solution.py:278
  47.9 22.2 %collective-permute-start.5 = (bf16[3,512,256]{2,1,0:T(8,128)(2,1)S(1)}, bf16[3,512,256]{2,1,0:T(8,128)(2,1)S(1)}, u32[]{:S(2)}, u32[]{:S(2)}) collective-permute-start(bf16[3,512,256]{2,1,0:T(8,128)(2,1)S(1)} %collective-permute-done.3.refs_13_.refs_6_), channel_id=1, source_target_pairs={{0,16},{4,20},{8,24},{12,28},{16,0},{20,4},{24,8},{28,12},{1,17},{... | collective-permute-start | bytes 2359304 | tf_op jit(solution)/shard_map/ppermute | solution.py:278
  48.4 21.7 %collective-permute-start.4 = (bf16[3,512,256]{2,1,0:T(8,128)(2,1)S(1)}, bf16[3,512,256]{2,1,0:T(8,128)(2,1)S(1)}, u32[]{:S(2)}, u32[]{:S(2)}) collective-permute-start(bf16[3,512,256]{2,1,0:T(8,128)(2,1)S(1)} %collective-permute-done.3.refs_13_.refs_6_), channel_id=1, source_target_pairs={{0,8},{4,12},{8,0},{12,4},{16,24},{20,28},{24,16},{28,20},{1,9},{5... | collective-permute-start | bytes 2359304 | tf_op jit(solution)/shard_map/ppermute | solution.py:278
  49.0 21.2 %collective-permute-start.6 = (bf16[3,512,256]{2,1,0:T(8,128)(2,1)S(1)}, bf16[3,512,256]{2,1,0:T(8,128)(2,1)}, u32[]{:S(2)}, u32[]{:S(2)}) collective-permute-start(bf16[3,512,256]{2,1,0:T(8,128)(2,1)S(1)} %constant_dynamic-slice_fusion), channel_id=1, source_target_pairs={{0,3},{1,0},{2,1},{3,2},{4,7},{5,4},{6,5},{7,6},{8,11},{9,8},{10,9... | collective-permute-start | bytes 2359304 | tf_op jit(solution)/shard_map/ppermute | solution.py:370
  53.3 16.9 %collective-permute-start.8 = (bf16[3,512,256]{2,1,0:T(8,128)(2,1)}, bf16[3,512,256]{2,1,0:T(8,128)(2,1)S(1)}, u32[]{:S(2)}, u32[]{:S(2)}) collective-permute-start(bf16[3,512,256]{2,1,0:T(8,128)(2,1)} %copy-done.9), channel_id=1, source_target_pairs={{0,4},{4,0},{8,12},{12,8},{16,20},{20,16},{24,28},{28,24},{1,5},{5... | collective-permute-start | bytes 2359304 | tf_op jit(solution)/shard_map/ppermute | solution.py:278
  53.3 16.9 %collective-permute-start.10 = (bf16[3,512,256]{2,1,0:T(8,128)(2,1)S(1)}, bf16[3,512,256]{2,1,0:T(8,128)(2,1)S(1)}, u32[]{:S(2)}, u32[]{:S(2)}) collective-permute-start(bf16[3,512,256]{2,1,0:T(8,128)(2,1)S(1)} %collective-permute-done.3.refs_13_.refs_6_), channel_id=1, source_target_pairs={{0,4},{4,0},{8,12},{12,8},{16,20},{20,16},{24,28},{28,24},{1,5},{5... | collective-permute-start | bytes 2359304 | tf_op jit(solution)/shard_map/ppermute | solution.py:278
  71.2 5.1 %collective-permute-start.12 = (bf16[3,512,256]{2,1,0:T(8,128)(2,1)}, bf16[3,512,256]{2,1,0:T(8,128)(2,1)}, u32[]{:S(2)}, u32[]{:S(2)}) collective-permute-start(bf16[3,512,256]{2,1,0:T(8,128)(2,1)} %collective-permute-done.6.refs_12_.refs_11_), channel_id=1, source_target_pairs={{0,4},{4,0},{8,12},{12,8},{16,20},{20,16},{24,28},{28,24},{1,5},{5... | collective-permute-start | bytes 2359304 | tf_op jit(solution)/shard_map/ppermute | solution.py:278
  71.9 21.9 %collective-permute-start.11 = (bf16[3,512,256]{2,1,0:T(8,128)(2,1)S(1)}, bf16[3,512,256]{2,1,0:T(8,128)(2,1)}, u32[]{:S(2)}, u32[]{:S(2)}) collective-permute-start(bf16[3,512,256]{2,1,0:T(8,128)(2,1)S(1)} %collective-permute-done.3.refs_13_.refs_6_), channel_id=1, source_target_pairs={{0,3},{1,0},{2,1},{3,2},{4,7},{5,4},{6,5},{7,6},{8,11},{9,8},{10,9... | collective-permute-start | bytes 2359304 | tf_op jit(solution)/shard_map/ppermute | solution.py:376
  76.3 17.5 %collective-permute-start.16 = (bf16[3,512,256]{2,1,0:T(8,128)(2,1)S(1)}, bf16[3,512,256]{2,1,0:T(8,128)(2,1)S(1)}, u32[]{:S(2)}, u32[]{:S(2)}) collective-permute-start(bf16[3,512,256]{2,1,0:T(8,128)(2,1)S(1)} %collective-permute-done.5.refs_16_.refs_9_), channel_id=1, source_target_pairs={{0,4},{4,0},{8,12},{12,8},{16,20},{20,16},{24,28},{28,24},{1,5},{5... | collective-permute-start | bytes 2359304 | tf_op jit(solution)/shard_map/ppermute | solution.py:278
  77.3 16.5 %collective-permute-start.15 = (bf16[3,512,256]{2,1,0:T(8,128)(2,1)S(1)}, bf16[3,512,256]{2,1,0:T(8,128)(2,1)S(1)}, u32[]{:S(2)}, u32[]{:S(2)}) collective-permute-start(bf16[3,512,256]{2,1,0:T(8,128)(2,1)S(1)} %collective-permute-done.4.refs_15_.refs_8_), channel_id=1, source_target_pairs={{0,4},{4,0},{8,12},{12,8},{16,20},{20,16},{24,28},{28,24},{1,5},{5... | collective-permute-start | bytes 2359304 | tf_op jit(solution)/shard_map/ppermute | solution.py:278
  77.6 16.1 %collective-permute-start.14 = (bf16[3,256,256]{2,1,0:T(8,128)(2,1)}, bf16[3,256,256]{2,1,0:T(8,128)(2,1)}, u32[]{:S(2)}, u32[]{:S(2)}) collective-permute-start(bf16[3,256,256]{2,1,0:T(8,128)(2,1)} %slice.7), channel_id=1, source_target_pairs={{0,16},{4,20},{8,24},{12,28},{16,0},{20,4},{24,8},{28,12},{1,17},{... | collective-permute-start | bytes 1179656 | tf_op jit(solution)/shard_map/ppermute | solution.py:278
  79.2 14.6 %collective-permute-start.13 = (bf16[3,256,256]{2,1,0:T(8,128)(2,1)S(1)}, bf16[3,256,256]{2,1,0:T(8,128)(2,1)}, u32[]{:S(2)}, u32[]{:S(2)}) collective-permute-start(bf16[3,256,256]{2,1,0:T(8,128)(2,1)S(1)} %slice.6), channel_id=1, source_target_pairs={{0,8},{4,12},{8,0},{12,4},{16,24},{20,28},{24,16},{28,20},{1,9},{5... | collective-permute-start | bytes 1179656 | tf_op jit(solution)/shard_map/ppermute | solution.py:278
  94.4 22.0 %collective-permute-start.22 = (bf16[3,512,256]{2,1,0:T(8,128)(2,1)S(1)}, bf16[3,512,256]{2,1,0:T(8,128)(2,1)S(1)}, u32[]{:S(2)}, u32[]{:S(2)}) collective-permute-start(bf16[3,512,256]{2,1,0:T(8,128)(2,1)S(1)} %copy-done.16), channel_id=1, source_target_pairs={{3,0},{0,1},{1,2},{2,3},{7,4},{4,5},{5,6},{6,7},{11,8},{8,9},{9,10... | collective-permute-start | bytes 2359304 | tf_op jit(solution)/shard_map/ppermute | solution.py:390
  94.4 22.0 %collective-permute-start.21 = (bf16[3,512,256]{2,1,0:T(8,128)(2,1)}, bf16[3,512,256]{2,1,0:T(8,128)(2,1)S(1)}, u32[]{:S(2)}, u32[]{:S(2)}) collective-permute-start(bf16[3,512,256]{2,1,0:T(8,128)(2,1)} %collective-permute-done.11.refs_16_.refs_5_), channel_id=1, source_target_pairs={{0,16},{4,20},{8,24},{12,28},{16,0},{20,4},{24,8},{28,12},{1,17},{... | collective-permute-start | bytes 2359304 | tf_op jit(solution)/shard_map/ppermute | solution.py:278
  95.8 20.7 %collective-permute-start.20 = (bf16[3,512,256]{2,1,0:T(8,128)(2,1)}, bf16[3,512,256]{2,1,0:T(8,128)(2,1)S(1)}, u32[]{:S(2)}, u32[]{:S(2)}) collective-permute-start(bf16[3,512,256]{2,1,0:T(8,128)(2,1)} %collective-permute-done.11.refs_16_.refs_5_), channel_id=1, source_target_pairs={{0,8},{4,12},{8,0},{12,4},{16,24},{20,28},{24,16},{28,20},{1,9},{5... | collective-permute-start | bytes 2359304 | tf_op jit(solution)/shard_map/ppermute | solution.py:278
  97.3 20.4 %collective-permute-start.19 = (bf16[3,512,256]{2,1,0:T(8,128)(2,1)}, bf16[3,512,256]{2,1,0:T(8,128)(2,1)S(1)}, u32[]{:S(2)}, u32[]{:S(2)}) collective-permute-start(bf16[3,512,256]{2,1,0:T(8,128)(2,1)} %collective-permute-done.11.refs_16_.refs_5_), channel_id=1, source_target_pairs={{0,4},{4,0},{8,12},{12,8},{16,20},{20,16},{24,28},{28,24},{1,5},{5... | collective-permute-start | bytes 2359304 | tf_op jit(solution)/shard_map/ppermute | solution.py:278
  116.6 3.5 %collective-permute-start.24 = (bf16[3,512,256]{2,1,0:T(8,128)(2,1)S(1)}, bf16[3,512,256]{2,1,0:T(8,128)(2,1)}, u32[]{:S(2)}, u32[]{:S(2)}) collective-permute-start(bf16[3,512,256]{2,1,0:T(8,128)(2,1)S(1)} %collective-permute-done.21.refs_19_.refs_8_), channel_id=1, source_target_pairs={{0,4},{4,0},{8,12},{12,8},{16,20},{20,16},{24,28},{28,24},{1,5},{5... | collective-permute-start | bytes 2359304 | tf_op jit(solution)/shard_map/ppermute | solution.py:278
  117.0 4.2 %collective-permute-start.25 = (bf16[3,512,256]{2,1,0:T(8,128)(2,1)S(1)}, bf16[3,512,256]{2,1,0:T(8,128)(2,1)}, u32[]{:S(2)}, u32[]{:S(2)}) collective-permute-start(bf16[3,512,256]{2,1,0:T(8,128)(2,1)S(1)} %collective-permute-done.22.refs_20_.refs_9_), channel_id=1, source_target_pairs={{0,4},{4,0},{8,12},{12,8},{16,20},{20,16},{24,28},{28,24},{1,5},{5... | collective-permute-start | bytes 2359304 | tf_op jit(solution)/shard_map/ppermute | solution.py:278
  129.6 31.0 %all-to-all-start = ((bf16[8,2,256,256]{3,2,1,0:T(8,128)(2,1)}), bf16[8,2,256,256]{3,2,1,0:T(8,128)(2,1)S(1)}, u32[]{:S(2)}, u32[]{:S(2)}) async-start(bf16[8,2,256,256]{3,2,1,0:T(8,128)(2,1)} %bitcast.17), calls=%async_computation | async-start | bytes 4194304 | tf_op jit(solution)/shard_map/all_to_all | solution.py:395
  (25 other events, 329.4 us)

commit v14 on v13

--- a/solution.py
+++ b/solution.py
@@ -23,25 +23,28 @@
     return packed
 
 
-def list_task(base, span, total, steps, phased, pair, tasks, counts):
+def list_task(bases, span, steps, phased, pair, tasks, counts):
     source, klass, lag, place = pair
     half = steps // 2
-    start = lax.rem(lag - base + total, total)
-    first = jnp.where(start < span, start, start - total)
-    whole = (first > -half) & (first < span - half)
-    lower = (first >= span - half) & (first < span)
-    upper_half = (first > -steps) & (first <= -half)
-    row = jnp.maximum(first + half - 1, 0)
     number = 2 * klass if phased else 0
-    at = counts[number]
-    tasks[number, at] = pack(0, source, klass, row, place)
-    counts[number] = at + jnp.where(whole, 1, 0)
-    at = counts[number + 1]
-    second = jnp.where(upper_half, 1, 0)
-    row = jnp.maximum(first + half - 1 + half * second, 0)
-    tasks[number + 1, at] = pack(second, source, klass, row, place)
-    counts[number + 1] = at + jnp.where(lower | upper_half, 1, 0)
-    return whole | lower | upper_half
+    touched = None
+    for slot, base in enumerate(bases):
+        first = lag - base
+        whole = (first > -half) & (first < span - half)
+        lower = (first >= span - half) & (first < span)
+        higher = (first > -steps) & (first <= -half)
+        second = jnp.where(higher, 1, 0)
+        row = slot * (span + half - 1) + half - 1
+        at = counts[number]
+        tasks[number, at] = pack(0, source, klass, jnp.maximum(row + first, 0), place)
+        counts[number] = at + jnp.where(whole, 1, 0)
+        at = counts[number + 1]
+        begin = jnp.maximum(row + first + half * second, 0)
+        tasks[number + 1, at] = pack(second, source, klass, begin, place)
+        counts[number + 1] = at + jnp.where(lower | higher, 1, 0)
+        active = whole | lower | higher
+        touched = active if touched is None else touched | active
+    return touched
 
 
 def run_list(number, width, tasks, counts, hist, table, acc):
@@ -75,7 +78,7 @@
 
 
 def window_kernel(config, *refs):
-    served, local, begun, narrow, places, total, rows, height, owned = config
+    served, local, begun, narrow, places, shards, rows, height, owned = config
     refs = list(refs)
     where = refs.pop(0)
     served_refs = [refs.pop(0) for _ in range(3 if served else 0)]
@@ -85,12 +88,13 @@
     before = [refs.pop(0) for _ in range((bool(served) + bool(local)) if begun else 0)]
     outs = [refs.pop(0) for _ in range(bool(served) + bool(local))]
     table, hist, acc, prior, tasks, counts, used, sems, ends, served_sems = refs
-    base, group = where[0], where[1]
+    group = where[0]
+    bases = [where[1 + n] for n in range(shards)]
     classes, _, panels = table.shape
     steps = hist.shape[2] // panels
     margin = (steps // 2 - 1) * panels
-    span = (table.shape[1] - 2 * margin) // panels
-    phased = bool(local) or span * panels > rows
+    span = rows // panels
+    phased = bool(local) or shards > 1
 
     pltpu.make_async_copy(hist_ref, hist, ends.at[0]).start()
     near = acc.at[pl.ds(served, owned)] if local else None
@@ -98,7 +102,8 @@
         pltpu.make_async_copy(before[-1], near, ends.at[1]).start()
     for k in range(classes):
         for (slot, mask, first), piece in zip(places, pieces):
-            start = pl.multiple_of(margin + slot * rows + (group ^ mask) * height + first, 16)
+            start = margin + slot * (rows + margin) + (group ^ mask) * height + first
+            start = pl.multiple_of(start, 16)
             pltpu.make_async_copy(
                 piece.at[k], table.at[k, pl.ds(start, piece.shape[1]), :], sems.at[k]
             ).start()
@@ -108,8 +113,8 @@
     for k in range(classes):
         counts[2 * k] = 0
         counts[2 * k + 1] = 0
-        table[k, pl.ds(0, margin), :] = ends_of_table
-        table[k, pl.ds(margin + span * panels, margin), :] = ends_of_table
+        for n in range(shards + 1):
+            table[k, pl.ds(n * (rows + margin), margin), :] = ends_of_table
 
     def served_copy(i, back):
         ends_of = (acc.at[i], outs[0].at[i]) if back else (before[0].at[i], acc.at[i])
@@ -128,7 +133,7 @@
                 source, lag, klass = (ref[c, i] for ref in served_refs)
                 place = i * slots + c
                 pair = (source, klass, lag, place)
-                touched = list_task(base, span, total, steps, phased, pair, tasks, counts)
+                touched = list_task(bases, span, steps, phased, pair, tasks, counts)
                 used[place] = jnp.where(touched, 1, 0)
                 if begun and not narrow:
                     @pl.when(touched)
@@ -140,7 +145,7 @@
         def _(i):
             source, lag, klass, target = (ref[i] for ref in local_refs)
             pair = (source, klass, lag, target + served)
-            list_task(base, span, total, steps, phased, pair, tasks, counts)
+            list_task(bases, span, steps, phased, pair, tasks, counts)
 
     pltpu.make_async_copy(hist_ref, hist, ends.at[0]).wait()
     if local and begun:
@@ -153,7 +158,7 @@
                 served_copy(i, False).wait()
 
     def wait_class(k):
-        inner = table.at[k, pl.ds(margin, span * panels), :]
+        inner = table.at[k, pl.ds(margin, shards * rows), :]
         pltpu.make_async_copy(inner, inner, sems.at[k]).wait()
 
     def run_lists(number):
@@ -188,7 +193,7 @@
         pltpu.make_async_copy(near, outs[-1], ends.at[1]).wait()
 
 
-def window_sums(shard, group, served, local, hist_t, shards, sums, lanes, rows, narrow=False):
+def window_sums(numbers, group, served, local, hist_t, shards, sums, rows, narrow=False):
     owned, excite, depth = hist_t.shape
     pieces = [(slot, *piece) for slot, found in enumerate(shards) for piece in found]
     classes, _, panels = pieces[0][3].shape
@@ -202,12 +207,13 @@
         sums is not None,
         narrow,
         tuple(piece[:3] for piece in pieces),
-        lanes * rows // panels,
+        len(shards),
         rows,
         max(first + value.shape[1] for _, _, first, value in pieces),
         targets,
     )
-    operands = [jnp.stack([shard * (rows // panels), group]).astype(jnp.int32), *served, *local]
+    bases = [number * (rows // panels) for number in numbers]
+    operands = [jnp.stack([group, *bases]).astype(jnp.int32), *served, *local]
     wide = [hist_t, *[piece[3] for piece in pieces]]
     before = list(sums) if sums is not None else []
     outs = [
@@ -215,7 +221,7 @@
         for n in (places, targets)
         if n
     ]
-    depth_of_table = len(shards) * rows + 2 * (steps // 2 - 1) * panels
+    depth_of_table = len(shards) * rows + (len(shards) + 1) * (steps // 2 - 1) * panels
     return pl.pallas_call(
         functools.partial(window_kernel, config),
         out_shape=outs,
@@ -226,7 +232,7 @@
             pltpu.VMEM(hist_t.shape, hist_t.dtype),
             pltpu.VMEM((places + targets, excite, panels), jnp.float32),
             pltpu.VMEM((places if narrow else 1, excite, panels), jnp.float32),
-            pltpu.SMEM((2 * classes, pairs + 1), jnp.int32),
+            pltpu.SMEM((2 * classes, 2 * pairs + 1), jnp.int32),
             pltpu.SMEM((2 * classes,), jnp.int32),
             pltpu.SMEM((max(places, 1),), jnp.int32),
             pltpu.SemaphoreType.DMA((classes,)),
@@ -312,7 +318,14 @@
     group = lax.axis_index("grp")
     lane = lax.axis_index("lag")
     lanes = lax.axis_size("lag")
-    ring = [(i, (i - 1) % lanes) for i in range(lanes)]
+    order = list(range(0, lanes, 2)) + list(range(1, lanes, 2))[::-1]
+    ring = [(order[(i + 1) % lanes], order[i]) for i in range(lanes)]
+
+    def ahead(step):
+        number = lane
+        for at, to in [(i, order[(order.index(i) + step) % lanes]) for i in range(lanes)]:
+            number = jnp.where(lane == at, to, number)
+        return number
     served = (send_patch.T, send_lag.T, send_class.T)
     local = (local_src, local_lag, local_class, local_target)
 
@@ -323,10 +336,10 @@
         return lax.dynamic_slice(weights, (0, index * height, 0), (classes, height, panels))
 
     def add_shards(first, end, served, local, sums, **options):
-        shard = lax.rem(lane + first, lanes)
+        numbers = [ahead(step) for step in range(first, end)]
         shards = rounds[first - 1 : end - 1]
         return window_sums(
-            shard, group, served, local, hist_t, shards, [sums], lanes, rows, **options
+            numbers, group, served, local, hist_t, shards, [sums], rows, **options
         )[0]
 
     own = part(group)
@@ -357,7 +370,7 @@
     own, corner = tie(own, corner)
     own = lax.ppermute(own, "lag", ring)
     served_sums, near = window_sums(
-        lane, group * 0, served, local, hist_t, [[(0, 0, weights)]], None, lanes, rows
+        [lane], group * 0, served, local, hist_t, [[(0, 0, weights)]], None, rows
     )
     trio, own, corner, served_sums, near = tie(trio, own, corner, served_sums, near)
     held, across, along = trio

time: 164 us -> 165 us (level)
  starting transfers between devices: 34.8 us -> 21.8 us
  waiting for transfers between devices: 46.4 us -> 55.3 us
  local copies, waits for them, and re-layouts: 13.2 us -> 15.2 us
    ppermute x3, starting transfers between devices: 13.8 us -> 4.44 us  [per_device(): own = lax.ppermute(own, 'lag', ring)]
    ppermute x3, waiting for transfers between devices: 12.9 us -> 16.3 us  [per_device(): own = lax.ppermute(own, 'lag', ring)]
    ppermute x21, waiting for transfers between devices: 3.54 us -> 6.87 us  [swap(): return lax.ppermute(value, 'grp', [(i, i ^ bit) for i in range(peers)])]
    ppermute x1, starting transfers between devices: 4.28 us -> 1.2 us  [per_device(): diagonal = lax.ppermute(corner, 'lag', ring)]
    ppermute x1, waiting for transfers between devices: 16.4 us -> 18.9 us  [per_device(): diagonal = lax.ppermute(corner, 'lag', ring)]
    unnamed x45 -> x43, local copies, waits for them, and re-layouts: 10 us -> 11.9 us
  transfers between devices with their start and end apart: 27 -> 27, of which waited for: 8 -> 12; matrix products, arithmetic and copies ran while one was open for 7% -> 7% of each run, Pallas kernels for 34% -> 34%
where the time goes in v14:
time: 165 us; the launch traced here: 164 us
  Pallas kernels  68.6 us (42%)
  waiting for transfers between devices  55.3 us (34%)
  starting transfers between devices  21.8 us (13%)
  local copies, waits for them, and re-layouts  15.2 us (9%)
  other arithmetic  3.15 us (2%)
    pallas_call x5, Pallas kernels, window_sums(): pl.pallas_call(functools.partial(window_kernel, config), out_shape=outs,...  66.2 us
    ppermute x1, waiting for transfers between devices, per_device(): diagonal = lax.ppermute(corner, 'lag', ring)  18.9 us
    ppermute x3, waiting for transfers between devices, per_device(): own = lax.ppermute(own, 'lag', ring)  16.3 us
    unnamed x43, local copies, waits for them, and re-layouts  11.9 us
    ppermute x21, starting transfers between devices, swap(): return lax.ppermute(value, 'grp', [(i, i ^ bit) for i in range(peers)])  11.6 us
    all_to_all x1, waiting for transfers between devices, per_device(): lax.all_to_all(contribution.reshape(peers, slots, *contribution.shape[1:]...  9.07 us
    ppermute x21, waiting for transfers between devices, swap(): return lax.ppermute(value, 'grp', [(i, i ^ bit) for i in range(peers)])  6.87 us
    ppermute x3, starting transfers between devices, per_device(): own = lax.ppermute(own, 'lag', ring)  4.44 us
  transfers between devices with their start and end apart: 27, of which 12 were waited for; matrix products, arithmetic and copies ran while one was open for 7% of the time, Pallas kernels for 34%

profile of v14, /device:TPU:0, one launch (start us, length us, event | category | flops | bytes accessed | tf_op | source)
XLA Modules:
  0.0 164.5 jit_solution(9992909232780566687)
XLA Ops:
  1.2 3.1 %collective-permute-start = (bf16[3,512,256]{2,1,0:T(8,128)(2,1)S(1)}, bf16[3,512,256]{2,1,0:T(8,128)(2,1)S(1)}, u32[]{:S(2)}, u32[]{:S(2)}) collective-permute-start(bf16[3,512,256]{2,1,0:T(8,128)(2,1)S(1)} %constant_dynamic-slice_fusion.1), channel_id=1, source_target_pairs={{2,0},{3,2},{1,3},{0,1},{6,4},{7,6},{5,7},{4,5},{10,8},{11,10},{9,... | collective-permute-start | bytes 2359304 | tf_op jit(solution)/shard_map/ppermute | solution.py:366
  4.3 6.3 %copy.16 = bf16[4,2048,256]{1,2,0:T(8,128)(2,1)} copy(bf16[4,2048,256]{2,1,0:T(8,128)(2,1)} %param.13) | data formatting | bytes 8388608 | tf_op args[1]
  11.1 11.7 %collective-permute-done.refs_6_.refs_5_ = bf16[3,512,256]{2,1,0:T(8,128)(2,1)S(1)} collective-permute-done((bf16[3,512,256]{2,1,0:T(8,128)(2,1)S(1)}, bf16[3,512,256]{2,1,0:T(8,128)(2,1)S(1)}, u32[]{:S(2)}, u32[]{:S(2)}) %collective-permute-start) | collective-permute-done | bytes 786464 | tf_op jit(solution)/shard_map/ppermute | solution.py:366
  22.8 1.6 collective-permute-start.2
  24.4 1.5 collective-permute-start.1
  25.9 2.1 %constant_dynamic-slice_fusion = bf16[3,512,256]{2,1,0:T(8,128)(2,1)} fusion(bf16[3,4096,256]{2,1,0:T(8,128)(2,1)} %refs_9_.1, s32[]{:T(128)S(6)} %select_n.64), kind=kLoop, calls=%fused_computation.5 | loop fusion | bytes 1572868 | tf_op jit(solution)/shard_map/dynamic_slice | solution.py:336
  28.7 13.3 %shard_map.118 = (f32[16,256,256]{2,1,0:T(8,128)}, f32[4,256,256]{2,1,0:T(8,128)}) custom-call(s32[2]{0:T(128)} %pad_add_fusion.1.refs_0_, s32[2,8]{1,0:T(2,128)} %bitcast.18, s32[2,8]{1,0:T(2,128)} %bitcast.21, s32[2,8]{1,0:T(2,128)} %bitcast.24, s32[48]{0:T(128)} %refs_1_.3, s32[48]{0:T(128)} %refs_2_.3, s32[48]{0:T(128)} %refs_3_.3, s32[48]{0:T(128)} %refs_4_.5, ...), custom_call_target="tpu_custom_call" | custom-call | flops 17179869184 | bytes 10485760 | tf_op jit(solution)/shard_map/pallas_call | solution.py:225
  42.0 4.7 %collective-permute-done.3.refs_13_.refs_6_ = bf16[3,512,256]{2,1,0:T(8,128)(2,1)S(1)} collective-permute-done((bf16[3,512,256]{2,1,0:T(8,128)(2,1)S(1)}, bf16[3,512,256]{2,1,0:T(8,128)(2,1)S(1)}, u32[]{:S(2)}, u32[]{:S(2)}) %collective-permute-start.3) | collective-permute-done | bytes 786464 | tf_op jit(solution)/shard_map/ppermute | solution.py:371
  50.7 18.9 %collective-permute-done.6.refs_12_.refs_11_ = bf16[3,512,256]{2,1,0:T(8,128)(2,1)} collective-permute-done((bf16[3,512,256]{2,1,0:T(8,128)(2,1)}, bf16[3,512,256]{2,1,0:T(8,128)(2,1)}, u32[]{:S(2)}, u32[]{:S(2)}) %collective-permute-start.6) | collective-permute-done | bytes 786464 | tf_op jit(solution)/shard_map/ppermute | solution.py:383
  71.8 1.4 collective-permute-done.12.refs_13_.refs_12_
  73.9 1.3 collective-permute-start.14
  75.1 1.5 collective-permute-start.13
  76.6 15.9 %shard_map.119.refs_24_ = f32[4,256,256]{2,1,0:T(8,128)} custom-call(s32[2]{0:T(128)} %pad_add_fusion.2.refs_0_, s32[48]{0:T(128)} %refs_1_.3, s32[48]{0:T(128)} %refs_2_.3, s32[48]{0:T(128)} %refs_3_.3, s32[48]{0:T(128)} %refs_4_.5, bf16[4,256,2048]{2,1,0:T(8,128)(2,1)} %bitcast.13, ...), custom_call_target="tpu_custom_call", output_to_operand_aliasing={{}: (14, {})} | custom-call | flops 12884901888 | bytes 10485760 | tf_op jit(solution)/shard_map/pallas_call | solution.py:225
  95.2 1.5 collective-permute-start.21
  96.7 1.5 collective-permute-start.20
  99.6 10.9 %shard_map.120.refs_13_ = f32[16,256,256]{2,1,0:T(8,128)} custom-call(s32[3]{0:T(128)} %pad_add_fusion.3.refs_0_, s32[2,8]{1,0:T(2,128)} %bitcast.19, s32[2,8]{1,0:T(2,128)} %bitcast.22, s32[2,8]{1,0:T(2,128)} %bitcast.25, bf16[4,256,2048]{2,1,0:T(8,128)(2,1)} %bitcast.14, bf16[3,512,256]{2,1,0:T(8,128)(2,1)} %copy-done.7, ...), custom_call_target="tpu_custom_call", output_to_operand_aliasing={{}: (23, {})} | custom-call | flops 4294967296 | bytes 16777216 | tf_op jit(solution)/shard_map/pallas_call | solution.py:225
  110.5 4.1 %collective-permute-done.22.refs_20_.refs_9_ = bf16[3,512,256]{2,1,0:T(8,128)(2,1)S(1)} collective-permute-done((bf16[3,512,256]{2,1,0:T(8,128)(2,1)}, bf16[3,512,256]{2,1,0:T(8,128)(2,1)S(1)}, u32[]{:S(2)}, u32[]{:S(2)}) %collective-permute-start.22) | collective-permute-done | bytes 786464 | tf_op jit(solution)/shard_map/ppermute | solution.py:403
  115.1 1.2 collective-permute-done.20.refs_18_.refs_7_
  117.5 1.2 collective-permute-done.23.refs_21_.refs_10_
  121.0 9.5 %shard_map.122 = bf16[16,256,256]{2,1,0:T(8,128)(2,1)} custom-call(s32[2]{0:T(128)} %pad_add_fusion.4.refs_0_, s32[2,8]{1,0:T(2,128)} %bitcast.20, s32[2,8]{1,0:T(2,128)} %bitcast.23, s32[2,8]{1,0:T(2,128)} %bitcast.26, bf16[4,256,2048]{2,1,0:T(8,128)(2,1)} %bitcast.15, bf16[3,512,256]{2,1,0:T(8,128)(2,1)} %collective-permute-done.11.refs_16_.refs_5_, ...), custom_call_target="tpu_custom_call" | custom-call | flops 4294967296 | bytes 10485760 | tf_op jit(solution)/shard_map/pallas_call | solution.py:225
  130.5 3.8 %all-to-all-start = ((bf16[8,2,256,256]{3,2,1,0:T(8,128)(2,1)}), bf16[8,2,256,256]{3,2,1,0:T(8,128)(2,1)S(1)}, u32[]{:S(2)}, u32[]{:S(2)}) async-start(bf16[8,2,256,256]{3,2,1,0:T(8,128)(2,1)} %bitcast.17), calls=%async_computation | async-start | bytes 4194304 | tf_op jit(solution)/shard_map/all_to_all | solution.py:408
  134.9 16.7 %shard_map.121.near_ref = f32[4,256,256]{2,1,0:T(8,128)} custom-call(s32[3]{0:T(128)} %pad_add_fusion.refs_0_, s32[48]{0:T(128)} %refs_1_.3, s32[48]{0:T(128)} %refs_2_.3, s32[48]{0:T(128)} %refs_3_.3, s32[48]{0:T(128)} %refs_4_.5, bf16[4,256,2048]{2,1,0:T(8,128)(2,1)} %bitcast.16, bf16[3,512,256]{2,1,0:T(8,128)(2,1)} %copy-done.6, ...), custom_call_target="tpu_custom_call", output_to_operand_aliasing={{}: (24, {})} | custom-call | flops 12884901888 | bytes 16777216 | tf_op jit(solution)/shard_map/pallas_call | solution.py:225
  151.6 9.1 %all-to-all-done.recv_ref = bf16[8,2,256,256]{3,2,1,0:T(8,128)(2,1)S(1)} async-done(((bf16[8,2,256,256]{3,2,1,0:T(8,128)(2,1)}), bf16[8,2,256,256]{3,2,1,0:T(8,128)(2,1)S(1)}, u32[]{:S(2)}, u32[]{:S(2)}) %all-to-all-start) | async-done | bytes 2097184 | tf_op jit(solution)/shard_map/all_to_all | solution.py:408
  161.9 2.4 %shard_map.123 = bf16[4,256,256]{2,1,0:T(8,128)(2,1)} custom-call(s32[2,8]{1,0:T(2,128)S(1)} %bitcast.11, f32[4,256,256]{2,1,0:T(8,128)S(1)} %copy-done, bf16[8,2,256,256]{3,2,1,0:T(8,128)(2,1)S(1)} %all-to-all-done.recv_ref, bf16[4,256,256]{2,1,0:T(8,128)(2,1)S(1)} %copy-done.1, bf16[4,256,256]{2,1,0:T(8,128)(2,1)S(1)} %copy-done.2), custom_call_target="tpu_custom_call" | custom-call | tf_op jit(solution)/shard_map/pallas_call | solution.py:273
  (88 shorter events, 19.2 us)
Async XLA Ops:
  1.2 21.6 %collective-permute-start = (bf16[3,512,256]{2,1,0:T(8,128)(2,1)S(1)}, bf16[3,512,256]{2,1,0:T(8,128)(2,1)S(1)}, u32[]{:S(2)}, u32[]{:S(2)}) collective-permute-start(bf16[3,512,256]{2,1,0:T(8,128)(2,1)S(1)} %constant_dynamic-slice_fusion.1), channel_id=1, source_target_pairs={{2,0},{3,2},{1,3},{0,1},{6,4},{7,6},{5,7},{4,5},{10,8},{11,10},{9,... | collective-permute-start | bytes 2359304 | tf_op jit(solution)/shard_map/ppermute | solution.py:366
  22.8 23.9 %collective-permute-start.2 = (bf16[3,512,256]{2,1,0:T(8,128)(2,1)S(1)}, bf16[3,512,256]{2,1,0:T(8,128)(2,1)}, u32[]{:S(2)}, u32[]{:S(2)}) collective-permute-start(bf16[3,512,256]{2,1,0:T(8,128)(2,1)S(1)} %collective-permute-done.refs_6_.refs_5_), channel_id=1, source_target_pairs={{0,16},{4,20},{8,24},{12,28},{16,0},{20,4},{24,8},{28,12},{1,17},{... | collective-permute-start | bytes 2359304 | tf_op jit(solution)/shard_map/ppermute | solution.py:284
  24.4 22.3 %collective-permute-start.1 = (bf16[3,512,256]{2,1,0:T(8,128)(2,1)S(1)}, bf16[3,512,256]{2,1,0:T(8,128)(2,1)S(1)}, u32[]{:S(2)}, u32[]{:S(2)}) collective-permute-start(bf16[3,512,256]{2,1,0:T(8,128)(2,1)S(1)} %collective-permute-done.refs_6_.refs_5_), channel_id=1, source_target_pairs={{0,8},{4,12},{8,0},{12,4},{16,24},{20,28},{24,16},{28,20},{1,9},{5... | collective-permute-start | bytes 2359304 | tf_op jit(solution)/shard_map/ppermute | solution.py:284
  28.0 18.7 %collective-permute-start.3 = (bf16[3,512,256]{2,1,0:T(8,128)(2,1)S(1)}, bf16[3,512,256]{2,1,0:T(8,128)(2,1)S(1)}, u32[]{:S(2)}, u32[]{:S(2)}) collective-permute-start(bf16[3,512,256]{2,1,0:T(8,128)(2,1)S(1)} %collective-permute-done.refs_6_.refs_5_), channel_id=1, source_target_pairs={{2,0},{3,2},{1,3},{0,1},{6,4},{7,6},{5,7},{4,5},{10,8},{11,10},{9,... | collective-permute-start | bytes 2359304 | tf_op jit(solution)/shard_map/ppermute | solution.py:371
  46.7 3.4 %collective-permute-start.7 = (bf16[3,512,256]{2,1,0:T(8,128)(2,1)S(1)}, bf16[3,512,256]{2,1,0:T(8,128)(2,1)S(1)}, u32[]{:S(2)}, u32[]{:S(2)}) collective-permute-start(bf16[3,512,256]{2,1,0:T(8,128)(2,1)S(1)} %collective-permute-done.refs_6_.refs_5_), channel_id=1, source_target_pairs={{0,4},{4,0},{8,12},{12,8},{16,20},{20,16},{24,28},{28,24},{1,5},{5... | collective-permute-start | bytes 2359304 | tf_op jit(solution)/shard_map/ppermute | solution.py:284
  47.6 21.9 %collective-permute-start.5 = (bf16[3,512,256]{2,1,0:T(8,128)(2,1)S(1)}, bf16[3,512,256]{2,1,0:T(8,128)(2,1)S(1)}, u32[]{:S(2)}, u32[]{:S(2)}) collective-permute-start(bf16[3,512,256]{2,1,0:T(8,128)(2,1)S(1)} %collective-permute-done.3.refs_13_.refs_6_), channel_id=1, source_target_pairs={{0,16},{4,20},{8,24},{12,28},{16,0},{20,4},{24,8},{28,12},{1,17},{... | collective-permute-start | bytes 2359304 | tf_op jit(solution)/shard_map/ppermute | solution.py:284
  48.1 21.4 %collective-permute-start.4 = (bf16[3,512,256]{2,1,0:T(8,128)(2,1)S(1)}, bf16[3,512,256]{2,1,0:T(8,128)(2,1)S(1)}, u32[]{:S(2)}, u32[]{:S(2)}) collective-permute-start(bf16[3,512,256]{2,1,0:T(8,128)(2,1)S(1)} %collective-permute-done.3.refs_13_.refs_6_), channel_id=1, source_target_pairs={{0,8},{4,12},{8,0},{12,4},{16,24},{20,28},{24,16},{28,20},{1,9},{5... | collective-permute-start | bytes 2359304 | tf_op jit(solution)/shard_map/ppermute | solution.py:284
  49.0 20.6 %collective-permute-start.6 = (bf16[3,512,256]{2,1,0:T(8,128)(2,1)}, bf16[3,512,256]{2,1,0:T(8,128)(2,1)}, u32[]{:S(2)}, u32[]{:S(2)}) collective-permute-start(bf16[3,512,256]{2,1,0:T(8,128)(2,1)} %constant_dynamic-slice_fusion), channel_id=1, source_target_pairs={{2,0},{3,2},{1,3},{0,1},{6,4},{7,6},{5,7},{4,5},{10,8},{11,10},{9,... | collective-permute-start | bytes 2359304 | tf_op jit(solution)/shard_map/ppermute | solution.py:383
  50.2 19.4 %collective-permute-start.8 = (bf16[3,512,256]{2,1,0:T(8,128)(2,1)}, bf16[3,512,256]{2,1,0:T(8,128)(2,1)S(1)}, u32[]{:S(2)}, u32[]{:S(2)}) collective-permute-start(bf16[3,512,256]{2,1,0:T(8,128)(2,1)} %copy-done.9), channel_id=1, source_target_pairs={{0,4},{4,0},{8,12},{12,8},{16,20},{20,16},{24,28},{28,24},{1,5},{5... | collective-permute-start | bytes 2359304 | tf_op jit(solution)/shard_map/ppermute | solution.py:284
  50.4 19.2 %collective-permute-start.10 = (bf16[3,512,256]{2,1,0:T(8,128)(2,1)S(1)}, bf16[3,512,256]{2,1,0:T(8,128)(2,1)S(1)}, u32[]{:S(2)}, u32[]{:S(2)}) collective-permute-start(bf16[3,512,256]{2,1,0:T(8,128)(2,1)S(1)} %collective-permute-done.3.refs_13_.refs_6_), channel_id=1, source_target_pairs={{0,4},{4,0},{8,12},{12,8},{16,20},{20,16},{24,28},{28,24},{1,5},{5... | collective-permute-start | bytes 2359304 | tf_op jit(solution)/shard_map/ppermute | solution.py:284
  71.2 21.3 %collective-permute-start.11 = (bf16[3,512,256]{2,1,0:T(8,128)(2,1)S(1)}, bf16[3,512,256]{2,1,0:T(8,128)(2,1)}, u32[]{:S(2)}, u32[]{:S(2)}) collective-permute-start(bf16[3,512,256]{2,1,0:T(8,128)(2,1)S(1)} %collective-permute-done.3.refs_13_.refs_6_), channel_id=1, source_target_pairs={{2,0},{3,2},{1,3},{0,1},{6,4},{7,6},{5,7},{4,5},{10,8},{11,10},{9,... | collective-permute-start | bytes 2359304 | tf_op jit(solution)/shard_map/ppermute | solution.py:389
  73.2 19.4 %collective-permute-start.16 = (bf16[3,512,256]{2,1,0:T(8,128)(2,1)S(1)}, bf16[3,512,256]{2,1,0:T(8,128)(2,1)S(1)}, u32[]{:S(2)}, u32[]{:S(2)}) collective-permute-start(bf16[3,512,256]{2,1,0:T(8,128)(2,1)S(1)} %collective-permute-done.5.refs_16_.refs_9_), channel_id=1, source_target_pairs={{0,4},{4,0},{8,12},{12,8},{16,20},{20,16},{24,28},{28,24},{1,5},{5... | collective-permute-start | bytes 2359304 | tf_op jit(solution)/shard_map/ppermute | solution.py:284
  73.4 19.2 %collective-permute-start.15 = (bf16[3,512,256]{2,1,0:T(8,128)(2,1)S(1)}, bf16[3,512,256]{2,1,0:T(8,128)(2,1)S(1)}, u32[]{:S(2)}, u32[]{:S(2)}) collective-permute-start(bf16[3,512,256]{2,1,0:T(8,128)(2,1)S(1)} %collective-permute-done.4.refs_15_.refs_8_), channel_id=1, source_target_pairs={{0,4},{4,0},{8,12},{12,8},{16,20},{20,16},{24,28},{28,24},{1,5},{5... | collective-permute-start | bytes 2359304 | tf_op jit(solution)/shard_map/ppermute | solution.py:284
  73.9 18.7 %collective-permute-start.14 = (bf16[3,256,256]{2,1,0:T(8,128)(2,1)S(1)}, bf16[3,256,256]{2,1,0:T(8,128)(2,1)S(1)}, u32[]{:S(2)}, u32[]{:S(2)}) collective-permute-start(bf16[3,256,256]{2,1,0:T(8,128)(2,1)S(1)} %slice.7), channel_id=1, source_target_pairs={{0,16},{4,20},{8,24},{12,28},{16,0},{20,4},{24,8},{28,12},{1,17},{... | collective-permute-start | bytes 1179656 | tf_op jit(solution)/shard_map/ppermute | solution.py:284
  75.1 17.4 %collective-permute-start.13 = (bf16[3,256,256]{2,1,0:T(8,128)(2,1)S(1)}, bf16[3,256,256]{2,1,0:T(8,128)(2,1)}, u32[]{:S(2)}, u32[]{:S(2)}) collective-permute-start(bf16[3,256,256]{2,1,0:T(8,128)(2,1)S(1)} %slice.6), channel_id=1, source_target_pairs={{0,8},{4,12},{8,0},{12,4},{16,24},{20,28},{24,16},{28,20},{1,9},{5... | collective-permute-start | bytes 1179656 | tf_op jit(solution)/shard_map/ppermute | solution.py:284
  93.5 5.3 %collective-permute-start.17 = (bf16[3,256,256]{2,1,0:T(8,128)(2,1)}, bf16[3,256,256]{2,1,0:T(8,128)(2,1)S(1)}, u32[]{:S(2)}, u32[]{:S(2)}) collective-permute-start(bf16[3,256,256]{2,1,0:T(8,128)(2,1)} %collective-permute-done.13.refs_19_.refs_12_), channel_id=1, source_target_pairs={{0,4},{4,0},{8,12},{12,8},{16,20},{20,16},{24,28},{28,24},{1,5},{5... | collective-permute-start | bytes 1179656 | tf_op jit(solution)/shard_map/ppermute | solution.py:284
  94.4 5.2 %collective-permute-start.18 = (bf16[3,256,256]{2,1,0:T(8,128)(2,1)S(1)}, bf16[3,256,256]{2,1,0:T(8,128)(2,1)}, u32[]{:S(2)}, u32[]{:S(2)}) collective-permute-start(bf16[3,256,256]{2,1,0:T(8,128)(2,1)S(1)} %collective-permute-done.14.refs_20_.refs_13_), channel_id=1, source_target_pairs={{0,4},{4,0},{8,12},{12,8},{16,20},{20,16},{24,28},{28,24},{1,5},{5... | collective-permute-start | bytes 1179656 | tf_op jit(solution)/shard_map/ppermute | solution.py:284
  94.4 20.2 %collective-permute-start.22 = (bf16[3,512,256]{2,1,0:T(8,128)(2,1)}, bf16[3,512,256]{2,1,0:T(8,128)(2,1)S(1)}, u32[]{:S(2)}, u32[]{:S(2)}) collective-permute-start(bf16[3,512,256]{2,1,0:T(8,128)(2,1)} %constant_dynamic-slice_fusion), channel_id=1, source_target_pairs={{0,2},{2,3},{3,1},{1,0},{4,6},{6,7},{7,5},{5,4},{8,10},{10,11},{11... | collective-permute-start | bytes 2359304 | tf_op jit(solution)/shard_map/ppermute | solution.py:403
  95.2 19.9 %collective-permute-start.21 = (bf16[3,512,256]{2,1,0:T(8,128)(2,1)}, bf16[3,512,256]{2,1,0:T(8,128)(2,1)S(1)}, u32[]{:S(2)}, u32[]{:S(2)}) collective-permute-start(bf16[3,512,256]{2,1,0:T(8,128)(2,1)} %collective-permute-done.11.refs_16_.refs_5_), channel_id=1, source_target_pairs={{0,16},{4,20},{8,24},{12,28},{16,0},{20,4},{24,8},{28,12},{1,17},{... | collective-permute-start | bytes 2359304 | tf_op jit(solution)/shard_map/ppermute | solution.py:284
  96.7 19.6 %collective-permute-start.20 = (bf16[3,512,256]{2,1,0:T(8,128)(2,1)}, bf16[3,512,256]{2,1,0:T(8,128)(2,1)S(1)}, u32[]{:S(2)}, u32[]{:S(2)}) collective-permute-start(bf16[3,512,256]{2,1,0:T(8,128)(2,1)} %collective-permute-done.11.refs_16_.refs_5_), channel_id=1, source_target_pairs={{0,8},{4,12},{8,0},{12,4},{16,24},{20,28},{24,16},{28,20},{1,9},{5... | collective-permute-start | bytes 2359304 | tf_op jit(solution)/shard_map/ppermute | solution.py:284
  99.6 17.9 %collective-permute-start.19 = (bf16[3,512,256]{2,1,0:T(8,128)(2,1)}, bf16[3,512,256]{2,1,0:T(8,128)(2,1)S(1)}, u32[]{:S(2)}, u32[]{:S(2)}) collective-permute-start(bf16[3,512,256]{2,1,0:T(8,128)(2,1)} %collective-permute-done.11.refs_16_.refs_5_), channel_id=1, source_target_pairs={{0,4},{4,0},{8,12},{12,8},{16,20},{20,16},{24,28},{28,24},{1,5},{5... | collective-permute-start | bytes 2359304 | tf_op jit(solution)/shard_map/ppermute | solution.py:284
  116.3 3.5 %collective-permute-start.24 = (bf16[3,512,256]{2,1,0:T(8,128)(2,1)S(1)}, bf16[3,512,256]{2,1,0:T(8,128)(2,1)}, u32[]{:S(2)}, u32[]{:S(2)}) collective-permute-start(bf16[3,512,256]{2,1,0:T(8,128)(2,1)S(1)} %collective-permute-done.21.refs_19_.refs_8_), channel_id=1, source_target_pairs={{0,4},{4,0},{8,12},{12,8},{16,20},{20,16},{24,28},{28,24},{1,5},{5... | collective-permute-start | bytes 2359304 | tf_op jit(solution)/shard_map/ppermute | solution.py:284
  116.8 4.2 %collective-permute-start.25 = (bf16[3,512,256]{2,1,0:T(8,128)(2,1)S(1)}, bf16[3,512,256]{2,1,0:T(8,128)(2,1)}, u32[]{:S(2)}, u32[]{:S(2)}) collective-permute-start(bf16[3,512,256]{2,1,0:T(8,128)(2,1)S(1)} %collective-permute-done.22.refs_20_.refs_9_), channel_id=1, source_target_pairs={{0,4},{4,0},{8,12},{12,8},{16,20},{20,16},{24,28},{28,24},{1,5},{5... | collective-permute-start | bytes 2359304 | tf_op jit(solution)/shard_map/ppermute | solution.py:284
  130.5 30.2 %all-to-all-start = ((bf16[8,2,256,256]{3,2,1,0:T(8,128)(2,1)}), bf16[8,2,256,256]{3,2,1,0:T(8,128)(2,1)S(1)}, u32[]{:S(2)}, u32[]{:S(2)}) async-start(bf16[8,2,256,256]{3,2,1,0:T(8,128)(2,1)} %bitcast.17), calls=%async_computation | async-start | bytes 4194304 | tf_op jit(solution)/shard_map/all_to_all | solution.py:408
  (24 other events, 294.7 us)

commit v15 on v14

--- a/solution.py
+++ b/solution.py
@@ -367,7 +367,6 @@
     own, hist_t, opposite = tie(own, hist_t, group ^ 6)
     corner = part(opposite)
     trio = neighbours(own)
-    own, corner = tie(own, corner)
     own = lax.ppermute(own, "lag", ring)
     served_sums, near = window_sums(
         [lane], group * 0, served, local, hist_t, [[(0, 0, weights)]], None, rows

time: 165 us -> 162 us (0.982)
  waiting for transfers between devices: 55.3 us -> 49.8 us
  starting transfers between devices: 21.8 us -> 25.3 us
    ppermute x1, starting transfers between devices: 1.2 us -> 4.9 us  [per_device(): diagonal = lax.ppermute(corner, 'lag', ring)]
    ppermute x21, starting transfers between devices: 11.6 us -> 8.78 us  [swap(): return lax.ppermute(value, 'grp', [(i, i ^ bit) for i in range(peers)])]
    ppermute x21, waiting for transfers between devices: 6.87 us -> 4.18 us  [swap(): return lax.ppermute(value, 'grp', [(i, i ^ bit) for i in range(peers)])]
    ppermute x1, waiting for transfers between devices: 18.9 us -> 16.7 us  [per_device(): diagonal = lax.ppermute(corner, 'lag', ring)]
    ppermute x3, starting transfers between devices: 4.44 us -> 6.4 us  [per_device(): own = lax.ppermute(own, 'lag', ring)]
  transfers between devices with their start and end apart: 27 -> 27, of which waited for: 12 -> 9; matrix products, arithmetic and copies ran while one was open for 7% -> 7% of each run, Pallas kernels for 34% -> 35%
where the time goes in v15:
time: 162 us; the launch traced here: 161 us
  Pallas kernels  67.5 us (42%)
  waiting for transfers between devices  49.8 us (31%)
  starting transfers between devices  25.3 us (16%)
  local copies, waits for them, and re-layouts  15.2 us (9%)
  other arithmetic  3.15 us (2%)
    pallas_call x5, Pallas kernels, window_sums(): pl.pallas_call(functools.partial(window_kernel, config), out_shape=outs,...  65.1 us
    ppermute x1, waiting for transfers between devices, per_device(): diagonal = lax.ppermute(corner, 'lag', ring)  16.7 us
    ppermute x3, waiting for transfers between devices, per_device(): own = lax.ppermute(own, 'lag', ring)  15.6 us
    unnamed x43, local copies, waits for them, and re-layouts  11.9 us
    ppermute x21, starting transfers between devices, swap(): return lax.ppermute(value, 'grp', [(i, i ^ bit) for i in range(peers)])  8.78 us
    all_to_all x1, waiting for transfers between devices, per_device(): lax.all_to_all(contribution.reshape(peers, slots, *contribution.shape[1:]...  7.77 us
    ppermute x3, starting transfers between devices, per_device(): own = lax.ppermute(own, 'lag', ring)  6.4 us
    ppermute x1, waiting for transfers between devices, per_device(): diagonal = lax.ppermute(corner, 'lag', [(j, i) for i, j in ring])  5.54 us
  transfers between devices with their start and end apart: 27, of which 9 were waited for; matrix products, arithmetic and copies ran while one was open for 7% of the time, Pallas kernels for 35%

profile of v15, /device:TPU:0, one launch (start us, length us, event | category | flops | bytes accessed | tf_op | source)
XLA Modules:
  0.0 161.4 jit_solution(3628276299432263051)
XLA Ops:
  0.0 1.2 constant_dynamic-slice_fusion.1
  1.2 3.1 %collective-permute-start = (bf16[3,512,256]{2,1,0:T(8,128)(2,1)S(1)}, bf16[3,512,256]{2,1,0:T(8,128)(2,1)S(1)}, u32[]{:S(2)}, u32[]{:S(2)}) collective-permute-start(bf16[3,512,256]{2,1,0:T(8,128)(2,1)S(1)} %constant_dynamic-slice_fusion.1), channel_id=1, source_target_pairs={{2,0},{3,2},{1,3},{0,1},{6,4},{7,6},{5,7},{4,5},{10,8},{11,10},{9,... | collective-permute-start | bytes 2359304 | tf_op jit(solution)/shard_map/ppermute | solution.py:366
  4.3 6.3 %copy.16 = bf16[4,2048,256]{1,2,0:T(8,128)(2,1)} copy(bf16[4,2048,256]{2,1,0:T(8,128)(2,1)} %param.13) | data formatting | bytes 8388608 | tf_op args[1]
  11.1 11.7 %collective-permute-done.refs_6_.refs_5_ = bf16[3,512,256]{2,1,0:T(8,128)(2,1)S(1)} collective-permute-done((bf16[3,512,256]{2,1,0:T(8,128)(2,1)S(1)}, bf16[3,512,256]{2,1,0:T(8,128)(2,1)S(1)}, u32[]{:S(2)}, u32[]{:S(2)}) %collective-permute-start) | collective-permute-done | bytes 786464 | tf_op jit(solution)/shard_map/ppermute | solution.py:366
  23.7 1.5 collective-permute-start.2
  25.2 1.5 collective-permute-start.1
  26.7 14.3 %shard_map.118 = (f32[16,256,256]{2,1,0:T(8,128)}, f32[4,256,256]{2,1,0:T(8,128)}) custom-call(s32[2]{0:T(128)} %pad_add_fusion.1.refs_0_, s32[2,8]{1,0:T(2,128)} %bitcast.18, s32[2,8]{1,0:T(2,128)} %bitcast.21, s32[2,8]{1,0:T(2,128)} %bitcast.24, s32[48]{0:T(128)} %refs_1_.3, s32[48]{0:T(128)} %refs_2_.3, s32[48]{0:T(128)} %refs_3_.3, s32[48]{0:T(128)} %refs_4_.5, ...), custom_call_target="tpu_custom_call" | custom-call | flops 17179869184 | bytes 10485760 | tf_op jit(solution)/shard_map/pallas_call | solution.py:225
  41.0 2.1 %constant_dynamic-slice_fusion = bf16[3,512,256]{2,1,0:T(8,128)(2,1)} fusion(bf16[3,4096,256]{2,1,0:T(8,128)(2,1)} %refs_9_.1, s32[]{:T(128)S(6)} %select_n.64), kind=kLoop, calls=%fused_computation.5 | loop fusion | bytes 1572868 | tf_op jit(solution)/shard_map/dynamic_slice | solution.py:336
  44.6 1.5 collective-permute-start.4
  46.1 4.9 %collective-permute-start.6 = (bf16[3,512,256]{2,1,0:T(8,128)(2,1)}, bf16[3,512,256]{2,1,0:T(8,128)(2,1)}, u32[]{:S(2)}, u32[]{:S(2)}) collective-permute-start(bf16[3,512,256]{2,1,0:T(8,128)(2,1)} %constant_dynamic-slice_fusion), channel_id=1, source_target_pairs={{2,0},{3,2},{1,3},{0,1},{6,4},{7,6},{5,7},{4,5},{10,8},{11,10},{9,... | collective-permute-start | bytes 2359304 | tf_op jit(solution)/shard_map/ppermute | solution.py:382
  51.5 16.7 %collective-permute-done.6.refs_12_.refs_11_ = bf16[3,512,256]{2,1,0:T(8,128)(2,1)} collective-permute-done((bf16[3,512,256]{2,1,0:T(8,128)(2,1)}, bf16[3,512,256]{2,1,0:T(8,128)(2,1)}, u32[]{:S(2)}, u32[]{:S(2)}) %collective-permute-start.6) | collective-permute-done | bytes 786464 | tf_op jit(solution)/shard_map/ppermute | solution.py:382
  69.9 2.5 %collective-permute-start.11 = (bf16[3,512,256]{2,1,0:T(8,128)(2,1)S(1)}, bf16[3,512,256]{2,1,0:T(8,128)(2,1)}, u32[]{:S(2)}, u32[]{:S(2)}) collective-permute-start(bf16[3,512,256]{2,1,0:T(8,128)(2,1)S(1)} %collective-permute-done.3.refs_13_.refs_6_), channel_id=1, source_target_pairs={{2,0},{3,2},{1,3},{0,1},{6,4},{7,6},{5,7},{4,5},{10,8},{11,10},{9,... | collective-permute-start | bytes 2359304 | tf_op jit(solution)/shard_map/ppermute | solution.py:388
  74.0 12.8 %shard_map.119.refs_24_ = f32[4,256,256]{2,1,0:T(8,128)} custom-call(s32[2]{0:T(128)} %pad_add_fusion.2.refs_0_, s32[48]{0:T(128)} %refs_1_.3, s32[48]{0:T(128)} %refs_2_.3, s32[48]{0:T(128)} %refs_3_.3, s32[48]{0:T(128)} %refs_4_.5, bf16[4,256,2048]{2,1,0:T(8,128)(2,1)} %bitcast.13, ...), custom_call_target="tpu_custom_call", output_to_operand_aliasing={{}: (14, {})} | custom-call | flops 12884901888 | bytes 10485760 | tf_op jit(solution)/shard_map/pallas_call | solution.py:225
  86.9 3.9 %collective-permute-done.11.refs_16_.refs_5_ = bf16[3,512,256]{2,1,0:T(8,128)(2,1)} collective-permute-done((bf16[3,512,256]{2,1,0:T(8,128)(2,1)S(1)}, bf16[3,512,256]{2,1,0:T(8,128)(2,1)}, u32[]{:S(2)}, u32[]{:S(2)}) %collective-permute-start.11) | collective-permute-done | bytes 786464 | tf_op jit(solution)/shard_map/ppermute | solution.py:388
  96.0 11.3 %shard_map.120.refs_13_ = f32[16,256,256]{2,1,0:T(8,128)} custom-call(s32[3]{0:T(128)} %pad_add_fusion.3.refs_0_, s32[2,8]{1,0:T(2,128)} %bitcast.19, s32[2,8]{1,0:T(2,128)} %bitcast.22, s32[2,8]{1,0:T(2,128)} %bitcast.25, bf16[4,256,2048]{2,1,0:T(8,128)(2,1)} %bitcast.14, bf16[3,512,256]{2,1,0:T(8,128)(2,1)} %copy-done.7, ...), custom_call_target="tpu_custom_call", output_to_operand_aliasing={{}: (23, {})} | custom-call | flops 4294967296 | bytes 16777216 | tf_op jit(solution)/shard_map/pallas_call | solution.py:225
  107.3 5.5 %collective-permute-done.22.refs_20_.refs_9_ = bf16[3,512,256]{2,1,0:T(8,128)(2,1)S(1)} collective-permute-done((bf16[3,512,256]{2,1,0:T(8,128)(2,1)}, bf16[3,512,256]{2,1,0:T(8,128)(2,1)S(1)}, u32[]{:S(2)}, u32[]{:S(2)}) %collective-permute-start.22) | collective-permute-done | bytes 786464 | tf_op jit(solution)/shard_map/ppermute | solution.py:402
  114.9 1.2 collective-permute-done.23.refs_21_.refs_10_
  116.0 1.1 collective-permute-done.24.refs_22_.refs_11_
  118.3 8.4 %shard_map.122 = bf16[16,256,256]{2,1,0:T(8,128)(2,1)} custom-call(s32[2]{0:T(128)} %pad_add_fusion.4.refs_0_, s32[2,8]{1,0:T(2,128)} %bitcast.20, s32[2,8]{1,0:T(2,128)} %bitcast.23, s32[2,8]{1,0:T(2,128)} %bitcast.26, bf16[4,256,2048]{2,1,0:T(8,128)(2,1)} %bitcast.15, bf16[3,512,256]{2,1,0:T(8,128)(2,1)} %collective-permute-done.11.refs_16_.refs_5_, ...), custom_call_target="tpu_custom_call" | custom-call | flops 4294967296 | bytes 10485760 | tf_op jit(solution)/shard_map/pallas_call | solution.py:225
  126.7 4.3 %all-to-all-start = ((bf16[8,2,256,256]{3,2,1,0:T(8,128)(2,1)}), bf16[8,2,256,256]{3,2,1,0:T(8,128)(2,1)S(1)}, u32[]{:S(2)}, u32[]{:S(2)}) async-start(bf16[8,2,256,256]{3,2,1,0:T(8,128)(2,1)} %bitcast.17), calls=%async_computation | async-start | bytes 4194304 | tf_op jit(solution)/shard_map/all_to_all | solution.py:407
  131.5 18.3 %shard_map.121.near_ref = f32[4,256,256]{2,1,0:T(8,128)} custom-call(s32[3]{0:T(128)} %pad_add_fusion.refs_0_, s32[48]{0:T(128)} %refs_1_.3, s32[48]{0:T(128)} %refs_2_.3, s32[48]{0:T(128)} %refs_3_.3, s32[48]{0:T(128)} %refs_4_.5, bf16[4,256,2048]{2,1,0:T(8,128)(2,1)} %bitcast.16, bf16[3,512,256]{2,1,0:T(8,128)(2,1)} %copy-done.6, ...), custom_call_target="tpu_custom_call", output_to_operand_aliasing={{}: (24, {})} | custom-call | flops 12884901888 | bytes 16777216 | tf_op jit(solution)/shard_map/pallas_call | solution.py:225
  149.8 7.8 %all-to-all-done.recv_ref = bf16[8,2,256,256]{3,2,1,0:T(8,128)(2,1)S(1)} async-done(((bf16[8,2,256,256]{3,2,1,0:T(8,128)(2,1)}), bf16[8,2,256,256]{3,2,1,0:T(8,128)(2,1)S(1)}, u32[]{:S(2)}, u32[]{:S(2)}) %all-to-all-start) | async-done | bytes 2097184 | tf_op jit(solution)/shard_map/all_to_all | solution.py:407
  157.6 1.2 copy-done
  158.8 2.4 %shard_map.123 = bf16[4,256,256]{2,1,0:T(8,128)(2,1)} custom-call(s32[2,8]{1,0:T(2,128)S(1)} %bitcast.11, f32[4,256,256]{2,1,0:T(8,128)S(1)} %copy-done, bf16[8,2,256,256]{3,2,1,0:T(8,128)(2,1)S(1)} %all-to-all-done.recv_ref, bf16[4,256,256]{2,1,0:T(8,128)(2,1)S(1)} %copy-done.1, bf16[4,256,256]{2,1,0:T(8,128)(2,1)S(1)} %copy-done.2), custom_call_target="tpu_custom_call" | custom-call | tf_op jit(solution)/shard_map/pallas_call | solution.py:273
  (88 shorter events, 15.6 us)
Async XLA Ops:
  1.2 21.6 %collective-permute-start = (bf16[3,512,256]{2,1,0:T(8,128)(2,1)S(1)}, bf16[3,512,256]{2,1,0:T(8,128)(2,1)S(1)}, u32[]{:S(2)}, u32[]{:S(2)}) collective-permute-start(bf16[3,512,256]{2,1,0:T(8,128)(2,1)S(1)} %constant_dynamic-slice_fusion.1), channel_id=1, source_target_pairs={{2,0},{3,2},{1,3},{0,1},{6,4},{7,6},{5,7},{4,5},{10,8},{11,10},{9,... | collective-permute-start | bytes 2359304 | tf_op jit(solution)/shard_map/ppermute | solution.py:366
  22.8 20.3 %collective-permute-start.3 = (bf16[3,512,256]{2,1,0:T(8,128)(2,1)S(1)}, bf16[3,512,256]{2,1,0:T(8,128)(2,1)S(1)}, u32[]{:S(2)}, u32[]{:S(2)}) collective-permute-start(bf16[3,512,256]{2,1,0:T(8,128)(2,1)S(1)} %collective-permute-done.refs_6_.refs_5_), channel_id=1, source_target_pairs={{2,0},{3,2},{1,3},{0,1},{6,4},{7,6},{5,7},{4,5},{10,8},{11,10},{9,... | collective-permute-start | bytes 2359304 | tf_op jit(solution)/shard_map/ppermute | solution.py:370
  23.7 19.5 %collective-permute-start.2 = (bf16[3,512,256]{2,1,0:T(8,128)(2,1)S(1)}, bf16[3,512,256]{2,1,0:T(8,128)(2,1)}, u32[]{:S(2)}, u32[]{:S(2)}) collective-permute-start(bf16[3,512,256]{2,1,0:T(8,128)(2,1)S(1)} %collective-permute-done.refs_6_.refs_5_), channel_id=1, source_target_pairs={{0,16},{4,20},{8,24},{12,28},{16,0},{20,4},{24,8},{28,12},{1,17},{... | collective-permute-start | bytes 2359304 | tf_op jit(solution)/shard_map/ppermute | solution.py:284
  25.2 17.9 %collective-permute-start.1 = (bf16[3,512,256]{2,1,0:T(8,128)(2,1)S(1)}, bf16[3,512,256]{2,1,0:T(8,128)(2,1)S(1)}, u32[]{:S(2)}, u32[]{:S(2)}) collective-permute-start(bf16[3,512,256]{2,1,0:T(8,128)(2,1)S(1)} %collective-permute-done.refs_6_.refs_5_), channel_id=1, source_target_pairs={{0,8},{4,12},{8,0},{12,4},{16,24},{20,28},{24,16},{28,20},{1,9},{5... | collective-permute-start | bytes 2359304 | tf_op jit(solution)/shard_map/ppermute | solution.py:284
  43.1 7.9 %collective-permute-start.7 = (bf16[3,512,256]{2,1,0:T(8,128)(2,1)S(1)}, bf16[3,512,256]{2,1,0:T(8,128)(2,1)S(1)}, u32[]{:S(2)}, u32[]{:S(2)}) collective-permute-start(bf16[3,512,256]{2,1,0:T(8,128)(2,1)S(1)} %collective-permute-done.refs_6_.refs_5_), channel_id=1, source_target_pairs={{0,4},{4,0},{8,12},{12,8},{16,20},{20,16},{24,28},{28,24},{1,5},{5... | collective-permute-start | bytes 2359304 | tf_op jit(solution)/shard_map/ppermute | solution.py:284
  44.1 7.0 %collective-permute-start.9 = (bf16[3,512,256]{2,1,0:T(8,128)(2,1)}, bf16[3,512,256]{2,1,0:T(8,128)(2,1)S(1)}, u32[]{:S(2)}, u32[]{:S(2)}) collective-permute-start(bf16[3,512,256]{2,1,0:T(8,128)(2,1)} %collective-permute-done.2.refs_10_.refs_9_), channel_id=1, source_target_pairs={{0,4},{4,0},{8,12},{12,8},{16,20},{20,16},{24,28},{28,24},{1,5},{5... | collective-permute-start | bytes 2359304 | tf_op jit(solution)/shard_map/ppermute | solution.py:284
  44.1 24.2 %collective-permute-start.5 = (bf16[3,512,256]{2,1,0:T(8,128)(2,1)S(1)}, bf16[3,512,256]{2,1,0:T(8,128)(2,1)S(1)}, u32[]{:S(2)}, u32[]{:S(2)}) collective-permute-start(bf16[3,512,256]{2,1,0:T(8,128)(2,1)S(1)} %collective-permute-done.3.refs_13_.refs_6_), channel_id=1, source_target_pairs={{0,16},{4,20},{8,24},{12,28},{16,0},{20,4},{24,8},{28,12},{1,17},{... | collective-permute-start | bytes 2359304 | tf_op jit(solution)/shard_map/ppermute | solution.py:284
  44.6 23.6 %collective-permute-start.4 = (bf16[3,512,256]{2,1,0:T(8,128)(2,1)S(1)}, bf16[3,512,256]{2,1,0:T(8,128)(2,1)S(1)}, u32[]{:S(2)}, u32[]{:S(2)}) collective-permute-start(bf16[3,512,256]{2,1,0:T(8,128)(2,1)S(1)} %collective-permute-done.3.refs_13_.refs_6_), channel_id=1, source_target_pairs={{0,8},{4,12},{8,0},{12,4},{16,24},{20,28},{24,16},{28,20},{1,9},{5... | collective-permute-start | bytes 2359304 | tf_op jit(solution)/shard_map/ppermute | solution.py:284
  46.1 22.1 %collective-permute-start.6 = (bf16[3,512,256]{2,1,0:T(8,128)(2,1)}, bf16[3,512,256]{2,1,0:T(8,128)(2,1)}, u32[]{:S(2)}, u32[]{:S(2)}) collective-permute-start(bf16[3,512,256]{2,1,0:T(8,128)(2,1)} %constant_dynamic-slice_fusion), channel_id=1, source_target_pairs={{2,0},{3,2},{1,3},{0,1},{6,4},{7,6},{5,7},{4,5},{10,8},{11,10},{9,... | collective-permute-start | bytes 2359304 | tf_op jit(solution)/shard_map/ppermute | solution.py:382
  51.0 17.2 %collective-permute-start.8 = (bf16[3,512,256]{2,1,0:T(8,128)(2,1)}, bf16[3,512,256]{2,1,0:T(8,128)(2,1)S(1)}, u32[]{:S(2)}, u32[]{:S(2)}) collective-permute-start(bf16[3,512,256]{2,1,0:T(8,128)(2,1)} %copy-done.9), channel_id=1, source_target_pairs={{0,4},{4,0},{8,12},{12,8},{16,20},{20,16},{24,28},{28,24},{1,5},{5... | collective-permute-start | bytes 2359304 | tf_op jit(solution)/shard_map/ppermute | solution.py:284
  51.1 17.2 %collective-permute-start.10 = (bf16[3,512,256]{2,1,0:T(8,128)(2,1)S(1)}, bf16[3,512,256]{2,1,0:T(8,128)(2,1)S(1)}, u32[]{:S(2)}, u32[]{:S(2)}) collective-permute-start(bf16[3,512,256]{2,1,0:T(8,128)(2,1)S(1)} %collective-permute-done.3.refs_13_.refs_6_), channel_id=1, source_target_pairs={{0,4},{4,0},{8,12},{12,8},{16,20},{20,16},{24,28},{28,24},{1,5},{5... | collective-permute-start | bytes 2359304 | tf_op jit(solution)/shard_map/ppermute | solution.py:284
  69.9 20.9 %collective-permute-start.11 = (bf16[3,512,256]{2,1,0:T(8,128)(2,1)S(1)}, bf16[3,512,256]{2,1,0:T(8,128)(2,1)}, u32[]{:S(2)}, u32[]{:S(2)}) collective-permute-start(bf16[3,512,256]{2,1,0:T(8,128)(2,1)S(1)} %collective-permute-done.3.refs_13_.refs_6_), channel_id=1, source_target_pairs={{2,0},{3,2},{1,3},{0,1},{6,4},{7,6},{5,7},{4,5},{10,8},{11,10},{9,... | collective-permute-start | bytes 2359304 | tf_op jit(solution)/shard_map/ppermute | solution.py:388
  72.4 18.4 %collective-permute-start.16 = (bf16[3,512,256]{2,1,0:T(8,128)(2,1)S(1)}, bf16[3,512,256]{2,1,0:T(8,128)(2,1)S(1)}, u32[]{:S(2)}, u32[]{:S(2)}) collective-permute-start(bf16[3,512,256]{2,1,0:T(8,128)(2,1)S(1)} %collective-permute-done.5.refs_16_.refs_9_), channel_id=1, source_target_pairs={{0,4},{4,0},{8,12},{12,8},{16,20},{20,16},{24,28},{28,24},{1,5},{5... | collective-permute-start | bytes 2359304 | tf_op jit(solution)/shard_map/ppermute | solution.py:284
  72.7 18.1 %collective-permute-start.15 = (bf16[3,512,256]{2,1,0:T(8,128)(2,1)S(1)}, bf16[3,512,256]{2,1,0:T(8,128)(2,1)S(1)}, u32[]{:S(2)}, u32[]{:S(2)}) collective-permute-start(bf16[3,512,256]{2,1,0:T(8,128)(2,1)S(1)} %collective-permute-done.4.refs_15_.refs_8_), channel_id=1, source_target_pairs={{0,4},{4,0},{8,12},{12,8},{16,20},{20,16},{24,28},{28,24},{1,5},{5... | collective-permute-start | bytes 2359304 | tf_op jit(solution)/shard_map/ppermute | solution.py:284
  73.1 17.7 %collective-permute-start.14 = (bf16[3,256,256]{2,1,0:T(8,128)(2,1)S(1)}, bf16[3,256,256]{2,1,0:T(8,128)(2,1)S(1)}, u32[]{:S(2)}, u32[]{:S(2)}) collective-permute-start(bf16[3,256,256]{2,1,0:T(8,128)(2,1)S(1)} %slice.7), channel_id=1, source_target_pairs={{0,16},{4,20},{8,24},{12,28},{16,0},{20,4},{24,8},{28,12},{1,17},{... | collective-permute-start | bytes 1179656 | tf_op jit(solution)/shard_map/ppermute | solution.py:284
  73.4 17.4 %collective-permute-start.13 = (bf16[3,256,256]{2,1,0:T(8,128)(2,1)S(1)}, bf16[3,256,256]{2,1,0:T(8,128)(2,1)}, u32[]{:S(2)}, u32[]{:S(2)}) collective-permute-start(bf16[3,256,256]{2,1,0:T(8,128)(2,1)S(1)} %slice.6), channel_id=1, source_target_pairs={{0,8},{4,12},{8,0},{12,4},{16,24},{20,28},{24,16},{28,20},{1,9},{5... | collective-permute-start | bytes 1179656 | tf_op jit(solution)/shard_map/ppermute | solution.py:284
  91.7 3.4 %collective-permute-start.17 = (bf16[3,256,256]{2,1,0:T(8,128)(2,1)}, bf16[3,256,256]{2,1,0:T(8,128)(2,1)S(1)}, u32[]{:S(2)}, u32[]{:S(2)}) collective-permute-start(bf16[3,256,256]{2,1,0:T(8,128)(2,1)} %collective-permute-done.13.refs_19_.refs_12_), channel_id=1, source_target_pairs={{0,4},{4,0},{8,12},{12,8},{16,20},{20,16},{24,28},{28,24},{1,5},{5... | collective-permute-start | bytes 1179656 | tf_op jit(solution)/shard_map/ppermute | solution.py:284
  92.7 20.2 %collective-permute-start.22 = (bf16[3,512,256]{2,1,0:T(8,128)(2,1)}, bf16[3,512,256]{2,1,0:T(8,128)(2,1)S(1)}, u32[]{:S(2)}, u32[]{:S(2)}) collective-permute-start(bf16[3,512,256]{2,1,0:T(8,128)(2,1)} %constant_dynamic-slice_fusion), channel_id=1, source_target_pairs={{0,2},{2,3},{3,1},{1,0},{4,6},{6,7},{7,5},{5,4},{8,10},{10,11},{11... | collective-permute-start | bytes 2359304 | tf_op jit(solution)/shard_map/ppermute | solution.py:402
  93.7 19.9 %collective-permute-start.21 = (bf16[3,512,256]{2,1,0:T(8,128)(2,1)}, bf16[3,512,256]{2,1,0:T(8,128)(2,1)S(1)}, u32[]{:S(2)}, u32[]{:S(2)}) collective-permute-start(bf16[3,512,256]{2,1,0:T(8,128)(2,1)} %collective-permute-done.11.refs_16_.refs_5_), channel_id=1, source_target_pairs={{0,16},{4,20},{8,24},{12,28},{16,0},{20,4},{24,8},{28,12},{1,17},{... | collective-permute-start | bytes 2359304 | tf_op jit(solution)/shard_map/ppermute | solution.py:284
  93.9 19.6 %collective-permute-start.20 = (bf16[3,512,256]{2,1,0:T(8,128)(2,1)}, bf16[3,512,256]{2,1,0:T(8,128)(2,1)S(1)}, u32[]{:S(2)}, u32[]{:S(2)}) collective-permute-start(bf16[3,512,256]{2,1,0:T(8,128)(2,1)} %collective-permute-done.11.refs_16_.refs_5_), channel_id=1, source_target_pairs={{0,8},{4,12},{8,0},{12,4},{16,24},{20,28},{24,16},{28,20},{1,9},{5... | collective-permute-start | bytes 2359304 | tf_op jit(solution)/shard_map/ppermute | solution.py:284
  96.0 18.9 %collective-permute-start.19 = (bf16[3,512,256]{2,1,0:T(8,128)(2,1)}, bf16[3,512,256]{2,1,0:T(8,128)(2,1)S(1)}, u32[]{:S(2)}, u32[]{:S(2)}) collective-permute-start(bf16[3,512,256]{2,1,0:T(8,128)(2,1)} %collective-permute-done.11.refs_16_.refs_5_), channel_id=1, source_target_pairs={{0,4},{4,0},{8,12},{12,8},{16,20},{20,16},{24,28},{28,24},{1,5},{5... | collective-permute-start | bytes 2359304 | tf_op jit(solution)/shard_map/ppermute | solution.py:284
  113.6 3.5 %collective-permute-start.24 = (bf16[3,512,256]{2,1,0:T(8,128)(2,1)S(1)}, bf16[3,512,256]{2,1,0:T(8,128)(2,1)}, u32[]{:S(2)}, u32[]{:S(2)}) collective-permute-start(bf16[3,512,256]{2,1,0:T(8,128)(2,1)S(1)} %collective-permute-done.21.refs_19_.refs_8_), channel_id=1, source_target_pairs={{0,4},{4,0},{8,12},{12,8},{16,20},{20,16},{24,28},{28,24},{1,5},{5... | collective-permute-start | bytes 2359304 | tf_op jit(solution)/shard_map/ppermute | solution.py:284
  114.1 4.2 %collective-permute-start.25 = (bf16[3,512,256]{2,1,0:T(8,128)(2,1)S(1)}, bf16[3,512,256]{2,1,0:T(8,128)(2,1)}, u32[]{:S(2)}, u32[]{:S(2)}) collective-permute-start(bf16[3,512,256]{2,1,0:T(8,128)(2,1)S(1)} %collective-permute-done.22.refs_20_.refs_9_), channel_id=1, source_target_pairs={{0,4},{4,0},{8,12},{12,8},{16,20},{20,16},{24,28},{28,24},{1,5},{5... | collective-permute-start | bytes 2359304 | tf_op jit(solution)/shard_map/ppermute | solution.py:284
  126.7 30.9 %all-to-all-start = ((bf16[8,2,256,256]{3,2,1,0:T(8,128)(2,1)}), bf16[8,2,256,256]{3,2,1,0:T(8,128)(2,1)S(1)}, u32[]{:S(2)}, u32[]{:S(2)}) async-start(bf16[8,2,256,256]{3,2,1,0:T(8,128)(2,1)} %bitcast.17), calls=%async_computation | async-start | bytes 4194304 | tf_op jit(solution)/shard_map/all_to_all | solution.py:407
  (24 other events, 269.8 us)

commit v16 on v15

--- a/solution.py
+++ b/solution.py
@@ -23,10 +23,10 @@
     return packed
 
 
-def list_task(bases, span, steps, phased, pair, tasks, counts):
+def list_task(bases, span, steps, pair, tasks, counts):
     source, klass, lag, place = pair
     half = steps // 2
-    number = 2 * klass if phased else 0
+    number = 2 * klass
     touched = None
     for slot, base in enumerate(bases):
         first = lag - base
@@ -94,7 +94,6 @@
     steps = hist.shape[2] // panels
     margin = (steps // 2 - 1) * panels
     span = rows // panels
-    phased = bool(local) or shards > 1
 
     pltpu.make_async_copy(hist_ref, hist, ends.at[0]).start()
     near = acc.at[pl.ds(served, owned)] if local else None
@@ -133,7 +132,7 @@
                 source, lag, klass = (ref[c, i] for ref in served_refs)
                 place = i * slots + c
                 pair = (source, klass, lag, place)
-                touched = list_task(bases, span, steps, phased, pair, tasks, counts)
+                touched = list_task(bases, span, steps, pair, tasks, counts)
                 used[place] = jnp.where(touched, 1, 0)
                 if begun and not narrow:
                     @pl.when(touched)
@@ -145,7 +144,7 @@
         def _(i):
             source, lag, klass, target = (ref[i] for ref in local_refs)
             pair = (source, klass, lag, target + served)
-            list_task(bases, span, steps, phased, pair, tasks, counts)
+            list_task(bases, span, steps, pair, tasks, counts)
 
     pltpu.make_async_copy(hist_ref, hist, ends.at[0]).wait()
     if local and begun:
@@ -165,15 +164,10 @@
         run_list(number, steps, tasks, counts, hist, table, acc)
         run_list(number + 1, steps // 2, tasks, counts, hist, table, acc)
 
-    if phased:
-        @pl.loop(0, classes)
-        def _(k):
-            wait_class(k)
-            run_lists(2 * k)
-    else:
-        for k in range(classes):
-            wait_class(k)
-        run_lists(0)
+    @pl.loop(0, classes)
+    def _(k):
+        wait_class(k)
+        run_lists(2 * k)
 
     if narrow:
         prior_copy.wait()
@@ -364,14 +358,16 @@
         return [(m ^ 6, 0, v) for m, v in zip(masks, held)]
 
     own = lax.ppermute(own, "lag", ring)
-    own, hist_t, opposite = tie(own, hist_t, group ^ 6)
-    corner = part(opposite)
+    own, hist_t = tie(own, hist_t)
     trio = neighbours(own)
     own = lax.ppermute(own, "lag", ring)
     served_sums, near = window_sums(
         [lane], group * 0, served, local, hist_t, [[(0, 0, weights)]], None, rows
     )
-    trio, own, corner, served_sums, near = tie(trio, own, corner, served_sums, near)
+    opposite, near = tie(group ^ 6, near)
+    corner = part(opposite)
+    diagonal = lax.ppermute(corner, "lag", ring)
+    trio, own, served_sums, near = tie(trio, own, served_sums, near)
     held, across, along = trio
     found, across = tie(with_other_core(held, peers), across)
     found += with_other_core(across, peers)
@@ -379,7 +375,6 @@
     held, across, along = neighbours(own)
     more, held = tie(more, held)
     found += more
-    diagonal = lax.ppermute(corner, "lag", ring)
     held = with_other_core(held, peers)
     across, along, own, diagonal, found, held = tie(across, along, own, diagonal, found, held)
     diagonal = with_other_core(corners(diagonal), peers)

time: 162 us -> 163 us (level)
    ppermute x21, starting transfers between devices: 8.78 us -> 13.2 us  [swap(): return lax.ppermute(value, 'grp', [(i, i ^ bit) for i in range(peers)])]
    ppermute x21, waiting for transfers between devices: 4.18 us -> 8.37 us  [swap(): return lax.ppermute(value, 'grp', [(i, i ^ bit) for i in range(peers)])]
    ppermute x1, waiting for transfers between devices: 5.54 us -> 2.7 us  [per_device(): diagonal = lax.ppermute(corner, 'lag', [(j, i) for i, j in ring])]
    ppermute x1, waiting for transfers between devices: 16.7 us -> 14.8 us  [per_device(): diagonal = lax.ppermute(corner, 'lag', ring)]
    unnamed x43 -> x39, local copies, waits for them, and re-layouts: 11.9 us -> 11 us
  transfers between devices with their start and end apart: 27 -> 27, of which waited for: 9 -> 14; matrix products, arithmetic and copies ran while one was open for 7% -> 7% of each run, Pallas kernels for 35% -> 35%
where the time goes in v16:
time: 163 us; the launch traced here: 162 us
  Pallas kernels  69 us (42%)
  waiting for transfers between devices  50.1 us (31%)
  starting transfers between devices  25.3 us (16%)
  local copies, waits for them, and re-layouts  14.4 us (9%)
  other arithmetic  3.14 us (2%)
    pallas_call x5, Pallas kernels, window_sums(): pl.pallas_call(functools.partial(window_kernel, config), out_shape=outs,...  66.7 us
    ppermute x3, waiting for transfers between devices, per_device(): own = lax.ppermute(own, 'lag', ring)  16.1 us
    ppermute x1, waiting for transfers between devices, per_device(): diagonal = lax.ppermute(corner, 'lag', ring)  14.8 us
    ppermute x21, starting transfers between devices, swap(): return lax.ppermute(value, 'grp', [(i, i ^ bit) for i in range(peers)])  13.2 us
    unnamed x39, local copies, waits for them, and re-layouts  11 us
    ppermute x21, waiting for transfers between devices, swap(): return lax.ppermute(value, 'grp', [(i, i ^ bit) for i in range(peers)])  8.37 us
    all_to_all x1, waiting for transfers between devices, per_device(): lax.all_to_all(contribution.reshape(peers, slots, *contribution.shape[1:]...  8.1 us
    ppermute x3, starting transfers between devices, per_device(): own = lax.ppermute(own, 'lag', ring)  4.95 us
  transfers between devices with their start and end apart: 27, of which 14 were waited for; matrix products, arithmetic and copies ran while one was open for 7% of the time, Pallas kernels for 35%

profile of v16, /device:TPU:0, one launch (start us, length us, event | category | flops | bytes accessed | tf_op | source)
XLA Modules:
  0.0 162.3 jit_solution(8194128062938121327)
XLA Ops:
  1.2 3.1 %collective-permute-start = (bf16[3,512,256]{2,1,0:T(8,128)(2,1)S(1)}, bf16[3,512,256]{2,1,0:T(8,128)(2,1)S(1)}, u32[]{:S(2)}, u32[]{:S(2)}) collective-permute-start(bf16[3,512,256]{2,1,0:T(8,128)(2,1)S(1)} %constant_dynamic-slice_fusion.1), channel_id=1, source_target_pairs={{2,0},{3,2},{1,3},{0,1},{6,4},{7,6},{5,7},{4,5},{10,8},{11,10},{9,... | collective-permute-start | bytes 2359304 | tf_op jit(solution)/shard_map/ppermute | solution.py:360
  4.3 6.3 %copy.16 = bf16[4,2048,256]{1,2,0:T(8,128)(2,1)} copy(bf16[4,2048,256]{2,1,0:T(8,128)(2,1)} %param.13) | data formatting | bytes 8388608 | tf_op args[1]
  11.2 11.7 %collective-permute-done.refs_6_.refs_5_ = bf16[3,512,256]{2,1,0:T(8,128)(2,1)S(1)} collective-permute-done((bf16[3,512,256]{2,1,0:T(8,128)(2,1)S(1)}, bf16[3,512,256]{2,1,0:T(8,128)(2,1)S(1)}, u32[]{:S(2)}, u32[]{:S(2)}) %collective-permute-start) | collective-permute-done | bytes 786464 | tf_op jit(solution)/shard_map/ppermute | solution.py:360
  23.7 1.5 collective-permute-start.2
  25.2 1.5 collective-permute-start.1
  26.7 12.6 %shard_map.118 = (f32[16,256,256]{2,1,0:T(8,128)}, f32[4,256,256]{2,1,0:T(8,128)}) custom-call(s32[2]{0:T(128)} %pad_add_fusion.1.refs_0_, s32[2,8]{1,0:T(2,128)} %bitcast.18, s32[2,8]{1,0:T(2,128)} %bitcast.21, s32[2,8]{1,0:T(2,128)} %bitcast.24, s32[48]{0:T(128)} %refs_1_.3, s32[48]{0:T(128)} %refs_2_.3, s32[48]{0:T(128)} %refs_3_.3, s32[48]{0:T(128)} %refs_4_.5, ...), custom_call_target="tpu_custom_call" | custom-call | flops 17179869184 | bytes 10485760 | tf_op jit(solution)/shard_map/pallas_call | solution.py:219
  39.2 3.2 %collective-permute-done.3.refs_13_.refs_6_ = bf16[3,512,256]{2,1,0:T(8,128)(2,1)S(1)} collective-permute-done((bf16[3,512,256]{2,1,0:T(8,128)(2,1)S(1)}, bf16[3,512,256]{2,1,0:T(8,128)(2,1)S(1)}, u32[]{:S(2)}, u32[]{:S(2)}) %collective-permute-start.3) | collective-permute-done | bytes 786464 | tf_op jit(solution)/shard_map/ppermute | solution.py:363
  43.5 2.1 %constant_dynamic-slice_fusion = bf16[3,512,256]{2,1,0:T(8,128)(2,1)} fusion(bf16[3,4096,256]{2,1,0:T(8,128)(2,1)} %refs_9_.1, s32[]{:T(128)S(6)} %select_n.64), kind=kLoop, calls=%fused_computation.5 | loop fusion | bytes 1572868 | tf_op jit(solution)/shard_map/dynamic_slice | solution.py:330
  45.6 3.4 %collective-permute-start.6 = (bf16[3,512,256]{2,1,0:T(8,128)(2,1)}, bf16[3,512,256]{2,1,0:T(8,128)(2,1)}, u32[]{:S(2)}, u32[]{:S(2)}) collective-permute-start(bf16[3,512,256]{2,1,0:T(8,128)(2,1)} %constant_dynamic-slice_fusion), channel_id=1, source_target_pairs={{2,0},{3,2},{1,3},{0,1},{6,4},{7,6},{5,7},{4,5},{10,8},{11,10},{9,... | collective-permute-start | bytes 2359304 | tf_op jit(solution)/shard_map/ppermute | solution.py:369
  49.5 1.5 collective-permute-start.4
  51.5 14.8 %collective-permute-done.6.refs_12_.refs_11_ = bf16[3,512,256]{2,1,0:T(8,128)(2,1)} collective-permute-done((bf16[3,512,256]{2,1,0:T(8,128)(2,1)}, bf16[3,512,256]{2,1,0:T(8,128)(2,1)}, u32[]{:S(2)}, u32[]{:S(2)}) %collective-permute-start.6) | collective-permute-done | bytes 786464 | tf_op jit(solution)/shard_map/ppermute | solution.py:369
  66.3 1.9 %collective-permute-done.5.refs_16_.refs_9_ = bf16[3,512,256]{2,1,0:T(8,128)(2,1)S(1)} collective-permute-done((bf16[3,512,256]{2,1,0:T(8,128)(2,1)S(1)}, bf16[3,512,256]{2,1,0:T(8,128)(2,1)S(1)}, u32[]{:S(2)}, u32[]{:S(2)}) %collective-permute-start.5) | collective-permute-done | bytes 786464 | tf_op jit(solution)/shard_map/ppermute | solution.py:278
  72.8 1.5 collective-permute-start.14
  74.3 1.5 collective-permute-start.13
  75.8 14.0 %shard_map.119.refs_24_ = f32[4,256,256]{2,1,0:T(8,128)} custom-call(s32[2]{0:T(128)} %pad_add_fusion.2.refs_0_, s32[48]{0:T(128)} %refs_1_.3, s32[48]{0:T(128)} %refs_2_.3, s32[48]{0:T(128)} %refs_3_.3, s32[48]{0:T(128)} %refs_4_.5, bf16[4,256,2048]{2,1,0:T(8,128)(2,1)} %bitcast.13, ...), custom_call_target="tpu_custom_call", output_to_operand_aliasing={{}: (14, {})} | custom-call | flops 12884901888 | bytes 10485760 | tf_op jit(solution)/shard_map/pallas_call | solution.py:219
  92.9 1.5 collective-permute-start.21
  94.4 1.5 collective-permute-start.20
  97.2 13.1 %shard_map.120.refs_13_ = f32[16,256,256]{2,1,0:T(8,128)} custom-call(s32[3]{0:T(128)} %pad_add_fusion.3.refs_0_, s32[2,8]{1,0:T(2,128)} %bitcast.19, s32[2,8]{1,0:T(2,128)} %bitcast.22, s32[2,8]{1,0:T(2,128)} %bitcast.25, bf16[4,256,2048]{2,1,0:T(8,128)(2,1)} %bitcast.14, bf16[3,512,256]{2,1,0:T(8,128)(2,1)} %copy-done.7, ...), custom_call_target="tpu_custom_call", output_to_operand_aliasing={{}: (23, {})} | custom-call | flops 4294967296 | bytes 16777216 | tf_op jit(solution)/shard_map/pallas_call | solution.py:219
  110.3 2.7 %collective-permute-done.22.refs_20_.refs_9_ = bf16[3,512,256]{2,1,0:T(8,128)(2,1)S(1)} collective-permute-done((bf16[3,512,256]{2,1,0:T(8,128)(2,1)}, bf16[3,512,256]{2,1,0:T(8,128)(2,1)S(1)}, u32[]{:S(2)}, u32[]{:S(2)}) %collective-permute-start.22) | collective-permute-done | bytes 786464 | tf_op jit(solution)/shard_map/ppermute | solution.py:397
  118.9 9.4 %shard_map.122 = bf16[16,256,256]{2,1,0:T(8,128)(2,1)} custom-call(s32[2]{0:T(128)} %pad_add_fusion.4.refs_0_, s32[2,8]{1,0:T(2,128)} %bitcast.20, s32[2,8]{1,0:T(2,128)} %bitcast.23, s32[2,8]{1,0:T(2,128)} %bitcast.26, bf16[4,256,2048]{2,1,0:T(8,128)(2,1)} %bitcast.15, bf16[3,512,256]{2,1,0:T(8,128)(2,1)} %collective-permute-done.11.refs_16_.refs_5_, ...), custom_call_target="tpu_custom_call" | custom-call | flops 4294967296 | bytes 10485760 | tf_op jit(solution)/shard_map/pallas_call | solution.py:219
  128.3 3.8 %all-to-all-start = ((bf16[8,2,256,256]{3,2,1,0:T(8,128)(2,1)}), bf16[8,2,256,256]{3,2,1,0:T(8,128)(2,1)S(1)}, u32[]{:S(2)}, u32[]{:S(2)}) async-start(bf16[8,2,256,256]{3,2,1,0:T(8,128)(2,1)} %bitcast.17), calls=%async_computation | async-start | bytes 4194304 | tf_op jit(solution)/shard_map/all_to_all | solution.py:402
  132.8 17.7 %shard_map.121.near_ref = f32[4,256,256]{2,1,0:T(8,128)} custom-call(s32[3]{0:T(128)} %pad_add_fusion.refs_0_, s32[48]{0:T(128)} %refs_1_.3, s32[48]{0:T(128)} %refs_2_.3, s32[48]{0:T(128)} %refs_3_.3, s32[48]{0:T(128)} %refs_4_.5, bf16[4,256,2048]{2,1,0:T(8,128)(2,1)} %bitcast.16, bf16[3,512,256]{2,1,0:T(8,128)(2,1)} %copy-done.6, ...), custom_call_target="tpu_custom_call", output_to_operand_aliasing={{}: (24, {})} | custom-call | flops 12884901888 | bytes 16777216 | tf_op jit(solution)/shard_map/pallas_call | solution.py:219
  150.4 8.1 %all-to-all-done.recv_ref = bf16[8,2,256,256]{3,2,1,0:T(8,128)(2,1)S(1)} async-done(((bf16[8,2,256,256]{3,2,1,0:T(8,128)(2,1)}), bf16[8,2,256,256]{3,2,1,0:T(8,128)(2,1)S(1)}, u32[]{:S(2)}, u32[]{:S(2)}) %all-to-all-start) | async-done | bytes 2097184 | tf_op jit(solution)/shard_map/all_to_all | solution.py:402
  159.8 2.4 %shard_map.123 = bf16[4,256,256]{2,1,0:T(8,128)(2,1)} custom-call(s32[2,8]{1,0:T(2,128)S(1)} %bitcast.11, f32[4,256,256]{2,1,0:T(8,128)S(1)} %copy-done, bf16[8,2,256,256]{3,2,1,0:T(8,128)(2,1)S(1)} %all-to-all-done.recv_ref, bf16[4,256,256]{2,1,0:T(8,128)(2,1)S(1)} %copy-done.1, bf16[4,256,256]{2,1,0:T(8,128)(2,1)S(1)} %copy-done.2), custom_call_target="tpu_custom_call" | custom-call | tf_op jit(solution)/shard_map/pallas_call | solution.py:267
  (84 shorter events, 21.4 us)
Async XLA Ops:
  1.2 21.6 %collective-permute-start = (bf16[3,512,256]{2,1,0:T(8,128)(2,1)S(1)}, bf16[3,512,256]{2,1,0:T(8,128)(2,1)S(1)}, u32[]{:S(2)}, u32[]{:S(2)}) collective-permute-start(bf16[3,512,256]{2,1,0:T(8,128)(2,1)S(1)} %constant_dynamic-slice_fusion.1), channel_id=1, source_target_pairs={{2,0},{3,2},{1,3},{0,1},{6,4},{7,6},{5,7},{4,5},{10,8},{11,10},{9,... | collective-permute-start | bytes 2359304 | tf_op jit(solution)/shard_map/ppermute | solution.py:360
  22.8 19.6 %collective-permute-start.3 = (bf16[3,512,256]{2,1,0:T(8,128)(2,1)S(1)}, bf16[3,512,256]{2,1,0:T(8,128)(2,1)S(1)}, u32[]{:S(2)}, u32[]{:S(2)}) collective-permute-start(bf16[3,512,256]{2,1,0:T(8,128)(2,1)S(1)} %collective-permute-done.refs_6_.refs_5_), channel_id=1, source_target_pairs={{2,0},{3,2},{1,3},{0,1},{6,4},{7,6},{5,7},{4,5},{10,8},{11,10},{9,... | collective-permute-start | bytes 2359304 | tf_op jit(solution)/shard_map/ppermute | solution.py:363
  23.7 18.8 %collective-permute-start.2 = (bf16[3,512,256]{2,1,0:T(8,128)(2,1)S(1)}, bf16[3,512,256]{2,1,0:T(8,128)(2,1)}, u32[]{:S(2)}, u32[]{:S(2)}) collective-permute-start(bf16[3,512,256]{2,1,0:T(8,128)(2,1)S(1)} %collective-permute-done.refs_6_.refs_5_), channel_id=1, source_target_pairs={{0,16},{4,20},{8,24},{12,28},{16,0},{20,4},{24,8},{28,12},{1,17},{... | collective-permute-start | bytes 2359304 | tf_op jit(solution)/shard_map/ppermute | solution.py:278
  25.2 17.9 %collective-permute-start.1 = (bf16[3,512,256]{2,1,0:T(8,128)(2,1)S(1)}, bf16[3,512,256]{2,1,0:T(8,128)(2,1)S(1)}, u32[]{:S(2)}, u32[]{:S(2)}) collective-permute-start(bf16[3,512,256]{2,1,0:T(8,128)(2,1)S(1)} %collective-permute-done.refs_6_.refs_5_), channel_id=1, source_target_pairs={{0,8},{4,12},{8,0},{12,4},{16,24},{20,28},{24,16},{28,20},{1,9},{5... | collective-permute-start | bytes 2359304 | tf_op jit(solution)/shard_map/ppermute | solution.py:278
  43.0 8.0 %collective-permute-start.7 = (bf16[3,512,256]{2,1,0:T(8,128)(2,1)S(1)}, bf16[3,512,256]{2,1,0:T(8,128)(2,1)}, u32[]{:S(2)}, u32[]{:S(2)}) collective-permute-start(bf16[3,512,256]{2,1,0:T(8,128)(2,1)S(1)} %collective-permute-done.refs_6_.refs_5_), channel_id=1, source_target_pairs={{0,4},{4,0},{8,12},{12,8},{16,20},{20,16},{24,28},{28,24},{1,5},{5... | collective-permute-start | bytes 2359304 | tf_op jit(solution)/shard_map/ppermute | solution.py:278
  43.0 8.0 %collective-permute-start.9 = (bf16[3,512,256]{2,1,0:T(8,128)(2,1)}, bf16[3,512,256]{2,1,0:T(8,128)(2,1)}, u32[]{:S(2)}, u32[]{:S(2)}) collective-permute-start(bf16[3,512,256]{2,1,0:T(8,128)(2,1)} %collective-permute-done.2.refs_10_.refs_9_), channel_id=1, source_target_pairs={{0,4},{4,0},{8,12},{12,8},{16,20},{20,16},{24,28},{28,24},{1,5},{5... | collective-permute-start | bytes 2359304 | tf_op jit(solution)/shard_map/ppermute | solution.py:278
  45.6 20.7 %collective-permute-start.6 = (bf16[3,512,256]{2,1,0:T(8,128)(2,1)}, bf16[3,512,256]{2,1,0:T(8,128)(2,1)}, u32[]{:S(2)}, u32[]{:S(2)}) collective-permute-start(bf16[3,512,256]{2,1,0:T(8,128)(2,1)} %constant_dynamic-slice_fusion), channel_id=1, source_target_pairs={{2,0},{3,2},{1,3},{0,1},{6,4},{7,6},{5,7},{4,5},{10,8},{11,10},{9,... | collective-permute-start | bytes 2359304 | tf_op jit(solution)/shard_map/ppermute | solution.py:369
  49.0 19.2 %collective-permute-start.5 = (bf16[3,512,256]{2,1,0:T(8,128)(2,1)S(1)}, bf16[3,512,256]{2,1,0:T(8,128)(2,1)S(1)}, u32[]{:S(2)}, u32[]{:S(2)}) collective-permute-start(bf16[3,512,256]{2,1,0:T(8,128)(2,1)S(1)} %collective-permute-done.3.refs_13_.refs_6_), channel_id=1, source_target_pairs={{0,16},{4,20},{8,24},{12,28},{16,0},{20,4},{24,8},{28,12},{1,17},{... | collective-permute-start | bytes 2359304 | tf_op jit(solution)/shard_map/ppermute | solution.py:278
  49.5 19.0 %collective-permute-start.4 = (bf16[3,512,256]{2,1,0:T(8,128)(2,1)S(1)}, bf16[3,512,256]{2,1,0:T(8,128)(2,1)S(1)}, u32[]{:S(2)}, u32[]{:S(2)}) collective-permute-start(bf16[3,512,256]{2,1,0:T(8,128)(2,1)S(1)} %collective-permute-done.3.refs_13_.refs_6_), channel_id=1, source_target_pairs={{0,8},{4,12},{8,0},{12,4},{16,24},{20,28},{24,16},{28,20},{1,9},{5... | collective-permute-start | bytes 2359304 | tf_op jit(solution)/shard_map/ppermute | solution.py:278
  51.0 17.5 %collective-permute-start.8 = (bf16[3,512,256]{2,1,0:T(8,128)(2,1)}, bf16[3,512,256]{2,1,0:T(8,128)(2,1)S(1)}, u32[]{:S(2)}, u32[]{:S(2)}) collective-permute-start(bf16[3,512,256]{2,1,0:T(8,128)(2,1)} %copy-done.9), channel_id=1, source_target_pairs={{0,4},{4,0},{8,12},{12,8},{16,20},{20,16},{24,28},{28,24},{1,5},{5... | collective-permute-start | bytes 2359304 | tf_op jit(solution)/shard_map/ppermute | solution.py:278
  51.0 17.5 %collective-permute-start.10 = (bf16[3,512,256]{2,1,0:T(8,128)(2,1)S(1)}, bf16[3,512,256]{2,1,0:T(8,128)(2,1)S(1)}, u32[]{:S(2)}, u32[]{:S(2)}) collective-permute-start(bf16[3,512,256]{2,1,0:T(8,128)(2,1)S(1)} %collective-permute-done.3.refs_13_.refs_6_), channel_id=1, source_target_pairs={{0,4},{4,0},{8,12},{12,8},{16,20},{20,16},{24,28},{28,24},{1,5},{5... | collective-permute-start | bytes 2359304 | tf_op jit(solution)/shard_map/ppermute | solution.py:278
  70.1 20.9 %collective-permute-start.11 = (bf16[3,512,256]{2,1,0:T(8,128)(2,1)S(1)}, bf16[3,512,256]{2,1,0:T(8,128)(2,1)}, u32[]{:S(2)}, u32[]{:S(2)}) collective-permute-start(bf16[3,512,256]{2,1,0:T(8,128)(2,1)S(1)} %collective-permute-done.3.refs_13_.refs_6_), channel_id=1, source_target_pairs={{2,0},{3,2},{1,3},{0,1},{6,4},{7,6},{5,7},{4,5},{10,8},{11,10},{9,... | collective-permute-start | bytes 2359304 | tf_op jit(solution)/shard_map/ppermute | solution.py:383
  72.1 18.9 %collective-permute-start.16 = (bf16[3,512,256]{2,1,0:T(8,128)(2,1)S(1)}, bf16[3,512,256]{2,1,0:T(8,128)(2,1)S(1)}, u32[]{:S(2)}, u32[]{:S(2)}) collective-permute-start(bf16[3,512,256]{2,1,0:T(8,128)(2,1)S(1)} %collective-permute-done.5.refs_16_.refs_9_), channel_id=1, source_target_pairs={{0,4},{4,0},{8,12},{12,8},{16,20},{20,16},{24,28},{28,24},{1,5},{5... | collective-permute-start | bytes 2359304 | tf_op jit(solution)/shard_map/ppermute | solution.py:278
  72.3 18.7 %collective-permute-start.15 = (bf16[3,512,256]{2,1,0:T(8,128)(2,1)S(1)}, bf16[3,512,256]{2,1,0:T(8,128)(2,1)S(1)}, u32[]{:S(2)}, u32[]{:S(2)}) collective-permute-start(bf16[3,512,256]{2,1,0:T(8,128)(2,1)S(1)} %collective-permute-done.4.refs_15_.refs_8_), channel_id=1, source_target_pairs={{0,4},{4,0},{8,12},{12,8},{16,20},{20,16},{24,28},{28,24},{1,5},{5... | collective-permute-start | bytes 2359304 | tf_op jit(solution)/shard_map/ppermute | solution.py:278
  72.8 18.2 %collective-permute-start.14 = (bf16[3,256,256]{2,1,0:T(8,128)(2,1)S(1)}, bf16[3,256,256]{2,1,0:T(8,128)(2,1)S(1)}, u32[]{:S(2)}, u32[]{:S(2)}) collective-permute-start(bf16[3,256,256]{2,1,0:T(8,128)(2,1)S(1)} %slice.7), channel_id=1, source_target_pairs={{0,16},{4,20},{8,24},{12,28},{16,0},{20,4},{24,8},{28,12},{1,17},{... | collective-permute-start | bytes 1179656 | tf_op jit(solution)/shard_map/ppermute | solution.py:278
  74.3 16.7 %collective-permute-start.13 = (bf16[3,256,256]{2,1,0:T(8,128)(2,1)S(1)}, bf16[3,256,256]{2,1,0:T(8,128)(2,1)}, u32[]{:S(2)}, u32[]{:S(2)}) collective-permute-start(bf16[3,256,256]{2,1,0:T(8,128)(2,1)S(1)} %slice.6), channel_id=1, source_target_pairs={{0,8},{4,12},{8,0},{12,4},{16,24},{20,28},{24,16},{28,20},{1,9},{5... | collective-permute-start | bytes 1179656 | tf_op jit(solution)/shard_map/ppermute | solution.py:278
  92.0 4.5 %collective-permute-start.17 = (bf16[3,256,256]{2,1,0:T(8,128)(2,1)}, bf16[3,256,256]{2,1,0:T(8,128)(2,1)S(1)}, u32[]{:S(2)}, u32[]{:S(2)}) collective-permute-start(bf16[3,256,256]{2,1,0:T(8,128)(2,1)} %collective-permute-done.13.refs_19_.refs_12_), channel_id=1, source_target_pairs={{0,4},{4,0},{8,12},{12,8},{16,20},{20,16},{24,28},{28,24},{1,5},{5... | collective-permute-start | bytes 1179656 | tf_op jit(solution)/shard_map/ppermute | solution.py:278
  92.9 4.4 %collective-permute-start.18 = (bf16[3,256,256]{2,1,0:T(8,128)(2,1)S(1)}, bf16[3,256,256]{2,1,0:T(8,128)(2,1)}, u32[]{:S(2)}, u32[]{:S(2)}) collective-permute-start(bf16[3,256,256]{2,1,0:T(8,128)(2,1)S(1)} %collective-permute-done.14.refs_20_.refs_13_), channel_id=1, source_target_pairs={{0,4},{4,0},{8,12},{12,8},{16,20},{20,16},{24,28},{28,24},{1,5},{5... | collective-permute-start | bytes 1179656 | tf_op jit(solution)/shard_map/ppermute | solution.py:278
  92.9 20.2 %collective-permute-start.22 = (bf16[3,512,256]{2,1,0:T(8,128)(2,1)}, bf16[3,512,256]{2,1,0:T(8,128)(2,1)S(1)}, u32[]{:S(2)}, u32[]{:S(2)}) collective-permute-start(bf16[3,512,256]{2,1,0:T(8,128)(2,1)} %constant_dynamic-slice_fusion), channel_id=1, source_target_pairs={{0,2},{2,3},{3,1},{1,0},{4,6},{6,7},{7,5},{5,4},{8,10},{10,11},{11... | collective-permute-start | bytes 2359304 | tf_op jit(solution)/shard_map/ppermute | solution.py:397
  92.9 20.2 %collective-permute-start.21 = (bf16[3,512,256]{2,1,0:T(8,128)(2,1)}, bf16[3,512,256]{2,1,0:T(8,128)(2,1)S(1)}, u32[]{:S(2)}, u32[]{:S(2)}) collective-permute-start(bf16[3,512,256]{2,1,0:T(8,128)(2,1)} %collective-permute-done.11.refs_16_.refs_5_), channel_id=1, source_target_pairs={{0,16},{4,20},{8,24},{12,28},{16,0},{20,4},{24,8},{28,12},{1,17},{... | collective-permute-start | bytes 2359304 | tf_op jit(solution)/shard_map/ppermute | solution.py:278
  94.4 19.9 %collective-permute-start.20 = (bf16[3,512,256]{2,1,0:T(8,128)(2,1)}, bf16[3,512,256]{2,1,0:T(8,128)(2,1)S(1)}, u32[]{:S(2)}, u32[]{:S(2)}) collective-permute-start(bf16[3,512,256]{2,1,0:T(8,128)(2,1)} %collective-permute-done.11.refs_16_.refs_5_), channel_id=1, source_target_pairs={{0,8},{4,12},{8,0},{12,4},{16,24},{20,28},{24,16},{28,20},{1,9},{5... | collective-permute-start | bytes 2359304 | tf_op jit(solution)/shard_map/ppermute | solution.py:278
  97.2 18.2 %collective-permute-start.19 = (bf16[3,512,256]{2,1,0:T(8,128)(2,1)}, bf16[3,512,256]{2,1,0:T(8,128)(2,1)S(1)}, u32[]{:S(2)}, u32[]{:S(2)}) collective-permute-start(bf16[3,512,256]{2,1,0:T(8,128)(2,1)} %collective-permute-done.11.refs_16_.refs_5_), channel_id=1, source_target_pairs={{0,4},{4,0},{8,12},{12,8},{16,20},{20,16},{24,28},{28,24},{1,5},{5... | collective-permute-start | bytes 2359304 | tf_op jit(solution)/shard_map/ppermute | solution.py:278
  114.8 4.2 %collective-permute-start.25 = (bf16[3,512,256]{2,1,0:T(8,128)(2,1)S(1)}, bf16[3,512,256]{2,1,0:T(8,128)(2,1)}, u32[]{:S(2)}, u32[]{:S(2)}) collective-permute-start(bf16[3,512,256]{2,1,0:T(8,128)(2,1)S(1)} %collective-permute-done.22.refs_20_.refs_9_), channel_id=1, source_target_pairs={{0,4},{4,0},{8,12},{12,8},{16,20},{20,16},{24,28},{28,24},{1,5},{5... | collective-permute-start | bytes 2359304 | tf_op jit(solution)/shard_map/ppermute | solution.py:278
  128.3 30.2 %all-to-all-start = ((bf16[8,2,256,256]{3,2,1,0:T(8,128)(2,1)}), bf16[8,2,256,256]{3,2,1,0:T(8,128)(2,1)S(1)}, u32[]{:S(2)}, u32[]{:S(2)}) async-start(bf16[8,2,256,256]{3,2,1,0:T(8,128)(2,1)} %bitcast.17), calls=%async_computation | async-start | bytes 4194304 | tf_op jit(solution)/shard_map/all_to_all | solution.py:402
  (22 other events, 250.2 us)

commit v17 on v15

--- a/solution.py
+++ b/solution.py
@@ -371,7 +371,9 @@
     served_sums, near = window_sums(
         [lane], group * 0, served, local, hist_t, [[(0, 0, weights)]], None, rows
     )
-    trio, own, corner, served_sums, near = tie(trio, own, corner, served_sums, near)
+    corner, near = tie(corner, near)
+    diagonal = lax.ppermute(corner, "lag", ring)
+    trio, own, served_sums, near = tie(trio, own, served_sums, near)
     held, across, along = trio
     found, across = tie(with_other_core(held, peers), across)
     found += with_other_core(across, peers)
@@ -379,7 +381,6 @@
     held, across, along = neighbours(own)
     more, held = tie(more, held)
     found += more
-    diagonal = lax.ppermute(corner, "lag", ring)
     held = with_other_core(held, peers)
     across, along, own, diagonal, found, held = tie(across, along, own, diagonal, found, held)
     diagonal = with_other_core(corners(diagonal), peers)

time: 162 us -> 163 us (level)
  waiting for transfers between devices: 49.8 us -> 52.9 us
    ppermute x21, waiting for transfers between devices: 4.18 us -> 8.55 us  [swap(): return lax.ppermute(value, 'grp', [(i, i ^ bit) for i in range(peers)])]
    ppermute x3, starting transfers between devices: 6.4 us -> 4.53 us  [per_device(): own = lax.ppermute(own, 'lag', ring)]
    ppermute x1, starting transfers between devices: 4.9 us -> 6.67 us  [per_device(): diagonal = lax.ppermute(corner, 'lag', ring)]
  transfers between devices with their start and end apart: 27 -> 27, of which waited for: 9 -> 12; matrix products, arithmetic and copies ran while one was open for 7% -> 7% of each run, Pallas kernels for 35% -> 34%
where the time goes in v17:
time: 163 us; the launch traced here: 164 us
  Pallas kernels  68.4 us (42%)
  waiting for transfers between devices  52.9 us (32%)
  starting transfers between devices  24.3 us (15%)
  local copies, waits for them, and re-layouts  14.7 us (9%)
  other arithmetic  3.15 us (2%)
    pallas_call x5, Pallas kernels, window_sums(): pl.pallas_call(functools.partial(window_kernel, config), out_shape=outs,...  66 us
    ppermute x3, waiting for transfers between devices, per_device(): own = lax.ppermute(own, 'lag', ring)  16.9 us
    ppermute x1, waiting for transfers between devices, per_device(): diagonal = lax.ppermute(corner, 'lag', ring)  16.4 us
    unnamed x43, local copies, waits for them, and re-layouts  11.4 us
    ppermute x21, starting transfers between devices, swap(): return lax.ppermute(value, 'grp', [(i, i ^ bit) for i in range(peers)])  9.31 us
    ppermute x21, waiting for transfers between devices, swap(): return lax.ppermute(value, 'grp', [(i, i ^ bit) for i in range(peers)])  8.55 us
    ppermute x1, starting transfers between devices, per_device(): diagonal = lax.ppermute(corner, 'lag', ring)  6.67 us
    all_to_all x1, waiting for transfers between devices, per_device(): lax.all_to_all(contribution.reshape(peers, slots, *contribution.shape[1:]...  6.3 us
  transfers between devices with their start and end apart: 27, of which 12 were waited for; matrix products, arithmetic and copies ran while one was open for 7% of the time, Pallas kernels for 34%

profile of v17, /device:TPU:0, one launch (start us, length us, event | category | flops | bytes accessed | tf_op | source)
XLA Modules:
  0.0 163.9 jit_solution(8186587932528948036)
XLA Ops:
  1.2 3.1 %collective-permute-start = (bf16[3,512,256]{2,1,0:T(8,128)(2,1)S(1)}, bf16[3,512,256]{2,1,0:T(8,128)(2,1)S(1)}, u32[]{:S(2)}, u32[]{:S(2)}) collective-permute-start(bf16[3,512,256]{2,1,0:T(8,128)(2,1)S(1)} %constant_dynamic-slice_fusion.1), channel_id=1, source_target_pairs={{2,0},{3,2},{1,3},{0,1},{6,4},{7,6},{5,7},{4,5},{10,8},{11,10},{9,... | collective-permute-start | bytes 2359304 | tf_op jit(solution)/shard_map/ppermute | solution.py:366
  4.3 6.3 %copy.16 = bf16[4,2048,256]{1,2,0:T(8,128)(2,1)} copy(bf16[4,2048,256]{2,1,0:T(8,128)(2,1)} %param.13) | data formatting | bytes 8388608 | tf_op args[1]
  11.1 11.7 %collective-permute-done.refs_6_.refs_5_ = bf16[3,512,256]{2,1,0:T(8,128)(2,1)S(1)} collective-permute-done((bf16[3,512,256]{2,1,0:T(8,128)(2,1)S(1)}, bf16[3,512,256]{2,1,0:T(8,128)(2,1)S(1)}, u32[]{:S(2)}, u32[]{:S(2)}) %collective-permute-start) | collective-permute-done | bytes 786464 | tf_op jit(solution)/shard_map/ppermute | solution.py:366
  23.7 1.5 collective-permute-start.2
  25.2 1.5 collective-permute-start.1
  26.7 13.9 %shard_map.118 = (f32[16,256,256]{2,1,0:T(8,128)}, f32[4,256,256]{2,1,0:T(8,128)}) custom-call(s32[2]{0:T(128)} %pad_add_fusion.1.refs_0_, s32[2,8]{1,0:T(2,128)} %bitcast.18, s32[2,8]{1,0:T(2,128)} %bitcast.21, s32[2,8]{1,0:T(2,128)} %bitcast.24, s32[48]{0:T(128)} %refs_1_.3, s32[48]{0:T(128)} %refs_2_.3, s32[48]{0:T(128)} %refs_3_.3, s32[48]{0:T(128)} %refs_4_.5, ...), custom_call_target="tpu_custom_call" | custom-call | flops 17179869184 | bytes 10485760 | tf_op jit(solution)/shard_map/pallas_call | solution.py:225
  40.6 2.1 %constant_dynamic-slice_fusion = bf16[3,512,256]{2,1,0:T(8,128)(2,1)} fusion(bf16[3,4096,256]{2,1,0:T(8,128)(2,1)} %refs_9_.1, s32[]{:T(128)S(6)} %select_n.64), kind=kLoop, calls=%fused_computation.5 | loop fusion | bytes 1572868 | tf_op jit(solution)/shard_map/dynamic_slice | solution.py:336
  43.9 6.7 %collective-permute-start.6 = (bf16[3,512,256]{2,1,0:T(8,128)(2,1)}, bf16[3,512,256]{2,1,0:T(8,128)(2,1)}, u32[]{:S(2)}, u32[]{:S(2)}) collective-permute-start(bf16[3,512,256]{2,1,0:T(8,128)(2,1)} %constant_dynamic-slice_fusion), channel_id=1, source_target_pairs={{2,0},{3,2},{1,3},{0,1},{6,4},{7,6},{5,7},{4,5},{10,8},{11,10},{9,... | collective-permute-start | bytes 2359304 | tf_op jit(solution)/shard_map/ppermute | solution.py:375
  51.2 16.4 %collective-permute-done.6.refs_12_.refs_11_ = bf16[3,512,256]{2,1,0:T(8,128)(2,1)} collective-permute-done((bf16[3,512,256]{2,1,0:T(8,128)(2,1)}, bf16[3,512,256]{2,1,0:T(8,128)(2,1)}, u32[]{:S(2)}, u32[]{:S(2)}) %collective-permute-start.6) | collective-permute-done | bytes 786464 | tf_op jit(solution)/shard_map/ppermute | solution.py:375
  67.6 1.9 %collective-permute-done.5.refs_16_.refs_9_ = bf16[3,512,256]{2,1,0:T(8,128)(2,1)S(1)} collective-permute-done((bf16[3,512,256]{2,1,0:T(8,128)(2,1)S(1)}, bf16[3,512,256]{2,1,0:T(8,128)(2,1)S(1)}, u32[]{:S(2)}, u32[]{:S(2)}) %collective-permute-start.5) | collective-permute-done | bytes 786464 | tf_op jit(solution)/shard_map/ppermute | solution.py:284
  71.8 1.3 collective-permute-done.12.refs_13_.refs_12_
  73.8 1.8 %collective-permute-start.14 = (bf16[3,256,256]{2,1,0:T(8,128)(2,1)S(1)}, bf16[3,256,256]{2,1,0:T(8,128)(2,1)S(1)}, u32[]{:S(2)}, u32[]{:S(2)}) collective-permute-start(bf16[3,256,256]{2,1,0:T(8,128)(2,1)S(1)} %slice.7), channel_id=1, source_target_pairs={{0,16},{4,20},{8,24},{12,28},{16,0},{20,4},{24,8},{28,12},{1,17},{... | collective-permute-start | bytes 1179656 | tf_op jit(solution)/shard_map/ppermute | solution.py:284
  75.8 11.0 %shard_map.119.refs_24_ = f32[4,256,256]{2,1,0:T(8,128)} custom-call(s32[2]{0:T(128)} %pad_add_fusion.2.refs_0_, s32[48]{0:T(128)} %refs_1_.3, s32[48]{0:T(128)} %refs_2_.3, s32[48]{0:T(128)} %refs_3_.3, s32[48]{0:T(128)} %refs_4_.5, bf16[4,256,2048]{2,1,0:T(8,128)(2,1)} %bitcast.13, ...), custom_call_target="tpu_custom_call", output_to_operand_aliasing={{}: (14, {})} | custom-call | flops 12884901888 | bytes 10485760 | tf_op jit(solution)/shard_map/pallas_call | solution.py:225
  86.8 5.2 %collective-permute-done.11.refs_16_.refs_5_ = bf16[3,512,256]{2,1,0:T(8,128)(2,1)} collective-permute-done((bf16[3,512,256]{2,1,0:T(8,128)(2,1)S(1)}, bf16[3,512,256]{2,1,0:T(8,128)(2,1)}, u32[]{:S(2)}, u32[]{:S(2)}) %collective-permute-start.11) | collective-permute-done | bytes 786464 | tf_op jit(solution)/shard_map/ppermute | solution.py:389
  93.9 1.8 %collective-permute-start.21 = (bf16[3,512,256]{2,1,0:T(8,128)(2,1)}, bf16[3,512,256]{2,1,0:T(8,128)(2,1)S(1)}, u32[]{:S(2)}, u32[]{:S(2)}) collective-permute-start(bf16[3,512,256]{2,1,0:T(8,128)(2,1)} %collective-permute-done.11.refs_16_.refs_5_), channel_id=1, source_target_pairs={{0,16},{4,20},{8,24},{12,28},{16,0},{20,4},{24,8},{28,12},{1,17},{... | collective-permute-start | bytes 2359304 | tf_op jit(solution)/shard_map/ppermute | solution.py:284
  97.3 12.0 %shard_map.120.refs_13_ = f32[16,256,256]{2,1,0:T(8,128)} custom-call(s32[3]{0:T(128)} %pad_add_fusion.3.refs_0_, s32[2,8]{1,0:T(2,128)} %bitcast.19, s32[2,8]{1,0:T(2,128)} %bitcast.22, s32[2,8]{1,0:T(2,128)} %bitcast.25, bf16[4,256,2048]{2,1,0:T(8,128)(2,1)} %bitcast.14, bf16[3,512,256]{2,1,0:T(8,128)(2,1)} %copy-done.7, ...), custom_call_target="tpu_custom_call", output_to_operand_aliasing={{}: (23, {})} | custom-call | flops 4294967296 | bytes 16777216 | tf_op jit(solution)/shard_map/pallas_call | solution.py:225
  109.2 4.8 %collective-permute-done.22.refs_20_.refs_9_ = bf16[3,512,256]{2,1,0:T(8,128)(2,1)S(1)} collective-permute-done((bf16[3,512,256]{2,1,0:T(8,128)(2,1)}, bf16[3,512,256]{2,1,0:T(8,128)(2,1)S(1)}, u32[]{:S(2)}, u32[]{:S(2)}) %collective-permute-start.22) | collective-permute-done | bytes 786464 | tf_op jit(solution)/shard_map/ppermute | solution.py:403
  114.0 1.5 collective-permute-done.20.refs_18_.refs_7_
  116.7 1.2 collective-permute-done.23.refs_21_.refs_10_
  120.2 9.7 %shard_map.122 = bf16[16,256,256]{2,1,0:T(8,128)(2,1)} custom-call(s32[2]{0:T(128)} %pad_add_fusion.4.refs_0_, s32[2,8]{1,0:T(2,128)} %bitcast.20, s32[2,8]{1,0:T(2,128)} %bitcast.23, s32[2,8]{1,0:T(2,128)} %bitcast.26, bf16[4,256,2048]{2,1,0:T(8,128)(2,1)} %bitcast.15, bf16[3,512,256]{2,1,0:T(8,128)(2,1)} %collective-permute-done.11.refs_16_.refs_5_, ...), custom_call_target="tpu_custom_call" | custom-call | flops 4294967296 | bytes 10485760 | tf_op jit(solution)/shard_map/pallas_call | solution.py:225
  129.9 3.8 %all-to-all-start = ((bf16[8,2,256,256]{3,2,1,0:T(8,128)(2,1)}), bf16[8,2,256,256]{3,2,1,0:T(8,128)(2,1)S(1)}, u32[]{:S(2)}, u32[]{:S(2)}) async-start(bf16[8,2,256,256]{3,2,1,0:T(8,128)(2,1)} %bitcast.17), calls=%async_computation | async-start | bytes 4194304 | tf_op jit(solution)/shard_map/all_to_all | solution.py:408
  134.3 19.5 %shard_map.121.near_ref = f32[4,256,256]{2,1,0:T(8,128)} custom-call(s32[3]{0:T(128)} %pad_add_fusion.refs_0_, s32[48]{0:T(128)} %refs_1_.3, s32[48]{0:T(128)} %refs_2_.3, s32[48]{0:T(128)} %refs_3_.3, s32[48]{0:T(128)} %refs_4_.5, bf16[4,256,2048]{2,1,0:T(8,128)(2,1)} %bitcast.16, bf16[3,512,256]{2,1,0:T(8,128)(2,1)} %copy-done.6, ...), custom_call_target="tpu_custom_call", output_to_operand_aliasing={{}: (24, {})} | custom-call | flops 12884901888 | bytes 16777216 | tf_op jit(solution)/shard_map/pallas_call | solution.py:225
  153.8 6.3 %all-to-all-done.recv_ref = bf16[8,2,256,256]{3,2,1,0:T(8,128)(2,1)S(1)} async-done(((bf16[8,2,256,256]{3,2,1,0:T(8,128)(2,1)}), bf16[8,2,256,256]{3,2,1,0:T(8,128)(2,1)S(1)}, u32[]{:S(2)}, u32[]{:S(2)}) %all-to-all-start) | async-done | bytes 2097184 | tf_op jit(solution)/shard_map/all_to_all | solution.py:408
  161.4 2.4 %shard_map.123 = bf16[4,256,256]{2,1,0:T(8,128)(2,1)} custom-call(s32[2,8]{1,0:T(2,128)S(1)} %bitcast.11, f32[4,256,256]{2,1,0:T(8,128)S(1)} %copy-done, bf16[8,2,256,256]{3,2,1,0:T(8,128)(2,1)S(1)} %all-to-all-done.recv_ref, bf16[4,256,256]{2,1,0:T(8,128)(2,1)S(1)} %copy-done.1, bf16[4,256,256]{2,1,0:T(8,128)(2,1)S(1)} %copy-done.2), custom_call_target="tpu_custom_call" | custom-call | tf_op jit(solution)/shard_map/pallas_call | solution.py:273
  (88 shorter events, 16.4 us)
Async XLA Ops:
  1.2 21.6 %collective-permute-start = (bf16[3,512,256]{2,1,0:T(8,128)(2,1)S(1)}, bf16[3,512,256]{2,1,0:T(8,128)(2,1)S(1)}, u32[]{:S(2)}, u32[]{:S(2)}) collective-permute-start(bf16[3,512,256]{2,1,0:T(8,128)(2,1)S(1)} %constant_dynamic-slice_fusion.1), channel_id=1, source_target_pairs={{2,0},{3,2},{1,3},{0,1},{6,4},{7,6},{5,7},{4,5},{10,8},{11,10},{9,... | collective-permute-start | bytes 2359304 | tf_op jit(solution)/shard_map/ppermute | solution.py:366
  22.8 19.8 %collective-permute-start.3 = (bf16[3,512,256]{2,1,0:T(8,128)(2,1)S(1)}, bf16[3,512,256]{2,1,0:T(8,128)(2,1)S(1)}, u32[]{:S(2)}, u32[]{:S(2)}) collective-permute-start(bf16[3,512,256]{2,1,0:T(8,128)(2,1)S(1)} %collective-permute-done.refs_6_.refs_5_), channel_id=1, source_target_pairs={{2,0},{3,2},{1,3},{0,1},{6,4},{7,6},{5,7},{4,5},{10,8},{11,10},{9,... | collective-permute-start | bytes 2359304 | tf_op jit(solution)/shard_map/ppermute | solution.py:370
  23.7 19.0 %collective-permute-start.2 = (bf16[3,512,256]{2,1,0:T(8,128)(2,1)S(1)}, bf16[3,512,256]{2,1,0:T(8,128)(2,1)}, u32[]{:S(2)}, u32[]{:S(2)}) collective-permute-start(bf16[3,512,256]{2,1,0:T(8,128)(2,1)S(1)} %collective-permute-done.refs_6_.refs_5_), channel_id=1, source_target_pairs={{0,16},{4,20},{8,24},{12,28},{16,0},{20,4},{24,8},{28,12},{1,17},{... | collective-permute-start | bytes 2359304 | tf_op jit(solution)/shard_map/ppermute | solution.py:284
  25.2 17.9 %collective-permute-start.1 = (bf16[3,512,256]{2,1,0:T(8,128)(2,1)S(1)}, bf16[3,512,256]{2,1,0:T(8,128)(2,1)S(1)}, u32[]{:S(2)}, u32[]{:S(2)}) collective-permute-start(bf16[3,512,256]{2,1,0:T(8,128)(2,1)S(1)} %collective-permute-done.refs_6_.refs_5_), channel_id=1, source_target_pairs={{0,8},{4,12},{8,0},{12,4},{16,24},{20,28},{24,16},{28,20},{1,9},{5... | collective-permute-start | bytes 2359304 | tf_op jit(solution)/shard_map/ppermute | solution.py:284
  43.0 7.6 %collective-permute-start.7 = (bf16[3,512,256]{2,1,0:T(8,128)(2,1)S(1)}, bf16[3,512,256]{2,1,0:T(8,128)(2,1)S(1)}, u32[]{:S(2)}, u32[]{:S(2)}) collective-permute-start(bf16[3,512,256]{2,1,0:T(8,128)(2,1)S(1)} %collective-permute-done.refs_6_.refs_5_), channel_id=1, source_target_pairs={{0,4},{4,0},{8,12},{12,8},{16,20},{20,16},{24,28},{28,24},{1,5},{5... | collective-permute-start | bytes 2359304 | tf_op jit(solution)/shard_map/ppermute | solution.py:284
  43.0 7.6 %collective-permute-start.9 = (bf16[3,512,256]{2,1,0:T(8,128)(2,1)}, bf16[3,512,256]{2,1,0:T(8,128)(2,1)S(1)}, u32[]{:S(2)}, u32[]{:S(2)}) collective-permute-start(bf16[3,512,256]{2,1,0:T(8,128)(2,1)} %collective-permute-done.2.refs_10_.refs_9_), channel_id=1, source_target_pairs={{0,4},{4,0},{8,12},{12,8},{16,20},{20,16},{24,28},{28,24},{1,5},{5... | collective-permute-start | bytes 2359304 | tf_op jit(solution)/shard_map/ppermute | solution.py:284
  43.9 23.7 %collective-permute-start.6 = (bf16[3,512,256]{2,1,0:T(8,128)(2,1)}, bf16[3,512,256]{2,1,0:T(8,128)(2,1)}, u32[]{:S(2)}, u32[]{:S(2)}) collective-permute-start(bf16[3,512,256]{2,1,0:T(8,128)(2,1)} %constant_dynamic-slice_fusion), channel_id=1, source_target_pairs={{2,0},{3,2},{1,3},{0,1},{6,4},{7,6},{5,7},{4,5},{10,8},{11,10},{9,... | collective-permute-start | bytes 2359304 | tf_op jit(solution)/shard_map/ppermute | solution.py:375
  50.6 18.9 %collective-permute-start.5 = (bf16[3,512,256]{2,1,0:T(8,128)(2,1)S(1)}, bf16[3,512,256]{2,1,0:T(8,128)(2,1)S(1)}, u32[]{:S(2)}, u32[]{:S(2)}) collective-permute-start(bf16[3,512,256]{2,1,0:T(8,128)(2,1)S(1)} %collective-permute-done.3.refs_13_.refs_6_), channel_id=1, source_target_pairs={{0,16},{4,20},{8,24},{12,28},{16,0},{20,4},{24,8},{28,12},{1,17},{... | collective-permute-start | bytes 2359304 | tf_op jit(solution)/shard_map/ppermute | solution.py:284
  50.6 18.9 %collective-permute-start.4 = (bf16[3,512,256]{2,1,0:T(8,128)(2,1)S(1)}, bf16[3,512,256]{2,1,0:T(8,128)(2,1)S(1)}, u32[]{:S(2)}, u32[]{:S(2)}) collective-permute-start(bf16[3,512,256]{2,1,0:T(8,128)(2,1)S(1)} %collective-permute-done.3.refs_13_.refs_6_), channel_id=1, source_target_pairs={{0,8},{4,12},{8,0},{12,4},{16,24},{20,28},{24,16},{28,20},{1,9},{5... | collective-permute-start | bytes 2359304 | tf_op jit(solution)/shard_map/ppermute | solution.py:284
  50.6 18.9 %collective-permute-start.8 = (bf16[3,512,256]{2,1,0:T(8,128)(2,1)}, bf16[3,512,256]{2,1,0:T(8,128)(2,1)S(1)}, u32[]{:S(2)}, u32[]{:S(2)}) collective-permute-start(bf16[3,512,256]{2,1,0:T(8,128)(2,1)} %copy-done.9), channel_id=1, source_target_pairs={{0,4},{4,0},{8,12},{12,8},{16,20},{20,16},{24,28},{28,24},{1,5},{5... | collective-permute-start | bytes 2359304 | tf_op jit(solution)/shard_map/ppermute | solution.py:284
  50.7 18.8 %collective-permute-start.10 = (bf16[3,512,256]{2,1,0:T(8,128)(2,1)S(1)}, bf16[3,512,256]{2,1,0:T(8,128)(2,1)S(1)}, u32[]{:S(2)}, u32[]{:S(2)}) collective-permute-start(bf16[3,512,256]{2,1,0:T(8,128)(2,1)S(1)} %collective-permute-done.3.refs_13_.refs_6_), channel_id=1, source_target_pairs={{0,4},{4,0},{8,12},{12,8},{16,20},{20,16},{24,28},{28,24},{1,5},{5... | collective-permute-start | bytes 2359304 | tf_op jit(solution)/shard_map/ppermute | solution.py:284
  71.1 20.9 %collective-permute-start.11 = (bf16[3,512,256]{2,1,0:T(8,128)(2,1)S(1)}, bf16[3,512,256]{2,1,0:T(8,128)(2,1)}, u32[]{:S(2)}, u32[]{:S(2)}) collective-permute-start(bf16[3,512,256]{2,1,0:T(8,128)(2,1)S(1)} %collective-permute-done.3.refs_13_.refs_6_), channel_id=1, source_target_pairs={{2,0},{3,2},{1,3},{0,1},{6,4},{7,6},{5,7},{4,5},{10,8},{11,10},{9,... | collective-permute-start | bytes 2359304 | tf_op jit(solution)/shard_map/ppermute | solution.py:389
  73.1 18.9 %collective-permute-start.16 = (bf16[3,512,256]{2,1,0:T(8,128)(2,1)S(1)}, bf16[3,512,256]{2,1,0:T(8,128)(2,1)S(1)}, u32[]{:S(2)}, u32[]{:S(2)}) collective-permute-start(bf16[3,512,256]{2,1,0:T(8,128)(2,1)S(1)} %collective-permute-done.5.refs_16_.refs_9_), channel_id=1, source_target_pairs={{0,4},{4,0},{8,12},{12,8},{16,20},{20,16},{24,28},{28,24},{1,5},{5... | collective-permute-start | bytes 2359304 | tf_op jit(solution)/shard_map/ppermute | solution.py:284
  73.3 18.7 %collective-permute-start.15 = (bf16[3,512,256]{2,1,0:T(8,128)(2,1)S(1)}, bf16[3,512,256]{2,1,0:T(8,128)(2,1)S(1)}, u32[]{:S(2)}, u32[]{:S(2)}) collective-permute-start(bf16[3,512,256]{2,1,0:T(8,128)(2,1)S(1)} %collective-permute-done.4.refs_15_.refs_8_), channel_id=1, source_target_pairs={{0,4},{4,0},{8,12},{12,8},{16,20},{20,16},{24,28},{28,24},{1,5},{5... | collective-permute-start | bytes 2359304 | tf_op jit(solution)/shard_map/ppermute | solution.py:284
  73.8 18.2 %collective-permute-start.14 = (bf16[3,256,256]{2,1,0:T(8,128)(2,1)S(1)}, bf16[3,256,256]{2,1,0:T(8,128)(2,1)S(1)}, u32[]{:S(2)}, u32[]{:S(2)}) collective-permute-start(bf16[3,256,256]{2,1,0:T(8,128)(2,1)S(1)} %slice.7), channel_id=1, source_target_pairs={{0,16},{4,20},{8,24},{12,28},{16,0},{20,4},{24,8},{28,12},{1,17},{... | collective-permute-start | bytes 1179656 | tf_op jit(solution)/shard_map/ppermute | solution.py:284
  75.5 16.5 %collective-permute-start.13 = (bf16[3,256,256]{2,1,0:T(8,128)(2,1)S(1)}, bf16[3,256,256]{2,1,0:T(8,128)(2,1)}, u32[]{:S(2)}, u32[]{:S(2)}) collective-permute-start(bf16[3,256,256]{2,1,0:T(8,128)(2,1)S(1)} %slice.6), channel_id=1, source_target_pairs={{0,8},{4,12},{8,0},{12,4},{16,24},{20,28},{24,16},{28,20},{1,9},{5... | collective-permute-start | bytes 1179656 | tf_op jit(solution)/shard_map/ppermute | solution.py:284
  93.0 3.6 %collective-permute-start.17 = (bf16[3,256,256]{2,1,0:T(8,128)(2,1)}, bf16[3,256,256]{2,1,0:T(8,128)(2,1)S(1)}, u32[]{:S(2)}, u32[]{:S(2)}) collective-permute-start(bf16[3,256,256]{2,1,0:T(8,128)(2,1)} %collective-permute-done.13.refs_19_.refs_12_), channel_id=1, source_target_pairs={{0,4},{4,0},{8,12},{12,8},{16,20},{20,16},{24,28},{28,24},{1,5},{5... | collective-permute-start | bytes 1179656 | tf_op jit(solution)/shard_map/ppermute | solution.py:284
  93.9 20.2 %collective-permute-start.22 = (bf16[3,512,256]{2,1,0:T(8,128)(2,1)}, bf16[3,512,256]{2,1,0:T(8,128)(2,1)S(1)}, u32[]{:S(2)}, u32[]{:S(2)}) collective-permute-start(bf16[3,512,256]{2,1,0:T(8,128)(2,1)} %constant_dynamic-slice_fusion), channel_id=1, source_target_pairs={{0,2},{2,3},{3,1},{1,0},{4,6},{6,7},{7,5},{5,4},{8,10},{10,11},{11... | collective-permute-start | bytes 2359304 | tf_op jit(solution)/shard_map/ppermute | solution.py:403
  93.9 20.2 %collective-permute-start.21 = (bf16[3,512,256]{2,1,0:T(8,128)(2,1)}, bf16[3,512,256]{2,1,0:T(8,128)(2,1)S(1)}, u32[]{:S(2)}, u32[]{:S(2)}) collective-permute-start(bf16[3,512,256]{2,1,0:T(8,128)(2,1)} %collective-permute-done.11.refs_16_.refs_5_), channel_id=1, source_target_pairs={{0,16},{4,20},{8,24},{12,28},{16,0},{20,4},{24,8},{28,12},{1,17},{... | collective-permute-start | bytes 2359304 | tf_op jit(solution)/shard_map/ppermute | solution.py:284
  95.6 19.9 %collective-permute-start.20 = (bf16[3,512,256]{2,1,0:T(8,128)(2,1)}, bf16[3,512,256]{2,1,0:T(8,128)(2,1)S(1)}, u32[]{:S(2)}, u32[]{:S(2)}) collective-permute-start(bf16[3,512,256]{2,1,0:T(8,128)(2,1)} %collective-permute-done.11.refs_16_.refs_5_), channel_id=1, source_target_pairs={{0,8},{4,12},{8,0},{12,4},{16,24},{20,28},{24,16},{28,20},{1,9},{5... | collective-permute-start | bytes 2359304 | tf_op jit(solution)/shard_map/ppermute | solution.py:284
  97.3 19.4 %collective-permute-start.19 = (bf16[3,512,256]{2,1,0:T(8,128)(2,1)}, bf16[3,512,256]{2,1,0:T(8,128)(2,1)S(1)}, u32[]{:S(2)}, u32[]{:S(2)}) collective-permute-start(bf16[3,512,256]{2,1,0:T(8,128)(2,1)} %collective-permute-done.11.refs_16_.refs_5_), channel_id=1, source_target_pairs={{0,4},{4,0},{8,12},{12,8},{16,20},{20,16},{24,28},{28,24},{1,5},{5... | collective-permute-start | bytes 2359304 | tf_op jit(solution)/shard_map/ppermute | solution.py:284
  115.5 3.5 %collective-permute-start.24 = (bf16[3,512,256]{2,1,0:T(8,128)(2,1)S(1)}, bf16[3,512,256]{2,1,0:T(8,128)(2,1)}, u32[]{:S(2)}, u32[]{:S(2)}) collective-permute-start(bf16[3,512,256]{2,1,0:T(8,128)(2,1)S(1)} %collective-permute-done.21.refs_19_.refs_8_), channel_id=1, source_target_pairs={{0,4},{4,0},{8,12},{12,8},{16,20},{20,16},{24,28},{28,24},{1,5},{5... | collective-permute-start | bytes 2359304 | tf_op jit(solution)/shard_map/ppermute | solution.py:284
  116.0 4.2 %collective-permute-start.25 = (bf16[3,512,256]{2,1,0:T(8,128)(2,1)S(1)}, bf16[3,512,256]{2,1,0:T(8,128)(2,1)}, u32[]{:S(2)}, u32[]{:S(2)}) collective-permute-start(bf16[3,512,256]{2,1,0:T(8,128)(2,1)S(1)} %collective-permute-done.22.refs_20_.refs_9_), channel_id=1, source_target_pairs={{0,4},{4,0},{8,12},{12,8},{16,20},{20,16},{24,28},{28,24},{1,5},{5... | collective-permute-start | bytes 2359304 | tf_op jit(solution)/shard_map/ppermute | solution.py:284
  129.9 30.2 %all-to-all-start = ((bf16[8,2,256,256]{3,2,1,0:T(8,128)(2,1)}), bf16[8,2,256,256]{3,2,1,0:T(8,128)(2,1)S(1)}, u32[]{:S(2)}, u32[]{:S(2)}) async-start(bf16[8,2,256,256]{3,2,1,0:T(8,128)(2,1)} %bitcast.17), calls=%async_computation | async-start | bytes 4194304 | tf_op jit(solution)/shard_map/all_to_all | solution.py:408
  (24 other events, 270.3 us)
